TPU v7x, 128 devices: a whole 4x4x4 slice. The times are simulated.
128 devices in a mesh: section: 2 (over y_lo), tensor: 2 (over y_hi), wide: 32 (over x, z, core).
Axes of the slice: x: 4, y: 4 (y_hi: 2, y_lo: 2; y = y_hi * 2 + y_lo), z: 4, core: 2. Of those that a mesh axis runs over, the one named last changes fastest.
Arguments:
- x_in: bfloat16 [2, 4096, 1024], P(None, ('tensor', 'wide')), may hold values from -6 to 6
- out_cot: bfloat16 [2, 4096, 1024], P(None, ('tensor', 'wide')), may hold values from -6 to 6
- image_ids: int32 [2, 4096], replicated, may hold values from 0 to 2, as said below
- w_qkv: bfloat16 [2, 1024, 3, 1024], P('section', 'wide', None, 'tensor'), may hold values from -1 to 1, as said below
- w_out: bfloat16 [2, 1024, 1024], P('section', ('tensor', 'wide')), may hold values from -0.5 to 0.5
- w_fc1: bfloat16 [2, 1024, 4096], P('section', 'wide', 'tensor'), may hold values from -0.1875 to 0.1875
- w_fc2: bfloat16 [2, 4096, 1024], P('section', ('tensor', 'wide')), may hold values from -0.09375 to 0.09375
- gains: bfloat16 [2, 2, 1024], P('section', None, 'wide'), may hold values from 0.5 to 1.5
- shifts: bfloat16 [2, 4, 1024], P('section', None, 'wide'), may hold values from -1.5 to 1.5
- layer_scales: bfloat16 [2, 2, 1024], P('section', None, 'wide'), may hold values from 0.5 to 1.5
- qv_bias: bfloat16 [2, 2, 1024], P('section', None, ('tensor', 'wide')), may hold values from -1.5 to 1.5
- fc1_bias: bfloat16 [2, 4096], P('section', ('tensor', 'wide')), may hold values from -1.5 to 1.5
Outputs:
- section_outputs: bfloat16 [2, 2, 4096, 1024], P('section', None, ('tensor', 'wide'))
- input_grads: float32 [2, 2, 4096, 1024], P('section', None, ('tensor', 'wide'))
- g_w_qkv: float32 [2, 1024, 3, 1024], P('section', 'wide', None, 'tensor')
- g_w_out: float32 [2, 1024, 1024], P('section', ('tensor', 'wide'))
- g_w_fc1: float32 [2, 1024, 4096], P('section', 'wide', 'tensor')
- g_w_fc2: float32 [2, 4096, 1024], P('section', ('tensor', 'wide'))
- g_gains: float32 [2, 2, 1024], P('section', None, 'wide')
- g_shifts: float32 [2, 4, 1024], P('section', None, 'wide')
- g_layer_scales: float32 [2, 2, 1024], P('section', None, 'wide')
- g_qv_bias: float32 [2, 2, 1024], P('section', None, ('tensor', 'wide'))
- g_fc1_bias: float32 [2, 4096], P('section', ('tensor', 'wide'))
Inputs may be any that keep to these rules, and one draw needn't show every extreme that they name: `image_ids`: each micro-batch packs three images in order: image 0 ends and image 2 begins at boundaries that lie within 4096/12 tokens of 4096/3 and of 2 * 4096/3; image 1 lies between. `w_qkv`: projection weights of order 1024^-0.5.
All inputs are finite; a program needn't handle non-finite values.
Results may differ from a plain program's by a relative error of at most 0.035.
Values may be sent and summed in bfloat16 or wider, within the bound.
No kernel may reach another device: no remote copies, remote signals or barrier semaphores. Data moves between devices by JAX's collectives and lax.ppermute only.
A program may use at most 192 MiB of HBM per device.

v0:
```python
import jax
import jax.numpy as jnp
from jax import lax
from jax.sharding import PartitionSpec as P

HEAD = 64


EPS = 1e-06
NEG_FILL = -1e30
ROOT_HALF = 0.7071067811865476
INV_ROOT_TAU = 0.3989422804014327


def passed_along(block, axis, distance):
    devices = range(lax.axis_size(axis))
    route = [(i - distance, i) for i in devices if i - distance in devices]
    return lax.ppermute(block, axis, route)


def layer_norm(rows_in, gain_row, shift_row):
    centre = jnp.mean(rows_in, axis=-1, keepdims=True)
    centred = rows_in - centre
    spread = jnp.mean(centred * centred, axis=-1, keepdims=True)
    rstd_rows = lax.rsqrt(spread + EPS)
    normal_rows = centred * rstd_rows
    return (normal_rows * gain_row + shift_row, normal_rows, rstd_rows)


def norm_back(grad_rows, normal_rows, rstd_rows, gain_row):
    scaled = grad_rows * gain_row
    first_mean = jnp.mean(scaled, axis=-1, keepdims=True)
    second_mean = jnp.mean(scaled * normal_rows, axis=-1, keepdims=True)
    return rstd_rows * (scaled - first_mean - normal_rows * second_mean)


def gelu_value(pre_act):
    return 0.5 * pre_act * (1.0 + lax.erf(pre_act * ROOT_HALF))


def gelu_slope(pre_act):
    return (
        0.5 * (1.0 + lax.erf(pre_act * ROOT_HALF))
        + pre_act * jnp.exp(-0.5 * pre_act * pre_act) * INV_ROOT_TAU
    )


def add_all(totals, terms):
    return tuple((total_now + term_now for total_now, term_now in zip(totals, terms)))


def image_rows(image_ids, micro_idx, wide_idx, tensor_count, wide_count, rows_dev):
    row_ids = lax.dynamic_index_in_dim(image_ids, micro_idx, 0, keepdims=False)
    id_grid = row_ids.reshape(tensor_count, wide_count, rows_dev)
    query_ids = lax.dynamic_index_in_dim(id_grid, wide_idx, 1, keepdims=False).reshape(
        tensor_count * rows_dev
    )
    key_ids = jnp.transpose(id_grid, (1, 0, 2)).reshape(tensor_count * wide_count * rows_dev)
    return (query_ids, key_ids)


def gather_keys(qkv_rows):
    return (
        lax.all_gather(qkv_rows[:, 1], "wide", axis=0, tiled=True),
        lax.all_gather(qkv_rows[:, 2], "wide", axis=0, tiled=True),
    )


def key_blocks(key_rows, value_rows, key_ids, heads_dev):
    total_keys = key_rows.shape[0]
    block_keys = 1024
    count_blocks = total_keys // block_keys
    return (
        key_rows.reshape(count_blocks, block_keys, heads_dev, HEAD),
        value_rows.reshape(count_blocks, block_keys, heads_dev, HEAD),
        key_ids.reshape(count_blocks, block_keys),
    )


def block_scores(queries, key_part, same_image, score_scale):
    scores = (
        jnp.einsum("qhd,khd->hqk", queries, key_part, preferred_element_type=jnp.float32)
        * score_scale
    )
    return jnp.where(same_image[None], scores, NEG_FILL)


def attend_forward(queries, blocks, query_ids, score_scale):
    heads_dev = queries.shape[1]
    count_rows = queries.shape[0]

    def sum_step(carried, block_part):
        running_top, running_total = carried
        key_part, value_part, id_part = block_part
        scores = block_scores(
            queries, key_part, query_ids[:, None] == id_part[None, :], score_scale
        )
        new_top = jnp.maximum(running_top, jnp.max(scores, axis=-1))
        new_total = running_total * jnp.exp(running_top - new_top) + jnp.sum(
            jnp.exp(scores - new_top[..., None]), axis=-1
        )
        return ((new_top, new_total), None)

    start_top = jnp.full((heads_dev, count_rows), NEG_FILL, jnp.float32)
    (last_top, last_total), unused = lax.scan(
        sum_step, (start_top, jnp.zeros_like(start_top)), blocks
    )
    log_total = last_top + jnp.log(last_total)

    def out_step(running, block_part):
        key_part, value_part, id_part = block_part
        scores = block_scores(
            queries, key_part, query_ids[:, None] == id_part[None, :], score_scale
        )
        probability = jnp.exp(scores - log_total[..., None]).astype(jnp.bfloat16)
        return (
            running
            + jnp.einsum(
                "hqk,khd->qhd", probability, value_part, preferred_element_type=jnp.float32
            ),
            None,
        )

    mixture, unused = lax.scan(out_step, jnp.zeros(queries.shape, jnp.float32), blocks)
    return (mixture, log_total)


def attend_backward(queries, blocks, query_ids, log_total, delta_rows, grad_out, score_scale):

    def grad_step(running, block_part):
        key_part, value_part, id_part = block_part
        scores = block_scores(
            queries, key_part, query_ids[:, None] == id_part[None, :], score_scale
        )
        probability = jnp.exp(scores - log_total[..., None])
        grad_probs = jnp.einsum(
            "qhd,khd->hqk", grad_out, value_part, preferred_element_type=jnp.float32
        )
        grad_scores = (probability * (grad_probs - delta_rows[..., None])).astype(jnp.bfloat16)
        running = running + jnp.einsum(
            "hqk,khd->qhd", grad_scores, key_part, preferred_element_type=jnp.float32
        )
        grad_keys = jnp.einsum(
            "hqk,qhd->khd", grad_scores, queries, preferred_element_type=jnp.float32
        )
        grad_values = jnp.einsum(
            "hqk,qhd->khd",
            probability.astype(jnp.bfloat16),
            grad_out,
            preferred_element_type=jnp.float32,
        )
        return (running, (grad_keys, grad_values))

    grad_queries, key_terms = lax.scan(grad_step, jnp.zeros(queries.shape, jnp.float32), blocks)
    grad_keys, grad_values = key_terms
    head_width = queries.shape[1] * queries.shape[2]
    return (grad_queries, grad_keys.reshape(-1, head_width), grad_values.reshape(-1, head_width))


def layer_forward(layer_in, query_ids, key_ids, weight_set, score_scale):
    wqkv, wout, wone, wtwo, gain_rows, shift_rows, scale_rows, qv_rows, fc1_row = weight_set
    normed_a, hat_a, rstd_a = layer_norm(layer_in, gain_rows[0], shift_rows[0])
    attn_rows = lax.all_gather(normed_a.astype(jnp.bfloat16), "tensor", axis=0, tiled=True)
    count_rows = attn_rows.shape[0]
    head_width = wqkv.shape[2]
    heads_dev = head_width // HEAD
    bias_three = jnp.stack([qv_rows[0], jnp.zeros_like(qv_rows[0]), qv_rows[1]])
    qkv_rows = (
        jnp.einsum("rd,dcj->rcj", attn_rows, wqkv, preferred_element_type=jnp.float32) + bias_three
    ).astype(jnp.bfloat16)
    key_rows, value_rows = gather_keys(qkv_rows)
    queries = qkv_rows[:, 0].reshape(count_rows, heads_dev, HEAD)
    blocks = key_blocks(key_rows, value_rows, key_ids, heads_dev)
    attn_full, log_total = attend_forward(queries, blocks, query_ids, score_scale)
    attn_full = attn_full.reshape(count_rows, head_width)
    attn_low = attn_full.astype(jnp.bfloat16)
    proj_rows = lax.psum_scatter(
        jnp.dot(attn_low, wout, preferred_element_type=jnp.float32).astype(jnp.bfloat16),
        "tensor",
        scatter_dimension=0,
        tiled=True,
    ).astype(jnp.float32)
    branch_a = proj_rows + shift_rows[1]
    middle = layer_in + scale_rows[0] * branch_a
    normed_c, hat_c, rstd_c = layer_norm(middle, gain_rows[1], shift_rows[2])
    mlp_rows = lax.all_gather(normed_c.astype(jnp.bfloat16), "tensor", axis=0, tiled=True)
    pre_act = jnp.dot(mlp_rows, wone, preferred_element_type=jnp.float32) + fc1_row
    act_low = gelu_value(pre_act).astype(jnp.bfloat16)
    mlp_out = lax.psum_scatter(
        jnp.dot(act_low, wtwo, preferred_element_type=jnp.float32).astype(jnp.bfloat16),
        "tensor",
        scatter_dimension=0,
        tiled=True,
    ).astype(jnp.float32)
    branch_m = mlp_out + shift_rows[3]
    layer_out = middle + scale_rows[1] * branch_m
    kept = {
        "hat_a": hat_a,
        "rstd_a": rstd_a,
        "attn_rows": attn_rows,
        "qkv_rows": qkv_rows,
        "log_total": log_total,
        "attn_full": attn_full,
        "attn_low": attn_low,
        "branch_a": branch_a,
        "hat_c": hat_c,
        "rstd_c": rstd_c,
        "mlp_rows": mlp_rows,
        "pre_act": pre_act,
        "act_low": act_low,
        "branch_m": branch_m,
        "query_ids": query_ids,
        "key_ids": key_ids,
    }
    return (layer_out, kept)


def mlp_backward(grad_in, kept, weight_set):
    wqkv, wout, wone, wtwo, gain_rows, shift_rows, scale_rows, qv_rows, fc1_row = weight_set
    grad_m = grad_in * scale_rows[1]
    scale_term = jnp.sum(grad_in * kept["branch_m"], axis=0)
    bias_term = jnp.sum(grad_m, axis=0)
    grad_rows = lax.all_gather(grad_m.astype(jnp.bfloat16), "tensor", axis=0, tiled=True)
    term_two = jnp.einsum(
        "rf,rd->fd", kept["act_low"], grad_rows, preferred_element_type=jnp.float32
    )
    grad_act = jnp.einsum("rd,fd->rf", grad_rows, wtwo, preferred_element_type=jnp.float32)
    grad_pre = (grad_act * gelu_slope(kept["pre_act"])).astype(jnp.bfloat16)
    term_bias = jnp.sum(grad_pre.astype(jnp.float32), axis=0)
    term_one = jnp.einsum(
        "rd,rf->df", kept["mlp_rows"], grad_pre, preferred_element_type=jnp.float32
    )
    grad_norm = lax.psum_scatter(
        jnp.einsum("rf,df->rd", grad_pre, wone, preferred_element_type=jnp.float32).astype(
            jnp.bfloat16
        ),
        "tensor",
        scatter_dimension=0,
        tiled=True,
    ).astype(jnp.float32)
    gain_term = jnp.sum(grad_norm * kept["hat_c"], axis=0)
    shift_term = jnp.sum(grad_norm, axis=0)
    grad_mid = grad_in + norm_back(grad_norm, kept["hat_c"], kept["rstd_c"], gain_rows[1])
    return (
        grad_mid,
        (term_one, term_two, term_bias),
        (gain_term, shift_term, bias_term, scale_term),
    )


def attn_backward(grad_mid, kept, weight_set, score_scale, key_rows, value_rows):
    wqkv, wout, wone, wtwo, gain_rows, shift_rows, scale_rows, qv_rows, fc1_row = weight_set
    grad_a = grad_mid * scale_rows[0]
    scale_term = jnp.sum(grad_mid * kept["branch_a"], axis=0)
    bias_term = jnp.sum(grad_a, axis=0)
    grad_rows = lax.all_gather(grad_a.astype(jnp.bfloat16), "tensor", axis=0, tiled=True)
    term_out = jnp.einsum(
        "rj,rd->jd", kept["attn_low"], grad_rows, preferred_element_type=jnp.float32
    )
    grad_attn = jnp.einsum("rd,jd->rj", grad_rows, wout, preferred_element_type=jnp.float32).astype(
        jnp.bfloat16
    )
    count_rows = grad_attn.shape[0]
    head_width = grad_attn.shape[1]
    heads_dev = head_width // HEAD
    delta_rows = jnp.sum(
        (grad_attn.astype(jnp.float32) * kept["attn_full"]).reshape(count_rows, heads_dev, HEAD),
        axis=-1,
    ).T
    queries = kept["qkv_rows"][:, 0].reshape(count_rows, heads_dev, HEAD)
    grad_heads = grad_attn.reshape(count_rows, heads_dev, HEAD)
    blocks = key_blocks(key_rows, value_rows, kept["key_ids"], heads_dev)
    grad_q, grad_k, grad_v = attend_backward(
        queries, blocks, kept["query_ids"], kept["log_total"], delta_rows, grad_heads, score_scale
    )
    own_k, own_v = (
        lax.psum_scatter(
            (grad_k * score_scale).astype(jnp.bfloat16), "wide", scatter_dimension=0, tiled=True
        ).astype(jnp.float32),
        lax.psum_scatter(
            grad_v.astype(jnp.bfloat16), "wide", scatter_dimension=0, tiled=True
        ).astype(jnp.float32),
    )
    grad_qkv = jnp.stack(
        [
            (grad_q * score_scale).reshape(count_rows, head_width).astype(jnp.bfloat16),
            own_k.astype(jnp.bfloat16),
            own_v.astype(jnp.bfloat16),
        ],
        axis=1,
    )
    bias_qv = jnp.stack(
        [
            jnp.sum(grad_qkv[:, 0].astype(jnp.float32), axis=0),
            jnp.sum(grad_qkv[:, 2].astype(jnp.float32), axis=0),
        ]
    )
    term_qkv = jnp.einsum(
        "rd,rcj->dcj", kept["attn_rows"], grad_qkv, preferred_element_type=jnp.float32
    )
    grad_norm = lax.psum_scatter(
        jnp.einsum("rcj,dcj->rd", grad_qkv, wqkv, preferred_element_type=jnp.float32).astype(
            jnp.bfloat16
        ),
        "tensor",
        scatter_dimension=0,
        tiled=True,
    ).astype(jnp.float32)
    gain_term = jnp.sum(grad_norm * kept["hat_a"], axis=0)
    shift_term = jnp.sum(grad_norm, axis=0)
    grad_x = grad_mid + norm_back(grad_norm, kept["hat_a"], kept["rstd_a"], gain_rows[0])
    return (grad_x, (term_qkv, term_out, bias_qv), (gain_term, shift_term, bias_term, scale_term))


def body(
    x_in,
    out_cot,
    image_ids,
    w_qkv,
    w_out,
    w_fc1,
    w_fc2,
    gains,
    shifts,
    layer_scales,
    qv_bias,
    fc1_bias,
):
    tensor_count = lax.axis_size("tensor")
    wide_count = lax.axis_size("wide")
    section_idx = lax.axis_index("section")
    wide_idx = lax.axis_index("wide")
    micro_count = x_in.shape[0]
    rows_dev = x_in.shape[1]
    model_width = x_in.shape[2]
    gathered = (
        lax.all_gather(w_qkv[0], "wide", axis=0, tiled=True),
        lax.all_gather(w_out[0], "wide", axis=0, tiled=True),
        lax.all_gather(w_fc1[0], "wide", axis=0, tiled=True),
        lax.all_gather(w_fc2[0], "wide", axis=0, tiled=True),
        lax.all_gather(gains[0], "wide", axis=1, tiled=True),
        lax.all_gather(shifts[0], "wide", axis=1, tiled=True),
        lax.all_gather(layer_scales[0], "wide", axis=1, tiled=True),
        lax.all_gather(qv_bias[0], "wide", axis=1, tiled=True),
        lax.all_gather(fc1_bias[0], "wide", axis=0, tiled=True),
    )
    weight_set = gathered[:4] + tuple((small_arr.astype(jnp.float32) for small_arr in gathered[4:]))
    score_scale = HEAD ** (-0.5)
    sent_rows = jnp.zeros((rows_dev, model_width), jnp.bfloat16)
    layer_outs = []
    kept_all = []
    for step_fwd in range(micro_count + 1):
        micro_idx = jnp.clip(step_fwd - section_idx, 0, micro_count - 1)
        own_input = x_in[min(step_fwd, micro_count - 1)]
        layer_in = jnp.where(section_idx == 0, own_input, sent_rows).astype(jnp.float32)
        query_ids, key_ids = image_rows(
            image_ids, micro_idx, wide_idx, tensor_count, wide_count, rows_dev
        )
        layer_out, kept = layer_forward(layer_in, query_ids, key_ids, weight_set, score_scale)
        out_low = layer_out.astype(jnp.bfloat16)
        layer_outs.append(out_low)
        kept_all.append(kept)
        if step_fwd < micro_count:
            sent_rows = passed_along(out_low, "section", 1)
    section_outputs = lax.dynamic_slice_in_dim(jnp.stack(layer_outs), section_idx, micro_count, 0)[
        None
    ]
    head_width = weight_set[0].shape[2]
    hidden_dev = weight_set[2].shape[1]
    mlp_sums = (
        jnp.zeros((model_width, hidden_dev), jnp.float32),
        jnp.zeros((hidden_dev, model_width), jnp.float32),
        jnp.zeros((hidden_dev,), jnp.float32),
    )
    attn_sums = (
        jnp.zeros((model_width, 3, head_width), jnp.float32),
        jnp.zeros((head_width, model_width), jnp.float32),
        jnp.zeros((2, head_width), jnp.float32),
    )
    mlp_vectors = tuple((jnp.zeros((model_width,), jnp.float32) for unused in range(4)))
    attn_vectors = tuple((jnp.zeros((model_width,), jnp.float32) for unused in range(4)))
    back_rows = jnp.zeros((rows_dev, model_width), jnp.bfloat16)
    input_list = []
    for step_back in range(micro_count + 1):
        micro_idx = micro_count - step_back - section_idx
        in_range = (micro_idx >= 0) & (micro_idx < micro_count)
        own_cot = out_cot[max(micro_count - 1 - step_back, 0)]
        grad_in = jnp.where(section_idx == 1, own_cot, back_rows).astype(jnp.float32)
        grad_in = jnp.where(in_range, grad_in, 0.0)
        kept = kept_all[micro_count - step_back]
        grad_mid, mlp_terms, mlp_vec = mlp_backward(grad_in, kept, weight_set)
        mlp_sums = add_all(mlp_sums, mlp_terms)
        mlp_vectors = add_all(mlp_vectors, mlp_vec)
        key_rows, value_rows = gather_keys(kept["qkv_rows"])
        grad_x, attn_terms, attn_vec = attn_backward(
            grad_mid, kept, weight_set, score_scale, key_rows, value_rows
        )
        attn_sums = add_all(attn_sums, attn_terms)
        attn_vectors = add_all(attn_vectors, attn_vec)
        input_list.append(grad_x)
        if step_back < micro_count:
            back_rows = passed_along(grad_x.astype(jnp.bfloat16), "section", -1)
    input_grads = lax.dynamic_slice_in_dim(
        jnp.stack(input_list[::-1]), section_idx, micro_count, 0
    )[None]
    gain_grad = jnp.stack([attn_vectors[0], mlp_vectors[0]])
    shift_grad = jnp.stack([attn_vectors[1], attn_vectors[2], mlp_vectors[1], mlp_vectors[2]])
    scale_grad = jnp.stack([attn_vectors[3], mlp_vectors[3]])
    gain_grad, shift_grad, scale_grad = (
        lax.psum(gain_grad.astype(jnp.bfloat16), "tensor").astype(jnp.float32),
        lax.psum(shift_grad.astype(jnp.bfloat16), "tensor").astype(jnp.float32),
        lax.psum(scale_grad.astype(jnp.bfloat16), "tensor").astype(jnp.float32),
    )
    summed = (
        lax.psum_scatter(
            attn_sums[0].astype(jnp.bfloat16), "wide", scatter_dimension=0, tiled=True
        ).astype(jnp.float32),
        lax.psum_scatter(
            attn_sums[1].astype(jnp.bfloat16), "wide", scatter_dimension=0, tiled=True
        ).astype(jnp.float32),
        lax.psum_scatter(
            mlp_sums[0].astype(jnp.bfloat16), "wide", scatter_dimension=0, tiled=True
        ).astype(jnp.float32),
        lax.psum_scatter(
            mlp_sums[1].astype(jnp.bfloat16), "wide", scatter_dimension=0, tiled=True
        ).astype(jnp.float32),
        lax.psum_scatter(
            mlp_sums[2].astype(jnp.bfloat16), "wide", scatter_dimension=0, tiled=True
        ).astype(jnp.float32),
        lax.psum_scatter(
            attn_sums[2].T.astype(jnp.bfloat16), "wide", scatter_dimension=0, tiled=True
        ).astype(jnp.float32),
        lax.psum_scatter(
            gain_grad.T.astype(jnp.bfloat16), "wide", scatter_dimension=0, tiled=True
        ).astype(jnp.float32),
        lax.psum_scatter(
            shift_grad.T.astype(jnp.bfloat16), "wide", scatter_dimension=0, tiled=True
        ).astype(jnp.float32),
        lax.psum_scatter(
            scale_grad.T.astype(jnp.bfloat16), "wide", scatter_dimension=0, tiled=True
        ).astype(jnp.float32),
    )
    return (
        section_outputs,
        input_grads,
        summed[0][None],
        summed[1][None],
        summed[2][None],
        summed[3][None],
        summed[6].T[None],
        summed[7].T[None],
        summed[8].T[None],
        summed[5].T[None],
        summed[4][None],
    )


def solution(mesh):
    in_specs = (
        P(None, ("tensor", "wide"), None),
        P(None, ("tensor", "wide"), None),
        P(),
        P("section", "wide", None, "tensor"),
        P("section", ("tensor", "wide"), None),
        P("section", "wide", "tensor"),
        P("section", ("tensor", "wide"), None),
        P("section", None, "wide"),
        P("section", None, "wide"),
        P("section", None, "wide"),
        P("section", None, ("tensor", "wide")),
        P("section", ("tensor", "wide")),
    )
    out_specs = (
        P("section", None, ("tensor", "wide"), None),
        P("section", None, ("tensor", "wide"), None),
        P("section", "wide", None, "tensor"),
        P("section", ("tensor", "wide"), None),
        P("section", "wide", "tensor"),
        P("section", ("tensor", "wide"), None),
        P("section", None, "wide"),
        P("section", None, "wide"),
        P("section", None, "wide"),
        P("section", None, ("tensor", "wide")),
        P("section", ("tensor", "wide")),
    )
    return jax.shard_map(body, mesh=mesh, in_specs=in_specs, out_specs=out_specs, check_vma=False)
```

profile of v0, /device:TPU:0, one launch (start us, length us, event | category | flops | bytes accessed | tf_op | source)
XLA Modules:
  0.0 2479.1 jit_solution(15132927794652367660)
XLA Ops:
  8.8 26.3 %all-gather.2 = bf16[1,4,1024]{1,0,2:T(2,128)(2,1)S(1)} all-gather(bf16[1,4,32]{1,0,2:T(2,128)(2,1)S(1)} %copy.269), channel_id=4, replica_groups=mesh['section'=2,'tensor'=2,'wide'=32] {'wide'}, dimensions={2}, use_global_device_ids=true | all-gather | bytes 8448 | tf_op jit(solution)/shard_map/all_gather | solution.py:342
  36.4 24.2 all-gather.1
  61.8 22.8 all-gather.4
  92.6 22.9 slice_reduce_fusion
  133.1 43.0 %all-gather.28.cloned.1.call-done = bf16[4096,1,512]{2,0,1:T(8,128)(2,1)} async-done(((bf16[128,1,512]{2,0,1:T(8,128)(2,1)}), bf16[4096,1,512]{2,0,1:T(8,128)(2,1)}) %all-gather.28.cloned.1.call-update) | async-done | bytes 4194320 | tf_op jit(solution)/shard_map/all_gather | solution.py:65
  197.2 27.4 %all-gather.30.cloned.1.call-done = bf16[4096,1,512]{2,0,1:T(8,128)(2,1)} async-done(((bf16[128,1,512]{2,0,1:T(8,128)(2,1)}), bf16[4096,1,512]{2,0,1:T(8,128)(2,1)}) %all-gather.30.cloned.1.call-update) | async-done | bytes 4194320 | tf_op jit(solution)/shard_map/all_gather | solution.py:64
  245.7 30.0 %while.126 = (s32[]{:T(128)}, f32[8,128]{1,0:T(8,128)S(1)}, f32[8,128]{1,0:T(8,128)S(1)}, s32[2,64]{1,0:T(2,128)}, s32[4,1024]{1,0:T(4,128)S(1)}, /*index=5*/bf1...) while((s32[]{:T(128)}, f32[8,128]{1,0:T(8,128)S(1)}, ...), condition=%wide.wide.region_5.6_spmd.clone, body=%wide.wide.region_2.5_spmd.clone.sunk | while | flops 141693952 | bytes 10027648 | solution.py:105
  293.6 24.1 all-gather
  319.8 65.7 %all-reduce = bf16[2048]{0:T(1024)(128)(2,1)S(1)} all-reduce(bf16[2048]{0:T(1024)(128)(2,1)S(1)} %dynamic-update-slice), channel_id=11, replica_groups=mesh['section'=2,'tensor'=2,'wide'=32] {'wide'}, use_global_device_ids=true, to_apply=%add | all-reduce | flops 2048 | bytes 8192
  443.0 45.7 %all-gather.38.cloned.1.call-done = bf16[4096,1,512]{2,0,1:T(8,128)(2,1)} async-done(((bf16[128,1,512]{2,0,1:T(8,128)(2,1)}), bf16[4096,1,512]{2,0,1:T(8,128)(2,1)}) %all-gather.38.cloned.1.call-update) | async-done | bytes 4194320 | tf_op jit(solution)/shard_map/all_gather | solution.py:65
  509.7 27.3 %all-gather.40.cloned.1.call-done = bf16[4096,1,512]{2,0,1:T(8,128)(2,1)} async-done(((bf16[128,1,512]{2,0,1:T(8,128)(2,1)}), bf16[4096,1,512]{2,0,1:T(8,128)(2,1)}) %all-gather.40.cloned.1.call-update) | async-done | bytes 4194320 | tf_op jit(solution)/shard_map/all_gather | solution.py:64
  558.0 33.3 %while.128 = (s32[]{:T(128)}, f32[8,128]{1,0:T(8,128)S(1)}, f32[8,128]{1,0:T(8,128)S(1)}, s32[2,64]{1,0:T(2,128)}, s32[4,1024]{1,0:T(4,128)}, /*index=5*/bf16[4,...) while((s32[]{:T(128)}, f32[8,128]{1,0:T(8,128)S(1)}, ...), condition=%wide.wide.region_17.18_spmd.clone, body=%wide.wide.region_14.17_spmd.clone.sunk | while | flops 141693952 | bytes 10027648 | solution.py:105
  675.5 46.5 %all-gather.42.cloned.1.call-done = bf16[4096,1,512]{2,0,1:T(8,128)(2,1)} async-done(((bf16[128,1,512]{2,0,1:T(8,128)(2,1)}), bf16[4096,1,512]{2,0,1:T(8,128)(2,1)}) %all-gather.42.cloned.1.call-update) | async-done | bytes 4194320 | tf_op jit(solution)/shard_map/all_gather | solution.py:65
  743.0 27.4 %all-gather.44.cloned.1.call-done = bf16[4096,1,512]{2,0,1:T(8,128)(2,1)} async-done(((bf16[128,1,512]{2,0,1:T(8,128)(2,1)}), bf16[4096,1,512]{2,0,1:T(8,128)(2,1)}) %all-gather.44.cloned.1.call-update) | async-done | bytes 4194320 | tf_op jit(solution)/shard_map/all_gather | solution.py:64
  791.3 30.4 %while.130 = (s32[]{:T(128)}, f32[8,128]{1,0:T(8,128)S(1)}, f32[8,128]{1,0:T(8,128)S(1)}, s32[2,64]{1,0:T(2,128)}, s32[4,1024]{1,0:T(4,128)S(1)}, /*index=5*/bf1...) while((s32[]{:T(128)}, f32[8,128]{1,0:T(8,128)S(1)}, ...), condition=%wide.wide.region_29.30_spmd.clone, body=%wide.wide.region_26.29_spmd.clone.sunk | while | flops 141693952 | bytes 10027648 | solution.py:105
  920.9 54.8 %while.132 = (s32[]{:T(128)}, f32[128,8,64]{0,2,1:T(8,128)}, f32[4,1024,8,64]{1,3,2,0:T(8,128)}, bf16[4,1024,8,64]{1,3,2,0:T(8,128)(2,1)}, bf16[4,1024,8,64]{1,3...) while((s32[]{:T(128)}, f32[128,8,64]{0,2,1:T(8,128)}, ...), condition=%wide.wide.region_41.42_spmd.clone, body=%wide.wide.region_40.41_spmd.clone.sunk | while | flops 681836544 | bytes 63384536 | solution.py:154
  1028.2 51.0 %reduce-scatter.51.cloned.1.call-done = bf16[128,512]{1,0:T(8,128)(2,1)} async-done(((bf16[4096,512]{1,0:T(8,128)(2,1)}), bf16[128,512]{1,0:T(8,128)(2,1)}) %reduce-scatter.51.cloned.1.call-update) | async-done | bytes 131088 | tf_op jit(solution)/shard_map/reduce_scatter | solution.py:280
  1079.1 84.9 %reduce-scatter.49.cloned.1.call-done = bf16[128,512]{1,0:T(8,128)(2,1)} async-done(((bf16[4096,512]{1,0:T(8,128)(2,1)}), bf16[128,512]{1,0:T(8,128)(2,1)}) %reduce-scatter.49.cloned.1.call-update) | async-done | bytes 131088 | tf_op jit(solution)/shard_map/reduce_scatter | solution.py:277
  1241.2 54.5 %while.133 = (s32[]{:T(128)}, f32[128,8,64]{0,2,1:T(8,128)}, f32[4,1024,8,64]{1,3,2,0:T(8,128)}, bf16[4,1024,8,64]{1,3,2,0:T(8,128)(2,1)}, bf16[4,1024,8,64]{1,3...) while((s32[]{:T(128)}, f32[128,8,64]{0,2,1:T(8,128)}, ...), condition=%wide.wide.region_52.53_spmd.clone, body=%wide.wide.region_51.52_spmd.clone.sunk | while | flops 681836544 | bytes 62337972 | solution.py:154
  1348.5 50.8 %reduce-scatter.59.cloned.1.call-done = bf16[128,512]{1,0:T(8,128)(2,1)} async-done(((bf16[4096,512]{1,0:T(8,128)(2,1)}), bf16[128,512]{1,0:T(8,128)(2,1)}) %reduce-scatter.59.cloned.1.call-update) | async-done | bytes 131088 | tf_op jit(solution)/shard_map/reduce_scatter | solution.py:280
  1399.3 85.0 %reduce-scatter.57.cloned.1.call-done = bf16[128,512]{1,0:T(8,128)(2,1)} async-done(((bf16[4096,512]{1,0:T(8,128)(2,1)}), bf16[128,512]{1,0:T(8,128)(2,1)}) %reduce-scatter.57.cloned.1.call-update) | async-done | bytes 131088 | tf_op jit(solution)/shard_map/reduce_scatter | solution.py:277
  1561.7 51.4 %while.134 = (s32[]{:T(128)}, f32[128,8,64]{0,2,1:T(8,128)S(1)}, f32[4,1024,8,64]{1,3,2,0:T(8,128)}, bf16[4,1024,8,64]{1,3,2,0:T(8,128)(2,1)}, bf16[4,1024,8,64]...) while((s32[]{:T(128)}, f32[128,8,64]{0,2,1:T(8,128)S(1)}, ...), condition=%wide.wide.region_63.64_spmd.clone, body=%wide.wide.region_62.63_spmd.clone.sunk | while | flops 681836544 | bytes 61240104 | solution.py:154
  1672.0 44.6 %reduce-scatter.67.cloned.1.call-done = bf16[128,512]{1,0:T(8,128)(2,1)} async-done(((bf16[4096,512]{1,0:T(8,128)(2,1)}), bf16[128,512]{1,0:T(8,128)(2,1)}) %reduce-scatter.67.cloned.1.call-update) | async-done | bytes 131088 | tf_op jit(solution)/shard_map/reduce_scatter | solution.py:280
  1716.6 84.8 %reduce-scatter.65.cloned.1.call-done = bf16[128,512]{1,0:T(8,128)(2,1)} async-done(((bf16[4096,512]{1,0:T(8,128)(2,1)}), bf16[128,512]{1,0:T(8,128)(2,1)}) %reduce-scatter.65.cloned.1.call-update) | async-done | bytes 131088 | tf_op jit(solution)/shard_map/reduce_scatter | solution.py:277
  1845.8 63.2 %all-reduce.1 = bf16[2048]{0:T(1024)(128)(2,1)S(1)} all-reduce(bf16[2048]{0:T(1024)(128)(2,1)S(1)} %add_convert_fusion.10), channel_id=43, replica_groups=mesh['section'=2,'tensor'=2,'wide'=32] {'wide'}, use_global_device_ids=true, to_apply=%region_113.114.clone | all-reduce | flops 2048 | bytes 8192
  1910.4 69.1 %reduce-scatter.73.cloned.1.call-done = bf16[16,1024]{1,0:T(8,128)(2,1)} async-done(((bf16[512,1024]{1,0:T(8,128)(2,1)}), bf16[16,1024]{1,0:T(8,128)(2,1)}) %reduce-scatter.73.cloned.1.call-update) | async-done | bytes 32784 | tf_op jit(solution)/shard_map/reduce_scatter | solution.py:418
  1980.9 84.1 %reduce-scatter.77.cloned.1.call-done = bf16[64,1024]{1,0:T(8,128)(2,1)} async-done(((bf16[2048,1024]{1,0:T(8,128)(2,1)}), bf16[64,1024]{1,0:T(8,128)(2,1)}) %reduce-scatter.77.cloned.1.call-update) | async-done | bytes 131088 | tf_op jit(solution)/shard_map/reduce_scatter | solution.py:424
  2066.6 83.3 %reduce-scatter.75.cloned.1.call-done = bf16[32,2048]{1,0:T(8,128)(2,1)} async-done(((bf16[1024,2048]{1,0:T(8,128)(2,1)}), bf16[32,2048]{1,0:T(8,128)(2,1)}) %reduce-scatter.75.cloned.1.call-update) | async-done | bytes 131088 | tf_op jit(solution)/shard_map/reduce_scatter | solution.py:421
  2151.6 75.2 %reduce-scatter.79.cloned.1.call-done = bf16[16,2]{1,0:T(8,128)(2,1)} async-done(((bf16[512,2]{1,0:T(8,128)(2,1)}), bf16[16,2]{1,0:T(8,128)(2,1)}) %reduce-scatter.79.cloned.1.call-update) | async-done | bytes 80
  2229.1 77.7 %reduce-scatter.81.cloned.1.call-done = bf16[32,2]{1,0:T(8,128)(2,1)} async-done(((bf16[1024,2]{1,0:T(8,128)(2,1)}), bf16[32,2]{1,0:T(8,128)(2,1)}) %reduce-scatter.81.cloned.1.call-update) | async-done | bytes 144
  2307.6 79.3 %reduce-scatter.83.cloned.1.call-done = bf16[32,4]{1,0:T(8,128)(2,1)} async-done(((bf16[1024,4]{1,0:T(8,128)(2,1)}), bf16[32,4]{1,0:T(8,128)(2,1)}) %reduce-scatter.83.cloned.1.call-update) | async-done | bytes 272
  2395.8 74.8 %reduce-scatter.71.cloned.1.call-done = bf16[32,3,512]{2,0,1:T(8,128)(2,1)} async-done(((bf16[1024,3,512]{2,0,1:T(8,128)(2,1)}), bf16[32,3,512]{2,0,1:T(8,128)(2,1)}) %reduce-scatter.71.cloned.1.call-update) | async-done | bytes 98320 | tf_op jit(solution)/shard_map/reduce_scatter | solution.py:415
  (1084 shorter events, 1092.0 us)
Async XLA Ops:
  7.2 119.4 %all-gather.26.cloned.1.call-start = ((), (), s32[]{:S(2)}) async-start(), calls=%async_computation.48 | async-start | bytes 3244032 | tf_op jit(solution)/shard_map/all_gather | solution.py:337
  7.9 168.1 %all-gather.28.cloned.1.call-start = ((), (), s32[]{:S(2)}) async-start(), calls=%async_computation.49 | async-start | bytes 4325376 | tf_op jit(solution)/shard_map/all_gather | solution.py:65
  130.4 94.2 %all-gather.30.cloned.1.call-start = ((), (), s32[]{:S(2)}) async-start(), calls=%async_computation.50 | async-start | bytes 4325376 | tf_op jit(solution)/shard_map/all_gather | solution.py:64
  131.2 158.5 %all-gather.32.cloned.1.call-start = ((), (), s32[]{:S(2)}) async-start(), calls=%async_computation.51 | async-start | bytes 1081344 | tf_op jit(solution)/shard_map/all_gather | solution.py:338
  131.7 260.0 %reduce-scatter.35.cloned.1.call-start = ((), (), s32[]{:S(2)}) async-start(), calls=%async_computation.26 | async-start | bytes 393216 | tf_op jit(solution)/shard_map/reduce_scatter | solution.py:177
  292.1 110.1 %all-gather.34.cloned.1.call-start = ((), (), s32[]{:S(2)}) async-start(), calls=%async_computation.52 | async-start | bytes 4325376 | tf_op jit(solution)/shard_map/all_gather | solution.py:339
  292.7 114.2 %all-gather.36.cloned.1.call-start = ((), (), s32[]{:S(2)}) async-start(), calls=%async_computation.53 | async-start | bytes 4325376 | tf_op jit(solution)/shard_map/all_gather | solution.py:340
  293.4 129.7 %reduce-scatter.37.cloned.1.call-start = ((), (), s32[]{:S(2)}) async-start(), calls=%async_computation.27 | async-start | bytes 393216 | tf_op jit(solution)/shard_map/reduce_scatter | solution.py:189
  411.0 77.6 %all-gather.38.cloned.1.call-start = ((), (), s32[]{:S(2)}) async-start(), calls=%async_computation.54 | async-start | bytes 4325376 | tf_op jit(solution)/shard_map/all_gather | solution.py:65
  440.8 96.3 %all-gather.40.cloned.1.call-start = ((), (), s32[]{:S(2)}) async-start(), calls=%async_computation.55 | async-start | bytes 4325376 | tf_op jit(solution)/shard_map/all_gather | solution.py:64
  441.4 183.1 %reduce-scatter.39.cloned.1.call-start = ((), (), s32[]{:S(2)}) async-start(), calls=%async_computation.28 | async-start | bytes 393216 | tf_op jit(solution)/shard_map/reduce_scatter | solution.py:177
  641.6 80.4 %all-gather.42.cloned.1.call-start = ((), (), s32[]{:S(2)}) async-start(), calls=%async_computation.56 | async-start | bytes 4325376 | tf_op jit(solution)/shard_map/all_gather | solution.py:65
  674.1 96.2 %all-gather.44.cloned.1.call-start = ((), (), s32[]{:S(2)}) async-start(), calls=%async_computation.57 | async-start | bytes 4325376 | tf_op jit(solution)/shard_map/all_gather | solution.py:64
  674.7 177.2 %reduce-scatter.43.cloned.1.call-start = ((), (), s32[]{:S(2)}) async-start(), calls=%async_computation.30 | async-start | bytes 393216 | tf_op jit(solution)/shard_map/reduce_scatter | solution.py:177
  879.8 199.3 %reduce-scatter.51.cloned.1.call-start = ((), (), s32[]{:S(2)}) async-start(), calls=%async_computation.34 | async-start | bytes 4325376 | tf_op jit(solution)/shard_map/reduce_scatter | solution.py:280
  997.5 166.6 %reduce-scatter.49.cloned.1.call-start = ((), (), s32[]{:S(2)}) async-start(), calls=%async_computation.33 | async-start | bytes 4325376 | tf_op jit(solution)/shard_map/reduce_scatter | solution.py:277
  1026.4 156.7 %reduce-scatter.53.cloned.1.call-start = ((), (), s32[]{:S(2)}) async-start(), calls=%async_computation.35 | async-start | bytes 393216 | tf_op jit(solution)/shard_map/reduce_scatter | solution.py:301
  1208.7 190.6 %reduce-scatter.59.cloned.1.call-start = ((), (), s32[]{:S(2)}) async-start(), calls=%async_computation.38 | async-start | bytes 4325376 | tf_op jit(solution)/shard_map/reduce_scatter | solution.py:280
  1317.6 166.7 %reduce-scatter.57.cloned.1.call-start = ((), (), s32[]{:S(2)}) async-start(), calls=%async_computation.37 | async-start | bytes 4325376 | tf_op jit(solution)/shard_map/reduce_scatter | solution.py:277
  1346.8 156.6 %reduce-scatter.61.cloned.1.call-start = ((), (), s32[]{:S(2)}) async-start(), calls=%async_computation.39 | async-start | bytes 393216 | tf_op jit(solution)/shard_map/reduce_scatter | solution.py:301
  1488.2 56.8 %reduce-scatter.63.cloned.1.call-start = ((), (), s32[]{:S(2)}) async-start(), calls=%async_computation.40 | async-start | bytes 393216 | tf_op jit(solution)/shard_map/reduce_scatter | solution.py:233
  1530.3 186.3 %reduce-scatter.67.cloned.1.call-start = ((), (), s32[]{:S(2)}) async-start(), calls=%async_computation.42 | async-start | bytes 4325376 | tf_op jit(solution)/shard_map/reduce_scatter | solution.py:280
  1635.0 166.4 %reduce-scatter.65.cloned.1.call-start = ((), (), s32[]{:S(2)}) async-start(), calls=%async_computation.41 | async-start | bytes 4325376 | tf_op jit(solution)/shard_map/reduce_scatter | solution.py:277
  1663.9 169.5 %reduce-scatter.69.cloned.1.call-start = ((), (), s32[]{:S(2)}) async-start(), calls=%async_computation.43 | async-start | bytes 393216 | tf_op jit(solution)/shard_map/reduce_scatter | solution.py:301
  1804.2 105.4 %reduce-scatter.85.cloned.1.call-start = ((), (), s32[]{:S(2)}) async-start(), calls=%async_computation.61 | async-start | bytes 270336
  1806.8 172.7 %reduce-scatter.73.cloned.1.call-start = ((), (), s32[]{:S(2)}) async-start(), calls=%async_computation.45 | async-start | bytes 1081344 | tf_op jit(solution)/shard_map/reduce_scatter | solution.py:418
  1811.0 253.9 %reduce-scatter.77.cloned.1.call-start = ((), (), s32[]{:S(2)}) async-start(), calls=%async_computation.47 | async-start | bytes 4325376 | tf_op jit(solution)/shard_map/reduce_scatter | solution.py:424
  1816.6 333.3 %reduce-scatter.75.cloned.1.call-start = ((), (), s32[]{:S(2)}) async-start(), calls=%async_computation.46 | async-start | bytes 4325376 | tf_op jit(solution)/shard_map/reduce_scatter | solution.py:421
  1823.6 403.1 %reduce-scatter.79.cloned.1.call-start = ((), (), s32[]{:S(2)}) async-start(), calls=%async_computation.58 | async-start | bytes 135168
  1833.4 473.4 %reduce-scatter.81.cloned.1.call-start = ((), (), s32[]{:S(2)}) async-start(), calls=%async_computation.59 | async-start | bytes 270336
  1835.6 551.3 %reduce-scatter.83.cloned.1.call-start = ((), (), s32[]{:S(2)}) async-start(), calls=%async_computation.60 | async-start | bytes 270336
  1836.7 633.9 %reduce-scatter.71.cloned.1.call-start = ((), (), s32[]{:S(2)}) async-start(), calls=%async_computation.44 | async-start | bytes 3244032 | tf_op jit(solution)/shard_map/reduce_scatter | solution.py:415
  (268 other events, 7393.5 us)
Sparse Core Ops, SparseCore 0:
  10.4 48.3 all-gather.25
  130.6 45.4 all-gather.27
  178.9 45.6 all-gather.29
  226.8 42.1 all-gather.31
  292.2 14.9 reduce-scatter.34
  309.6 45.7 all-gather.33
  358.0 45.7 all-gather.35
  440.9 47.7 all-gather.37
  491.3 45.6 all-gather.39
  609.4 15.0 reduce-scatter.38
  641.7 15.1 reduce-scatter.40
  674.3 47.6 all-gather.41
  724.7 45.6 all-gather.43
  836.9 15.0 reduce-scatter.42
  871.4 15.1 reduce-scatter.46
  889.3 15.0 reduce-scatter.44
  997.6 81.4 reduce-scatter.50
  1082.8 81.2 reduce-scatter.48
  1168.1 14.9 reduce-scatter.52
  1317.7 81.5 reduce-scatter.58
  1402.9 81.3 reduce-scatter.56
  1488.3 14.9 reduce-scatter.60
  1635.1 81.4 reduce-scatter.66
  1720.1 81.2 reduce-scatter.64
  1822.8 76.3 reduce-scatter.84
  1902.6 76.8 reduce-scatter.72
  1983.6 81.3 reduce-scatter.76
  2068.6 81.2 reduce-scatter.74
  2154.2 72.4 reduce-scatter.78
  2230.5 76.2 reduce-scatter.80
  2310.6 76.2 reduce-scatter.82
  2390.8 79.7 reduce-scatter.70
  (4 shorter events, 55.7 us)
where the time goes:
time: 2490 us; the launch traced here: 2480 us
  waiting for transfers between devices  1310 us (53%)
  local copies, waits for them, and re-layouts  365 us (15%)
  matrix products  333 us (13%)
  blocking collectives  322 us (13%)
  other arithmetic  120 us (5%)
    reduce_scatter x3, waiting for transfers between devices, attn_backward(): lax.psum_scatter((grad_k * score_scale).astype(jnp.bfloat16), 'wide', sca...  255 us
    unnamed x40, waiting for transfers between devices  237 us
    reduce_scatter x3, waiting for transfers between devices, attn_backward(): lax.psum_scatter(grad_v.astype(jnp.bfloat16), 'wide', scatter_dimension=0...  146 us
    all_gather x3, waiting for transfers between devices, gather_keys(): lax.all_gather(qkv_rows[:, 2], 'wide', axis=0, tiled=True)  135 us
    unnamed x2, blocking collectives  129 us
    unnamed x359, local copies, waits for them, and re-layouts  87.6 us
    reduce_scatter x1, waiting for transfers between devices, body(): lax.psum_scatter(mlp_sums[1].astype(jnp.bfloat16), 'wide', scatter_dimens...  84.1 us
    reduce_scatter x1, waiting for transfers between devices, body(): lax.psum_scatter(mlp_sums[0].astype(jnp.bfloat16), 'wide', scatter_dimens...  83.3 us
  transfers between devices with their start and end apart: 40, of which 33 were waited for; matrix products, arithmetic and copies ran while one was open for 14% of the time, Pallas kernels for 0%

commit v1 on v0

v1 whole, which is shorter than its diff:
```python
import jax
import jax.numpy as jnp
from jax import lax
from jax.experimental import pallas as pl
from jax.experimental.pallas import tpu as pltpu
from jax.sharding import PartitionSpec as P

HEAD = 64
EPS = 1e-06
NEG_FILL = -1e30
ROOT_HALF = 0.7071067811865476
INV_ROOT_TAU = 0.3989422804014327
SCALE = HEAD ** (-0.5)
BF = jnp.bfloat16
F32 = jnp.float32
MIB = 1024 * 1024

ROWS = 64
BOTH = 128
WIDE = 32
HEADS_DEV = 8
QUARTERS = 4
HALF_W = 512
MODEL = 1024
HIDDEN = 2048
SEND_ROWS = 144
BLOCKS_Q = 4
CHUNKS = 8


def params(limit=56):
    return pltpu.CompilerParams(vmem_limit_bytes=limit * MIB)


def cost(flops, moved):
    return pl.CostEstimate(flops=int(flops), bytes_accessed=int(moved), transcendentals=0)


def whole(shape):
    count = len(shape)
    return pl.BlockSpec(shape, lambda *g: (0,) * count)


def swap(block, axis):
    return lax.ppermute(block, axis, [(0, 1), (1, 0)])


def nt(left, right):
    return lax.dot_general(left, right, (((1,), (1,)), ((), ())), preferred_element_type=F32)


def tn(left, right):
    return lax.dot_general(left, right, (((0,), (0,)), ((), ())), preferred_element_type=F32)


def nn(left, right):
    return jnp.dot(left, right, preferred_element_type=F32)


def low_lanes(shape):
    return lax.broadcasted_iota(jnp.int32, shape, len(shape) - 1) < HEAD


def turn(tile):
    return pltpu.roll(tile, HEAD, 1)


def pack_heads(tile, out_ref, pair, row0):
    rolled = turn(tile)
    for quarter in range(QUARTERS):
        first = slice(quarter * 32, quarter * 32 + 16)
        second = slice(quarter * 32 + 16, quarter * 32 + 32)
        mask = low_lanes((16, 128))
        even = jnp.where(mask, tile[first], rolled[second])
        odd = jnp.where(mask, rolled[first], tile[second])
        out_ref[(2 * pair) * QUARTERS + quarter, row0 : row0 + 16, :] = even.astype(BF)
        out_ref[(2 * pair + 1) * QUARTERS + quarter, row0 : row0 + 16, :] = odd.astype(BF)


def unpack_heads(in_ref, row0):
    mask = low_lanes((16, 128))
    columns = []
    for pair in range(HEADS_DEV // 2):
        pieces = []
        for quarter in range(QUARTERS):
            even = in_ref[(2 * pair) * QUARTERS + quarter, row0 : row0 + 16, :].astype(F32)
            odd = in_ref[(2 * pair + 1) * QUARTERS + quarter, row0 : row0 + 16, :].astype(F32)
            pieces.append(jnp.where(mask, even, turn(odd)))
            pieces.append(jnp.where(mask, turn(even), odd))
        columns.append(jnp.concatenate(pieces, axis=0))
    return jnp.concatenate(columns, axis=1)


def qkv_kernel(own_ref, other_ref, weight_ref, bias_ref, out_ref):
    rows = jnp.concatenate([own_ref[...], other_ref[...]], axis=0)

    def project(which):
        weight = weight_ref[:, which * 32 : which * 32 + 32, :].reshape(MODEL, HALF_W)
        return nn(rows, weight)

    queries = project(0) + bias_ref[0:1, :]
    keys = project(1)
    values = project(2) + bias_ref[1:2, :]
    mask = low_lanes((BOTH, 128))
    for pair in range(HEADS_DEV // 2):
        columns = slice(pair * 128, pair * 128 + 128)
        key_tile, value_tile, query_tile = keys[:, columns], values[:, columns], queries[:, columns]
        even = jnp.where(mask, key_tile, turn(value_tile)).astype(BF)
        odd = jnp.where(mask, turn(key_tile), value_tile).astype(BF)
        for quarter in range(QUARTERS):
            out_ref[(2 * pair) * QUARTERS + quarter, 0:BOTH, :] = even
            out_ref[(2 * pair + 1) * QUARTERS + quarter, 0:BOTH, :] = odd
        pack_heads(query_tile, out_ref, pair, BOTH)


def qkv_call(own, other, weight, bias):
    return pl.pallas_call(
        qkv_kernel,
        grid=(1,),
        in_specs=[whole((ROWS, MODEL)), whole((ROWS, MODEL)), whole((WIDE, 96, HALF_W)), whole((2, HALF_W))],
        out_specs=whole((WIDE, SEND_ROWS, 128)),
        out_shape=jax.ShapeDtypeStruct((WIDE, SEND_ROWS, 128), BF),
        compiler_params=params(),
        cost_estimate=cost(2 * BOTH * MODEL * 1536, 5e6),
    )(own, other, weight, bias)


def query_tiles(packed):
    mask = low_lanes((128, 128))
    return jnp.concatenate(
        [jnp.where(mask, packed, 0.0), jnp.where(mask, turn(packed), 0.0)], axis=0
    )


def key_chunk(recv_ref, chunk):
    half, group = chunk // 4, chunk % 4
    block = recv_ref[group * 8 : group * 8 + 8, half * ROWS : half * ROWS + ROWS, :]
    return block.reshape(512, 128)


def lane_tiles(fn, block):
    return fn(fn(block[:, 0:128], block[:, 128:256]), fn(block[:, 256:384], block[:, 384:512]))


def attend_kernel(
    flag_ref, recv_ref, key_id_ref, query_id_ref, out_ref, keep_ref, lse_ref,
    score_ref, top_ref, total_ref, acc_ref,
):
    at = pl.program_id(0)
    packed = recv_ref[pl.ds(at * 8, 8), BOTH : BOTH + 16, :].astype(F32).reshape(128, 128)
    queries = (query_tiles(packed) * SCALE).astype(BF)
    query_ids = query_id_ref[0]
    top_ref[...] = jnp.full((256, 128), NEG_FILL, F32)
    total_ref[...] = jnp.zeros((256, 128), F32)
    acc_ref[...] = jnp.zeros((256, 128), F32)
    for chunk in range(CHUNKS):

        @pl.when(flag_ref[at, chunk] != 0)
        def _():
            scores = nt(queries, key_chunk(recv_ref, chunk))
            scores = jnp.where(query_ids == key_id_ref[chunk], scores, NEG_FILL)
            score_ref[chunk] = scores
            top_ref[...] = jnp.maximum(top_ref[...], lane_tiles(jnp.maximum, scores))

    top = jnp.max(top_ref[...], axis=1, keepdims=True)
    for chunk in range(CHUNKS):

        @pl.when(flag_ref[at, chunk] != 0)
        def _():
            expo = jnp.exp(score_ref[chunk] - top)
            total_ref[...] += lane_tiles(jnp.add, expo)
            acc_ref[...] += nn(expo.astype(BF), key_chunk(recv_ref, chunk))

    total = jnp.sum(total_ref[...], axis=1, keepdims=True)
    mixture = acc_ref[...] / total
    lse_ref[...] = top + jnp.log(total)
    mask = low_lanes((128, 128))
    joined = jnp.where(mask, turn(mixture[:128]), mixture[128:]).reshape(8, 16, 128)
    keep_ref[...] = joined
    out_ref[...] = joined.astype(BF)


def attend_call(flags, recv, key_ids, query_ids):
    return pl.pallas_call(
        attend_kernel,
        grid_spec=pltpu.PrefetchScalarGridSpec(
            num_scalar_prefetch=1,
            grid=(BLOCKS_Q,),
            in_specs=[
                pl.BlockSpec((WIDE, SEND_ROWS, 128), lambda i, f: (0, 0, 0)),
                pl.BlockSpec((CHUNKS, 1, 512), lambda i, f: (0, 0, 0)),
                pl.BlockSpec((1, 256, 1), lambda i, f: (i, 0, 0)),
            ],
            out_specs=[
                pl.BlockSpec((8, 16, 128), lambda i, f: (i, 0, 0)),
                pl.BlockSpec((8, 16, 128), lambda i, f: (i, 0, 0)),
                pl.BlockSpec((256, 1), lambda i, f: (i, 0)),
            ],
            scratch_shapes=[
                pltpu.VMEM((CHUNKS, 256, 512), F32),
                pltpu.VMEM((256, 128), F32),
                pltpu.VMEM((256, 128), F32),
                pltpu.VMEM((256, 128), F32),
            ],
        ),
        out_shape=[
            jax.ShapeDtypeStruct((WIDE, 16, 128), BF),
            jax.ShapeDtypeStruct((WIDE, 16, 128), F32),
            jax.ShapeDtypeStruct((1024, 1), F32),
        ],
        compiler_params=params(),
        cost_estimate=cost(4 * 1024 * 4096 * 256, 2e6),
    )(flags, recv, key_ids, query_ids)


def attend_back_kernel(
    flag_ref, recv_ref, grad_ref, keep_ref, lse_ref, key_id_ref, query_id_ref, out_ref,
    key_grad_ref, query_grad_ref,
):
    at = pl.program_id(0)

    @pl.when(at == 0)
    def _():
        key_grad_ref[...] = jnp.zeros((WIDE, BOTH, 128), F32)

    mask = low_lanes((128, 128))
    packed = recv_ref[pl.ds(at * 8, 8), BOTH : BOTH + 16, :].astype(F32).reshape(128, 128)
    queries = (query_tiles(packed) * SCALE).astype(BF)
    grads = grad_ref[...].astype(F32).reshape(128, 128)
    grad_tile = jnp.concatenate(
        [jnp.where(mask, 0.0, turn(grads)), jnp.where(mask, 0.0, grads)], axis=0
    ).astype(BF)
    product = grads * keep_ref[...].reshape(128, 128)
    delta = jnp.concatenate(
        [
            jnp.sum(jnp.where(mask, product, 0.0), axis=1, keepdims=True),
            jnp.sum(jnp.where(mask, 0.0, product), axis=1, keepdims=True),
        ],
        axis=0,
    )
    lse = lse_ref[...]
    query_ids = query_id_ref[0]
    both = jnp.concatenate([queries, grad_tile], axis=0)
    query_grad_ref[...] = jnp.zeros((256, 128), F32)
    for chunk in range(CHUNKS):

        @pl.when(flag_ref[at, chunk] != 0)
        def _():
            half, group = chunk // 4, chunk % 4
            keys = key_chunk(recv_ref, chunk)
            scores = nt(queries, keys)
            scores = jnp.where(query_ids == key_id_ref[chunk], scores, NEG_FILL)
            chance = jnp.exp(scores - lse)
            grad_scores = (chance * (nt(grad_tile, keys) - delta)).astype(BF)
            query_grad_ref[...] += nn(grad_scores, keys)
            stacked = jnp.concatenate([grad_scores, chance.astype(BF)], axis=0)
            key_grad_ref[group * 8 : group * 8 + 8, half * ROWS : half * ROWS + ROWS, :] += tn(
                stacked, both
            ).reshape(8, ROWS, 128)

    query_grad = query_grad_ref[...] * SCALE
    joined = jnp.where(mask, query_grad[:128], turn(query_grad[128:]))
    out_ref[pl.ds(at * 8, 8), BOTH : BOTH + 16, :] = joined.astype(BF).reshape(8, 16, 128)

    @pl.when(at == BLOCKS_Q - 1)
    def _():
        out_ref[:, 0:BOTH, :] = key_grad_ref[...].astype(BF)


def attend_back_call(flags, recv, grads, keep, lse, key_ids, query_ids):
    return pl.pallas_call(
        attend_back_kernel,
        grid_spec=pltpu.PrefetchScalarGridSpec(
            num_scalar_prefetch=1,
            grid=(BLOCKS_Q,),
            in_specs=[
                pl.BlockSpec((WIDE, SEND_ROWS, 128), lambda i, f: (0, 0, 0)),
                pl.BlockSpec((8, 16, 128), lambda i, f: (i, 0, 0)),
                pl.BlockSpec((8, 16, 128), lambda i, f: (i, 0, 0)),
                pl.BlockSpec((256, 1), lambda i, f: (i, 0)),
                pl.BlockSpec((CHUNKS, 1, 512), lambda i, f: (0, 0, 0)),
                pl.BlockSpec((1, 256, 1), lambda i, f: (i, 0, 0)),
            ],
            out_specs=pl.BlockSpec((WIDE, SEND_ROWS, 128), lambda i, f: (0, 0, 0)),
            scratch_shapes=[
                pltpu.VMEM((WIDE, BOTH, 128), F32),
                pltpu.VMEM((256, 128), F32),
            ],
        ),
        out_shape=jax.ShapeDtypeStruct((WIDE, SEND_ROWS, 128), BF),
        compiler_params=params(),
        cost_estimate=cost(10 * 1024 * 4096 * 256, 3e6),
    )(flags, recv, grads, keep, lse, key_ids, query_ids)


def out_kernel(recv_ref, weight_ref, mixture_ref, own_ref, other_ref):
    mixture = unpack_heads(recv_ref, 0).astype(BF)
    mixture_ref[...] = mixture
    result = nn(mixture, weight_ref[...].reshape(HALF_W, MODEL))
    own_ref[...] = result[:ROWS]
    other_ref[...] = result[ROWS:].astype(BF)


def out_call(recv, weights):
    return pl.pallas_call(
        out_kernel,
        grid=(1,),
        in_specs=[whole((WIDE, 16, 128)), pl.BlockSpec((WIDE, 16, MODEL), lambda i: (0, 8, 0))],
        out_specs=[whole((BOTH, HALF_W)), whole((ROWS, MODEL)), whole((ROWS, MODEL))],
        out_shape=[
            jax.ShapeDtypeStruct((BOTH, HALF_W), BF),
            jax.ShapeDtypeStruct((ROWS, MODEL), F32),
            jax.ShapeDtypeStruct((ROWS, MODEL), BF),
        ],
        compiler_params=params(),
        cost_estimate=cost(2 * BOTH * HALF_W * MODEL, 2e6),
    )(recv, weights)


def mlp_kernel(own_ref, other_ref, bias_ref, one_ref, two_ref, pre_ref, act_ref, own_out, other_out, acc_ref):
    at = pl.program_id(0)
    rows = jnp.concatenate([own_ref[...], other_ref[...]], axis=0)
    pre = nn(rows, one_ref[...].reshape(MODEL, MODEL)) + bias_ref[...]
    act = (0.5 * pre * (1.0 + lax.erf(pre * ROOT_HALF))).astype(BF)
    pre_ref[...] = pre
    act_ref[...] = act
    part = nn(act, two_ref[...].reshape(MODEL, MODEL))

    @pl.when(at == 0)
    def _():
        acc_ref[...] = part

    @pl.when(at == 1)
    def _():
        result = acc_ref[...] + part
        own_out[...] = result[:ROWS]
        other_out[...] = result[ROWS:].astype(BF)


def mlp_call(own, other, bias, weights):
    return pl.pallas_call(
        mlp_kernel,
        grid=(2,),
        in_specs=[
            whole((ROWS, MODEL)),
            whole((ROWS, MODEL)),
            pl.BlockSpec((1, MODEL), lambda j: (0, j)),
            pl.BlockSpec((WIDE, 32, MODEL), lambda j: (0, 2 + j, 0)),
            pl.BlockSpec((16, 64, MODEL), lambda j: (j, 0, 0)),
        ],
        out_specs=[
            pl.BlockSpec((BOTH, MODEL), lambda j: (0, j)),
            pl.BlockSpec((BOTH, MODEL), lambda j: (0, j)),
            whole((ROWS, MODEL)),
            whole((ROWS, MODEL)),
        ],
        out_shape=[
            jax.ShapeDtypeStruct((BOTH, HIDDEN), F32),
            jax.ShapeDtypeStruct((BOTH, HIDDEN), BF),
            jax.ShapeDtypeStruct((ROWS, MODEL), F32),
            jax.ShapeDtypeStruct((ROWS, MODEL), BF),
        ],
        scratch_shapes=[pltpu.VMEM((BOTH, MODEL), F32)],
        compiler_params=params(),
        cost_estimate=cost(4 * BOTH * HIDDEN * MODEL, 10e6),
    )(own, other, bias, weights, weights)


def mlp_back_kernel(
    own_ref, other_ref, c_own_ref, c_other_ref, pre_ref, act_ref, one_ref, two_ref,
    grad_ref, bias_ref, own_out, other_out, acc_ref,
):
    at = pl.program_id(0)
    rows = jnp.concatenate([own_ref[...], other_ref[...]], axis=0)
    normed = jnp.concatenate([c_own_ref[...], c_other_ref[...]], axis=0)
    pre = pre_ref[...]
    slope = 0.5 * (1.0 + lax.erf(pre * ROOT_HALF)) + pre * jnp.exp(-0.5 * pre * pre) * INV_ROOT_TAU
    grad_pre = (nt(rows, two_ref[...].reshape(MODEL, MODEL)) * slope).astype(BF)
    bias_ref[...] = jnp.sum(grad_pre.astype(F32), axis=0, keepdims=True)
    part = nt(grad_pre, one_ref[...].reshape(MODEL, MODEL))
    grad_two = tn(act_ref[...], rows).astype(BF).reshape(16, 64, MODEL)
    grad_one = tn(normed, grad_pre).astype(BF).reshape(WIDE, 32, MODEL)

    @pl.when(at == 0)
    def _():
        acc_ref[...] = part
        grad_ref[0:16, 0:64, :] = grad_two
        grad_ref[:, 64:96, :] = grad_one

    @pl.when(at == 1)
    def _():
        result = acc_ref[...] + part
        own_out[...] = result[:ROWS]
        other_out[...] = result[ROWS:].astype(BF)
        grad_ref[16:32, 0:64, :] = grad_two
        grad_ref[:, 96:128, :] = grad_one


def mlp_back_call(own, other, c_own, c_other, pre, act, weights):
    return pl.pallas_call(
        mlp_back_kernel,
        grid=(2,),
        in_specs=[
            whole((ROWS, MODEL)),
            whole((ROWS, MODEL)),
            whole((ROWS, MODEL)),
            whole((ROWS, MODEL)),
            pl.BlockSpec((BOTH, MODEL), lambda j: (0, j)),
            pl.BlockSpec((BOTH, MODEL), lambda j: (0, j)),
            pl.BlockSpec((WIDE, 32, MODEL), lambda j: (0, 2 + j, 0)),
            pl.BlockSpec((16, 64, MODEL), lambda j: (j, 0, 0)),
        ],
        out_specs=[
            whole((WIDE, 128, MODEL)),
            pl.BlockSpec((1, MODEL), lambda j: (0, j)),
            whole((ROWS, MODEL)),
            whole((ROWS, MODEL)),
        ],
        out_shape=[
            jax.ShapeDtypeStruct((WIDE, 128, MODEL), BF),
            jax.ShapeDtypeStruct((1, HIDDEN), F32),
            jax.ShapeDtypeStruct((ROWS, MODEL), F32),
            jax.ShapeDtypeStruct((ROWS, MODEL), BF),
        ],
        scratch_shapes=[pltpu.VMEM((BOTH, MODEL), F32)],
        compiler_params=params(),
        cost_estimate=cost(8 * BOTH * HIDDEN * MODEL, 20e6),
    )(own, other, c_own, c_other, pre, act, weights, weights)


def out_back_kernel(own_ref, other_ref, mixture_ref, weight_ref, send_ref, grad_ref):
    rows = jnp.concatenate([own_ref[...], other_ref[...]], axis=0)
    grad_mix = nt(rows, weight_ref[...].reshape(HALF_W, MODEL))
    for pair in range(HEADS_DEV // 2):
        pack_heads(grad_mix[:, pair * 128 : pair * 128 + 128], send_ref, pair, 0)
    grad_ref[...] = tn(mixture_ref[...], rows).astype(BF).reshape(WIDE, 16, MODEL)


def out_back_call(own, other, mixture, weights):
    return pl.pallas_call(
        out_back_kernel,
        grid=(1,),
        in_specs=[
            whole((ROWS, MODEL)),
            whole((ROWS, MODEL)),
            whole((BOTH, HALF_W)),
            pl.BlockSpec((WIDE, 16, MODEL), lambda i: (0, 8, 0)),
        ],
        out_specs=[whole((WIDE, 16, 128)), whole((WIDE, 16, MODEL))],
        out_shape=[
            jax.ShapeDtypeStruct((WIDE, 16, 128), BF),
            jax.ShapeDtypeStruct((WIDE, 16, MODEL), BF),
        ],
        compiler_params=params(),
        cost_estimate=cost(4 * BOTH * HALF_W * MODEL, 3e6),
    )(own, other, mixture, weights)


def qkv_back_kernel(recv_ref, own_ref, other_ref, weight_ref, grad_ref, bias_ref, own_out, other_out):
    rows = jnp.concatenate([own_ref[...], other_ref[...]], axis=0)
    grad_q = unpack_heads(recv_ref, BOTH).astype(BF)
    mask = low_lanes((BOTH, 128))
    key_columns, value_columns = [], []
    for pair in range(HEADS_DEV // 2):
        sums = []
        for head in (2 * pair, 2 * pair + 1):
            total = recv_ref[head * QUARTERS, 0:BOTH, :].astype(F32)
            for quarter in range(1, QUARTERS):
                total = total + recv_ref[head * QUARTERS + quarter, 0:BOTH, :].astype(F32)
            sums.append(total)
        key_columns.append(jnp.where(mask, sums[0], turn(sums[1])))
        value_columns.append(jnp.where(mask, turn(sums[0]), sums[1]))
    grad_k = jnp.concatenate(key_columns, axis=1).astype(BF)
    grad_v = jnp.concatenate(value_columns, axis=1).astype(BF)
    bias_ref[0:1, :] = jnp.sum(grad_q.astype(F32), axis=0, keepdims=True)
    bias_ref[1:2, :] = jnp.sum(grad_v.astype(F32), axis=0, keepdims=True)

    def weight(which):
        return weight_ref[:, which * 32 : which * 32 + 32, :].reshape(MODEL, HALF_W)

    result = nt(grad_q, weight(0)) + nt(grad_k, weight(1)) + nt(grad_v, weight(2))
    own_out[...] = result[:ROWS]
    other_out[...] = result[ROWS:].astype(BF)
    grad_ref[:, 0:32, 0:HALF_W] = tn(rows, grad_q).astype(BF).reshape(WIDE, 32, HALF_W)
    grad_ref[:, 0:32, HALF_W:MODEL] = tn(rows, grad_k).astype(BF).reshape(WIDE, 32, HALF_W)
    value_part = tn(rows, grad_v).astype(BF).reshape(WIDE, 32, HALF_W)
    grad_ref[:, 32:48, 0:HALF_W] = value_part[:, 0:16]
    grad_ref[:, 32:48, HALF_W:MODEL] = value_part[:, 16:32]


def qkv_back_call(recv, own, other, weight):
    return pl.pallas_call(
        qkv_back_kernel,
        grid=(1,),
        in_specs=[
            whole((WIDE, SEND_ROWS, 128)),
            whole((ROWS, MODEL)),
            whole((ROWS, MODEL)),
            whole((WIDE, 96, HALF_W)),
        ],
        out_specs=[
            whole((WIDE, 48, MODEL)),
            whole((2, HALF_W)),
            whole((ROWS, MODEL)),
            whole((ROWS, MODEL)),
        ],
        out_shape=[
            jax.ShapeDtypeStruct((WIDE, 48, MODEL), BF),
            jax.ShapeDtypeStruct((2, HALF_W), F32),
            jax.ShapeDtypeStruct((ROWS, MODEL), F32),
            jax.ShapeDtypeStruct((ROWS, MODEL), BF),
        ],
        compiler_params=params(),
        cost_estimate=cost(12 * BOTH * HALF_W * MODEL, 8e6),
    )(recv, own, other, weight)


def layer_norm(rows_in, gain_row, shift_row):
    centre = jnp.mean(rows_in, axis=-1, keepdims=True)
    centred = rows_in - centre
    spread = jnp.mean(centred * centred, axis=-1, keepdims=True)
    rstd_rows = lax.rsqrt(spread + EPS)
    normal_rows = centred * rstd_rows
    return ((normal_rows * gain_row + shift_row).astype(BF), normal_rows, rstd_rows)


def norm_back(grad_rows, normal_rows, rstd_rows, gain_row):
    scaled = grad_rows * gain_row
    first_mean = jnp.mean(scaled, axis=-1, keepdims=True)
    second_mean = jnp.mean(scaled * normal_rows, axis=-1, keepdims=True)
    return rstd_rows * (scaled - first_mean - normal_rows * second_mean)


def all_to_all(block):
    return lax.all_to_all(block, "wide", 0, 0, tiled=True)


def layer_forward(layer_in, ids, weights, small):
    flags, key_ids, query_ids = ids
    qkv_weight, rest_weight = weights
    gain_rows, shift_rows, scale_rows, qv_rows, fc1_row = small
    a_own, hat_a, rstd_a = layer_norm(layer_in, gain_rows[0], shift_rows[0])
    a_other = swap(a_own, "tensor")
    sent = qkv_call(a_own, a_other, qkv_weight, qv_rows)
    recv = all_to_all(sent)
    mix_sent, mix_keep, lse = attend_call(flags, recv, key_ids, query_ids)
    mixture, proj_own, proj_other = out_call(all_to_all(mix_sent), rest_weight)
    branch_a = proj_own + swap(proj_other, "tensor").astype(F32) + shift_rows[1]
    middle = layer_in + scale_rows[0] * branch_a
    c_own, hat_c, rstd_c = layer_norm(middle, gain_rows[1], shift_rows[2])
    c_other = swap(c_own, "tensor")
    pre, act, mlp_own, mlp_other = mlp_call(c_own, c_other, fc1_row, rest_weight)
    branch_m = mlp_own + swap(mlp_other, "tensor").astype(F32) + shift_rows[3]
    layer_out = middle + scale_rows[1] * branch_m
    kept = (
        a_own, a_other, hat_a, rstd_a, recv, mix_keep, lse, mixture, branch_a,
        c_own, c_other, hat_c, rstd_c, pre, act, branch_m,
    )
    return layer_out, kept


def column_sum(rows):
    return jnp.sum(rows, axis=0)


def mlp_backward(grad_in, kept, weights, small):
    (a_own, a_other, hat_a, rstd_a, recv, mix_keep, lse, mixture, branch_a,
     c_own, c_other, hat_c, rstd_c, pre, act, branch_m) = kept
    gain_rows, shift_rows, scale_rows, qv_rows, fc1_row = small
    grad_m = grad_in * scale_rows[1]
    low_m = grad_m.astype(BF)
    grad_pack, fc1_grad, norm_own, norm_other = mlp_back_call(
        low_m, swap(low_m, "tensor"), c_own, c_other, pre, act, weights[1]
    )
    grad_norm = norm_own + swap(norm_other, "tensor").astype(F32)
    grad_mid = grad_in + norm_back(grad_norm, hat_c, rstd_c, gain_rows[1])
    vectors = (
        column_sum(grad_norm * hat_c),
        column_sum(grad_norm),
        column_sum(grad_m),
        column_sum(grad_in * branch_m),
    )
    return grad_mid, grad_pack, fc1_grad, vectors


def attn_backward(grad_mid, kept, ids, weights, small):
    (a_own, a_other, hat_a, rstd_a, recv, mix_keep, lse, mixture, branch_a,
     c_own, c_other, hat_c, rstd_c, pre, act, branch_m) = kept
    flags, key_ids, query_ids = ids
    gain_rows, shift_rows, scale_rows, qv_rows, fc1_row = small
    grad_a = grad_mid * scale_rows[0]
    low_a = grad_a.astype(BF)
    mix_grad, out_pack = out_back_call(low_a, swap(low_a, "tensor"), mixture, weights[1])
    back = attend_back_call(flags, recv, all_to_all(mix_grad), mix_keep, lse, key_ids, query_ids)
    qkv_pack, qv_grad, norm_own, norm_other = qkv_back_call(
        all_to_all(back), a_own, a_other, weights[0]
    )
    grad_norm = norm_own + swap(norm_other, "tensor").astype(F32)
    grad_x = grad_mid + norm_back(grad_norm, hat_a, rstd_a, gain_rows[0])
    vectors = (
        column_sum(grad_norm * hat_a),
        column_sum(grad_norm),
        column_sum(grad_a),
        column_sum(grad_mid * branch_a),
    )
    return grad_x, qkv_pack, out_pack, qv_grad, vectors


def body(
    x_in, out_cot, image_ids, w_qkv, w_out, w_fc1, w_fc2, gains, shifts, layer_scales, qv_bias, fc1_bias
):
    section = lax.axis_index("section")
    tensor = lax.axis_index("tensor")
    wide = lax.axis_index("wide")
    is_first = section == 0

    def one(array):
        return lax.dynamic_index_in_dim(array, section, 0, keepdims=False)

    flat_small = jnp.concatenate(
        [
            gains.reshape(-1),
            shifts.reshape(-1),
            layer_scales.reshape(-1),
            qv_bias.reshape(-1),
            fc1_bias.reshape(-1),
            jnp.zeros((160,), BF),
        ]
    )
    small_block = jnp.concatenate(
        [flat_small.reshape(1, HALF_W), jnp.zeros((15, HALF_W), BF)], axis=0
    )
    pack_a = jnp.concatenate(
        [jnp.transpose(w_qkv[0], (1, 0, 2)).reshape(96, HALF_W), small_block], axis=0
    )
    pack_b = jnp.concatenate(
        [w_fc2[0], w_fc1[0][:, :MODEL], w_fc1[0][:, MODEL:], w_out[0]], axis=0
    )
    other_a = swap(pack_a, "section")
    other_b = swap(pack_b, "section")

    def gather(block):
        return lax.all_gather(block, "wide", axis=0, tiled=False)

    a_layers = (
        gather(jnp.where(is_first, pack_a, other_a)),
        gather(jnp.where(is_first, other_a, pack_a)),
    )
    b_layers = (
        gather(jnp.where(is_first, pack_b, other_b)),
        gather(jnp.where(is_first, other_b, pack_b)),
    )

    def small_rows(gathered):
        block = gathered[:, 96, :].astype(F32)

        def pick(start, count, width):
            part = block[:, start : start + count * width].reshape(WIDE, count, width)
            return jnp.transpose(part, (1, 0, 2)).reshape(count, WIDE * width)

        return (pick(0, 2, 32), pick(64, 4, 32), pick(192, 2, 32), pick(256, 2, 16), pick(288, 1, 64))

    small = tuple(small_rows(block) for block in a_layers)
    weights = tuple((a_layers[layer], b_layers[layer]) for layer in range(2))

    id_grid = one(image_ids).reshape(2, WIDE, ROWS)
    sorted_ids = jnp.where(tensor == 0, id_grid, id_grid[::-1])
    key_ids = sorted_ids.reshape(CHUNKS, 1, 512)
    quarter = lax.rem(wide, QUARTERS)
    half_ids = lax.dynamic_index_in_dim(sorted_ids, quarter // 2, 0, keepdims=False)
    quarter_ids = lax.dynamic_slice_in_dim(half_ids, lax.rem(quarter, 2) * 32, 32, 1)
    query_ids = jnp.transpose(quarter_ids.reshape(BLOCKS_Q, 8, 2, 16), (0, 2, 1, 3)).reshape(
        BLOCKS_Q, 256, 1
    )
    key_low, key_high = jnp.min(key_ids[:, 0], axis=1), jnp.max(key_ids[:, 0], axis=1)
    query_low, query_high = jnp.min(query_ids[..., 0], axis=1), jnp.max(query_ids[..., 0], axis=1)
    flags = (
        (query_low[:, None] <= key_high[None]) & (query_high[:, None] >= key_low[None])
    ).astype(jnp.int32)
    ids = (flags, key_ids, query_ids)

    rows = one(x_in).astype(F32)
    kept, outs = [], []
    for layer in range(2):
        layer_out, saved = layer_forward(rows, ids, weights[layer], small[layer])
        outs.append(layer_out.astype(BF))
        kept.append(saved)
        rows = outs[-1].astype(F32)

    def rs(pack):
        count = pack.shape[1]
        return lax.psum_scatter(
            pack.reshape(WIDE * count, MODEL), "wide", scatter_dimension=0, tiled=True
        )

    def small_shards(pairs):
        parts = [
            jnp.transpose(vector.reshape(count, WIDE, -1), (1, 0, 2)).reshape(WIDE, -1)
            for vector, count in pairs
        ]
        return jnp.concatenate(parts, axis=1).astype(BF)

    def padded(shards, count):
        return jnp.pad(shards[:, None, :], ((0, 0), (0, count - 1), (0, MODEL - shards.shape[1])))

    grad = one(out_cot).astype(F32)
    grad_mid1, mlp_pack1, fc1_grad1, mlp_vec1 = mlp_backward(grad, kept[1], weights[1], small[1])
    sum_mlp1 = rs(mlp_pack1)
    grad_x1, qkv_pack1, out_pack1, qv_grad1, attn_vec1 = attn_backward(
        grad_mid1, kept[1], ids, weights[1], small[1]
    )
    grad = grad_x1.astype(BF).astype(F32)
    grad_mid0, mlp_pack0, fc1_grad0, mlp_vec0 = mlp_backward(grad, kept[0], weights[0], small[0])
    small1 = small_shards(
        [(jnp.stack(mlp_vec1 + attn_vec1), 8), (qv_grad1, 2), (fc1_grad1, 1)]
    )
    small0 = small_shards([(jnp.stack(mlp_vec0), 4), (fc1_grad0, 1)])
    grad_x0, qkv_pack0, out_pack0, qv_grad0, attn_vec0 = attn_backward(
        grad_mid0, kept[0], ids, weights[0], small[0]
    )
    middle_pack = jnp.concatenate(
        [
            mlp_pack0,
            qkv_pack1,
            out_pack1,
            out_pack0,
            padded(jnp.concatenate([small1, small0], axis=1), 16),
        ],
        axis=1,
    )
    sum_mid = rs(middle_pack)
    last_small = small_shards([(jnp.stack(attn_vec0), 4), (qv_grad0, 2)])
    last_pack = jnp.concatenate([qkv_pack0, padded(last_small, 8)], axis=1)
    last_recv = lax.all_to_all(last_pack, "wide", 0, 0, tiled=True)
    sum_last = jnp.sum(last_recv.astype(F32), axis=0).astype(BF)

    def to_owner(first, second):
        own = jnp.where(is_first, first, second)
        away = jnp.where(is_first, second, first)
        return own.astype(F32) + swap(away, "section").astype(F32)

    mlp_total = to_owner(sum_mid[0:128], sum_mlp1)
    out_total = to_owner(sum_mid[192:208], sum_mid[176:192])
    qkv_total = to_owner(sum_last[0:48], sum_mid[128:176])
    tiny = sum_mid[208]
    tiny1 = tiny[:352]
    tiny_mlp0 = tiny[352:544]
    tiny_attn0 = sum_last[48][:160]
    tiny0 = jnp.concatenate([tiny_mlp0[:128], tiny_attn0, tiny_mlp0[128:]])
    tiny_total = to_owner(tiny0[None], tiny1[None])[0]
    norm_part = tiny_total[:256].astype(BF)
    norm_total = (norm_part.astype(F32) + swap(norm_part, "tensor").astype(F32)).reshape(8, 32)
    g_gains = jnp.stack([norm_total[4], norm_total[0]])
    g_shifts = jnp.stack([norm_total[5], norm_total[6], norm_total[1], norm_total[2]])
    g_scales = jnp.stack([norm_total[7], norm_total[3]])
    g_qv = tiny_total[256:288].reshape(2, 16)
    g_fc1_bias = tiny_total[288:352]
    g_fc2 = mlp_total[0:64]
    g_fc1 = jnp.concatenate([mlp_total[64:96], mlp_total[96:128]], axis=1)
    pairs = qkv_total[0:32]
    value_grad = jnp.concatenate([qkv_total[32:48, :HALF_W], qkv_total[32:48, HALF_W:]], axis=0)
    g_qkv = jnp.stack([pairs[:, :HALF_W], pairs[:, HALF_W:], value_grad], axis=1)

    def by_micro(first, second):
        own = jnp.where(is_first, first, second)
        came = swap(jnp.where(is_first, second, first), "section")
        return jnp.stack([jnp.where(is_first, own, came), jnp.where(is_first, came, own)])

    return (
        by_micro(outs[0], outs[1])[None],
        by_micro(grad_x0, grad_x1)[None],
        g_qkv[None],
        out_total[None],
        g_fc1[None],
        g_fc2[None],
        g_gains[None],
        g_shifts[None],
        g_scales[None],
        g_qv[None],
        g_fc1_bias[None],
    )


def solution(mesh):
    in_specs = (
        P(None, ("tensor", "wide"), None),
        P(None, ("tensor", "wide"), None),
        P(),
        P("section", "wide", None, "tensor"),
        P("section", ("tensor", "wide"), None),
        P("section", "wide", "tensor"),
        P("section", ("tensor", "wide"), None),
        P("section", None, "wide"),
        P("section", None, "wide"),
        P("section", None, "wide"),
        P("section", None, ("tensor", "wide")),
        P("section", ("tensor", "wide")),
    )
    out_specs = (
        P("section", None, ("tensor", "wide"), None),
        P("section", None, ("tensor", "wide"), None),
        P("section", "wide", None, "tensor"),
        P("section", ("tensor", "wide"), None),
        P("section", "wide", "tensor"),
        P("section", ("tensor", "wide"), None),
        P("section", None, "wide"),
        P("section", None, "wide"),
        P("section", None, "wide"),
        P("section", None, ("tensor", "wide")),
        P("section", ("tensor", "wide")),
    )
    return jax.shard_map(body, mesh=mesh, in_specs=in_specs, out_specs=out_specs, check_vma=False)
```

time: 2490 us -> 744 us (0.30)
  waiting for transfers between devices: 1310 us -> 343 us
  matrix products: 333 us -> 0 us
  local copies, waits for them, and re-layouts: 365 us -> 42 us
  blocking collectives: 322 us -> 88.4 us
  Pallas kernels: 0 us -> 121 us
  other arithmetic: 120 us -> 45.4 us
  starting transfers between devices: 10.2 us -> 77.8 us
    reduce_scatter x22 -> x2, waiting for transfers between devices: 837 us -> 107 us  [rs(): lax.psum_scatter(pack.reshape(WIDE * count, MODEL), 'wide', scatter_dimen...]
    dot_general x120 -> x0, matrix products: 333 us -> none  [the longest x24 75.9 us: block_scores(): jnp.einsum('qhd,khd->hqk', queries, key_part, preferred_element_type=jnp....]
    unnamed x40 -> x6, waiting for transfers between devices: 237 us -> 1.79 us
    all_gather x16 -> x0, blocking collectives: 187 us -> none  [the longest x1 26.3 us: body(): lax.all_gather(shifts[0], 'wide', axis=1, tiled=True)]
    convert_element_type x18 -> x0, local copies, waits for them, and re-layouts: 135 us -> none  [the longest x6 66.6 us: attn_backward(): (grad_k * score_scale).astype(jnp.bfloat16)]
    all_gather x10 -> x4, waiting for transfers between devices: 217 us -> 83.8 us  [gather(): return lax.all_gather(block, 'wide', axis=0, tiled=False)]
    unnamed x2 -> x0, blocking collectives: 129 us -> none
    pallas_call x0 -> x16, Pallas kernels: none -> 121 us  [the longest x2 30.4 us: attend_back_call(): pl.pallas_call(attend_back_kernel, grid_spec=pltpu.PrefetchScalarGridSpec...]
  transfers between devices with their start and end apart: 40 -> 35, of which waited for: 33 -> 29; matrix products, arithmetic and copies ran while one was open for 14% -> 8% of each run, Pallas kernels for 0% -> 8%
where the time goes in v1:
time: 744 us; the launch traced here: 733 us
  waiting for transfers between devices  343 us (46%)
  Pallas kernels  121 us (16%)
  blocking collectives  88.4 us (12%)
  starting transfers between devices  77.8 us (10%)
  other arithmetic  45.4 us (6%)
  local copies, waits for them, and re-layouts  42 us (6%)
  between operations  15.4 us (2%)
    reduce_scatter x2, waiting for transfers between devices, rs(): lax.psum_scatter(pack.reshape(WIDE * count, MODEL), 'wide', scatter_dimen...  107 us
    all_to_all x5, blocking collectives, all_to_all(): return lax.all_to_all(block, 'wide', 0, 0, tiled=True)  88.4 us
    all_gather x4, waiting for transfers between devices, gather(): return lax.all_gather(block, 'wide', axis=0, tiled=False)  83.8 us
    ppermute x25, waiting for transfers between devices, swap(): return lax.ppermute(block, axis, [(0, 1), (1, 0)])  73.6 us
    ppermute x25, starting transfers between devices, swap(): return lax.ppermute(block, axis, [(0, 1), (1, 0)])  59.7 us
    all_to_all x3, waiting for transfers between devices, all_to_all(): return lax.all_to_all(block, 'wide', 0, 0, tiled=True)  41.6 us
    all_to_all x1, waiting for transfers between devices, body(): last_recv = lax.all_to_all(last_pack, 'wide', 0, 0, tiled=True)  34.8 us
    pallas_call x2, Pallas kernels, attend_back_call(): pl.pallas_call(attend_back_kernel, grid_spec=pltpu.PrefetchScalarGridSpec...  30.4 us
  transfers between devices with their start and end apart: 35, of which 29 were waited for; matrix products, arithmetic and copies ran while one was open for 8% of the time, Pallas kernels for 8%

profile of v1, /device:TPU:0, one launch (start us, length us, event | category | flops | bytes accessed | tf_op | source)
XLA Modules:
  0.0 733.0 jit_solution(12648234502403172243)
XLA Ops:
  23.1 6.1 collective-permute-done.2
  33.9 33.4 %all-gather.9.cloned.1.call-done = bf16[3584,512]{1,0:T(8,128)(2,1)} async-done(((bf16[112,512]{1,0:T(8,128)(2,1)}), bf16[3584,512]{1,0:T(8,128)(2,1)}) %all-gather.9.cloned.1.call-update) | async-done | bytes 3670032 | tf_op jit(solution)/shard_map/all_gather | solution.py:643
  69.0 46.3 %all-gather.13.cloned.1.call-done = bf16[3584,512]{1,0:T(8,128)(2,1)} async-done(((bf16[112,512]{1,0:T(8,128)(2,1)}), bf16[3584,512]{1,0:T(8,128)(2,1)}) %all-gather.13.cloned.1.call-update) | async-done | bytes 3670032 | tf_op jit(solution)/shard_map/all_gather | solution.py:643
  129.6 5.1 all-to-all-start
  138.7 15.9 %all-to-all-done.recv_ref = bf16[32,144,128]{2,1,0:T(8,128)(2,1)S(1)} async-done(((bf16[32,144,128]{2,1,0:T(8,128)(2,1)}), bf16[32,144,128]{2,1,0:T(8,128)(2,1)S(1)}, u32[]{:S(2)}, u32[]{:S(2)}) %all-to-all-start) | async-done | bytes 1179680 | tf_op jit(solution)/shard_map/all_to_all | solution.py:535
  155.6 12.0 %shard_map.204 = (bf16[32,16,128]{2,1,0:T(8,128)(2,1)}, f32[32,16,128]{2,1,0:T(8,128)}, f32[1024,1]{1,0:T(8,128)}) custom-call(s32[4,8]{1,0:T(4,128)} %and_convert_fusion.flag_ref, bf16[32,144,128]{2,1,0:T(8,128)(2,1)} %copy-done.9, s32[8,1,512]{2,1,0:T(1,128)} %reshape.367.key_id_ref, s32[4,256,1]{2,1,0:T(8,128)} %reshape.389.query_id_ref), custom_call_target="tpu_custom_call" | custom-call | flops 4294967296 | bytes 2000000 | tf_op jit(solution)/shard_map/pallas_call | solution.py:184
  167.5 13.6 %all_to_all.45.recv_ref = bf16[32,16,128]{2,1,0:T(8,128)(2,1)} all-to-all(bf16[32,16,128]{2,1,0:T(8,128)(2,1)} %get-tuple-element.51), channel_id=1, replica_groups=mesh['section'=2,'tensor'=2,'wide'=32] {'wide'}, dimensions={0} | all-to-all | bytes 262144 | tf_op jit(solution)/shard_map/all_to_all | solution.py:535
  190.9 4.1 collective-permute-done.3
  203.7 5.4 shard_map.206
  228.5 27.0 %all_to_all.46.recv_ref = bf16[32,144,128]{2,1,0:T(8,128)(2,1)} all-to-all(bf16[32,144,128]{2,1,0:T(8,128)(2,1)} %shard_map.207), channel_id=1, replica_groups=mesh['section'=2,'tensor'=2,'wide'=32] {'wide'}, dimensions={0} | all-to-all | bytes 2359296 | tf_op jit(solution)/shard_map/all_to_all | solution.py:535
  255.4 12.0 %shard_map.208 = (bf16[32,16,128]{2,1,0:T(8,128)(2,1)}, f32[32,16,128]{2,1,0:T(8,128)}, f32[1024,1]{1,0:T(8,128)}) custom-call(s32[4,8]{1,0:T(4,128)} %and_convert_fusion.flag_ref, bf16[32,144,128]{2,1,0:T(8,128)(2,1)} %all_to_all.46.recv_ref, s32[8,1,512]{2,1,0:T(1,128)} %reshape.367.key_id_ref, s32[4,256,1]{2,1,0:T(8,128)} %reshape.389.query_id_ref), custom_call_target="tpu_custom_call" | custom-call | flops 4294967296 | bytes 2000000 | tf_op jit(solution)/shard_map/pallas_call | solution.py:184
  271.3 7.8 %all-to-all-done.3.recv_ref = bf16[32,16,128]{2,1,0:T(8,128)(2,1)S(1)} async-done(((bf16[32,16,128]{2,1,0:T(8,128)(2,1)}), bf16[32,16,128]{2,1,0:T(8,128)(2,1)S(1)}, u32[]{:S(2)}, u32[]{:S(2)}) %all-to-all-start.3) | async-done | bytes 131104 | tf_op jit(solution)/shard_map/all_to_all | solution.py:535
  298.1 5.5 shard_map.210
  318.6 12.3 %shard_map.211 = (bf16[32,128,1024]{2,1,0:T(8,128)(2,1)}, f32[1,2048]{1,0:T(1,128)}, f32[64,1024]{1,0:T(8,128)}, bf16[64,1024]{1,0:T(8,128)(2,1)}) custom-call(bf16[64,1024]{1,0:T(8,128)(2,1)} %copy-done.23, bf16[64,1024]{1,0:T(8,128)(2,1)} %copy-done.33, bf16[64,1024]{1,0:T(8,128)(2,1)} %copy-done.6, bf16[64,1024]{1,0:T(8,128)(2,1)} %copy-done.18, ...), custom_call_target="tpu_custom_call" | custom-call | flops 2147483648 | bytes 20000000 | tf_op jit(solution)/shard_map/pallas_call | solution.py:400
  350.4 12.6 %all_to_all.47.grad_ref = bf16[32,16,128]{2,1,0:T(8,128)(2,1)} all-to-all(bf16[32,16,128]{2,1,0:T(8,128)(2,1)} %get-tuple-element.66), channel_id=1, replica_groups=mesh['section'=2,'tensor'=2,'wide'=32] {'wide'}, dimensions={0} | all-to-all | bytes 262144 | tf_op jit(solution)/shard_map/all_to_all | solution.py:535
  363.0 15.2 %shard_map.213 = bf16[32,144,128]{2,1,0:T(8,128)(2,1)} custom-call(s32[4,8]{1,0:T(4,128)} %and_convert_fusion.flag_ref, bf16[32,144,128]{2,1,0:T(8,128)(2,1)} %all_to_all.46.recv_ref, bf16[32,16,128]{2,1,0:T(8,128)(2,1)} %all_to_all.47.grad_ref, f32[32,16,128]{2,1,0:T(8,128)} %get-tuple-element.67.keep_ref, f32[1024,1]{1,0:T(8,128)} %get-tuple-element.68.lse_ref, ...), custom_call_target="tpu_custom_call" | custom-call | flops 10737418240 | bytes 3000000 | tf_op jit(solution)/shard_map/pallas_call | solution.py:271
  382.8 17.8 %all-to-all-done.5.recv_ref = bf16[32,144,128]{2,1,0:T(8,128)(2,1)S(1)} async-done(((bf16[32,144,128]{2,1,0:T(8,128)(2,1)}), bf16[32,144,128]{2,1,0:T(8,128)(2,1)S(1)}, u32[]{:S(2)}, u32[]{:S(2)}) %all-to-all-start.5) | async-done | bytes 1179680 | tf_op jit(solution)/shard_map/all_to_all | solution.py:535
  401.7 6.1 shard_map.214
  425.0 12.3 %shard_map.215 = (bf16[32,128,1024]{2,1,0:T(8,128)(2,1)}, f32[1,2048]{1,0:T(1,128)}, f32[64,1024]{1,0:T(8,128)}, bf16[64,1024]{1,0:T(8,128)(2,1)}) custom-call(bf16[64,1024]{1,0:T(8,128)(2,1)} %copy-done.21, bf16[64,1024]{1,0:T(8,128)(2,1)} %copy-done.32, bf16[64,1024]{1,0:T(8,128)(2,1)} %copy-done.5, bf16[64,1024]{1,0:T(8,128)(2,1)} %copy-done.17, ...), custom_call_target="tpu_custom_call" | custom-call | flops 2147483648 | bytes 20000000 | tf_op jit(solution)/shard_map/pallas_call | solution.py:400
  440.6 8.4 %constant_dynamic-update-slice_fusion.11 = bf16[32,224,1024]{2,1,0:T(8,128)(2,1)} fusion(bf16[32,128,1024]{2,1,0:T(8,128)(2,1)} %get-tuple-element.83), kind=kLoop, calls=%fused_computation.133 | loop fusion | bytes 16777216
  453.6 5.4 collective-permute-done.17.other_ref
  467.2 11.5 %all_to_all.48.grad_ref = bf16[32,16,128]{2,1,0:T(8,128)(2,1)} all-to-all(bf16[32,16,128]{2,1,0:T(8,128)(2,1)S(1)} %copy-done.35), channel_id=1, replica_groups=mesh['section'=2,'tensor'=2,'wide'=32] {'wide'}, dimensions={0} | all-to-all | bytes 262144 | tf_op jit(solution)/shard_map/all_to_all | solution.py:535
  478.7 15.2 %shard_map.217 = bf16[32,144,128]{2,1,0:T(8,128)(2,1)} custom-call(s32[4,8]{1,0:T(4,128)} %and_convert_fusion.flag_ref, bf16[32,144,128]{2,1,0:T(8,128)(2,1)} %copy-done.9, bf16[32,16,128]{2,1,0:T(8,128)(2,1)} %all_to_all.48.grad_ref, f32[32,16,128]{2,1,0:T(8,128)} %get-tuple-element.77.keep_ref, f32[1024,1]{1,0:T(8,128)} %get-tuple-element.78.lse_ref, ...), custom_call_target="tpu_custom_call" | custom-call | flops 10737418240 | bytes 3000000 | tf_op jit(solution)/shard_map/pallas_call | solution.py:271
  493.9 23.8 %all_to_all.49.recv_ref = bf16[32,144,128]{2,1,0:T(8,128)(2,1)} all-to-all(bf16[32,144,128]{2,1,0:T(8,128)(2,1)} %shard_map.217), channel_id=1, replica_groups=mesh['section'=2,'tensor'=2,'wide'=32] {'wide'}, dimensions={0} | all-to-all | bytes 2359296 | tf_op jit(solution)/shard_map/all_to_all | solution.py:535
  517.7 6.2 shard_map.218
  525.9 5.5 collective-permute-done.18
  533.0 4.4 pad_maximum_fusion
  537.3 4.8 all-to-all-start.8
  550.6 4.5 collective-permute-done.19
  556.0 34.8 %all-to-all-done.8 = bf16[32,56,1024]{2,1,0:T(8,128)(2,1)} async-done(((bf16[32,56,1024]{2,1,0:T(8,128)(2,1)}), bf16[32,56,1024]{2,1,0:T(8,128)(2,1)}, u32[]{:S(2)}, u32[]{:S(2)}) %all-to-all-start.8) | async-done | bytes 3670048 | tf_op jit(solution)/shard_map/all_to_all | solution.py:734
  593.6 18.9 %reduce-scatter.3.cloned.1.call-done = bf16[224,1024]{1,0:T(8,128)(2,1)} async-done(((bf16[7168,1024]{1,0:T(8,128)(2,1)}), bf16[224,1024]{1,0:T(8,128)(2,1)}) %reduce-scatter.3.cloned.1.call-update) | async-done | bytes 458768 | tf_op jit(solution)/shard_map/reduce_scatter | solution.py:692
  620.1 88.5 %reduce-scatter.5.cloned.1.call-done = bf16[128,1024]{1,0:T(8,128)(2,1)} async-done(((bf16[4096,1024]{1,0:T(8,128)(2,1)}), bf16[128,1024]{1,0:T(8,128)(2,1)}) %reduce-scatter.5.cloned.1.call-update) | async-done | bytes 262160 | tf_op jit(solution)/shard_map/reduce_scatter | solution.py:692
  (342 shorter events, 215.4 us)
Async XLA Ops:
  7.2 60.1 %all-gather.9.cloned.1.call-start = ((), (), s32[]{:S(2)}) async-start(), calls=%async_computation.13 | async-start | bytes 3784704 | tf_op jit(solution)/shard_map/all_gather | solution.py:643
  18.7 96.6 %all-gather.13.cloned.1.call-start = ((), (), s32[]{:S(2)}) async-start(), calls=%async_computation.15 | async-start | bytes 3784704 | tf_op jit(solution)/shard_map/all_gather | solution.py:643
  19.4 165.8 %all-gather.11.cloned.1.call-start = ((), (), s32[]{:S(2)}) async-start(), calls=%async_computation.14 | async-start | bytes 9732096 | tf_op jit(solution)/shard_map/all_gather | solution.py:643
  21.3 8.0 %collective-permute-start.2 = (bf16[144,1024]{1,0:T(8,128)(2,1)S(1)}, bf16[144,1024]{1,0:T(8,128)(2,1)S(1)}, u32[]{:S(2)}, u32[]{:S(2)}) collective-permute-start(bf16[144,1024]{1,0:T(8,128)(2,1)S(1)} %pad_maximum_fusion.1), channel_id=1, source_target_pairs={{0,64},{64,0},{1,65},{65,1},{2,66},{66,2},{3,67},{67,3},{4,68},{68... | collective-permute-start | bytes 884744 | tf_op jit(solution)/shard_map/ppermute | solution.py:45
  31.2 240.1 %all-gather.15.cloned.1.call-start = ((), (), s32[]{:S(2)}) async-start(), calls=%async_computation.16 | async-start | bytes 9732096 | tf_op jit(solution)/shard_map/all_gather | solution.py:643
  117.9 7.2 collective-permute-start.1
  129.6 24.9 %all-to-all-start = ((bf16[32,144,128]{2,1,0:T(8,128)(2,1)}), bf16[32,144,128]{2,1,0:T(8,128)(2,1)S(1)}, u32[]{:S(2)}, u32[]{:S(2)}) async-start(bf16[32,144,128]{2,1,0:T(8,128)(2,1)} %shard_map.203), calls=%async_computation | async-start | bytes 2359296 | tf_op jit(solution)/shard_map/all_to_all | solution.py:535
  187.6 7.4 %collective-permute-start.3 = (bf16[64,1024]{1,0:T(8,128)(2,1)}, bf16[64,1024]{1,0:T(8,128)(2,1)S(1)}, u32[]{:S(2)}, u32[]{:S(2)}) collective-permute-start(bf16[64,1024]{1,0:T(8,128)(2,1)} %get-tuple-element.53), channel_id=1, source_target_pairs={{0,32},{32,0},{1,33},{33,1},{2,34},{34,2},{3,35},{35,3},{4,36},{36... | collective-permute-start | bytes 393224 | tf_op jit(solution)/shard_map/ppermute | solution.py:45
  196.5 6.6 collective-permute-start.4
  209.2 6.8 collective-permute-start.5
  217.4 6.6 collective-permute-start.6
  267.4 11.7 %all-to-all-start.3 = ((bf16[32,16,128]{2,1,0:T(8,128)(2,1)}), bf16[32,16,128]{2,1,0:T(8,128)(2,1)S(1)}, u32[]{:S(2)}, u32[]{:S(2)}) async-start(bf16[32,16,128]{2,1,0:T(8,128)(2,1)} %get-tuple-element.56), calls=%async_computation.3 | async-start | bytes 262144 | tf_op jit(solution)/shard_map/all_to_all | solution.py:535
  282.2 7.2 collective-permute-start.7
  290.9 6.6 collective-permute-start.8
  303.5 6.8 collective-permute-start.9
  311.4 6.6 collective-permute-start.11
  330.9 6.8 collective-permute-start.12
  340.1 6.6 collective-permute-start.13
  378.2 22.4 %all-to-all-start.5 = ((bf16[32,144,128]{2,1,0:T(8,128)(2,1)}), bf16[32,144,128]{2,1,0:T(8,128)(2,1)S(1)}, u32[]{:S(2)}, u32[]{:S(2)}) async-start(bf16[32,144,128]{2,1,0:T(8,128)(2,1)} %shard_map.213), calls=%async_computation.5 | async-start | bytes 2359296 | tf_op jit(solution)/shard_map/all_to_all | solution.py:535
  382.3 230.2 %reduce-scatter.3.cloned.1.call-start = ((), (), s32[]{:S(2)}) async-start(), calls=%async_computation.11 | async-start | bytes 15138816 | tf_op jit(solution)/shard_map/reduce_scatter | solution.py:692
  407.8 7.4 %collective-permute-start.14 = (bf16[64,1024]{1,0:T(8,128)(2,1)}, bf16[64,1024]{1,0:T(8,128)(2,1)S(1)}, u32[]{:S(2)}, u32[]{:S(2)}) collective-permute-start(bf16[64,1024]{1,0:T(8,128)(2,1)} %get-tuple-element.70), channel_id=1, source_target_pairs={{0,32},{32,0},{1,33},{33,1},{2,34},{34,2},{3,35},{35,3},{4,36},{36... | collective-permute-start | bytes 393224 | tf_op jit(solution)/shard_map/ppermute | solution.py:45
  417.7 6.6 collective-permute-start.15
  437.3 14.7 %collective-permute-start.16 = (bf16[64,1024]{1,0:T(8,128)(2,1)}, bf16[64,1024]{1,0:T(8,128)(2,1)S(1)}, u32[]{:S(2)}, u32[]{:S(2)}) collective-permute-start(bf16[64,1024]{1,0:T(8,128)(2,1)} %get-tuple-element.74), channel_id=1, source_target_pairs={{0,32},{32,0},{1,33},{33,1},{2,34},{34,2},{3,35},{35,3},{4,36},{36... | collective-permute-start | bytes 393224 | tf_op jit(solution)/shard_map/ppermute | solution.py:45
  466.3 242.3 %reduce-scatter.5.cloned.1.call-start = ((), (), s32[]{:S(2)}) async-start(), calls=%async_computation.12 | async-start | bytes 8650752 | tf_op jit(solution)/shard_map/reduce_scatter | solution.py:692
  523.9 7.5 %collective-permute-start.18 = (bf16[64,1024]{1,0:T(8,128)(2,1)}, bf16[64,1024]{1,0:T(8,128)(2,1)S(1)}, u32[]{:S(2)}, u32[]{:S(2)}) collective-permute-start(bf16[64,1024]{1,0:T(8,128)(2,1)} %get-tuple-element.80), channel_id=1, source_target_pairs={{0,32},{32,0},{1,33},{33,1},{2,34},{34,2},{3,35},{35,3},{4,36},{36... | collective-permute-start | bytes 393224 | tf_op jit(solution)/shard_map/ppermute | solution.py:45
  537.3 53.4 %all-to-all-start.8 = ((bf16[32,56,1024]{2,1,0:T(8,128)(2,1)}), bf16[32,56,1024]{2,1,0:T(8,128)(2,1)}, u32[]{:S(2)}, u32[]{:S(2)}) async-start(bf16[32,56,1024]{2,1,0:T(8,128)(2,1)} %pad_maximum_fusion), calls=%async_computation.8 | async-start | bytes 7340032 | tf_op jit(solution)/shard_map/all_to_all | solution.py:734
  542.3 7.5 %collective-permute-start.10 = (bf16[64,1024]{1,0:T(8,128)(2,1)S(1)}, bf16[64,1024]{1,0:T(8,128)(2,1)S(1)}, u32[]{:S(2)}, u32[]{:S(2)}) collective-permute-start(bf16[64,1024]{1,0:T(8,128)(2,1)S(1)} %get-tuple-element.141), channel_id=1, source_target_pairs={{0,64},{64,0},{1,65},{65,1},{2,66},{66,2},{3,67},{67,3},{4,68},{68... | collective-permute-start | bytes 393224 | tf_op jit(solution)/shard_map/ppermute | solution.py:45
  545.7 9.3 %collective-permute-start.19 = (f32[64,1024]{1,0:T(8,128)S(1)}, f32[64,1024]{1,0:T(8,128)S(1)}, u32[]{:S(2)}, u32[]{:S(2)}) collective-permute-start(f32[64,1024]{1,0:T(8,128)S(1)} %get-tuple-element.139), channel_id=1, source_target_pairs={{0,64},{64,0},{1,65},{65,1},{2,66},{66,2},{3,67},{67,3},{4,68},{68... | collective-permute-start | bytes 786440 | tf_op jit(solution)/shard_map/ppermute | solution.py:45
  614.7 96.4 %collective-permute-start.23 = (bf16[1,352]{1,0:T(2,128)(2,1)S(1)}, bf16[1,352]{1,0:T(2,128)(2,1)S(1)}, u32[]{:S(2)}, u32[]{:S(2)}) collective-permute-start(bf16[1,352]{1,0:T(2,128)(2,1)S(1)} %broadcast_select_fusion.11), channel_id=1, source_target_pairs={{0,64},{64,0},{1,65},{65,1},{2,66},{66,2},{3,67},{67,3},{4,68},{68... | collective-permute-start | bytes 2120 | tf_op jit(solution)/shard_map/ppermute | solution.py:45
  617.1 103.0 %collective-permute-start.21 = (bf16[16,1024]{1,0:T(8,128)(2,1)S(1)}, bf16[16,1024]{1,0:T(8,128)(2,1)S(1)}, u32[]{:S(2)}, u32[]{:S(2)}) collective-permute-start(bf16[16,1024]{1,0:T(8,128)(2,1)S(1)} %broadcast_select_fusion.10), channel_id=1, source_target_pairs={{0,64},{64,0},{1,65},{65,1},{2,66},{66,2},{3,67},{67,3},{4,68},{68... | collective-permute-start | bytes 98312 | tf_op jit(solution)/shard_map/ppermute | solution.py:45
  618.4 103.0 %collective-permute-start.20 = (bf16[48,1024]{1,0:T(8,128)(2,1)S(1)}, bf16[48,1024]{1,0:T(8,128)(2,1)S(1)}, u32[]{:S(2)}, u32[]{:S(2)}) collective-permute-start(bf16[48,1024]{1,0:T(8,128)(2,1)S(1)} %broadcast_select_fusion.9), channel_id=1, source_target_pairs={{0,64},{64,0},{1,65},{65,1},{2,66},{66,2},{3,67},{67,3},{4,68},{68... | collective-permute-start | bytes 294920 | tf_op jit(solution)/shard_map/ppermute | solution.py:45
  709.7 13.5 %collective-permute-start.22 = (bf16[128,1024]{1,0:T(8,128)(2,1)S(1)}, bf16[128,1024]{1,0:T(8,128)(2,1)S(1)}, u32[]{:S(2)}, u32[]{:S(2)}) collective-permute-start(bf16[128,1024]{1,0:T(8,128)(2,1)S(1)} %broadcast_select_fusion.2), channel_id=1, source_target_pairs={{0,64},{64,0},{1,65},{65,1},{2,66},{66,2},{3,67},{67,3},{4,68},{68... | collective-permute-start | bytes 786440 | tf_op jit(solution)/shard_map/ppermute | solution.py:45
  (41 other events, 597.3 us)
Sparse Core Ops, SparseCore 0:
  18.8 48.4 all-gather.8
  70.1 45.1 all-gather.12
  117.6 67.5 all-gather.10
  187.3 59.7 all-gather.14
  466.4 145.9 reduce-scatter.2
  616.5 92.0 reduce-scatter.4

commit v2 on v1

v2 whole, which is shorter than its diff:
```python
import jax
import jax.numpy as jnp
from jax import lax
from jax.experimental import pallas as pl
from jax.experimental.pallas import tpu as pltpu
from jax.sharding import PartitionSpec as P

HEAD = 64
EPS = 1e-06
NEG_FILL = -1e30
ROOT_HALF = 0.7071067811865476
INV_ROOT_TAU = 0.3989422804014327
SCALE = HEAD ** (-0.5)
BF = jnp.bfloat16
F32 = jnp.float32
MIB = 1024 * 1024

ROWS = 64
BOTH = 128
WIDE = 32
HEADS_DEV = 8
QUARTERS = 4
HALF_W = 512
MODEL = 1024
HIDDEN = 2048
SEND_ROWS = 144
BLOCKS_Q = 4
CHUNKS = 8


def params(limit=56):
    return pltpu.CompilerParams(vmem_limit_bytes=limit * MIB)


def cost(micros):
    return pl.CostEstimate(flops=int(micros * 1e9), bytes_accessed=100000, transcendentals=0)


def whole(shape):
    count = len(shape)
    return pl.BlockSpec(shape, lambda *g: (0,) * count)


def swap(block, axis):
    return lax.ppermute(block, axis, [(0, 1), (1, 0)])


def nt(left, right):
    return lax.dot_general(left, right, (((1,), (1,)), ((), ())), preferred_element_type=F32)


def tn(left, right):
    return lax.dot_general(left, right, (((0,), (0,)), ((), ())), preferred_element_type=F32)


def nn(left, right):
    return jnp.dot(left, right, preferred_element_type=F32)


def low_lanes(shape):
    return lax.broadcasted_iota(jnp.int32, shape, len(shape) - 1) < HEAD


def turn(tile):
    return pltpu.roll(tile, HEAD, 1)


def pack_heads(tile, out_ref, pair, row0):
    rolled = turn(tile)
    for quarter in range(QUARTERS):
        first = slice(quarter * 32, quarter * 32 + 16)
        second = slice(quarter * 32 + 16, quarter * 32 + 32)
        mask = low_lanes((16, 128))
        even = jnp.where(mask, tile[first], rolled[second])
        odd = jnp.where(mask, rolled[first], tile[second])
        out_ref[(2 * pair) * QUARTERS + quarter, row0 : row0 + 16, :] = even.astype(BF)
        out_ref[(2 * pair + 1) * QUARTERS + quarter, row0 : row0 + 16, :] = odd.astype(BF)


def unpack_heads(in_ref, row0):
    mask = low_lanes((16, 128))
    columns = []
    for pair in range(HEADS_DEV // 2):
        pieces = []
        for quarter in range(QUARTERS):
            even = in_ref[(2 * pair) * QUARTERS + quarter, row0 : row0 + 16, :].astype(F32)
            odd = in_ref[(2 * pair + 1) * QUARTERS + quarter, row0 : row0 + 16, :].astype(F32)
            pieces.append(jnp.where(mask, even, turn(odd)))
            pieces.append(jnp.where(mask, turn(even), odd))
        columns.append(jnp.concatenate(pieces, axis=0))
    return jnp.concatenate(columns, axis=1)


def norm_parts(rows_in):
    centre = jnp.mean(rows_in, axis=-1, keepdims=True)
    centred = rows_in - centre
    spread = jnp.mean(centred * centred, axis=-1, keepdims=True)
    rstd_rows = lax.rsqrt(spread + EPS)
    return centred * rstd_rows, rstd_rows


def norm_back(grad_rows, normal_rows, rstd_rows, gain_row):
    scaled = grad_rows * gain_row
    first_mean = jnp.mean(scaled, axis=-1, keepdims=True)
    second_mean = jnp.mean(scaled * normal_rows, axis=-1, keepdims=True)
    return rstd_rows * (scaled - first_mean - normal_rows * second_mean)


def joined(own_ref, recv_ref):
    recv = jnp.concatenate([recv_ref[ROWS:], recv_ref[:ROWS]], axis=0)
    return own_ref[...].astype(F32) + recv.astype(F32)


def column_sum(rows):
    return jnp.sum(rows[:ROWS], axis=0, keepdims=True) + jnp.sum(rows[ROWS:], axis=0, keepdims=True)


GAIN_A, GAIN_C, SHIFT_A, SHIFT_O, SHIFT_C, SHIFT_M, SCALE_A, SCALE_M = range(8)


def row_of(ref, at):
    return ref[at : at + 1, :]


def qkv_weight(ref, which):
    if which < 2:
        return ref[:, 0:32, which * HALF_W : which * HALF_W + HALF_W].reshape(MODEL, HALF_W)
    parts = [ref[:, 32:48, 0:HALF_W], ref[:, 32:48, HALF_W:MODEL]]
    return jnp.concatenate(parts, axis=1).reshape(MODEL, HALF_W)


def project_and_pack(rows, vec_ref, bias_ref, weight_ref, out_ref, rows_ref, normed_ref):
    rows_ref[...] = rows
    hat, _ = norm_parts(rows.astype(F32))
    normed = (hat * row_of(vec_ref, GAIN_A) + row_of(vec_ref, SHIFT_A)).astype(BF)
    normed_ref[...] = normed
    queries = nn(normed, qkv_weight(weight_ref, 0)) + bias_ref[0:1, :]
    keys = nn(normed, qkv_weight(weight_ref, 1))
    values = nn(normed, qkv_weight(weight_ref, 2)) + bias_ref[1:2, :]
    mask = low_lanes((BOTH, 128))
    for pair in range(HEADS_DEV // 2):
        columns = slice(pair * 128, pair * 128 + 128)
        key_tile, value_tile, query_tile = keys[:, columns], values[:, columns], queries[:, columns]
        even = jnp.where(mask, key_tile, turn(value_tile)).astype(BF)
        odd = jnp.where(mask, turn(key_tile), value_tile).astype(BF)
        for quarter in range(QUARTERS):
            out_ref[(2 * pair) * QUARTERS + quarter, 0:BOTH, :] = even
            out_ref[(2 * pair + 1) * QUARTERS + quarter, 0:BOTH, :] = odd
        pack_heads(query_tile, out_ref, pair, BOTH)


def qkv_first_kernel(own_ref, other_ref, vec_ref, bias_ref, weight_ref, out_ref, rows_ref, normed_ref):
    rows = jnp.concatenate([own_ref[...], other_ref[...]], axis=0)
    project_and_pack(rows, vec_ref, bias_ref, weight_ref, out_ref, rows_ref, normed_ref)


def qkv_next_kernel(
    middle_ref, mlp_own_ref, mlp_recv_ref, before_ref, vec_ref, bias_ref, weight_ref,
    out_ref, rows_ref, normed_ref,
):
    branch = joined(mlp_own_ref, mlp_recv_ref) + row_of(before_ref, SHIFT_M)
    rows = (middle_ref[...] + row_of(before_ref, SCALE_M) * branch).astype(BF)
    project_and_pack(rows, vec_ref, bias_ref, weight_ref, out_ref, rows_ref, normed_ref)


def qkv_block(index):
    return pl.BlockSpec((WIDE, 48, MODEL), lambda i: (0, index, 0))


def qkv_call(inputs, small, weight, block_at):
    vec, bias, _ = small
    first = len(inputs) == 2
    return pl.pallas_call(
        qkv_first_kernel if first else qkv_next_kernel,
        grid=(1,),
        in_specs=[whole(part.shape) for part in inputs]
        + [whole((8, MODEL)), whole((2, HALF_W)), qkv_block(block_at)],
        out_specs=[whole((WIDE, SEND_ROWS, 128)), whole((BOTH, MODEL)), whole((BOTH, MODEL))],
        out_shape=[
            jax.ShapeDtypeStruct((WIDE, SEND_ROWS, 128), BF),
            jax.ShapeDtypeStruct((BOTH, MODEL), BF),
            jax.ShapeDtypeStruct((BOTH, MODEL), BF),
        ],
        compiler_params=params(),
        cost_estimate=cost(5),
    )(*inputs, vec, bias, weight)


def query_tiles(packed):
    mask = low_lanes((128, 128))
    return jnp.concatenate(
        [jnp.where(mask, packed, 0.0), jnp.where(mask, turn(packed), 0.0)], axis=0
    )


def key_chunk(recv_ref, chunk):
    half, group = chunk // 4, chunk % 4
    block = recv_ref[group * 8 : group * 8 + 8, half * ROWS : half * ROWS + ROWS, :]
    return block.reshape(512, 128)


def lane_tiles(fn, block):
    return fn(fn(block[:, 0:128], block[:, 128:256]), fn(block[:, 256:384], block[:, 384:512]))


def attend_kernel(
    flag_ref, recv_ref, key_id_ref, query_id_ref, out_ref, keep_ref, lse_ref,
    score_ref, top_ref, total_ref, acc_ref,
):
    at = pl.program_id(0)
    packed = recv_ref[pl.ds(at * 8, 8), BOTH : BOTH + 16, :].astype(F32).reshape(128, 128)
    queries = (query_tiles(packed) * SCALE).astype(BF)
    query_ids = query_id_ref[0]
    top_ref[...] = jnp.full((256, 128), NEG_FILL, F32)
    total_ref[...] = jnp.zeros((256, 128), F32)
    acc_ref[...] = jnp.zeros((256, 128), F32)
    for chunk in range(CHUNKS):

        @pl.when(flag_ref[at, chunk] != 0)
        def _():
            scores = nt(queries, key_chunk(recv_ref, chunk))
            scores = jnp.where(query_ids == key_id_ref[chunk], scores, NEG_FILL)
            score_ref[chunk] = scores
            top_ref[...] = jnp.maximum(top_ref[...], lane_tiles(jnp.maximum, scores))

    top = jnp.max(top_ref[...], axis=1, keepdims=True)
    for chunk in range(CHUNKS):

        @pl.when(flag_ref[at, chunk] != 0)
        def _():
            expo = jnp.exp(score_ref[chunk] - top)
            total_ref[...] += lane_tiles(jnp.add, expo)
            acc_ref[...] += nn(expo.astype(BF), key_chunk(recv_ref, chunk))

    total = jnp.sum(total_ref[...], axis=1, keepdims=True)
    mixture = acc_ref[...] / total
    lse_ref[...] = top + jnp.log(total)
    mask = low_lanes((128, 128))
    joined = jnp.where(mask, turn(mixture[:128]), mixture[128:]).reshape(8, 16, 128)
    keep_ref[...] = joined
    out_ref[...] = joined.astype(BF)


def attend_call(flags, recv, key_ids, query_ids):
    return pl.pallas_call(
        attend_kernel,
        grid_spec=pltpu.PrefetchScalarGridSpec(
            num_scalar_prefetch=1,
            grid=(BLOCKS_Q,),
            in_specs=[
                pl.BlockSpec((WIDE, SEND_ROWS, 128), lambda i, f: (0, 0, 0)),
                pl.BlockSpec((CHUNKS, 1, 512), lambda i, f: (0, 0, 0)),
                pl.BlockSpec((1, 256, 1), lambda i, f: (i, 0, 0)),
            ],
            out_specs=[
                pl.BlockSpec((8, 16, 128), lambda i, f: (i, 0, 0)),
                pl.BlockSpec((8, 16, 128), lambda i, f: (i, 0, 0)),
                pl.BlockSpec((256, 1), lambda i, f: (i, 0)),
            ],
            scratch_shapes=[
                pltpu.VMEM((CHUNKS, 256, 512), F32),
                pltpu.VMEM((256, 128), F32),
                pltpu.VMEM((256, 128), F32),
                pltpu.VMEM((256, 128), F32),
            ],
        ),
        out_shape=[
            jax.ShapeDtypeStruct((WIDE, 16, 128), BF),
            jax.ShapeDtypeStruct((WIDE, 16, 128), F32),
            jax.ShapeDtypeStruct((1024, 1), F32),
        ],
        compiler_params=params(),
        cost_estimate=cost(12),
    )(flags, recv, key_ids, query_ids)


def attend_back_kernel(
    flag_ref, recv_ref, grad_ref, keep_ref, lse_ref, key_id_ref, query_id_ref, out_ref,
    key_grad_ref, query_grad_ref,
):
    at = pl.program_id(0)

    @pl.when(at == 0)
    def _():
        key_grad_ref[...] = jnp.zeros((WIDE, BOTH, 128), F32)

    mask = low_lanes((128, 128))
    packed = recv_ref[pl.ds(at * 8, 8), BOTH : BOTH + 16, :].astype(F32).reshape(128, 128)
    queries = (query_tiles(packed) * SCALE).astype(BF)
    grads = grad_ref[...].astype(F32).reshape(128, 128)
    grad_tile = jnp.concatenate(
        [jnp.where(mask, 0.0, turn(grads)), jnp.where(mask, 0.0, grads)], axis=0
    ).astype(BF)
    product = grads * keep_ref[...].reshape(128, 128)
    delta = jnp.concatenate(
        [
            jnp.sum(jnp.where(mask, product, 0.0), axis=1, keepdims=True),
            jnp.sum(jnp.where(mask, 0.0, product), axis=1, keepdims=True),
        ],
        axis=0,
    )
    lse = lse_ref[...]
    query_ids = query_id_ref[0]
    both = jnp.concatenate([queries, grad_tile], axis=0)
    query_grad_ref[...] = jnp.zeros((256, 128), F32)
    for chunk in range(CHUNKS):

        @pl.when(flag_ref[at, chunk] != 0)
        def _():
            half, group = chunk // 4, chunk % 4
            keys = key_chunk(recv_ref, chunk)
            scores = nt(queries, keys)
            scores = jnp.where(query_ids == key_id_ref[chunk], scores, NEG_FILL)
            chance = jnp.exp(scores - lse)
            grad_scores = (chance * (nt(grad_tile, keys) - delta)).astype(BF)
            query_grad_ref[...] += nn(grad_scores, keys)
            stacked = jnp.concatenate([grad_scores, chance.astype(BF)], axis=0)
            key_grad_ref[group * 8 : group * 8 + 8, half * ROWS : half * ROWS + ROWS, :] += tn(
                stacked, both
            ).reshape(8, ROWS, 128)

    query_grad = query_grad_ref[...] * SCALE
    joined = jnp.where(mask, query_grad[:128], turn(query_grad[128:]))
    out_ref[pl.ds(at * 8, 8), BOTH : BOTH + 16, :] = joined.astype(BF).reshape(8, 16, 128)

    @pl.when(at == BLOCKS_Q - 1)
    def _():
        out_ref[:, 0:BOTH, :] = key_grad_ref[...].astype(BF)


def attend_back_call(flags, recv, grads, keep, lse, key_ids, query_ids):
    return pl.pallas_call(
        attend_back_kernel,
        grid_spec=pltpu.PrefetchScalarGridSpec(
            num_scalar_prefetch=1,
            grid=(BLOCKS_Q,),
            in_specs=[
                pl.BlockSpec((WIDE, SEND_ROWS, 128), lambda i, f: (0, 0, 0)),
                pl.BlockSpec((8, 16, 128), lambda i, f: (i, 0, 0)),
                pl.BlockSpec((8, 16, 128), lambda i, f: (i, 0, 0)),
                pl.BlockSpec((256, 1), lambda i, f: (i, 0)),
                pl.BlockSpec((CHUNKS, 1, 512), lambda i, f: (0, 0, 0)),
                pl.BlockSpec((1, 256, 1), lambda i, f: (i, 0, 0)),
            ],
            out_specs=pl.BlockSpec((WIDE, SEND_ROWS, 128), lambda i, f: (0, 0, 0)),
            scratch_shapes=[
                pltpu.VMEM((WIDE, BOTH, 128), F32),
                pltpu.VMEM((256, 128), F32),
            ],
        ),
        out_shape=jax.ShapeDtypeStruct((WIDE, SEND_ROWS, 128), BF),
        compiler_params=params(),
        cost_estimate=cost(16),
    )(flags, recv, grads, keep, lse, key_ids, query_ids)


def out_kernel(recv_ref, weight_ref, mixture_ref, part_ref):
    mixture = unpack_heads(recv_ref, 0).astype(BF)
    mixture_ref[...] = mixture
    part_ref[...] = nn(mixture, weight_ref[...].reshape(HALF_W, MODEL)).astype(BF)


def out_call(recv, weights):
    return pl.pallas_call(
        out_kernel,
        grid=(1,),
        in_specs=[whole((WIDE, 16, 128)), pl.BlockSpec((WIDE, 16, MODEL), lambda i: (0, 8, 0))],
        out_specs=[whole((BOTH, HALF_W)), whole((BOTH, MODEL))],
        out_shape=[
            jax.ShapeDtypeStruct((BOTH, HALF_W), BF),
            jax.ShapeDtypeStruct((BOTH, MODEL), BF),
        ],
        compiler_params=params(),
        cost_estimate=cost(2.5),
    )(recv, weights)


def mlp_kernel(
    rows_ref, part_own_ref, part_recv_ref, vec_ref, bias_ref, one_ref, two_ref,
    middle_ref, normed_ref, pre_ref, act_ref, out_ref, acc_ref,
):
    at = pl.program_id(0)

    @pl.when(at == 0)
    def _():
        branch = joined(part_own_ref, part_recv_ref) + row_of(vec_ref, SHIFT_O)
        middle = rows_ref[...].astype(F32) + row_of(vec_ref, SCALE_A) * branch
        middle_ref[...] = middle
        hat, _ = norm_parts(middle)
        normed_ref[...] = (hat * row_of(vec_ref, GAIN_C) + row_of(vec_ref, SHIFT_C)).astype(BF)

    pre = nn(normed_ref[...], one_ref[...].reshape(MODEL, MODEL)) + bias_ref[...]
    act = (0.5 * pre * (1.0 + lax.erf(pre * ROOT_HALF))).astype(BF)
    pre_ref[...] = pre
    act_ref[...] = act
    part = nn(act, two_ref[...].reshape(MODEL, MODEL))

    @pl.when(at == 0)
    def _():
        acc_ref[...] = part

    @pl.when(at == 1)
    def _():
        out_ref[...] = (acc_ref[...] + part).astype(BF)


def mlp_call(rows, part_own, part_recv, small, weights):
    vec, _, bias = small
    return pl.pallas_call(
        mlp_kernel,
        grid=(2,),
        in_specs=[
            whole((BOTH, MODEL)),
            whole((BOTH, MODEL)),
            whole((BOTH, MODEL)),
            whole((8, MODEL)),
            pl.BlockSpec((1, MODEL), lambda j: (0, j)),
            pl.BlockSpec((WIDE, 32, MODEL), lambda j: (0, 2 + j, 0)),
            pl.BlockSpec((16, 64, MODEL), lambda j: (j, 0, 0)),
        ],
        out_specs=[
            whole((BOTH, MODEL)),
            whole((BOTH, MODEL)),
            pl.BlockSpec((BOTH, MODEL), lambda j: (0, j)),
            pl.BlockSpec((BOTH, MODEL), lambda j: (0, j)),
            whole((BOTH, MODEL)),
        ],
        out_shape=[
            jax.ShapeDtypeStruct((BOTH, MODEL), F32),
            jax.ShapeDtypeStruct((BOTH, MODEL), BF),
            jax.ShapeDtypeStruct((BOTH, HIDDEN), F32),
            jax.ShapeDtypeStruct((BOTH, HIDDEN), BF),
            jax.ShapeDtypeStruct((BOTH, MODEL), BF),
        ],
        scratch_shapes=[pltpu.VMEM((BOTH, MODEL), F32)],
        compiler_params=params(),
        cost_estimate=cost(7),
    )(rows, part_own, part_recv, vec, bias, weights, weights)


def mlp_back_steps(
    grad, vec_ref, mlp_own_ref, mlp_recv_ref, pre_ref, one_ref, two_ref,
    grad_ref, low_ref, grad_pre_ref, out_ref, sums_ref, acc_ref,
):
    at = pl.program_id(0)

    @pl.when(at == 0)
    def _():
        rows = grad()
        grad_ref[...] = rows
        rows = rows.astype(F32)
        scaled = rows * row_of(vec_ref, SCALE_M)
        low_ref[...] = scaled.astype(BF)
        branch = joined(mlp_own_ref, mlp_recv_ref) + row_of(vec_ref, SHIFT_M)
        sums_ref[...] = jnp.zeros((8, MODEL), F32)
        sums_ref[0:1, :] = column_sum(scaled)
        sums_ref[1:2, :] = column_sum(rows * branch)

    pre = pre_ref[...]
    slope = 0.5 * (1.0 + lax.erf(pre * ROOT_HALF)) + pre * jnp.exp(-0.5 * pre * pre) * INV_ROOT_TAU
    grad_pre = (nt(low_ref[...], two_ref[...].reshape(MODEL, MODEL)) * slope).astype(BF)
    grad_pre_ref[...] = grad_pre
    part = nt(grad_pre, one_ref[...].reshape(MODEL, MODEL))
    bias_sum = jnp.sum(grad_pre.astype(F32), axis=0, keepdims=True)

    @pl.when(at == 0)
    def _():
        acc_ref[...] = part
        sums_ref[2:3, :] = bias_sum

    @pl.when(at == 1)
    def _():
        out_ref[...] = (acc_ref[...] + part).astype(BF)
        sums_ref[3:4, :] = bias_sum


def mlp_back_first_kernel(own_ref, other_ref, *refs):
    mlp_back_steps(lambda: jnp.concatenate([own_ref[...], other_ref[...]], axis=0), *refs)


def mlp_back_next_kernel(middle_grad_ref, part_own_ref, part_recv_ref, rows_ref, after_ref, *refs):
    *refs, input_grad_ref, acc_ref = refs

    def grad():
        hat, rstd = norm_parts(rows_ref[...].astype(F32))
        grad_norm = joined(part_own_ref, part_recv_ref)
        total = middle_grad_ref[...] + norm_back(grad_norm, hat, rstd, row_of(after_ref, GAIN_A))
        input_grad_ref[...] = total[:ROWS]
        return total.astype(BF)

    mlp_back_steps(grad, *refs, acc_ref)


def mlp_back_call(inputs, small, mlp_own, mlp_recv, pre, weights):
    first = len(inputs) == 2
    extra = [] if first else [(ROWS, MODEL)]
    return pl.pallas_call(
        mlp_back_first_kernel if first else mlp_back_next_kernel,
        grid=(2,),
        in_specs=[whole(part.shape) for part in inputs]
        + [
            whole((8, MODEL)),
            whole((BOTH, MODEL)),
            whole((BOTH, MODEL)),
            pl.BlockSpec((BOTH, MODEL), lambda j: (0, j)),
            pl.BlockSpec((WIDE, 32, MODEL), lambda j: (0, 2 + j, 0)),
            pl.BlockSpec((16, 64, MODEL), lambda j: (j, 0, 0)),
        ],
        out_specs=[
            whole((BOTH, MODEL)),
            whole((BOTH, MODEL)),
            pl.BlockSpec((BOTH, MODEL), lambda j: (0, j)),
            whole((BOTH, MODEL)),
            whole((8, MODEL)),
        ]
        + [whole(shape) for shape in extra],
        out_shape=[
            jax.ShapeDtypeStruct((BOTH, MODEL), BF),
            jax.ShapeDtypeStruct((BOTH, MODEL), BF),
            jax.ShapeDtypeStruct((BOTH, HIDDEN), BF),
            jax.ShapeDtypeStruct((BOTH, MODEL), BF),
            jax.ShapeDtypeStruct((8, MODEL), F32),
        ]
        + [jax.ShapeDtypeStruct(shape, F32) for shape in extra],
        scratch_shapes=[pltpu.VMEM((BOTH, MODEL), F32)],
        compiler_params=params(),
        cost_estimate=cost(8),
    )(*inputs, small[0], mlp_own, mlp_recv, pre, weights, weights)


PACK_ROWS = 240


def buffer_args(buffer, count_inputs):
    if buffer is None:
        return [], [], {}
    return [buffer], [pl.BlockSpec(memory_space=pl.ANY)], {count_inputs: 0}


def mlp_weight_kernel(low_ref, normed_ref, act_ref, grad_pre_ref, after_ref, *refs):
    grad_ref = refs[-1]
    at = pl.program_id(0)
    grad_two = tn(act_ref[...], low_ref[...]).astype(BF).reshape(16, 64, MODEL)
    grad_one = tn(normed_ref[...], grad_pre_ref[...]).astype(BF).reshape(WIDE, 32, MODEL)

    @pl.when(at == 0)
    def _():
        grad_ref[0:16, 0:64, :] = grad_two
        grad_ref[:, 64:96, :] = grad_one

    @pl.when(at == 1)
    def _():
        grad_ref[16:32, 0:64, :] = grad_two
        grad_ref[:, 96:128, :] = grad_one


def mlp_weight_call(low, normed, act, grad_pre, after, buffer):
    more, more_specs, aliases = buffer_args(buffer, 5)
    rows = 128 if buffer is None else PACK_ROWS
    return pl.pallas_call(
        mlp_weight_kernel,
        grid=(2,),
        in_specs=[
            whole((BOTH, MODEL)),
            whole((BOTH, MODEL)),
            pl.BlockSpec((BOTH, MODEL), lambda j: (0, j)),
            pl.BlockSpec((BOTH, MODEL), lambda j: (0, j)),
            pl.BlockSpec(memory_space=pl.ANY),
        ]
        + more_specs,
        out_specs=whole((WIDE, 128, MODEL)),
        out_shape=jax.ShapeDtypeStruct((WIDE, rows, MODEL), BF),
        input_output_aliases=aliases,
        compiler_params=params(),
        cost_estimate=cost(8),
    )(low, normed, act, grad_pre, after, *more)


def out_back_kernel(
    grad_ref, part_own_ref, part_recv_ref, middle_ref, proj_own_ref, proj_recv_ref, vec_ref,
    weight_ref, middle_grad_ref, send_ref, low_ref, sums_ref,
):
    hat, rstd = norm_parts(middle_ref[...])
    grad_norm = joined(part_own_ref, part_recv_ref)
    total = grad_ref[...].astype(F32) + norm_back(grad_norm, hat, rstd, row_of(vec_ref, GAIN_C))
    middle_grad_ref[...] = total
    scaled = total * row_of(vec_ref, SCALE_A)
    rows = scaled.astype(BF)
    low_ref[...] = rows
    grad_mix = nt(rows, weight_ref[...].reshape(HALF_W, MODEL))
    for pair in range(HEADS_DEV // 2):
        pack_heads(grad_mix[:, pair * 128 : pair * 128 + 128], send_ref, pair, 0)
    branch = joined(proj_own_ref, proj_recv_ref) + row_of(vec_ref, SHIFT_O)
    sums_ref[...] = jnp.zeros((8, MODEL), F32)
    sums_ref[0:1, :] = column_sum(grad_norm * hat)
    sums_ref[1:2, :] = column_sum(grad_norm)
    sums_ref[2:3, :] = column_sum(scaled)
    sums_ref[3:4, :] = column_sum(total * branch)


def out_back_call(grad, part_own, part_recv, middle, proj_own, proj_recv, small, weights):
    return pl.pallas_call(
        out_back_kernel,
        grid=(1,),
        in_specs=[whole((BOTH, MODEL))] * 6
        + [whole((8, MODEL)), pl.BlockSpec((WIDE, 16, MODEL), lambda i: (0, 8, 0))],
        out_specs=[
            whole((BOTH, MODEL)), whole((WIDE, 16, 128)), whole((BOTH, MODEL)), whole((8, MODEL))
        ],
        out_shape=[
            jax.ShapeDtypeStruct((BOTH, MODEL), F32),
            jax.ShapeDtypeStruct((WIDE, 16, 128), BF),
            jax.ShapeDtypeStruct((BOTH, MODEL), BF),
            jax.ShapeDtypeStruct((8, MODEL), F32),
        ],
        compiler_params=params(),
        cost_estimate=cost(4),
    )(grad, part_own, part_recv, middle, proj_own, proj_recv, small[0], weights)


def out_weight_kernel(mixture_ref, low_ref, grad_ref):
    grad_ref[...] = tn(mixture_ref[...], low_ref[...]).astype(BF).reshape(WIDE, 16, MODEL)


def out_weight_last_kernel(mixture_ref, low_ref, *refs):
    *sums_refs, before_ref, buffer_ref, grad_ref = refs
    grad_ref[:, 0:16, :] = tn(mixture_ref[...], low_ref[...]).astype(BF).reshape(WIDE, 16, MODEL)
    parts = [ref[0:4, :] for ref in sums_refs] + [before_ref[0:12, :].astype(F32)]
    rows = jnp.concatenate(parts, axis=0).astype(BF)
    grad_ref[:, 16:48, :] = jnp.broadcast_to(rows[None], (WIDE, 32, MODEL))


def out_weight_call(mixture, low):
    return pl.pallas_call(
        out_weight_kernel,
        grid=(1,),
        in_specs=[whole((BOTH, HALF_W)), whole((BOTH, MODEL))],
        out_specs=pl.BlockSpec((WIDE, 16, MODEL), lambda i: (0, 8, 0)),
        out_shape=jax.ShapeDtypeStruct((WIDE, PACK_ROWS, MODEL), BF),
        compiler_params=params(),
        cost_estimate=cost(2),
    )(mixture, low)


def out_weight_last_call(mixture, low, sums, before, buffer):
    count = 3 + len(sums)
    return pl.pallas_call(
        out_weight_last_kernel,
        grid=(1,),
        in_specs=[whole((BOTH, HALF_W)), whole((BOTH, MODEL))]
        + [whole((8, MODEL)) for _ in sums]
        + [whole((16, MODEL)), pl.BlockSpec(memory_space=pl.ANY)],
        out_specs=pl.BlockSpec((WIDE, 48, MODEL), lambda i: (0, 4, 0)),
        out_shape=jax.ShapeDtypeStruct((WIDE, PACK_ROWS, MODEL), BF),
        input_output_aliases={count: 0},
        compiler_params=params(),
        cost_estimate=cost(3),
    )(mixture, low, *sums, before, buffer)


def qkv_back_kernel(recv_ref, rows_ref, vec_ref, weight_ref, part_ref, grads_ref, sums_ref):
    grad_q = unpack_heads(recv_ref, BOTH).astype(BF)
    mask = low_lanes((BOTH, 128))
    key_columns, value_columns = [], []
    for pair in range(HEADS_DEV // 2):
        sums = []
        for head in (2 * pair, 2 * pair + 1):
            total = recv_ref[head * QUARTERS, 0:BOTH, :].astype(F32)
            for quarter in range(1, QUARTERS):
                total = total + recv_ref[head * QUARTERS + quarter, 0:BOTH, :].astype(F32)
            sums.append(total)
        key_columns.append(jnp.where(mask, sums[0], turn(sums[1])))
        value_columns.append(jnp.where(mask, turn(sums[0]), sums[1]))
    grad_k = jnp.concatenate(key_columns, axis=1).astype(BF)
    grad_v = jnp.concatenate(value_columns, axis=1).astype(BF)
    grads_ref[:, 0:HALF_W] = grad_q
    grads_ref[:, HALF_W:MODEL] = grad_k
    grads_ref[:, MODEL : MODEL + HALF_W] = grad_v
    result = (
        nt(grad_q, qkv_weight(weight_ref, 0))
        + nt(grad_k, qkv_weight(weight_ref, 1))
        + nt(grad_v, qkv_weight(weight_ref, 2))
    )
    part_ref[...] = result.astype(BF)
    hat, _ = norm_parts(rows_ref[...].astype(F32))
    sums_ref[...] = jnp.zeros((8, MODEL), F32)
    sums_ref[0:1, :] = column_sum(result * hat)
    sums_ref[1:2, :] = column_sum(result)
    sums_ref[2:3, 0:HALF_W] = column_sum(grad_q.astype(F32))
    sums_ref[2:3, HALF_W:MODEL] = column_sum(grad_v.astype(F32))


def qkv_back_call(recv, rows, small, weight, block_at):
    return pl.pallas_call(
        qkv_back_kernel,
        grid=(1,),
        in_specs=[
            whole((WIDE, SEND_ROWS, 128)),
            whole((BOTH, MODEL)),
            whole((8, MODEL)),
            qkv_block(block_at),
        ],
        out_specs=[whole((BOTH, MODEL)), whole((BOTH, 3 * HALF_W)), whole((8, MODEL))],
        out_shape=[
            jax.ShapeDtypeStruct((BOTH, MODEL), BF),
            jax.ShapeDtypeStruct((BOTH, 3 * HALF_W), BF),
            jax.ShapeDtypeStruct((8, MODEL), F32),
        ],
        compiler_params=params(),
        cost_estimate=cost(5),
    )(recv, rows, small[0], weight)


def store_qkv_grads(normed_ref, grads_ref, grad_ref):
    rows = normed_ref[...]

    def part(which):
        grads = grads_ref[:, which * HALF_W : which * HALF_W + HALF_W]
        return tn(rows, grads).astype(BF).reshape(WIDE, 32, HALF_W)

    grad_ref[:, 0:32, 0:HALF_W] = part(0)
    grad_ref[:, 0:32, HALF_W:MODEL] = part(1)
    values = part(2)
    grad_ref[:, 32:48, 0:HALF_W] = values[:, 0:16]
    grad_ref[:, 32:48, HALF_W:MODEL] = values[:, 16:32]


def qkv_weight_kernel(normed_ref, grads_ref, buffer_ref, grad_ref):
    store_qkv_grads(normed_ref, grads_ref, grad_ref)


def qkv_weight_last_kernel(normed_ref, grads_ref, sums_ref, grad_ref):
    store_qkv_grads(normed_ref, grads_ref, grad_ref)
    grad_ref[:, 48:56, :] = jnp.broadcast_to(sums_ref[...].astype(BF)[None], (WIDE, 8, MODEL))


def qkv_weight_call(normed, grads, buffer):
    return pl.pallas_call(
        qkv_weight_kernel,
        grid=(1,),
        in_specs=[whole((BOTH, MODEL)), whole((BOTH, 3 * HALF_W)), pl.BlockSpec(memory_space=pl.ANY)],
        out_specs=qkv_block(3),
        out_shape=jax.ShapeDtypeStruct((WIDE, PACK_ROWS, MODEL), BF),
        input_output_aliases={2: 0},
        compiler_params=params(),
        cost_estimate=cost(4),
    )(normed, grads, buffer)


def qkv_weight_last_call(normed, grads, sums):
    return pl.pallas_call(
        qkv_weight_last_kernel,
        grid=(1,),
        in_specs=[whole((BOTH, MODEL)), whole((BOTH, 3 * HALF_W)), whole((8, MODEL))],
        out_specs=whole((WIDE, 56, MODEL)),
        out_shape=jax.ShapeDtypeStruct((WIDE, 56, MODEL), BF),
        compiler_params=params(),
        cost_estimate=cost(4),
    )(normed, grads, sums)


def all_to_all(block):
    return lax.all_to_all(block, "wide", 0, 0, tiled=True)


def layer_forward(inputs, ids, qkv, rest, small):
    flags, key_ids, query_ids = ids
    sent, rows, normed_a = qkv_call(inputs, small, *qkv)
    recv = all_to_all(sent)
    mix_sent, mix_keep, lse = attend_call(flags, recv, key_ids, query_ids)
    mixture, proj = out_call(all_to_all(mix_sent), rest)
    proj_recv = swap(proj, "tensor")
    middle, normed_c, pre, act, mlp = mlp_call(rows, proj, proj_recv, small, rest)
    mlp_recv = swap(mlp, "tensor")
    return dict(
        rows=rows, normed_a=normed_a, recv=recv, keep=mix_keep, lse=lse, mixture=mixture,
        proj=proj, proj_recv=proj_recv, middle=middle, normed_c=normed_c, pre=pre, act=act,
        mlp=mlp, mlp_recv=mlp_recv,
    )


def layer_backward(inputs, kept, ids, qkv, rest, small):
    flags, key_ids, query_ids = ids
    grad, low_m, grad_pre, part, mlp_sums, *input_grad = mlp_back_call(
        inputs, small, kept["mlp"], kept["mlp_recv"], kept["pre"], rest
    )
    middle_grad, mix_grad, low_a, out_sums = out_back_call(
        grad, part, swap(part, "tensor"), kept["middle"], kept["proj"], kept["proj_recv"], small, rest
    )
    back = attend_back_call(
        flags, kept["recv"], all_to_all(mix_grad), kept["keep"], kept["lse"], key_ids, query_ids
    )
    qkv_part, qkv_grads, qkv_sums = qkv_back_call(all_to_all(back), kept["rows"], small, *qkv)
    carried = (middle_grad, qkv_part, swap(qkv_part, "tensor"), kept["rows"])
    for_weights = dict(
        low_m=low_m, grad_pre=grad_pre, low_a=low_a, qkv_grads=qkv_grads,
        mlp_sums=mlp_sums, out_sums=out_sums, qkv_sums=qkv_sums,
    )
    return carried, for_weights, input_grad


def body(
    x_in, out_cot, image_ids, w_qkv, w_out, w_fc1, w_fc2, gains, shifts, layer_scales, qv_bias, fc1_bias
):
    section = lax.axis_index("section")
    tensor = lax.axis_index("tensor")
    wide = lax.axis_index("wide")
    is_first = section == 0

    def one(array):
        return lax.dynamic_index_in_dim(array, section, 0, keepdims=False)

    qkv = w_qkv[0]
    small_row = jnp.concatenate(
        [
            gains.reshape(-1),
            shifts.reshape(-1),
            layer_scales.reshape(-1),
            qv_bias.reshape(-1),
            fc1_bias.reshape(-1),
            jnp.zeros((672,), BF),
        ]
    ).reshape(1, MODEL)
    pack_a = jnp.concatenate(
        [
            jnp.concatenate([qkv[:, 0], qkv[:, 1]], axis=1),
            jnp.concatenate([qkv[0:16, 2], qkv[16:32, 2]], axis=1),
            small_row,
            jnp.zeros((15, MODEL), BF),
        ],
        axis=0,
    )
    pack_b = jnp.concatenate([w_fc2[0], w_fc1[0][:, :MODEL], w_fc1[0][:, MODEL:], w_out[0]], axis=0)
    own_rows, own_cot = one(x_in), one(out_cot)
    other_both = swap(jnp.concatenate([own_rows, own_cot], axis=0), "tensor")
    other_rows, other_cot = other_both[:ROWS], other_both[ROWS:]
    other_a = swap(pack_a, "section")
    pack_b = jnp.concatenate([pack_b, other_rows[:16]], axis=0)
    other_b = swap(pack_b, "section")

    def gather(block):
        return lax.all_gather(block, "wide", axis=0, tiled=False)

    def behind(block, rows):
        return jnp.concatenate([block[:144], rows], axis=0)

    attn_both = gather(
        jnp.where(
            is_first,
            jnp.concatenate([pack_a, pack_a[48:64], pack_a[48:64], other_a], axis=0),
            jnp.concatenate([other_a, other_a[48:64], other_a[48:64], pack_a], axis=0),
        )
    )
    rest_first = gather(behind(jnp.where(is_first, pack_b, other_b), attn_both[0, 48:64]))

    def rest_second(rows):
        return gather(behind(jnp.where(is_first, other_b, pack_b), rows))

    def small_rows(at):
        block = attn_both[:, at, :].astype(F32)
        vec = jnp.transpose(block[:, :256].reshape(WIDE, 8, 32), (1, 0, 2)).reshape(8, MODEL)
        bias = jnp.transpose(block[:, 256:288].reshape(WIDE, 2, 16), (1, 0, 2)).reshape(2, HALF_W)
        return vec, bias, block[:, 288:352].reshape(1, HIDDEN)

    small = (small_rows(48), small_rows(96 + 48))

    id_grid = one(image_ids).reshape(2, WIDE, ROWS)
    sorted_ids = jnp.where(tensor == 0, id_grid, id_grid[::-1])
    key_ids = sorted_ids.reshape(CHUNKS, 1, 512)
    quarter = lax.rem(wide, QUARTERS)
    half_ids = lax.dynamic_index_in_dim(sorted_ids, quarter // 2, 0, keepdims=False)
    quarter_ids = lax.dynamic_slice_in_dim(half_ids, lax.rem(quarter, 2) * 32, 32, 1)
    query_ids = jnp.transpose(quarter_ids.reshape(BLOCKS_Q, 8, 2, 16), (0, 2, 1, 3)).reshape(
        BLOCKS_Q, 256, 1
    )
    key_low, key_high = jnp.min(key_ids[:, 0], axis=1), jnp.max(key_ids[:, 0], axis=1)
    query_low, query_high = jnp.min(query_ids[..., 0], axis=1), jnp.max(query_ids[..., 0], axis=1)
    flags = (
        (query_low[:, None] <= key_high[None]) & (query_high[:, None] >= key_low[None])
    ).astype(jnp.int32)
    ids = (flags, key_ids, query_ids)

    qkv_parts = ((attn_both, 0), (attn_both, 2))
    kept0 = layer_forward((own_rows, other_rows), ids, qkv_parts[0], rest_first, small[0])
    rest = (rest_first, rest_second(kept0["proj"][:16]))
    kept1 = layer_forward(
        (kept0["middle"], kept0["mlp"], kept0["mlp_recv"], small[0][0]),
        ids, qkv_parts[1], rest[1], small[1],
    )
    branch1 = kept1["mlp"][:ROWS].astype(F32) + kept1["mlp_recv"][ROWS:].astype(F32)
    out1 = (
        kept1["middle"][:ROWS]
        + small[1][0][SCALE_M] * (branch1 + small[1][0][SHIFT_M])
    ).astype(BF)
    out0 = kept1["rows"][:ROWS]

    def rs(pack):
        return lax.psum_scatter(
            pack.reshape(WIDE * pack.shape[1], MODEL), "wide", scatter_dimension=0, tiled=True
        )

    carried1, back1, _ = layer_backward(
        (own_cot, other_cot), kept1, ids, qkv_parts[1], rest[1], small[1]
    )
    sum_mlp1 = rs(
        mlp_weight_call(
            back1["low_m"], kept1["normed_c"], kept1["act"], back1["grad_pre"], back1["out_sums"], None
        )
    )
    pack = out_weight_call(kept1["mixture"], back1["low_a"])
    pack = qkv_weight_call(kept1["normed_a"], back1["qkv_grads"], pack)

    carried0, back0, (grad_x1,) = layer_backward(
        carried1 + (small[1][0],), kept0, ids, qkv_parts[0], rest[0], small[0]
    )
    pack = mlp_weight_call(
        back0["low_m"], kept0["normed_c"], kept0["act"], back0["grad_pre"], back0["low_m"], pack
    )
    pack = out_weight_last_call(
        kept0["mixture"],
        back0["low_a"],
        (back1["mlp_sums"], back1["out_sums"], back1["qkv_sums"], back0["mlp_sums"], back0["out_sums"]),
        sum_mlp1,
        pack,
    )
    sum_mid = rs(pack)
    last_pack = qkv_weight_last_call(kept0["normed_a"], back0["qkv_grads"], back0["qkv_sums"])
    sum_last = jnp.sum(all_to_all(last_pack).astype(F32), axis=0)

    middle_grad0, part0, part_recv0, _ = carried0
    hat0, rstd0 = norm_parts(own_rows.astype(F32))
    grad_norm0 = part0[:ROWS].astype(F32) + part_recv0[ROWS:].astype(F32)
    grad_x0 = middle_grad0[:ROWS] + norm_back(grad_norm0, hat0, rstd0, small[0][0][GAIN_A])

    def lanes(rows, width):
        return lax.dynamic_slice_in_dim(rows, wide * width, width, rows.ndim - 1)

    def own_sums(mlp, outs, qkv_rows):
        norms = jnp.concatenate([mlp[0:2], outs, qkv_rows[0:2]], axis=0)
        pair = qkv_rows[2].reshape(2, HALF_W)
        return jnp.concatenate(
            [lanes(norms, 32).reshape(-1), lanes(pair, 16).reshape(-1), lanes(mlp[2:4].reshape(-1), 64)]
        )

    sums = sum_mid[208:228]
    mlp1, outs1, qkv1, mlp0, outs0 = (sums[at : at + 4] for at in range(0, 20, 4))
    mid0 = jnp.concatenate([sum_mid[0:128], sum_mid[192:208]], axis=0)
    mid1 = jnp.concatenate([sum_mlp1, sum_mid[128:144]], axis=0)
    mid_total = jnp.where(is_first, mid0, mid1).astype(F32) + swap(
        jnp.where(is_first, mid1, mid0), "section"
    ).astype(F32)

    def with_sums(rows, vector):
        return jnp.concatenate([rows, jnp.pad(vector, (0, 672)).reshape(1, MODEL)], axis=0)

    late0 = with_sums(sum_last[0:48].astype(BF), own_sums(mlp0, outs0, sum_last[48:52].astype(BF)))
    late1 = with_sums(sum_mid[144:192], own_sums(mlp1, outs1, qkv1))
    late_own = jnp.where(is_first, late0, late1)
    late_away = jnp.where(is_first, late1, late0)
    late_total = late_own.astype(F32) + swap(late_away, "section").astype(F32)
    own_part, away_part = late_own[48, 192:256], late_away[48, 192:256]
    across = lax.ppermute(away_part, ("section", "tensor"), [(0, 3), (3, 0), (1, 2), (2, 1)])
    heads_total = late_total[48, 192:256] + (
        swap(own_part, "tensor").astype(F32) + across.astype(F32)
    )
    mlp_total, out_total = mid_total[0:128], mid_total[128:144]
    qkv_total, tiny = late_total[0:48], late_total[48]
    norms = jnp.concatenate([tiny[0:192], heads_total]).reshape(8, 32)
    g_gains = jnp.stack([norms[6], norms[2]])
    g_shifts = jnp.stack([norms[7], norms[4], norms[3], norms[0]])
    g_scales = jnp.stack([norms[5], norms[1]])
    g_qv = tiny[256:288].reshape(2, 16)
    g_fc1_bias = tiny[288:352]
    g_fc2 = mlp_total[0:64]
    g_fc1 = jnp.concatenate([mlp_total[64:96], mlp_total[96:128]], axis=1)
    pairs = qkv_total[0:32]
    value_grad = jnp.concatenate([qkv_total[32:48, :HALF_W], qkv_total[32:48, HALF_W:]], axis=0)
    g_qkv = jnp.stack([pairs[:, :HALF_W], pairs[:, HALF_W:], value_grad], axis=1)

    def by_micro(first, second):
        own = jnp.where(is_first, first, second)
        came = swap(jnp.where(is_first, second, first), "section")
        return jnp.stack([jnp.where(is_first, own, came), jnp.where(is_first, came, own)])

    return (
        by_micro(out0, out1)[None],
        by_micro(grad_x0, grad_x1)[None],
        g_qkv[None],
        out_total[None],
        g_fc1[None],
        g_fc2[None],
        g_gains[None],
        g_shifts[None],
        g_scales[None],
        g_qv[None],
        g_fc1_bias[None],
    )


def solution(mesh):
    in_specs = (
        P(None, ("tensor", "wide"), None),
        P(None, ("tensor", "wide"), None),
        P(),
        P("section", "wide", None, "tensor"),
        P("section", ("tensor", "wide"), None),
        P("section", "wide", "tensor"),
        P("section", ("tensor", "wide"), None),
        P("section", None, "wide"),
        P("section", None, "wide"),
        P("section", None, "wide"),
        P("section", None, ("tensor", "wide")),
        P("section", ("tensor", "wide")),
    )
    out_specs = (
        P("section", None, ("tensor", "wide"), None),
        P("section", None, ("tensor", "wide"), None),
        P("section", "wide", None, "tensor"),
        P("section", ("tensor", "wide"), None),
        P("section", "wide", "tensor"),
        P("section", ("tensor", "wide"), None),
        P("section", None, "wide"),
        P("section", None, "wide"),
        P("section", None, "wide"),
        P("section", None, ("tensor", "wide")),
        P("section", ("tensor", "wide")),
    )
    return jax.shard_map(body, mesh=mesh, in_specs=in_specs, out_specs=out_specs, check_vma=False)
```

time: 744 us -> 589 us (0.79)
  waiting for transfers between devices: 343 us -> 201 us
  other arithmetic: 45.4 us -> 14.5 us
  blocking collectives: 88.4 us -> 112 us
  starting transfers between devices: 77.8 us -> 56.3 us
  Pallas kernels: 121 us -> 141 us
    reduce_scatter x2, waiting for transfers between devices: 107 us -> 20.5 us  [rs(): lax.psum_scatter(pack.reshape(WIDE * pack.shape[1], MODEL), 'wide', scatt...]
    all_to_all x1 -> x0, waiting for transfers between devices: 34.8 us -> none  [body(): last_recv = lax.all_to_all(last_pack, 'wide', 0, 0, tiled=True)]
    all_gather x4 -> x3, waiting for transfers between devices: 83.8 us -> 49.6 us  [gather(): return lax.all_gather(block, 'wide', axis=0, tiled=False)]
    all_to_all x3, waiting for transfers between devices: 41.6 us -> 75.6 us  [all_to_all(): return lax.all_to_all(block, 'wide', 0, 0, tiled=True)]
    all_to_all x5 -> x6, blocking collectives: 88.4 us -> 112 us  [all_to_all(): return lax.all_to_all(block, 'wide', 0, 0, tiled=True)]
    pallas_call x8 -> x14, Pallas kernels: 49.5 us -> 71.8 us  [the longest x2 15.8 us: mlp_weight_call(): pl.pallas_call(mlp_weight_kernel, grid=(2,), in_specs=[whole((BOTH, MODEL...]
    ppermute x25 -> x16, starting transfers between devices: 59.7 us -> 39.7 us  [swap(): return lax.ppermute(block, axis, [(0, 1), (1, 0)])]
    ppermute x25 -> x16, waiting for transfers between devices: 73.6 us -> 55 us  [swap(): return lax.ppermute(block, axis, [(0, 1), (1, 0)])]
  transfers between devices with their start and end apart: 35 -> 25, of which waited for: 29 -> 20; matrix products, arithmetic and copies ran while one was open for 8% -> 5% of each run, Pallas kernels for 8% -> 19%
where the time goes in v2:
time: 589 us; the launch traced here: 579 us
  waiting for transfers between devices  201 us (34%)
  Pallas kernels  141 us (24%)
  blocking collectives  112 us (19%)
  starting transfers between devices  56.3 us (10%)
  local copies, waits for them, and re-layouts  39.9 us (7%)
  between operations  14.6 us (2%)
  other arithmetic  14.5 us (2%)
    all_to_all x6, blocking collectives, all_to_all(): return lax.all_to_all(block, 'wide', 0, 0, tiled=True)  112 us
    all_to_all x3, waiting for transfers between devices, all_to_all(): return lax.all_to_all(block, 'wide', 0, 0, tiled=True)  75.6 us
    ppermute x16, waiting for transfers between devices, swap(): return lax.ppermute(block, axis, [(0, 1), (1, 0)])  55 us
    all_gather x3, waiting for transfers between devices, gather(): return lax.all_gather(block, 'wide', axis=0, tiled=False)  49.6 us
    ppermute x16, starting transfers between devices, swap(): return lax.ppermute(block, axis, [(0, 1), (1, 0)])  39.7 us
    pallas_call x2, Pallas kernels, attend_back_call(): pl.pallas_call(attend_back_kernel, grid_spec=pltpu.PrefetchScalarGridSpec...  30.5 us
    pallas_call x2, Pallas kernels, attend_call(): pl.pallas_call(attend_kernel, grid_spec=pltpu.PrefetchScalarGridSpec(num_...  23.9 us
    reduce_scatter x2, waiting for transfers between devices, rs(): lax.psum_scatter(pack.reshape(WIDE * pack.shape[1], MODEL), 'wide', scatt...  20.5 us
  transfers between devices with their start and end apart: 25, of which 20 were waited for; matrix products, arithmetic and copies ran while one was open for 5% of the time, Pallas kernels for 19%

profile of v2, /device:TPU:0, one launch (start us, length us, event | category | flops | bytes accessed | tf_op | source)
XLA Modules:
  0.0 578.9 jit_solution(14999329259447380413)
XLA Ops:
  31.3 6.1 %collective-permute-done.2 = bf16[160,1024]{1,0:T(8,128)(2,1)S(1)} collective-permute-done((bf16[160,1024]{1,0:T(8,128)(2,1)S(1)}, bf16[160,1024]{1,0:T(8,128)(2,1)S(1)}, u32[]{:S(2)}, u32[]{:S(2)}) %collective-permute-start.2) | collective-permute-done | bytes 327712 | tf_op jit(solution)/shard_map/ppermute | solution.py:45
  37.5 42.2 %all-gather.6.cloned.1.call-done.weight_ref = bf16[32,160,1024]{2,1,0:T(8,128)(2,1)} async-done(((bf16[1,160,1024]{2,1,0:T(8,128)(2,1)}), bf16[32,160,1024]{2,1,0:T(8,128)(2,1)}) %all-gather.6.cloned.1.call-update) | async-done | bytes 10485776 | tf_op jit(solution)/shard_map/all_gather | solution.py:842
  89.2 5.4 all-to-all-start
  98.6 18.1 %all-to-all-done.recv_ref = bf16[32,144,128]{2,1,0:T(8,128)(2,1)S(1)} async-done(((bf16[32,144,128]{2,1,0:T(8,128)(2,1)}), bf16[32,144,128]{2,1,0:T(8,128)(2,1)S(1)}, u32[]{:S(2)}, u32[]{:S(2)}) %all-to-all-start) | async-done | bytes 1179680 | tf_op jit(solution)/shard_map/all_to_all | solution.py:763
  117.7 12.0 %shard_map.204 = (bf16[32,16,128]{2,1,0:T(8,128)(2,1)}, f32[32,16,128]{2,1,0:T(8,128)}, f32[1024,1]{1,0:T(8,128)}) custom-call(s32[4,8]{1,0:T(4,128)} %and_convert_fusion.flag_ref, bf16[32,144,128]{2,1,0:T(8,128)(2,1)} %copy-done.5, s32[8,1,512]{2,1,0:T(1,128)} %reshape.365.key_id_ref, s32[4,256,1]{2,1,0:T(8,128)} %reshape.388.query_id_ref), custom_call_target="tpu_custom_call" | custom-call | flops 12000000000 | bytes 100000 | tf_op jit(solution)/shard_map/pallas_call | solution.py:245
  129.7 13.5 %all_to_all.45.recv_ref = bf16[32,16,128]{2,1,0:T(8,128)(2,1)} all-to-all(bf16[32,16,128]{2,1,0:T(8,128)(2,1)} %get-tuple-element.64), channel_id=1, replica_groups=mesh['section'=2,'tensor'=2,'wide'=32] {'wide'}, dimensions={0} | all-to-all | bytes 262144 | tf_op jit(solution)/shard_map/all_to_all | solution.py:763
  143.2 7.3 %all-gather.8.cloned.1.call-done = bf16[5120,1024]{1,0:T(8,128)(2,1)} async-done(((bf16[160,1024]{1,0:T(8,128)(2,1)}), bf16[5120,1024]{1,0:T(8,128)(2,1)}) %all-gather.8.cloned.1.call-update) | async-done | bytes 10485776 | tf_op jit(solution)/shard_map/all_gather | solution.py:842
  158.4 6.4 %collective-permute-done.3.part_recv_ref.proj_recv_ref = bf16[128,1024]{1,0:T(8,128)(2,1)S(1)} collective-permute-done((bf16[128,1024]{1,0:T(8,128)(2,1)}, bf16[128,1024]{1,0:T(8,128)(2,1)S(1)}, u32[]{:S(2)}, u32[]{:S(2)}) %collective-permute-start.3) | collective-permute-done | bytes 262176 | tf_op jit(solution)/shard_map/ppermute | solution.py:45
  165.4 5.9 %shard_map.206 = (f32[128,1024]{1,0:T(8,128)}, bf16[128,1024]{1,0:T(8,128)(2,1)}, f32[128,2048]{1,0:T(8,128)}, bf16[128,2048]{1,0:T(8,128)(2,1)}, bf16[128,1024]{1,0:T(8,128)(2,1)}) custom-call(bf16[128,1024]{1,0:T(8,128)(2,1)} %get-tuple-element.62.rows_ref, bf16[128,1024]{1,0:T(8,128)(2,1)} %get-tuple-element.65.part_own_ref.proj_own_ref, ...), custom_call_target="tpu_custom_call" | custom-call | flops 7000000000 | bytes 100000 | tf_op jit(solution)/shard_map/pallas_call | solution.py:409
  185.7 37.5 %all_to_all.46.recv_ref = bf16[32,144,128]{2,1,0:T(8,128)(2,1)} all-to-all(bf16[32,144,128]{2,1,0:T(8,128)(2,1)} %get-tuple-element.69), channel_id=1, replica_groups=mesh['section'=2,'tensor'=2,'wide'=32] {'wide'}, dimensions={0} | all-to-all | bytes 2359296 | tf_op jit(solution)/shard_map/all_to_all | solution.py:763
  223.3 12.0 %shard_map.208 = (bf16[32,16,128]{2,1,0:T(8,128)(2,1)}, f32[32,16,128]{2,1,0:T(8,128)}, f32[1024,1]{1,0:T(8,128)}) custom-call(s32[4,8]{1,0:T(4,128)} %and_convert_fusion.flag_ref, bf16[32,144,128]{2,1,0:T(8,128)(2,1)} %all_to_all.46.recv_ref, s32[8,1,512]{2,1,0:T(1,128)} %reshape.365.key_id_ref, s32[4,256,1]{2,1,0:T(8,128)} %reshape.388.query_id_ref), custom_call_target="tpu_custom_call" | custom-call | flops 12000000000 | bytes 100000 | tf_op jit(solution)/shard_map/pallas_call | solution.py:245
  235.2 12.4 %all_to_all.47.recv_ref = bf16[32,16,128]{2,1,0:T(8,128)(2,1)} all-to-all(bf16[32,16,128]{2,1,0:T(8,128)(2,1)} %get-tuple-element.70), channel_id=1, replica_groups=mesh['section'=2,'tensor'=2,'wide'=32] {'wide'}, dimensions={0} | all-to-all | bytes 262144 | tf_op jit(solution)/shard_map/all_to_all | solution.py:763
  253.8 6.2 %collective-permute-done.5.part_recv_ref.proj_recv_ref = bf16[128,1024]{1,0:T(8,128)(2,1)S(1)} collective-permute-done((bf16[128,1024]{1,0:T(8,128)(2,1)}, bf16[128,1024]{1,0:T(8,128)(2,1)S(1)}, u32[]{:S(2)}, u32[]{:S(2)}) %collective-permute-start.5) | collective-permute-done | bytes 262176 | tf_op jit(solution)/shard_map/ppermute | solution.py:45
  260.7 5.8 %shard_map.210 = (f32[128,1024]{1,0:T(8,128)}, bf16[128,1024]{1,0:T(8,128)(2,1)}, f32[128,2048]{1,0:T(8,128)}, bf16[128,2048]{1,0:T(8,128)(2,1)}, bf16[128,1024]{1,0:T(8,128)(2,1)}) custom-call(bf16[128,1024]{1,0:T(8,128)(2,1)} %get-tuple-element.68.rows_ref, bf16[128,1024]{1,0:T(8,128)(2,1)} %get-tuple-element.71.part_own_ref.proj_own_ref, ...), custom_call_target="tpu_custom_call" | custom-call | flops 7000000000 | bytes 100000 | tf_op jit(solution)/shard_map/pallas_call | solution.py:409
  269.7 6.1 %collective-permute-done.6.refs_2_ = bf16[128,1024]{1,0:T(8,128)(2,1)S(1)} collective-permute-done((bf16[128,1024]{1,0:T(8,128)(2,1)}, bf16[128,1024]{1,0:T(8,128)(2,1)S(1)}, u32[]{:S(2)}, u32[]{:S(2)}) %collective-permute-start.6) | collective-permute-done | bytes 262176 | tf_op jit(solution)/shard_map/ppermute | solution.py:45
  276.6 7.1 %shard_map.211 = (bf16[128,1024]{1,0:T(8,128)(2,1)}, bf16[128,1024]{1,0:T(8,128)(2,1)}, bf16[128,2048]{1,0:T(8,128)(2,1)}, bf16[128,1024]{1,0:T(8,128)(2,1)}, f32[8,1024]{1,0:T(8,128)}) custom-call(bf16[64,1024]{1,0:T(8,128)(2,1)} %copy-done.10, bf16[64,1024]{1,0:T(8,128)(2,1)} %get-tuple-element.145.other_ref, ...), custom_call_target="tpu_custom_call" | custom-call | flops 8000000000 | bytes 100000 | tf_op jit(solution)/shard_map/pallas_call | solution.py:497
  286.8 5.2 collective-permute-done.8.part_recv_ref
  296.3 8.0 %shard_map.220 = bf16[32,128,1024]{2,1,0:T(8,128)(2,1)} custom-call(bf16[128,1024]{1,0:T(8,128)(2,1)} %get-tuple-element.101.low_ref, bf16[128,1024]{1,0:T(8,128)(2,1)} %get-tuple-element.102.normed_ref, bf16[128,2048]{1,0:T(8,128)(2,1)} %get-tuple-element.103.act_ref, bf16[128,2048]{1,0:T(8,128)(2,1)} %get-tuple-element.104.grad_pre_ref, ...), custom_call_target="tpu_custom_call" | custom-call | flops 8000000000 | bytes 100000 | tf_op jit(solution)/shard_map/pallas_call | solution.py:560
  305.2 12.0 %all_to_all.48.grad_ref = bf16[32,16,128]{2,1,0:T(8,128)(2,1)} all-to-all(bf16[32,16,128]{2,1,0:T(8,128)(2,1)S(1)} %copy-done.15), channel_id=1, replica_groups=mesh['section'=2,'tensor'=2,'wide'=32] {'wide'}, dimensions={0} | all-to-all | bytes 262144 | tf_op jit(solution)/shard_map/all_to_all | solution.py:763
  317.2 15.2 %shard_map.213 = bf16[32,144,128]{2,1,0:T(8,128)(2,1)} custom-call(s32[4,8]{1,0:T(4,128)} %and_convert_fusion.flag_ref, bf16[32,144,128]{2,1,0:T(8,128)(2,1)} %all_to_all.46.recv_ref, bf16[32,16,128]{2,1,0:T(8,128)(2,1)} %all_to_all.48.grad_ref, f32[32,16,128]{2,1,0:T(8,128)} %get-tuple-element.79.keep_ref, f32[1024,1]{1,0:T(8,128)} %get-tuple-element.80.lse_ref, ...), custom_call_target="tpu_custom_call" | custom-call | flops 16000000000 | bytes 100000 | tf_op jit(solution)/shard_map/pallas_call | solution.py:332
  338.8 15.8 %all-to-all-done.5.recv_ref = bf16[32,144,128]{2,1,0:T(8,128)(2,1)S(1)} async-done(((bf16[32,144,128]{2,1,0:T(8,128)(2,1)}), bf16[32,144,128]{2,1,0:T(8,128)(2,1)S(1)}, u32[]{:S(2)}, u32[]{:S(2)}) %all-to-all-start.5) | async-done | bytes 1179680 | tf_op jit(solution)/shard_map/all_to_all | solution.py:763
  370.9 8.1 %shard_map.215 = (bf16[128,1024]{1,0:T(8,128)(2,1)}, bf16[128,1024]{1,0:T(8,128)(2,1)}, bf16[128,2048]{1,0:T(8,128)(2,1)}, bf16[128,1024]{1,0:T(8,128)(2,1)}, f32[8,1024]{1,0:T(8,128)}, /*index=5*/f32[64,1024]{1,0:T(8,128)}) custom-call(f32[128,1024]{1,0:T(8,128)} %get-tuple-element.77.middle_grad_ref, bf16[128,1024]{1,0:T(8,128)(2,1)} %get-tuple-element.81.part_own_ref, ...), custom_call_target="tpu_custom_call" | custom-call | flops 8000000000 | bytes 100000 | tf_op jit(solution)/shard_map/pallas_call | solution.py:497
  382.3 7.8 %shard_map.223.refs_6_ = bf16[32,240,1024]{2,1,0:T(8,128)(2,1)} custom-call(bf16[128,1024]{1,0:T(8,128)(2,1)} %get-tuple-element.105.low_ref.after_ref, bf16[128,1024]{1,0:T(8,128)(2,1)} %get-tuple-element.106.normed_ref, bf16[128,2048]{1,0:T(8,128)(2,1)} %get-tuple-element.107.act_ref, ...), custom_call_target="tpu_custom_call", output_to_operand_aliasing={{}: (5, {})} | custom-call | flops 8000000000 | bytes 100000 | tf_op jit(solution)/shard_map/pallas_call | solution.py:560
  399.0 13.0 %all_to_all.49.grad_ref = bf16[32,16,128]{2,1,0:T(8,128)(2,1)} all-to-all(bf16[32,16,128]{2,1,0:T(8,128)(2,1)S(1)} %copy-done.14), channel_id=1, replica_groups=mesh['section'=2,'tensor'=2,'wide'=32] {'wide'}, dimensions={0} | all-to-all | bytes 262144 | tf_op jit(solution)/shard_map/all_to_all | solution.py:763
  412.0 15.4 %shard_map.217 = bf16[32,144,128]{2,1,0:T(8,128)(2,1)} custom-call(s32[4,8]{1,0:T(4,128)} %and_convert_fusion.flag_ref, bf16[32,144,128]{2,1,0:T(8,128)(2,1)} %copy-done.5, bf16[32,16,128]{2,1,0:T(8,128)(2,1)} %all_to_all.49.grad_ref, f32[32,16,128]{2,1,0:T(8,128)} %get-tuple-element.87.keep_ref, f32[1024,1]{1,0:T(8,128)} %get-tuple-element.88.lse_ref, ...), custom_call_target="tpu_custom_call" | custom-call | flops 16000000000 | bytes 100000 | tf_op jit(solution)/shard_map/pallas_call | solution.py:332
  427.4 23.7 %all_to_all.50.recv_ref = bf16[32,144,128]{2,1,0:T(8,128)(2,1)} all-to-all(bf16[32,144,128]{2,1,0:T(8,128)(2,1)} %shard_map.217), channel_id=1, replica_groups=mesh['section'=2,'tensor'=2,'wide'=32] {'wide'}, dimensions={0} | all-to-all | bytes 2359296 | tf_op jit(solution)/shard_map/all_to_all | solution.py:763
  451.1 5.3 shard_map.218
  460.7 5.0 all-to-all-start.8
  471.8 5.0 collective-permute-done.11
  480.1 4.6 collective-permute-done.12
  485.5 41.6 %all-to-all-done.8 = bf16[32,56,1024]{2,1,0:T(8,128)(2,1)} async-done(((bf16[32,56,1024]{2,1,0:T(8,128)(2,1)}), bf16[32,56,1024]{2,1,0:T(8,128)(2,1)}, u32[]{:S(2)}, u32[]{:S(2)}) %all-to-all-start.8) | async-done | bytes 3670048 | tf_op jit(solution)/shard_map/all_to_all | solution.py:763
  530.2 20.2 %reduce-scatter.5.cloned.1.call-done = bf16[240,1024]{1,0:T(8,128)(2,1)} async-done(((bf16[7680,1024]{1,0:T(8,128)(2,1)}), bf16[240,1024]{1,0:T(8,128)(2,1)}) %reduce-scatter.5.cloned.1.call-update) | async-done | bytes 491536 | tf_op jit(solution)/shard_map/reduce_scatter | solution.py:898
  (249 shorter events, 154.2 us)
Async XLA Ops:
  7.2 72.6 %all-gather.6.cloned.1.call-start = ((), (), s32[]{:S(2)}) async-start(), calls=%async_computation.11 | async-start | bytes 10813440 | tf_op jit(solution)/shard_map/all_gather | solution.py:842
  12.7 5.2 collective-permute-start.1
  19.1 131.4 %all-gather.8.cloned.1.call-start = ((), (), s32[]{:S(2)}) async-start(), calls=%async_computation.14 | async-start | bytes 10813440 | tf_op jit(solution)/shard_map/all_gather | solution.py:842
  19.2 70.0 %copy-start.10 = (bf16[64,1024]{1,0:T(8,128)(2,1)}, bf16[64,1024]{1,0:T(8,128)(2,1)S(1)}, u32[]{:S(2)}) copy-start(bf16[64,1024]{1,0:T(8,128)(2,1)S(1)} %dynamic-slice_bitcast_fusion.own_ref) | copy-start | bytes 393220
  20.8 64.5 %copy-start.2 = (bf16[64,1024]{1,0:T(8,128)(2,1)}, bf16[64,1024]{1,0:T(8,128)(2,1)S(1)}, u32[]{:S(2)}) copy-start(bf16[64,1024]{1,0:T(8,128)(2,1)S(1)} %get-tuple-element.124.own_ref) | copy-start | bytes 393220
  20.8 8.9 %collective-permute-start = (bf16[128,1024]{1,0:T(8,128)(2,1)S(1)}, bf16[128,1024]{1,0:T(8,128)(2,1)S(1)}, u32[]{:S(2)}, u32[]{:S(2)}) collective-permute-start(bf16[128,1024]{1,0:T(8,128)(2,1)S(1)} %pad_maximum_fusion.4), channel_id=1, source_target_pairs={{0,32},{32,0},{1,33},{33,1},{2,34},{34,2},{3,35},{35,3},{4,36},{36... | collective-permute-start | bytes 786440 | tf_op jit(solution)/shard_map/ppermute | solution.py:45
  29.7 7.8 %collective-permute-start.2 = (bf16[160,1024]{1,0:T(8,128)(2,1)S(1)}, bf16[160,1024]{1,0:T(8,128)(2,1)S(1)}, u32[]{:S(2)}, u32[]{:S(2)}) collective-permute-start(bf16[160,1024]{1,0:T(8,128)(2,1)S(1)} %slice_dynamic-update-slice_fusion.2), channel_id=1, source_target_pairs={{0,64},{64,0},{1,65},{65,1},{2,66},{66,2},{3,67},{67,3},{4,68},{68... | collective-permute-start | bytes 983048 | tf_op jit(solution)/shard_map/ppermute | solution.py:45
  89.2 27.5 %all-to-all-start = ((bf16[32,144,128]{2,1,0:T(8,128)(2,1)}), bf16[32,144,128]{2,1,0:T(8,128)(2,1)S(1)}, u32[]{:S(2)}, u32[]{:S(2)}) async-start(bf16[32,144,128]{2,1,0:T(8,128)(2,1)} %get-tuple-element.63), calls=%async_computation | async-start | bytes 2359296 | tf_op jit(solution)/shard_map/all_to_all | solution.py:763
  94.7 152.9 %all-gather.10.cloned.1.call-start = ((), (), s32[]{:S(2)}) async-start(), calls=%async_computation.15 | async-start | bytes 10813440 | tf_op jit(solution)/shard_map/all_gather | solution.py:842
  154.4 240.4 %reduce-scatter.3.cloned.1.call-start = ((), (), s32[]{:S(2)}) async-start(), calls=%async_computation.12 | async-start | bytes 8650752 | tf_op jit(solution)/shard_map/reduce_scatter | solution.py:898
  154.5 10.3 %collective-permute-start.3 = (bf16[128,1024]{1,0:T(8,128)(2,1)}, bf16[128,1024]{1,0:T(8,128)(2,1)S(1)}, u32[]{:S(2)}, u32[]{:S(2)}) collective-permute-start(bf16[128,1024]{1,0:T(8,128)(2,1)} %get-tuple-element.65.part_own_ref.proj_own_ref), channel_id=1, source_target_pairs={{0,32},{32,0},{1,33},{33,1},{2,34},{34,2},{3,35},{35,3},{4,36},{36... | collective-permute-start | bytes 786440 | tf_op jit(solution)/shard_map/ppermute | solution.py:45
  171.3 9.4 %collective-permute-start.4 = (bf16[128,1024]{1,0:T(8,128)(2,1)}, bf16[128,1024]{1,0:T(8,128)(2,1)S(1)}, u32[]{:S(2)}, u32[]{:S(2)}) collective-permute-start(bf16[128,1024]{1,0:T(8,128)(2,1)} %get-tuple-element.67.mlp_own_ref.refs_1_), channel_id=1, source_target_pairs={{0,32},{32,0},{1,33},{33,1},{2,34},{34,2},{3,35},{35,3},{4,36},{36... | collective-permute-start | bytes 786440 | tf_op jit(solution)/shard_map/ppermute | solution.py:45
  250.0 10.0 %collective-permute-start.5 = (bf16[128,1024]{1,0:T(8,128)(2,1)}, bf16[128,1024]{1,0:T(8,128)(2,1)S(1)}, u32[]{:S(2)}, u32[]{:S(2)}) collective-permute-start(bf16[128,1024]{1,0:T(8,128)(2,1)} %get-tuple-element.71.part_own_ref.proj_own_ref), channel_id=1, source_target_pairs={{0,32},{32,0},{1,33},{33,1},{2,34},{34,2},{3,35},{35,3},{4,36},{36... | collective-permute-start | bytes 786440 | tf_op jit(solution)/shard_map/ppermute | solution.py:45
  266.6 9.3 %collective-permute-start.6 = (bf16[128,1024]{1,0:T(8,128)(2,1)}, bf16[128,1024]{1,0:T(8,128)(2,1)S(1)}, u32[]{:S(2)}, u32[]{:S(2)}) collective-permute-start(bf16[128,1024]{1,0:T(8,128)(2,1)} %get-tuple-element.73.refs_1_), channel_id=1, source_target_pairs={{0,32},{32,0},{1,33},{33,1},{2,34},{34,2},{3,35},{35,3},{4,36},{36... | collective-permute-start | bytes 786440 | tf_op jit(solution)/shard_map/ppermute | solution.py:45
  283.6 8.4 %collective-permute-start.8 = (bf16[128,1024]{1,0:T(8,128)(2,1)}, bf16[128,1024]{1,0:T(8,128)(2,1)S(1)}, u32[]{:S(2)}, u32[]{:S(2)}) collective-permute-start(bf16[128,1024]{1,0:T(8,128)(2,1)} %get-tuple-element.76.part_own_ref), channel_id=1, source_target_pairs={{0,32},{32,0},{1,33},{33,1},{2,34},{34,2},{3,35},{35,3},{4,36},{36... | collective-permute-start | bytes 786440 | tf_op jit(solution)/shard_map/ppermute | solution.py:45
  332.4 22.3 %all-to-all-start.5 = ((bf16[32,144,128]{2,1,0:T(8,128)(2,1)}), bf16[32,144,128]{2,1,0:T(8,128)(2,1)S(1)}, u32[]{:S(2)}, u32[]{:S(2)}) async-start(bf16[32,144,128]{2,1,0:T(8,128)(2,1)} %shard_map.213), calls=%async_computation.5 | async-start | bytes 2359296 | tf_op jit(solution)/shard_map/all_to_all | solution.py:763
  336.3 214.1 %reduce-scatter.5.cloned.1.call-start = ((), (), s32[]{:S(2)}) async-start(), calls=%async_computation.13 | async-start | bytes 16220160 | tf_op jit(solution)/shard_map/reduce_scatter | solution.py:898
  360.0 10.2 %collective-permute-start.9 = (bf16[128,1024]{1,0:T(8,128)(2,1)}, bf16[128,1024]{1,0:T(8,128)(2,1)S(1)}, u32[]{:S(2)}, u32[]{:S(2)}) collective-permute-start(bf16[128,1024]{1,0:T(8,128)(2,1)} %get-tuple-element.81.part_own_ref), channel_id=1, source_target_pairs={{0,32},{32,0},{1,33},{33,1},{2,34},{34,2},{3,35},{35,3},{4,36},{36... | collective-permute-start | bytes 786440 | tf_op jit(solution)/shard_map/ppermute | solution.py:45
  379.0 11.2 %collective-permute-start.10 = (bf16[128,1024]{1,0:T(8,128)(2,1)}, bf16[128,1024]{1,0:T(8,128)(2,1)S(1)}, u32[]{:S(2)}, u32[]{:S(2)}) collective-permute-start(bf16[128,1024]{1,0:T(8,128)(2,1)} %get-tuple-element.84.part_own_ref), channel_id=1, source_target_pairs={{0,32},{32,0},{1,33},{33,1},{2,34},{34,2},{3,35},{35,3},{4,36},{36... | collective-permute-start | bytes 786440 | tf_op jit(solution)/shard_map/ppermute | solution.py:45
  456.4 14.5 %copy-start.11 = (bf16[128,1024]{1,0:T(8,128)(2,1)S(1)}, bf16[128,1024]{1,0:T(8,128)(2,1)}, u32[]{:S(2)}) copy-start(bf16[128,1024]{1,0:T(8,128)(2,1)} %get-tuple-element.68.rows_ref) | copy-start | bytes 786436
  456.5 20.6 %copy-start.7 = (f32[64,1024]{1,0:T(8,128)S(1)}, f32[64,1024]{1,0:T(8,128)}, u32[]{:S(2)}) copy-start(f32[64,1024]{1,0:T(8,128)} %get-tuple-element.90) | copy-start | bytes 786436
  456.5 20.6 %copy-start.16 = (f32[128,1024]{1,0:T(8,128)S(1)}, f32[128,1024]{1,0:T(8,128)}, u32[]{:S(2)}) copy-start(f32[128,1024]{1,0:T(8,128)} %get-tuple-element.85) | copy-start | bytes 1572868
  460.7 100.0 %copy-start.4 = (bf16[128,1024]{1,0:T(8,128)(2,1)S(1)}, bf16[128,1024]{1,0:T(8,128)(2,1)}, u32[]{:S(2)}) copy-start(bf16[128,1024]{1,0:T(8,128)(2,1)} %reduce-scatter.3.cloned.1.call-done.refs_5_) | copy-start | bytes 786436
  460.7 66.5 %all-to-all-start.8 = ((bf16[32,56,1024]{2,1,0:T(8,128)(2,1)}), bf16[32,56,1024]{2,1,0:T(8,128)(2,1)}, u32[]{:S(2)}, u32[]{:S(2)}) async-start(bf16[32,56,1024]{2,1,0:T(8,128)(2,1)} %shard_map.219), calls=%async_computation.8 | async-start | bytes 7340032 | tf_op jit(solution)/shard_map/all_to_all | solution.py:763
  465.9 11.0 %collective-permute-start.11 = (bf16[128,1024]{1,0:T(8,128)(2,1)S(1)}, bf16[128,1024]{1,0:T(8,128)(2,1)S(1)}, u32[]{:S(2)}, u32[]{:S(2)}) collective-permute-start(bf16[128,1024]{1,0:T(8,128)(2,1)S(1)} %copy-done.12), channel_id=1, source_target_pairs={{0,32},{32,0},{1,33},{33,1},{2,34},{34,2},{3,35},{35,3},{4,36},{36... | collective-permute-start | bytes 786440 | tf_op jit(solution)/shard_map/ppermute | solution.py:45
  471.0 101.2 %copy-start.1 = (bf16[2,64,1024]{2,1,0:T(8,128)(2,1)S(1)}, bf16[2,64,1024]{2,1,0:T(8,128)(2,1)}, u32[]{:S(2)}) copy-start(bf16[2,64,1024]{2,1,0:T(8,128)(2,1)} %param.13) | copy-start | bytes 786436
  471.1 8.2 %collective-permute-start.7 = (bf16[64,1024]{1,0:T(8,128)(2,1)S(1)}, bf16[64,1024]{1,0:T(8,128)(2,1)S(1)}, u32[]{:S(2)}, u32[]{:S(2)}) collective-permute-start(bf16[64,1024]{1,0:T(8,128)(2,1)S(1)} %get-tuple-element.125), channel_id=1, source_target_pairs={{0,64},{64,0},{1,65},{65,1},{2,66},{66,2},{3,67},{67,3},{4,68},{68... | collective-permute-start | bytes 393224 | tf_op jit(solution)/shard_map/ppermute | solution.py:45
  477.3 7.4 %collective-permute-start.12 = (f32[64,1024]{1,0:T(8,128)S(1)}, f32[64,1024]{1,0:T(8,128)S(1)}, u32[]{:S(2)}, u32[]{:S(2)}) collective-permute-start(f32[64,1024]{1,0:T(8,128)S(1)} %get-tuple-element.121), channel_id=1, source_target_pairs={{0,64},{64,0},{1,65},{65,1},{2,66},{66,2},{3,67},{67,3},{4,68},{68... | collective-permute-start | bytes 786440 | tf_op jit(solution)/shard_map/ppermute | solution.py:45
  555.4 6.1 %collective-permute-start.13 = (bf16[49,1024]{1,0:T(8,128)(2,1)S(1)}, bf16[49,1024]{1,0:T(8,128)(2,1)S(1)}, u32[]{:S(2)}, u32[]{:S(2)}) collective-permute-start(bf16[49,1024]{1,0:T(8,128)(2,1)S(1)} %broadcast_select_fusion.8), channel_id=1, source_target_pairs={{0,64},{64,0},{1,65},{65,1},{2,66},{66,2},{3,67},{67,3},{4,68},{68... | collective-permute-start | bytes 301064 | tf_op jit(solution)/shard_map/ppermute | solution.py:45
  556.9 9.9 %collective-permute-start.16 = (bf16[64]{0:T(256)(128)(2,1)S(1)}, bf16[64]{0:T(256)(128)(2,1)S(1)}, u32[]{:S(2)}, u32[]{:S(2)}) collective-permute-start(bf16[64]{0:T(256)(128)(2,1)S(1)} %slice_bitcast_fusion.12), channel_id=1, source_target_pairs={{0,96},{96,0},{32,64},{64,32},{1,97},{97,1},{33,65},{65,33},{2,98}... | collective-permute-start | bytes 392 | tf_op jit(solution)/shard_map/ppermute | solution.py:962
  560.8 9.2 %collective-permute-start.14 = (bf16[144,1024]{1,0:T(8,128)(2,1)S(1)}, bf16[144,1024]{1,0:T(8,128)(2,1)S(1)}, u32[]{:S(2)}, u32[]{:S(2)}) collective-permute-start(bf16[144,1024]{1,0:T(8,128)(2,1)S(1)} %broadcast_select_fusion.1), channel_id=1, source_target_pairs={{0,64},{64,0},{1,65},{65,1},{2,66},{66,2},{3,67},{67,3},{4,68},{68... | collective-permute-start | bytes 884744 | tf_op jit(solution)/shard_map/ppermute | solution.py:45
  562.2 6.4 %collective-permute-start.15 = (bf16[64]{0:T(256)(128)(2,1)S(1)}, bf16[64]{0:T(256)(128)(2,1)S(1)}, u32[]{:S(2)}, u32[]{:S(2)}) collective-permute-start(bf16[64]{0:T(256)(128)(2,1)S(1)} %slice_bitcast_fusion.13), channel_id=1, source_target_pairs={{0,32},{32,0},{1,33},{33,1},{2,34},{34,2},{3,35},{35,3},{4,36},{36... | collective-permute-start | bytes 392 | tf_op jit(solution)/shard_map/ppermute | solution.py:45
  (21 other events, 116.6 us)
Sparse Core Ops, SparseCore 0:
  19.2 60.4 all-gather.5
  82.0 68.4 all-gather.7
  154.5 69.8 all-gather.9
  304.4 90.3 reduce-scatter.2
  399.1 151.3 reduce-scatter.4

commit v3 on v2

--- a/solution.py
+++ b/solution.py
@@ -77,14 +77,14 @@
         out_ref[(2 * pair + 1) * QUARTERS + quarter, row0 : row0 + 16, :] = odd.astype(BF)
 
 
-def unpack_heads(in_ref, row0):
+def unpack_heads(in_ref, row0, base=0):
     mask = low_lanes((16, 128))
     columns = []
     for pair in range(HEADS_DEV // 2):
         pieces = []
         for quarter in range(QUARTERS):
-            even = in_ref[(2 * pair) * QUARTERS + quarter, row0 : row0 + 16, :].astype(F32)
-            odd = in_ref[(2 * pair + 1) * QUARTERS + quarter, row0 : row0 + 16, :].astype(F32)
+            even = in_ref[base + (2 * pair) * QUARTERS + quarter, row0 : row0 + 16, :].astype(F32)
+            odd = in_ref[base + (2 * pair + 1) * QUARTERS + quarter, row0 : row0 + 16, :].astype(F32)
             pieces.append(jnp.where(mask, even, turn(odd)))
             pieces.append(jnp.where(mask, turn(even), odd))
         columns.append(jnp.concatenate(pieces, axis=0))
@@ -238,7 +238,8 @@
     mask = low_lanes((128, 128))
     joined = jnp.where(mask, turn(mixture[:128]), mixture[128:]).reshape(8, 16, 128)
     keep_ref[...] = joined
-    out_ref[...] = joined.astype(BF)
+    out_ref[0] = joined.astype(BF)
+    out_ref[1] = joined.astype(BF)
 
 
 def attend_call(flags, recv, key_ids, query_ids):
@@ -253,7 +254,7 @@
                 pl.BlockSpec((1, 256, 1), lambda i, f: (i, 0, 0)),
             ],
             out_specs=[
-                pl.BlockSpec((8, 16, 128), lambda i, f: (i, 0, 0)),
+                pl.BlockSpec((2, 8, 16, 128), lambda i, f: (0, i, 0, 0)),
                 pl.BlockSpec((8, 16, 128), lambda i, f: (i, 0, 0)),
                 pl.BlockSpec((256, 1), lambda i, f: (i, 0)),
             ],
@@ -265,7 +266,7 @@
             ],
         ),
         out_shape=[
-            jax.ShapeDtypeStruct((WIDE, 16, 128), BF),
+            jax.ShapeDtypeStruct((2, WIDE, 16, 128), BF),
             jax.ShapeDtypeStruct((WIDE, 16, 128), F32),
             jax.ShapeDtypeStruct((1024, 1), F32),
         ],
@@ -354,36 +355,24 @@
     )(flags, recv, grads, keep, lse, key_ids, query_ids)
 
 
-def out_kernel(recv_ref, weight_ref, mixture_ref, part_ref):
-    mixture = unpack_heads(recv_ref, 0).astype(BF)
-    mixture_ref[...] = mixture
-    part_ref[...] = nn(mixture, weight_ref[...].reshape(HALF_W, MODEL)).astype(BF)
-
-
-def out_call(recv, weights):
-    return pl.pallas_call(
-        out_kernel,
-        grid=(1,),
-        in_specs=[whole((WIDE, 16, 128)), pl.BlockSpec((WIDE, 16, MODEL), lambda i: (0, 8, 0))],
-        out_specs=[whole((BOTH, HALF_W)), whole((BOTH, MODEL))],
-        out_shape=[
-            jax.ShapeDtypeStruct((BOTH, HALF_W), BF),
-            jax.ShapeDtypeStruct((BOTH, MODEL), BF),
-        ],
-        compiler_params=params(),
-        cost_estimate=cost(2.5),
-    )(recv, weights)
-
-
 def mlp_kernel(
-    rows_ref, part_own_ref, part_recv_ref, vec_ref, bias_ref, one_ref, two_ref,
-    middle_ref, normed_ref, pre_ref, act_ref, out_ref, acc_ref,
+    place_ref, rows_ref, recv_ref, vec_ref, bias_ref, out_weight_ref, one_ref, two_ref,
+    mixture_ref, branch_ref, middle_ref, normed_ref, pre_ref, act_ref, out_ref, acc_ref,
 ):
     at = pl.program_id(0)
 
     @pl.when(at == 0)
     def _():
-        branch = joined(part_own_ref, part_recv_ref) + row_of(vec_ref, SHIFT_O)
+        tensor = place_ref[0]
+        own = unpack_heads(recv_ref, 0, tensor * WIDE).astype(BF)
+        partner = unpack_heads(recv_ref, 0, (1 - tensor) * WIDE).astype(BF)
+        partner = jnp.concatenate([partner[ROWS:], partner[:ROWS]], axis=0)
+        mixture_ref[...] = own
+        proj = nn(own, out_weight_ref[:, 0:16, :].reshape(HALF_W, MODEL)) + nn(
+            partner, out_weight_ref[:, 16:32, :].reshape(HALF_W, MODEL)
+        )
+        branch = proj + row_of(vec_ref, SHIFT_O)
+        branch_ref[...] = branch
         middle = rows_ref[...].astype(F32) + row_of(vec_ref, SCALE_A) * branch
         middle_ref[...] = middle
         hat, _ = norm_parts(middle)
@@ -404,21 +393,24 @@
         out_ref[...] = (acc_ref[...] + part).astype(BF)
 
 
-def mlp_call(rows, part_own, part_recv, small, weights):
+def mlp_call(place, rows, recv, small, weights):
     vec, _, bias = small
     return pl.pallas_call(
         mlp_kernel,
         grid=(2,),
         in_specs=[
+            pl.BlockSpec(memory_space=pltpu.SMEM),
             whole((BOTH, MODEL)),
-            whole((BOTH, MODEL)),
-            whole((BOTH, MODEL)),
+            whole((2 * WIDE, 16, 128)),
             whole((8, MODEL)),
             pl.BlockSpec((1, MODEL), lambda j: (0, j)),
+            pl.BlockSpec((WIDE, 32, MODEL), lambda j: (0, 4, 0)),
             pl.BlockSpec((WIDE, 32, MODEL), lambda j: (0, 2 + j, 0)),
             pl.BlockSpec((16, 64, MODEL), lambda j: (j, 0, 0)),
         ],
         out_specs=[
+            whole((BOTH, HALF_W)),
+            whole((BOTH, MODEL)),
             whole((BOTH, MODEL)),
             whole((BOTH, MODEL)),
             pl.BlockSpec((BOTH, MODEL), lambda j: (0, j)),
@@ -426,6 +418,8 @@
             whole((BOTH, MODEL)),
         ],
         out_shape=[
+            jax.ShapeDtypeStruct((BOTH, HALF_W), BF),
+            jax.ShapeDtypeStruct((BOTH, MODEL), F32),
             jax.ShapeDtypeStruct((BOTH, MODEL), F32),
             jax.ShapeDtypeStruct((BOTH, MODEL), BF),
             jax.ShapeDtypeStruct((BOTH, HIDDEN), F32),
@@ -434,8 +428,8 @@
         ],
         scratch_shapes=[pltpu.VMEM((BOTH, MODEL), F32)],
         compiler_params=params(),
-        cost_estimate=cost(7),
-    )(rows, part_own, part_recv, vec, bias, weights, weights)
+        cost_estimate=cost(8),
+    )(place, rows, recv, vec, bias, weights, weights, weights)
 
 
 def mlp_back_steps(
@@ -529,55 +523,99 @@
 
 
 PACK_ROWS = 240
-
-
-def buffer_args(buffer, count_inputs):
-    if buffer is None:
-        return [], [], {}
-    return [buffer], [pl.BlockSpec(memory_space=pl.ANY)], {count_inputs: 0}
-
-
-def mlp_weight_kernel(low_ref, normed_ref, act_ref, grad_pre_ref, after_ref, *refs):
-    grad_ref = refs[-1]
-    at = pl.program_id(0)
+CHIPS = WIDE // 2
+
+
+def store_split(place_ref, value, mine_ref, away_ref, pairs, rows, columns):
+    value = value.reshape(value.shape[0] // 2, 2, *value.shape[1:])
+    for core in range(2):
+
+        @pl.when(place_ref[1] == core)
+        def _():
+            mine_ref[pairs, rows, columns] = value[:, core]
+            away_ref[pairs, rows, columns] = value[:, 1 - core]
+
+
+EVERY = slice(None)
+
+
+def split_spec(rows, index):
+    return [pl.BlockSpec((CHIPS, rows, MODEL), lambda *g: (0, index, 0))] * 2
+
+
+def split_shape(rows):
+    return [jax.ShapeDtypeStruct((CHIPS, rows, MODEL), BF)] * 2
+
+
+ANYWHERE = pl.BlockSpec(memory_space=pl.ANY)
+SCALARS = pl.BlockSpec(memory_space=pltpu.SMEM)
+
+
+def mlp_weight_grads(low_ref, normed_ref, act_ref, grad_pre_ref):
     grad_two = tn(act_ref[...], low_ref[...]).astype(BF).reshape(16, 64, MODEL)
     grad_one = tn(normed_ref[...], grad_pre_ref[...]).astype(BF).reshape(WIDE, 32, MODEL)
-
-    @pl.when(at == 0)
-    def _():
-        grad_ref[0:16, 0:64, :] = grad_two
-        grad_ref[:, 64:96, :] = grad_one
-
-    @pl.when(at == 1)
-    def _():
-        grad_ref[16:32, 0:64, :] = grad_two
-        grad_ref[:, 96:128, :] = grad_one
-
-
-def mlp_weight_call(low, normed, act, grad_pre, after, buffer):
-    more, more_specs, aliases = buffer_args(buffer, 5)
-    rows = 128 if buffer is None else PACK_ROWS
+    return grad_two, grad_one
+
+
+MLP_WEIGHT_SPECS = [
+    whole((BOTH, MODEL)),
+    whole((BOTH, MODEL)),
+    pl.BlockSpec((BOTH, MODEL), lambda j: (0, j)),
+    pl.BlockSpec((BOTH, MODEL), lambda j: (0, j)),
+]
+
+
+def mlp_weight_kernel(low_ref, normed_ref, act_ref, grad_pre_ref, after_ref, grad_ref):
+    grad_two, grad_one = mlp_weight_grads(low_ref, normed_ref, act_ref, grad_pre_ref)
+    for at in range(2):
+
+        @pl.when(pl.program_id(0) == at)
+        def _():
+            grad_ref[16 * at : 16 * at + 16, 0:64, :] = grad_two
+            grad_ref[:, 64 + 32 * at : 96 + 32 * at, :] = grad_one
+
+
+def mlp_weight_call(low, normed, act, grad_pre, after):
     return pl.pallas_call(
         mlp_weight_kernel,
         grid=(2,),
-        in_specs=[
-            whole((BOTH, MODEL)),
-            whole((BOTH, MODEL)),
-            pl.BlockSpec((BOTH, MODEL), lambda j: (0, j)),
-            pl.BlockSpec((BOTH, MODEL), lambda j: (0, j)),
-            pl.BlockSpec(memory_space=pl.ANY),
-        ]
-        + more_specs,
+        in_specs=MLP_WEIGHT_SPECS + [ANYWHERE],
         out_specs=whole((WIDE, 128, MODEL)),
-        out_shape=jax.ShapeDtypeStruct((WIDE, rows, MODEL), BF),
-        input_output_aliases=aliases,
+        out_shape=jax.ShapeDtypeStruct((WIDE, 128, MODEL), BF),
         compiler_params=params(),
         cost_estimate=cost(8),
-    )(low, normed, act, grad_pre, after, *more)
+    )(low, normed, act, grad_pre, after)
+
+
+def mlp_weight_split_kernel(
+    place_ref, low_ref, normed_ref, act_ref, grad_pre_ref, mine_in, away_in, mine_ref, away_ref
+):
+    grad_two, grad_one = mlp_weight_grads(low_ref, normed_ref, act_ref, grad_pre_ref)
+    for at in range(2):
+
+        @pl.when(pl.program_id(0) == at)
+        def _():
+            half = slice(8 * at, 8 * at + 8)
+            store_split(place_ref, grad_two, mine_ref, away_ref, half, slice(0, 64), EVERY)
+            rows = slice(64 + 32 * at, 96 + 32 * at)
+            store_split(place_ref, grad_one, mine_ref, away_ref, EVERY, rows, EVERY)
+
+
+def mlp_weight_split_call(place, low, normed, act, grad_pre, pack):
+    return pl.pallas_call(
+        mlp_weight_split_kernel,
+        grid=(2,),
+        in_specs=[SCALARS] + MLP_WEIGHT_SPECS + [ANYWHERE] * 2,
+        out_specs=split_spec(128, 0),
+        out_shape=split_shape(PACK_ROWS),
+        input_output_aliases={5: 0, 6: 1},
+        compiler_params=params(),
+        cost_estimate=cost(8),
+    )(place, low, normed, act, grad_pre, *pack)
 
 
 def out_back_kernel(
-    grad_ref, part_own_ref, part_recv_ref, middle_ref, proj_own_ref, proj_recv_ref, vec_ref,
+    grad_ref, part_own_ref, part_recv_ref, middle_ref, branch_ref, vec_ref,
     weight_ref, middle_grad_ref, send_ref, low_ref, sums_ref,
 ):
     hat, rstd = norm_parts(middle_ref[...])
@@ -590,19 +628,18 @@
     grad_mix = nt(rows, weight_ref[...].reshape(HALF_W, MODEL))
     for pair in range(HEADS_DEV // 2):
         pack_heads(grad_mix[:, pair * 128 : pair * 128 + 128], send_ref, pair, 0)
-    branch = joined(proj_own_ref, proj_recv_ref) + row_of(vec_ref, SHIFT_O)
     sums_ref[...] = jnp.zeros((8, MODEL), F32)
     sums_ref[0:1, :] = column_sum(grad_norm * hat)
     sums_ref[1:2, :] = column_sum(grad_norm)
     sums_ref[2:3, :] = column_sum(scaled)
-    sums_ref[3:4, :] = column_sum(total * branch)
-
-
-def out_back_call(grad, part_own, part_recv, middle, proj_own, proj_recv, small, weights):
+    sums_ref[3:4, :] = column_sum(total * branch_ref[...])
+
+
+def out_back_call(grad, part_own, part_recv, middle, branch, small, weights):
     return pl.pallas_call(
         out_back_kernel,
         grid=(1,),
-        in_specs=[whole((BOTH, MODEL))] * 6
+        in_specs=[whole((BOTH, MODEL))] * 5
         + [whole((8, MODEL)), pl.BlockSpec((WIDE, 16, MODEL), lambda i: (0, 8, 0))],
         out_specs=[
             whole((BOTH, MODEL)), whole((WIDE, 16, 128)), whole((BOTH, MODEL)), whole((8, MODEL))
@@ -615,47 +652,51 @@
         ],
         compiler_params=params(),
         cost_estimate=cost(4),
-    )(grad, part_own, part_recv, middle, proj_own, proj_recv, small[0], weights)
-
-
-def out_weight_kernel(mixture_ref, low_ref, grad_ref):
-    grad_ref[...] = tn(mixture_ref[...], low_ref[...]).astype(BF).reshape(WIDE, 16, MODEL)
-
-
-def out_weight_last_kernel(mixture_ref, low_ref, *refs):
-    *sums_refs, before_ref, buffer_ref, grad_ref = refs
-    grad_ref[:, 0:16, :] = tn(mixture_ref[...], low_ref[...]).astype(BF).reshape(WIDE, 16, MODEL)
+    )(grad, part_own, part_recv, middle, branch, small[0], weights)
+
+
+def out_weight_kernel(place_ref, mixture_ref, low_ref, mine_ref, away_ref):
+    grad = tn(mixture_ref[...], low_ref[...]).astype(BF).reshape(WIDE, 16, MODEL)
+    store_split(place_ref, grad, mine_ref, away_ref, EVERY, EVERY, EVERY)
+
+
+def out_weight_last_kernel(place_ref, mixture_ref, low_ref, *refs):
+    *sums_refs, before_ref, mine_in, away_in, mine_ref, away_ref = refs
+    grad = tn(mixture_ref[...], low_ref[...]).astype(BF).reshape(WIDE, 16, MODEL)
+    store_split(place_ref, grad, mine_ref, away_ref, EVERY, slice(0, 16), EVERY)
     parts = [ref[0:4, :] for ref in sums_refs] + [before_ref[0:12, :].astype(F32)]
     rows = jnp.concatenate(parts, axis=0).astype(BF)
-    grad_ref[:, 16:48, :] = jnp.broadcast_to(rows[None], (WIDE, 32, MODEL))
-
-
-def out_weight_call(mixture, low):
+    rows = jnp.broadcast_to(rows[None], (CHIPS, 32, MODEL))
+    mine_ref[:, 16:48, :] = rows
+    away_ref[:, 16:48, :] = rows
+
+
+def out_weight_call(place, mixture, low):
     return pl.pallas_call(
         out_weight_kernel,
         grid=(1,),
-        in_specs=[whole((BOTH, HALF_W)), whole((BOTH, MODEL))],
-        out_specs=pl.BlockSpec((WIDE, 16, MODEL), lambda i: (0, 8, 0)),
-        out_shape=jax.ShapeDtypeStruct((WIDE, PACK_ROWS, MODEL), BF),
+        in_specs=[SCALARS, whole((BOTH, HALF_W)), whole((BOTH, MODEL))],
+        out_specs=split_spec(16, 8),
+        out_shape=split_shape(PACK_ROWS),
         compiler_params=params(),
         cost_estimate=cost(2),
-    )(mixture, low)
-
-
-def out_weight_last_call(mixture, low, sums, before, buffer):
-    count = 3 + len(sums)
+    )(place, mixture, low)
+
+
+def out_weight_last_call(place, mixture, low, sums, before, pack):
+    count = 4 + len(sums)
     return pl.pallas_call(
         out_weight_last_kernel,
         grid=(1,),
-        in_specs=[whole((BOTH, HALF_W)), whole((BOTH, MODEL))]
+        in_specs=[SCALARS, whole((BOTH, HALF_W)), whole((BOTH, MODEL))]
         + [whole((8, MODEL)) for _ in sums]
-        + [whole((16, MODEL)), pl.BlockSpec(memory_space=pl.ANY)],
-        out_specs=pl.BlockSpec((WIDE, 48, MODEL), lambda i: (0, 4, 0)),
-        out_shape=jax.ShapeDtypeStruct((WIDE, PACK_ROWS, MODEL), BF),
-        input_output_aliases={count: 0},
+        + [whole((16, MODEL)), ANYWHERE, ANYWHERE],
+        out_specs=split_spec(48, 4),
+        out_shape=split_shape(PACK_ROWS),
+        input_output_aliases={count: 0, count + 1: 1},
         compiler_params=params(),
         cost_estimate=cost(3),
-    )(mixture, low, *sums, before, buffer)
+    )(place, mixture, low, *sums, before, *pack)
 
 
 def qkv_back_kernel(recv_ref, rows_ref, vec_ref, weight_ref, part_ref, grads_ref, sums_ref):
@@ -711,71 +752,74 @@
     )(recv, rows, small[0], weight)
 
 
-def store_qkv_grads(normed_ref, grads_ref, grad_ref):
+def store_qkv_grads(place_ref, normed_ref, grads_ref, mine_ref, away_ref):
     rows = normed_ref[...]
 
     def part(which):
         grads = grads_ref[:, which * HALF_W : which * HALF_W + HALF_W]
         return tn(rows, grads).astype(BF).reshape(WIDE, 32, HALF_W)
 
-    grad_ref[:, 0:32, 0:HALF_W] = part(0)
-    grad_ref[:, 0:32, HALF_W:MODEL] = part(1)
+    low, high = slice(0, HALF_W), slice(HALF_W, MODEL)
+    store_split(place_ref, part(0), mine_ref, away_ref, EVERY, slice(0, 32), low)
+    store_split(place_ref, part(1), mine_ref, away_ref, EVERY, slice(0, 32), high)
     values = part(2)
-    grad_ref[:, 32:48, 0:HALF_W] = values[:, 0:16]
-    grad_ref[:, 32:48, HALF_W:MODEL] = values[:, 16:32]
-
-
-def qkv_weight_kernel(normed_ref, grads_ref, buffer_ref, grad_ref):
-    store_qkv_grads(normed_ref, grads_ref, grad_ref)
-
-
-def qkv_weight_last_kernel(normed_ref, grads_ref, sums_ref, grad_ref):
-    store_qkv_grads(normed_ref, grads_ref, grad_ref)
-    grad_ref[:, 48:56, :] = jnp.broadcast_to(sums_ref[...].astype(BF)[None], (WIDE, 8, MODEL))
-
-
-def qkv_weight_call(normed, grads, buffer):
+    store_split(place_ref, values[:, 0:16], mine_ref, away_ref, EVERY, slice(32, 48), low)
+    store_split(place_ref, values[:, 16:32], mine_ref, away_ref, EVERY, slice(32, 48), high)
+
+
+def qkv_weight_kernel(place_ref, normed_ref, grads_ref, mine_in, away_in, mine_ref, away_ref):
+    store_qkv_grads(place_ref, normed_ref, grads_ref, mine_ref, away_ref)
+
+
+def qkv_weight_last_kernel(place_ref, normed_ref, grads_ref, sums_ref, mine_ref, away_ref):
+    store_qkv_grads(place_ref, normed_ref, grads_ref, mine_ref, away_ref)
+    rows = jnp.broadcast_to(sums_ref[...].astype(BF)[None], (CHIPS, 8, MODEL))
+    mine_ref[:, 48:56, :] = rows
+    away_ref[:, 48:56, :] = rows
+
+
+def qkv_weight_call(place, normed, grads, pack):
     return pl.pallas_call(
         qkv_weight_kernel,
         grid=(1,),
-        in_specs=[whole((BOTH, MODEL)), whole((BOTH, 3 * HALF_W)), pl.BlockSpec(memory_space=pl.ANY)],
-        out_specs=qkv_block(3),
-        out_shape=jax.ShapeDtypeStruct((WIDE, PACK_ROWS, MODEL), BF),
-        input_output_aliases={2: 0},
+        in_specs=[SCALARS, whole((BOTH, MODEL)), whole((BOTH, 3 * HALF_W)), ANYWHERE, ANYWHERE],
+        out_specs=split_spec(48, 3),
+        out_shape=split_shape(PACK_ROWS),
+        input_output_aliases={3: 0, 4: 1},
         compiler_params=params(),
         cost_estimate=cost(4),
-    )(normed, grads, buffer)
-
-
-def qkv_weight_last_call(normed, grads, sums):
+    )(place, normed, grads, *pack)
+
+
+def qkv_weight_last_call(place, normed, grads, sums):
     return pl.pallas_call(
         qkv_weight_last_kernel,
         grid=(1,),
-        in_specs=[whole((BOTH, MODEL)), whole((BOTH, 3 * HALF_W)), whole((8, MODEL))],
-        out_specs=whole((WIDE, 56, MODEL)),
-        out_shape=jax.ShapeDtypeStruct((WIDE, 56, MODEL), BF),
+        in_specs=[SCALARS, whole((BOTH, MODEL)), whole((BOTH, 3 * HALF_W)), whole((8, MODEL))],
+        out_specs=split_spec(56, 0),
+        out_shape=split_shape(56),
         compiler_params=params(),
         cost_estimate=cost(4),
-    )(normed, grads, sums)
+    )(place, normed, grads, sums)
 
 
 def all_to_all(block):
     return lax.all_to_all(block, "wide", 0, 0, tiled=True)
 
 
-def layer_forward(inputs, ids, qkv, rest, small):
+def layer_forward(place, inputs, ids, qkv, rest, small):
     flags, key_ids, query_ids = ids
     sent, rows, normed_a = qkv_call(inputs, small, *qkv)
     recv = all_to_all(sent)
     mix_sent, mix_keep, lse = attend_call(flags, recv, key_ids, query_ids)
-    mixture, proj = out_call(all_to_all(mix_sent), rest)
-    proj_recv = swap(proj, "tensor")
-    middle, normed_c, pre, act, mlp = mlp_call(rows, proj, proj_recv, small, rest)
+    mix_recv = lax.all_to_all(
+        mix_sent.reshape(2 * WIDE, 16, 128), ("tensor", "wide"), 0, 0, tiled=True
+    )
+    mixture, branch, middle, normed_c, pre, act, mlp = mlp_call(place, rows, mix_recv, small, rest)
     mlp_recv = swap(mlp, "tensor")
     return dict(
         rows=rows, normed_a=normed_a, recv=recv, keep=mix_keep, lse=lse, mixture=mixture,
-        proj=proj, proj_recv=proj_recv, middle=middle, normed_c=normed_c, pre=pre, act=act,
-        mlp=mlp, mlp_recv=mlp_recv,
+        branch=branch, middle=middle, normed_c=normed_c, pre=pre, act=act, mlp=mlp, mlp_recv=mlp_recv,
     )
 
 
@@ -785,7 +829,7 @@
         inputs, small, kept["mlp"], kept["mlp_recv"], kept["pre"], rest
     )
     middle_grad, mix_grad, low_a, out_sums = out_back_call(
-        grad, part, swap(part, "tensor"), kept["middle"], kept["proj"], kept["proj_recv"], small, rest
+        grad, part, swap(part, "tensor"), kept["middle"], kept["branch"], small, rest
     )
     back = attend_back_call(
         flags, kept["recv"], all_to_all(mix_grad), kept["keep"], kept["lse"], key_ids, query_ids
@@ -810,59 +854,57 @@
     def one(array):
         return lax.dynamic_index_in_dim(array, section, 0, keepdims=False)
 
+    place = jnp.stack([tensor, lax.rem(wide, 2)]).astype(jnp.int32)
+
     qkv = w_qkv[0]
-    small_row = jnp.concatenate(
+    small_rows = jnp.concatenate(
         [
-            gains.reshape(-1),
-            shifts.reshape(-1),
-            layer_scales.reshape(-1),
-            qv_bias.reshape(-1),
-            fc1_bias.reshape(-1),
-            jnp.zeros((672,), BF),
-        ]
-    ).reshape(1, MODEL)
+            jnp.pad(jnp.concatenate([gains[0], shifts[0], layer_scales[0]], axis=0), ((0, 0), (0, 32))),
+            jnp.pad(qv_bias[0], ((0, 0), (0, 48))),
+            fc1_bias,
+        ],
+        axis=0,
+    )
     pack_a = jnp.concatenate(
         [
             jnp.concatenate([qkv[:, 0], qkv[:, 1]], axis=1),
             jnp.concatenate([qkv[0:16, 2], qkv[16:32, 2]], axis=1),
-            small_row,
-            jnp.zeros((15, MODEL), BF),
+            jnp.pad(small_rows, ((0, 5), (0, MODEL - 64))),
         ],
         axis=0,
     )
-    pack_b = jnp.concatenate([w_fc2[0], w_fc1[0][:, :MODEL], w_fc1[0][:, MODEL:], w_out[0]], axis=0)
     own_rows, own_cot = one(x_in), one(out_cot)
-    other_both = swap(jnp.concatenate([own_rows, own_cot], axis=0), "tensor")
-    other_rows, other_cot = other_both[:ROWS], other_both[ROWS:]
+    partner = swap(jnp.concatenate([own_rows, own_cot, w_out[0]], axis=0), "tensor")
+    other_rows, other_cot, other_out = partner[:ROWS], partner[ROWS:BOTH], partner[BOTH:]
+    pack_b = jnp.concatenate(
+        [w_fc2[0], w_fc1[0][:, :MODEL], w_fc1[0][:, MODEL:], w_out[0], other_out], axis=0
+    )
     other_a = swap(pack_a, "section")
-    pack_b = jnp.concatenate([pack_b, other_rows[:16]], axis=0)
     other_b = swap(pack_b, "section")
 
     def gather(block):
         return lax.all_gather(block, "wide", axis=0, tiled=False)
 
-    def behind(block, rows):
-        return jnp.concatenate([block[:144], rows], axis=0)
-
-    attn_both = gather(
-        jnp.where(
-            is_first,
-            jnp.concatenate([pack_a, pack_a[48:64], pack_a[48:64], other_a], axis=0),
-            jnp.concatenate([other_a, other_a[48:64], other_a[48:64], pack_a], axis=0),
-        )
-    )
-    rest_first = gather(behind(jnp.where(is_first, pack_b, other_b), attn_both[0, 48:64]))
+    def joined_a(first, second):
+        vectors = jnp.concatenate([first[48:64, :HALF_W], second[48:64, :HALF_W]], axis=1)
+        return jnp.concatenate([first[:48], second[:48], vectors], axis=0)
+
+    attn_both = gather(jnp.where(is_first, joined_a(pack_a, other_a), joined_a(other_a, pack_a)))
+
+    rest_first = gather(
+        jnp.concatenate([jnp.where(is_first, pack_b, other_b), attn_both[0, 96:112]], axis=0)
+    )
 
     def rest_second(rows):
-        return gather(behind(jnp.where(is_first, other_b, pack_b), rows))
-
-    def small_rows(at):
-        block = attn_both[:, at, :].astype(F32)
-        vec = jnp.transpose(block[:, :256].reshape(WIDE, 8, 32), (1, 0, 2)).reshape(8, MODEL)
-        bias = jnp.transpose(block[:, 256:288].reshape(WIDE, 2, 16), (1, 0, 2)).reshape(2, HALF_W)
-        return vec, bias, block[:, 288:352].reshape(1, HIDDEN)
-
-    small = (small_rows(48), small_rows(96 + 48))
+        return gather(jnp.concatenate([jnp.where(is_first, other_b, pack_b), rows], axis=0))
+
+    def small_of(layer):
+        block = attn_both[:, 96:107, layer * HALF_W : layer * HALF_W + 64].astype(F32)
+        vec = jnp.transpose(block[:, 0:8, 0:32], (1, 0, 2)).reshape(8, MODEL)
+        bias = jnp.transpose(block[:, 8:10, 0:16], (1, 0, 2)).reshape(2, HALF_W)
+        return vec, bias, block[:, 10].reshape(1, HIDDEN)
+
+    small = (small_of(0), small_of(1))
 
     id_grid = one(image_ids).reshape(2, WIDE, ROWS)
     sorted_ids = jnp.where(tensor == 0, id_grid, id_grid[::-1])
@@ -880,10 +922,11 @@
     ).astype(jnp.int32)
     ids = (flags, key_ids, query_ids)
 
-    qkv_parts = ((attn_both, 0), (attn_both, 2))
-    kept0 = layer_forward((own_rows, other_rows), ids, qkv_parts[0], rest_first, small[0])
-    rest = (rest_first, rest_second(kept0["proj"][:16]))
+    qkv_parts = ((attn_both, 0), (attn_both, 1))
+    kept0 = layer_forward(place, (own_rows, other_rows), ids, qkv_parts[0], rest_first, small[0])
+    rest = (rest_first, rest_second(kept0["mlp"][:16]))
     kept1 = layer_forward(
+        place,
         (kept0["middle"], kept0["mlp"], kept0["mlp_recv"], small[0][0]),
         ids, qkv_parts[1], rest[1], small[1],
     )
@@ -904,28 +947,42 @@
     )
     sum_mlp1 = rs(
         mlp_weight_call(
-            back1["low_m"], kept1["normed_c"], kept1["act"], back1["grad_pre"], back1["out_sums"], None
+            back1["low_m"], kept1["normed_c"], kept1["act"], back1["grad_pre"], back1["out_sums"]
         )
     )
-    pack = out_weight_call(kept1["mixture"], back1["low_a"])
-    pack = qkv_weight_call(kept1["normed_a"], back1["qkv_grads"], pack)
+    pack = out_weight_call(place, kept1["mixture"], back1["low_a"])
+    pack = qkv_weight_call(place, kept1["normed_a"], back1["qkv_grads"], pack)
 
     carried0, back0, (grad_x1,) = layer_backward(
         carried1 + (small[1][0],), kept0, ids, qkv_parts[0], rest[0], small[0]
     )
-    pack = mlp_weight_call(
-        back0["low_m"], kept0["normed_c"], kept0["act"], back0["grad_pre"], back0["low_m"], pack
+    pack = mlp_weight_split_call(
+        place, back0["low_m"], kept0["normed_c"], kept0["act"], back0["grad_pre"], pack
     )
     pack = out_weight_last_call(
+        place,
         kept0["mixture"],
         back0["low_a"],
         (back1["mlp_sums"], back1["out_sums"], back1["qkv_sums"], back0["mlp_sums"], back0["out_sums"]),
         sum_mlp1,
         pack,
     )
-    sum_mid = rs(pack)
-    last_pack = qkv_weight_last_call(kept0["normed_a"], back0["qkv_grads"], back0["qkv_sums"])
-    sum_last = jnp.sum(all_to_all(last_pack).astype(F32), axis=0)
+
+    same_core = [list(range(core, WIDE, 2)) for core in range(2)]
+
+    def over_chip(mine, away):
+        came = lax.ppermute(away, "wide", [(i, i ^ 1) for i in range(WIDE)])
+        return (mine.astype(F32) + came.astype(F32)).astype(BF)
+
+    sum_mid = lax.psum_scatter(
+        over_chip(*pack).reshape(CHIPS * PACK_ROWS, MODEL),
+        "wide", scatter_dimension=0, axis_index_groups=same_core, tiled=True,
+    )
+    last_pack = qkv_weight_last_call(place, kept0["normed_a"], back0["qkv_grads"], back0["qkv_sums"])
+    last_recv = lax.all_to_all(
+        over_chip(*last_pack), "wide", 0, 0, axis_index_groups=same_core, tiled=True
+    )
+    sum_last = jnp.sum(last_recv.astype(F32), axis=0)
 
     middle_grad0, part0, part_recv0, _ = carried0
     hat0, rstd0 = norm_parts(own_rows.astype(F32))

time: 589 us -> 542 us (0.920)
  blocking collectives: 112 us -> 81.5 us
  waiting for transfers between devices: 201 us -> 176 us
  other arithmetic: 14.5 us -> 35.2 us
  local copies, waits for them, and re-layouts: 39.9 us -> 32.7 us
    all_to_all x3 -> x2, waiting for transfers between devices: 75.6 us -> 34 us  [all_to_all(): return lax.all_to_all(block, 'wide', 0, 0, tiled=True)]
    all_to_all x0 -> x3, waiting for transfers between devices: none -> 38.9 us  [the longest x2 21.4 us: layer_forward(): lax.all_to_all(mix_sent.reshape(2 * WIDE, 16, 128), ('tensor', 'wide'), 0...]
    all_to_all x6 -> x4, blocking collectives: 112 us -> 81.5 us  [all_to_all(): return lax.all_to_all(block, 'wide', 0, 0, tiled=True)]
    reduce_scatter x2 -> x1, waiting for transfers between devices: 20.5 us -> 0.97 us  [rs(): lax.psum_scatter(pack.reshape(WIDE * pack.shape[1], MODEL), 'wide', scatt...]
    all_to_all x0 -> x3, starting transfers between devices: none -> 19.2 us  [the longest x2 14.2 us: layer_forward(): lax.all_to_all(mix_sent.reshape(2 * WIDE, 16, 128), ('tensor', 'wide'), 0...]
    convert_element_type x2 -> x3, other arithmetic: 0.07 us -> 17.5 us  [the longest x2 16.5 us: over_chip(): return (mine.astype(F32) + came.astype(F32)).astype(BF)]
    ppermute x16 -> x14, starting transfers between devices: 39.7 us -> 24.6 us  [swap(): return lax.ppermute(block, axis, [(0, 1), (1, 0)])]
    ppermute x0 -> x2, waiting for transfers between devices: none -> 12.7 us  [over_chip(): came = lax.ppermute(away, 'wide', [(i, i ^ 1) for i in range(WIDE)])]
  transfers between devices with their start and end apart: 25 -> 27, of which waited for: 20 -> 20; matrix products, arithmetic and copies ran while one was open for 5% -> 6% of each run, Pallas kernels for 19% -> 19%
where the time goes in v3:
time: 542 us; the launch traced here: 534 us
  waiting for transfers between devices  176 us (32%)
  Pallas kernels  139 us (26%)
  blocking collectives  81.5 us (15%)
  starting transfers between devices  54.5 us (10%)
  other arithmetic  35.2 us (6%)
  local copies, waits for them, and re-layouts  32.7 us (6%)
  between operations  14.8 us (3%)
    all_to_all x4, blocking collectives, all_to_all(): return lax.all_to_all(block, 'wide', 0, 0, tiled=True)  81.5 us
    ppermute x14, waiting for transfers between devices, swap(): return lax.ppermute(block, axis, [(0, 1), (1, 0)])  50.8 us
    all_gather x3, waiting for transfers between devices, gather(): return lax.all_gather(block, 'wide', axis=0, tiled=False)  38.7 us
    all_to_all x2, waiting for transfers between devices, all_to_all(): return lax.all_to_all(block, 'wide', 0, 0, tiled=True)  34 us
    pallas_call x2, Pallas kernels, attend_back_call(): pl.pallas_call(attend_back_kernel, grid_spec=pltpu.PrefetchScalarGridSpec...  30.3 us
    ppermute x14, starting transfers between devices, swap(): return lax.ppermute(block, axis, [(0, 1), (1, 0)])  24.6 us
    pallas_call x2, Pallas kernels, attend_call(): pl.pallas_call(attend_kernel, grid_spec=pltpu.PrefetchScalarGridSpec(num_...  24.1 us
    all_to_all x2, waiting for transfers between devices, layer_forward(): lax.all_to_all(mix_sent.reshape(2 * WIDE, 16, 128), ('tensor', 'wide'), 0...  21.4 us
  transfers between devices with their start and end apart: 27, of which 20 were waited for; matrix products, arithmetic and copies ran while one was open for 6% of the time, Pallas kernels for 19%

profile of v3, /device:TPU:0, one launch (start us, length us, event | category | flops | bytes accessed | tf_op | source)
XLA Modules:
  0.0 534.0 jit_solution(10865933876974123780)
XLA Ops:
  29.9 6.1 %collective-permute-done.2 = bf16[160,1024]{1,0:T(8,128)(2,1)S(1)} collective-permute-done((bf16[160,1024]{1,0:T(8,128)(2,1)S(1)}, bf16[160,1024]{1,0:T(8,128)(2,1)S(1)}, u32[]{:S(2)}, u32[]{:S(2)}) %collective-permute-start.2) | collective-permute-done | bytes 327712 | tf_op jit(solution)/shard_map/ppermute | solution.py:45
  36.1 33.8 %all-gather.6.cloned.1.call-done.weight_ref = bf16[32,112,1024]{2,1,0:T(8,128)(2,1)} async-done(((bf16[1,112,1024]{2,1,0:T(8,128)(2,1)}), bf16[32,112,1024]{2,1,0:T(8,128)(2,1)}) %all-gather.6.cloned.1.call-update) | async-done | bytes 7340048 | tf_op jit(solution)/shard_map/all_gather | solution.py:886
  78.8 5.1 all-to-all-start
  87.8 18.3 %all-to-all-done.recv_ref = bf16[32,144,128]{2,1,0:T(8,128)(2,1)S(1)} async-done(((bf16[32,144,128]{2,1,0:T(8,128)(2,1)}), bf16[32,144,128]{2,1,0:T(8,128)(2,1)S(1)}, u32[]{:S(2)}, u32[]{:S(2)}) %all-to-all-start) | async-done | bytes 1179680 | tf_op jit(solution)/shard_map/all_to_all | solution.py:807
  107.2 12.0 %shard_map.204 = (bf16[2,32,16,128]{3,2,1,0:T(8,128)(2,1)}, f32[32,16,128]{2,1,0:T(8,128)}, f32[1024,1]{1,0:T(8,128)}) custom-call(s32[4,8]{1,0:T(4,128)} %and_convert_fusion.flag_ref, bf16[32,144,128]{2,1,0:T(8,128)(2,1)} %copy-done.5, s32[8,1,512]{2,1,0:T(1,128)} %reshape.242.key_id_ref, s32[4,256,1]{2,1,0:T(8,128)} %reshape.261.query_id_ref), custom_call_target="tpu_custom_call" | custom-call | flops 12000000000 | bytes 100000 | tf_op jit(solution)/shard_map/pallas_call | solution.py:246
  119.2 7.1 %all-to-all-start.1 = ((bf16[64,16,128]{2,1,0:T(8,128)(2,1)}), bf16[64,16,128]{2,1,0:T(8,128)(2,1)S(1)}, u32[]{:S(2)}, u32[]{:S(2)}) async-start(bf16[64,16,128]{2,1,0:T(8,128)(2,1)} %bitcast.124), calls=%async_computation.1 | async-start | bytes 524288 | tf_op jit(solution)/shard_map/all_to_all | solution.py:815
  127.6 11.3 %all-to-all-done.1.recv_ref = bf16[64,16,128]{2,1,0:T(8,128)(2,1)S(1)} async-done(((bf16[64,16,128]{2,1,0:T(8,128)(2,1)}), bf16[64,16,128]{2,1,0:T(8,128)(2,1)S(1)}, u32[]{:S(2)}, u32[]{:S(2)}) %all-to-all-start.1) | async-done | bytes 262176 | tf_op jit(solution)/shard_map/all_to_all | solution.py:815
  143.8 7.1 %shard_map.205 = (bf16[128,512]{1,0:T(8,128)(2,1)}, f32[128,1024]{1,0:T(8,128)}, f32[128,1024]{1,0:T(8,128)}, bf16[128,1024]{1,0:T(8,128)(2,1)}, f32[128,2048]{1...) custom-call(s32[2]{0:T(128)} %pad_add_fusion.place_ref, bf16[128,1024]{1,0:T(8,128)(2,1)} %get-tuple-element.72.rows_ref, ...), custom_call_target="tpu_custom_call" | custom-call | flops 8000000000 | bytes 100000 | tf_op jit(solution)/shard_map/pallas_call | solution.py:398
  157.0 5.7 %collective-permute-done.3.mlp_recv_ref.refs_2_ = bf16[128,1024]{1,0:T(8,128)(2,1)S(1)} collective-permute-done((bf16[128,1024]{1,0:T(8,128)(2,1)}, bf16[128,1024]{1,0:T(8,128)(2,1)S(1)}, u32[]{:S(2)}, u32[]{:S(2)}) %collective-permute-start.3) | collective-permute-done | bytes 262176 | tf_op jit(solution)/shard_map/ppermute | solution.py:45
  167.6 27.5 %all_to_all.45.recv_ref = bf16[32,144,128]{2,1,0:T(8,128)(2,1)} all-to-all(bf16[32,144,128]{2,1,0:T(8,128)(2,1)} %get-tuple-element.78), channel_id=1, replica_groups=mesh['section'=2,'tensor'=2,'wide'=32] {'wide'}, dimensions={0} | all-to-all | bytes 2359296 | tf_op jit(solution)/shard_map/all_to_all | solution.py:807
  195.1 12.1 %shard_map.207 = (bf16[2,32,16,128]{3,2,1,0:T(8,128)(2,1)}, f32[32,16,128]{2,1,0:T(8,128)}, f32[1024,1]{1,0:T(8,128)}) custom-call(s32[4,8]{1,0:T(4,128)} %and_convert_fusion.flag_ref, bf16[32,144,128]{2,1,0:T(8,128)(2,1)} %all_to_all.45.recv_ref, s32[8,1,512]{2,1,0:T(1,128)} %reshape.242.key_id_ref, s32[4,256,1]{2,1,0:T(8,128)} %reshape.261.query_id_ref), custom_call_target="tpu_custom_call" | custom-call | flops 12000000000 | bytes 100000 | tf_op jit(solution)/shard_map/pallas_call | solution.py:246
  207.2 7.1 %all-to-all-start.3 = ((bf16[64,16,128]{2,1,0:T(8,128)(2,1)}), bf16[64,16,128]{2,1,0:T(8,128)(2,1)S(1)}, u32[]{:S(2)}, u32[]{:S(2)}) async-start(bf16[64,16,128]{2,1,0:T(8,128)(2,1)} %bitcast.125), calls=%async_computation.3 | async-start | bytes 524288 | tf_op jit(solution)/shard_map/all_to_all | solution.py:815
  215.1 10.1 %all-to-all-done.3.recv_ref = bf16[64,16,128]{2,1,0:T(8,128)(2,1)S(1)} async-done(((bf16[64,16,128]{2,1,0:T(8,128)(2,1)}), bf16[64,16,128]{2,1,0:T(8,128)(2,1)S(1)}, u32[]{:S(2)}, u32[]{:S(2)}) %all-to-all-start.3) | async-done | bytes 262176 | tf_op jit(solution)/shard_map/all_to_all | solution.py:815
  225.9 7.1 %shard_map.208 = (bf16[128,512]{1,0:T(8,128)(2,1)}, f32[128,1024]{1,0:T(8,128)}, f32[128,1024]{1,0:T(8,128)}, bf16[128,1024]{1,0:T(8,128)(2,1)}, f32[128,2048]{1...) custom-call(s32[2]{0:T(128)} %pad_add_fusion.place_ref, bf16[128,1024]{1,0:T(8,128)(2,1)} %get-tuple-element.77.rows_ref, ...), custom_call_target="tpu_custom_call" | custom-call | flops 8000000000 | bytes 100000 | tf_op jit(solution)/shard_map/pallas_call | solution.py:398
  234.5 8.6 %collective-permute-done.4.refs_2_ = bf16[128,1024]{1,0:T(8,128)(2,1)S(1)} collective-permute-done((bf16[128,1024]{1,0:T(8,128)(2,1)}, bf16[128,1024]{1,0:T(8,128)(2,1)S(1)}, u32[]{:S(2)}, u32[]{:S(2)}) %collective-permute-start.4) | collective-permute-done | bytes 262176 | tf_op jit(solution)/shard_map/ppermute | solution.py:45
  243.8 7.1 %shard_map.209 = (bf16[128,1024]{1,0:T(8,128)(2,1)}, bf16[128,1024]{1,0:T(8,128)(2,1)}, bf16[128,2048]{1,0:T(8,128)(2,1)}, bf16[128,1024]{1,0:T(8,128)(2,1)}, f32[8,1024]{1,0:T(8,128)}) custom-call(bf16[64,1024]{1,0:T(8,128)(2,1)} %copy-done.12, bf16[64,1024]{1,0:T(8,128)(2,1)} %get-tuple-element.167.other_ref, ...), custom_call_target="tpu_custom_call" | custom-call | flops 8000000000 | bytes 100000 | tf_op jit(solution)/shard_map/pallas_call | solution.py:491
  252.1 8.1 %collective-permute-done.6.part_recv_ref = bf16[128,1024]{1,0:T(8,128)(2,1)S(1)} collective-permute-done((bf16[128,1024]{1,0:T(8,128)(2,1)}, bf16[128,1024]{1,0:T(8,128)(2,1)S(1)}, u32[]{:S(2)}, u32[]{:S(2)}) %collective-permute-start.6) | collective-permute-done | bytes 262176 | tf_op jit(solution)/shard_map/ppermute | solution.py:45
  264.5 7.8 %shard_map.218 = bf16[32,128,1024]{2,1,0:T(8,128)(2,1)} custom-call(bf16[128,1024]{1,0:T(8,128)(2,1)} %get-tuple-element.113.low_ref, bf16[128,1024]{1,0:T(8,128)(2,1)} %get-tuple-element.114.normed_ref, bf16[128,2048]{1,0:T(8,128)(2,1)} %get-tuple-element.115.act_ref, bf16[128,2048]{1,0:T(8,128)(2,1)} %get-tuple-element.116.grad_pre_ref, ...), custom_call_target="tpu_custom_call" | custom-call | flops 8000000000 | bytes 100000 | tf_op jit(solution)/shard_map/pallas_call | solution.py:579
  273.2 11.9 %all_to_all.46.grad_ref = bf16[32,16,128]{2,1,0:T(8,128)(2,1)} all-to-all(bf16[32,16,128]{2,1,0:T(8,128)(2,1)S(1)} %copy-done.15), channel_id=1, replica_groups=mesh['section'=2,'tensor'=2,'wide'=32] {'wide'}, dimensions={0} | all-to-all | bytes 262144 | tf_op jit(solution)/shard_map/all_to_all | solution.py:807
  285.1 15.2 %shard_map.211 = bf16[32,144,128]{2,1,0:T(8,128)(2,1)} custom-call(s32[4,8]{1,0:T(4,128)} %and_convert_fusion.flag_ref, bf16[32,144,128]{2,1,0:T(8,128)(2,1)} %all_to_all.45.recv_ref, bf16[32,16,128]{2,1,0:T(8,128)(2,1)} %all_to_all.46.grad_ref, f32[32,16,128]{2,1,0:T(8,128)} %get-tuple-element.88.keep_ref, f32[1024,1]{1,0:T(8,128)} %get-tuple-element.89.lse_ref, ...), custom_call_target="tpu_custom_call" | custom-call | flops 16000000000 | bytes 100000 | tf_op jit(solution)/shard_map/pallas_call | solution.py:333
  306.9 15.7 %all-to-all-done.5.recv_ref = bf16[32,144,128]{2,1,0:T(8,128)(2,1)S(1)} async-done(((bf16[32,144,128]{2,1,0:T(8,128)(2,1)}), bf16[32,144,128]{2,1,0:T(8,128)(2,1)S(1)}, u32[]{:S(2)}, u32[]{:S(2)}) %all-to-all-start.5) | async-done | bytes 1179680 | tf_op jit(solution)/shard_map/all_to_all | solution.py:807
  332.9 5.2 collective-permute-done.7.part_recv_ref
  338.8 8.1 %shard_map.213 = (bf16[128,1024]{1,0:T(8,128)(2,1)}, bf16[128,1024]{1,0:T(8,128)(2,1)}, bf16[128,2048]{1,0:T(8,128)(2,1)}, bf16[128,1024]{1,0:T(8,128)(2,1)}, f32[8,1024]{1,0:T(8,128)}, /*index=5*/f32[64,1024]{1,0:T(8,128)}) custom-call(f32[128,1024]{1,0:T(8,128)} %get-tuple-element.86.middle_grad_ref, bf16[128,1024]{1,0:T(8,128)(2,1)} %get-tuple-element.90.part_own_ref, ...), custom_call_target="tpu_custom_call" | custom-call | flops 8000000000 | bytes 100000 | tf_op jit(solution)/shard_map/pallas_call | solution.py:491
  347.7 8.1 %shard_map.221 = (bf16[16,240,1024]{2,1,0:T(8,128)(2,1)}, bf16[16,240,1024]{2,1,0:T(8,128)(2,1)}) custom-call(s32[2]{0:T(128)} %pad_add_fusion.place_ref, bf16[128,1024]{1,0:T(8,128)(2,1)} %get-tuple-element.117.low_ref, bf16[128,1024]{1,0:T(8,128)(2,1)} %get-tuple-element.118.normed_ref, ...), custom_call_target="tpu_custom_call", output_to_operand_aliasing={{0}: (5, {}), {1}: (6, {})} | custom-call | flops 8000000000 | bytes 100000 | tf_op jit(solution)/shard_map/pallas_call | solution.py:605
  365.3 12.7 %collective-permute-done.12 = bf16[16,240,1024]{2,1,0:T(8,128)(2,1)} collective-permute-done((bf16[16,240,1024]{2,1,0:T(8,128)(2,1)}, bf16[16,240,1024]{2,1,0:T(8,128)(2,1)}, u32[]{:S(2)}, u32[]{:S(2)}) %collective-permute-start.12) | collective-permute-done | bytes 7864352 | tf_op jit(solution)/shard_map/ppermute | solution.py:974
  378.0 12.9 %add_convert_fusion = bf16[16,240,1024]{2,1,0:T(8,128)(2,1)} fusion(bf16[16,240,1024]{2,1,0:T(8,128)(2,1)} %collective-permute-done.12, bf16[16,240,1024]{2,1,0:T(8,128)(2,1)} %get-tuple-element.131), kind=kLoop, calls=%fused_computation | loop fusion | flops 15728640 | bytes 23592960 | tf_op jit(solution)/shard_map/convert_element_type | solution.py:975
  391.9 13.3 %all_to_all.47.grad_ref = bf16[32,16,128]{2,1,0:T(8,128)(2,1)} all-to-all(bf16[32,16,128]{2,1,0:T(8,128)(2,1)S(1)} %copy-done.14), channel_id=1, replica_groups=mesh['section'=2,'tensor'=2,'wide'=32] {'wide'}, dimensions={0} | all-to-all | bytes 262144 | tf_op jit(solution)/shard_map/all_to_all | solution.py:807
  405.1 15.2 %shard_map.215 = bf16[32,144,128]{2,1,0:T(8,128)(2,1)} custom-call(s32[4,8]{1,0:T(4,128)} %and_convert_fusion.flag_ref, bf16[32,144,128]{2,1,0:T(8,128)(2,1)} %copy-done.5, bf16[32,16,128]{2,1,0:T(8,128)(2,1)} %all_to_all.47.grad_ref, f32[32,16,128]{2,1,0:T(8,128)} %get-tuple-element.97.keep_ref, f32[1024,1]{1,0:T(8,128)} %get-tuple-element.98.lse_ref, ...), custom_call_target="tpu_custom_call" | custom-call | flops 16000000000 | bytes 100000 | tf_op jit(solution)/shard_map/pallas_call | solution.py:333
  420.3 28.9 %all_to_all.48.recv_ref = bf16[32,144,128]{2,1,0:T(8,128)(2,1)} all-to-all(bf16[32,144,128]{2,1,0:T(8,128)(2,1)} %shard_map.215), channel_id=1, replica_groups=mesh['section'=2,'tensor'=2,'wide'=32] {'wide'}, dimensions={0} | all-to-all | bytes 2359296 | tf_op jit(solution)/shard_map/all_to_all | solution.py:807
  466.7 5.0 all-to-all-start.8
  479.4 6.0 %collective-permute-done.10 = f32[64,1024]{1,0:T(8,128)S(1)} collective-permute-done((f32[64,1024]{1,0:T(8,128)S(1)}, f32[64,1024]{1,0:T(8,128)S(1)}, u32[]{:S(2)}, u32[]{:S(2)}) %collective-permute-start.10) | collective-permute-done | bytes 262176 | tf_op jit(solution)/shard_map/ppermute | solution.py:45
  486.3 17.5 %all-to-all-done.8 = bf16[16,56,1024]{2,1,0:T(8,128)(2,1)S(1)} async-done(((bf16[16,56,1024]{2,1,0:T(8,128)(2,1)}), bf16[16,56,1024]{2,1,0:T(8,128)(2,1)S(1)}, u32[]{:S(2)}, u32[]{:S(2)}) %all-to-all-start.8) | async-done | bytes 1835040 | tf_op jit(solution)/shard_map/all_to_all | solution.py:982
  (228 shorter events, 141.6 us)
Async XLA Ops:
  7.2 62.7 %all-gather.6.cloned.1.call-start = ((), (), s32[]{:S(2)}) async-start(), calls=%async_computation.11 | async-start | bytes 7569408 | tf_op jit(solution)/shard_map/all_gather | solution.py:886
  10.2 5.2 collective-permute-start.1
  16.2 127.6 %all-gather.8.cloned.1.call-start = ((), (), s32[]{:S(2)}) async-start(), calls=%async_computation.14 | async-start | bytes 11894784 | tf_op jit(solution)/shard_map/all_gather | solution.py:886
  16.3 62.5 %copy-start.12 = (bf16[64,1024]{1,0:T(8,128)(2,1)}, bf16[64,1024]{1,0:T(8,128)(2,1)S(1)}, u32[]{:S(2)}) copy-start(bf16[64,1024]{1,0:T(8,128)(2,1)S(1)} %dynamic-slice_bitcast_fusion.own_ref) | copy-start | bytes 393220
  17.9 56.8 %copy-start.2 = (bf16[64,1024]{1,0:T(8,128)(2,1)}, bf16[64,1024]{1,0:T(8,128)(2,1)S(1)}, u32[]{:S(2)}) copy-start(bf16[64,1024]{1,0:T(8,128)(2,1)S(1)} %get-tuple-element.146.own_ref) | copy-start | bytes 393220
  18.7 9.6 %collective-permute-start = (bf16[144,1024]{1,0:T(8,128)(2,1)S(1)}, bf16[144,1024]{1,0:T(8,128)(2,1)S(1)}, u32[]{:S(2)}, u32[]{:S(2)}) collective-permute-start(bf16[144,1024]{1,0:T(8,128)(2,1)S(1)} %pad_maximum_fusion.2), channel_id=1, source_target_pairs={{0,32},{32,0},{1,33},{33,1},{2,34},{34,2},{3,35},{35,3},{4,36},{36... | collective-permute-start | bytes 884744 | tf_op jit(solution)/shard_map/ppermute | solution.py:45
  28.3 7.8 %collective-permute-start.2 = (bf16[160,1024]{1,0:T(8,128)(2,1)S(1)}, bf16[160,1024]{1,0:T(8,128)(2,1)S(1)}, u32[]{:S(2)}, u32[]{:S(2)}) collective-permute-start(bf16[160,1024]{1,0:T(8,128)(2,1)S(1)} %slice_dynamic-update-slice_fusion.2), channel_id=1, source_target_pairs={{0,64},{64,0},{1,65},{65,1},{2,66},{66,2},{3,67},{67,3},{4,68},{68... | collective-permute-start | bytes 983048 | tf_op jit(solution)/shard_map/ppermute | solution.py:45
  78.8 27.3 %all-to-all-start = ((bf16[32,144,128]{2,1,0:T(8,128)(2,1)}), bf16[32,144,128]{2,1,0:T(8,128)(2,1)S(1)}, u32[]{:S(2)}, u32[]{:S(2)}) async-start(bf16[32,144,128]{2,1,0:T(8,128)(2,1)} %get-tuple-element.73), calls=%async_computation | async-start | bytes 2359296 | tf_op jit(solution)/shard_map/all_to_all | solution.py:807
  119.2 19.8 %all-to-all-start.1 = ((bf16[64,16,128]{2,1,0:T(8,128)(2,1)}), bf16[64,16,128]{2,1,0:T(8,128)(2,1)S(1)}, u32[]{:S(2)}, u32[]{:S(2)}) async-start(bf16[64,16,128]{2,1,0:T(8,128)(2,1)} %bitcast.124), calls=%async_computation.1 | async-start | bytes 524288 | tf_op jit(solution)/shard_map/all_to_all | solution.py:815
  126.3 98.9 %all-gather.10.cloned.1.call-start = ((), (), s32[]{:S(2)}) async-start(), calls=%async_computation.15 | async-start | bytes 11894784 | tf_op jit(solution)/shard_map/all_gather | solution.py:886
  152.4 10.3 %collective-permute-start.3 = (bf16[128,1024]{1,0:T(8,128)(2,1)}, bf16[128,1024]{1,0:T(8,128)(2,1)S(1)}, u32[]{:S(2)}, u32[]{:S(2)}) collective-permute-start(bf16[128,1024]{1,0:T(8,128)(2,1)} %get-tuple-element.76.mlp_own_ref.refs_1_), channel_id=1, source_target_pairs={{0,32},{32,0},{1,33},{33,1},{2,34},{34,2},{3,35},{35,3},{4,36},{36... | collective-permute-start | bytes 786440 | tf_op jit(solution)/shard_map/ppermute | solution.py:45
  207.2 18.0 %all-to-all-start.3 = ((bf16[64,16,128]{2,1,0:T(8,128)(2,1)}), bf16[64,16,128]{2,1,0:T(8,128)(2,1)S(1)}, u32[]{:S(2)}, u32[]{:S(2)}) async-start(bf16[64,16,128]{2,1,0:T(8,128)(2,1)} %bitcast.125), calls=%async_computation.3 | async-start | bytes 524288 | tf_op jit(solution)/shard_map/all_to_all | solution.py:815
  214.3 147.4 %reduce-scatter.3.cloned.1.call-start = ((), (), s32[]{:S(2)}) async-start(), calls=%async_computation.12 | async-start | bytes 8650752 | tf_op jit(solution)/shard_map/reduce_scatter | solution.py:941
  233.0 10.1 %collective-permute-start.4 = (bf16[128,1024]{1,0:T(8,128)(2,1)}, bf16[128,1024]{1,0:T(8,128)(2,1)S(1)}, u32[]{:S(2)}, u32[]{:S(2)}) collective-permute-start(bf16[128,1024]{1,0:T(8,128)(2,1)} %get-tuple-element.81.refs_1_), channel_id=1, source_target_pairs={{0,32},{32,0},{1,33},{33,1},{2,34},{34,2},{3,35},{35,3},{4,36},{36... | collective-permute-start | bytes 786440 | tf_op jit(solution)/shard_map/ppermute | solution.py:45
  250.9 9.3 %collective-permute-start.6 = (bf16[128,1024]{1,0:T(8,128)(2,1)}, bf16[128,1024]{1,0:T(8,128)(2,1)S(1)}, u32[]{:S(2)}, u32[]{:S(2)}) collective-permute-start(bf16[128,1024]{1,0:T(8,128)(2,1)} %get-tuple-element.84.part_own_ref), channel_id=1, source_target_pairs={{0,32},{32,0},{1,33},{33,1},{2,34},{34,2},{3,35},{35,3},{4,36},{36... | collective-permute-start | bytes 786440 | tf_op jit(solution)/shard_map/ppermute | solution.py:45
  300.2 22.3 %all-to-all-start.5 = ((bf16[32,144,128]{2,1,0:T(8,128)(2,1)}), bf16[32,144,128]{2,1,0:T(8,128)(2,1)S(1)}, u32[]{:S(2)}, u32[]{:S(2)}) async-start(bf16[32,144,128]{2,1,0:T(8,128)(2,1)} %shard_map.211), calls=%async_computation.5 | async-start | bytes 2359296 | tf_op jit(solution)/shard_map/all_to_all | solution.py:807
  304.2 200.2 %reduce-scatter.5.cloned.1.call-start = ((), (), s32[]{:S(2)}) async-start(), calls=%async_computation.13 | async-start | bytes 8355840 | tf_op jit(solution)/shard_map/reduce_scatter | solution.py:977
  327.8 10.2 %collective-permute-start.7 = (bf16[128,1024]{1,0:T(8,128)(2,1)}, bf16[128,1024]{1,0:T(8,128)(2,1)S(1)}, u32[]{:S(2)}, u32[]{:S(2)}) collective-permute-start(bf16[128,1024]{1,0:T(8,128)(2,1)} %get-tuple-element.90.part_own_ref), channel_id=1, source_target_pairs={{0,32},{32,0},{1,33},{33,1},{2,34},{34,2},{3,35},{35,3},{4,36},{36... | collective-permute-start | bytes 786440 | tf_op jit(solution)/shard_map/ppermute | solution.py:45
  346.8 9.6 %collective-permute-start.8 = (bf16[128,1024]{1,0:T(8,128)(2,1)}, bf16[128,1024]{1,0:T(8,128)(2,1)S(1)}, u32[]{:S(2)}, u32[]{:S(2)}) collective-permute-start(bf16[128,1024]{1,0:T(8,128)(2,1)} %get-tuple-element.93.part_own_ref), channel_id=1, source_target_pairs={{0,32},{32,0},{1,33},{33,1},{2,34},{34,2},{3,35},{35,3},{4,36},{36... | collective-permute-start | bytes 786440 | tf_op jit(solution)/shard_map/ppermute | solution.py:45
  365.3 12.8 %collective-permute-start.12 = (bf16[16,240,1024]{2,1,0:T(8,128)(2,1)}, bf16[16,240,1024]{2,1,0:T(8,128)(2,1)}, u32[]{:S(2)}, u32[]{:S(2)}) collective-permute-start(bf16[16,240,1024]{2,1,0:T(8,128)(2,1)} %get-tuple-element.132), channel_id=1, source_target_pairs={{0,1},{1,0},{2,3},{3,2},{4,5},{5,4},{6,7},{7,6},{8,9},{9,8},{10,11... | collective-permute-start | bytes 23592968 | tf_op jit(solution)/shard_map/ppermute | solution.py:974
  458.4 17.8 %copy-start.10 = (f32[64,1024]{1,0:T(8,128)S(1)}, f32[64,1024]{1,0:T(8,128)}, u32[]{:S(2)}) copy-start(f32[64,1024]{1,0:T(8,128)} %get-tuple-element.100) | copy-start | bytes 786436
  458.4 4.7 collective-permute-start.11
  459.9 15.1 %collective-permute-start.9 = (bf16[128,1024]{1,0:T(8,128)(2,1)S(1)}, bf16[128,1024]{1,0:T(8,128)(2,1)}, u32[]{:S(2)}, u32[]{:S(2)}) collective-permute-start(bf16[128,1024]{1,0:T(8,128)(2,1)S(1)} %copy-done.13), channel_id=1, source_target_pairs={{0,32},{32,0},{1,33},{33,1},{2,34},{34,2},{3,35},{35,3},{4,36},{36... | collective-permute-start | bytes 786440 | tf_op jit(solution)/shard_map/ppermute | solution.py:45
  466.7 47.6 %copy-start.4 = (bf16[128,1024]{1,0:T(8,128)(2,1)S(1)}, bf16[128,1024]{1,0:T(8,128)(2,1)}, u32[]{:S(2)}) copy-start(bf16[128,1024]{1,0:T(8,128)(2,1)} %reduce-scatter.3.cloned.1.call-done.refs_5_) | copy-start | bytes 786436
  466.7 37.1 %all-to-all-start.8 = ((bf16[16,56,1024]{2,1,0:T(8,128)(2,1)}), bf16[16,56,1024]{2,1,0:T(8,128)(2,1)S(1)}, u32[]{:S(2)}, u32[]{:S(2)}) async-start(bf16[16,56,1024]{2,1,0:T(8,128)(2,1)} %add_convert_fusion.1), calls=%async_computation.8 | async-start | bytes 3670016 | tf_op jit(solution)/shard_map/all_to_all | solution.py:982
  471.7 55.3 %copy-start.1 = (bf16[2,64,1024]{2,1,0:T(8,128)(2,1)S(1)}, bf16[2,64,1024]{2,1,0:T(8,128)(2,1)}, u32[]{:S(2)}) copy-start(bf16[2,64,1024]{2,1,0:T(8,128)(2,1)} %param.13) | copy-start | bytes 786436
  472.9 5.7 %collective-permute-start.5 = (bf16[64,1024]{1,0:T(8,128)(2,1)S(1)}, bf16[64,1024]{1,0:T(8,128)(2,1)S(1)}, u32[]{:S(2)}, u32[]{:S(2)}) collective-permute-start(bf16[64,1024]{1,0:T(8,128)(2,1)S(1)} %get-tuple-element.147), channel_id=1, source_target_pairs={{0,64},{64,0},{1,65},{65,1},{2,66},{66,2},{3,67},{67,3},{4,68},{68... | collective-permute-start | bytes 393224 | tf_op jit(solution)/shard_map/ppermute | solution.py:45
  477.4 8.0 %collective-permute-start.10 = (f32[64,1024]{1,0:T(8,128)S(1)}, f32[64,1024]{1,0:T(8,128)S(1)}, u32[]{:S(2)}, u32[]{:S(2)}) collective-permute-start(f32[64,1024]{1,0:T(8,128)S(1)} %get-tuple-element.143), channel_id=1, source_target_pairs={{0,64},{64,0},{1,65},{65,1},{2,66},{66,2},{3,67},{67,3},{4,68},{68... | collective-permute-start | bytes 786440 | tf_op jit(solution)/shard_map/ppermute | solution.py:45
  509.3 6.2 %collective-permute-start.13 = (bf16[49,1024]{1,0:T(8,128)(2,1)S(1)}, bf16[49,1024]{1,0:T(8,128)(2,1)S(1)}, u32[]{:S(2)}, u32[]{:S(2)}) collective-permute-start(bf16[49,1024]{1,0:T(8,128)(2,1)S(1)} %broadcast_select_fusion.7), channel_id=1, source_target_pairs={{0,64},{64,0},{1,65},{65,1},{2,66},{66,2},{3,67},{67,3},{4,68},{68... | collective-permute-start | bytes 301064 | tf_op jit(solution)/shard_map/ppermute | solution.py:45
  511.1 9.4 %collective-permute-start.16 = (bf16[64]{0:T(256)(128)(2,1)S(1)}, bf16[64]{0:T(256)(128)(2,1)S(1)}, u32[]{:S(2)}, u32[]{:S(2)}) collective-permute-start(bf16[64]{0:T(256)(128)(2,1)S(1)} %slice_bitcast_fusion.16), channel_id=1, source_target_pairs={{0,96},{96,0},{32,64},{64,32},{1,97},{97,1},{33,65},{65,33},{2,98}... | collective-permute-start | bytes 392 | tf_op jit(solution)/shard_map/ppermute | solution.py:1019
  514.4 10.4 %collective-permute-start.14 = (bf16[144,1024]{1,0:T(8,128)(2,1)S(1)}, bf16[144,1024]{1,0:T(8,128)(2,1)S(1)}, u32[]{:S(2)}, u32[]{:S(2)}) collective-permute-start(bf16[144,1024]{1,0:T(8,128)(2,1)S(1)} %broadcast_select_fusion.2), channel_id=1, source_target_pairs={{0,64},{64,0},{1,65},{65,1},{2,66},{66,2},{3,67},{67,3},{4,68},{68... | collective-permute-start | bytes 884744 | tf_op jit(solution)/shard_map/ppermute | solution.py:45
  516.3 7.2 %collective-permute-start.15 = (bf16[64]{0:T(256)(128)(2,1)S(1)}, bf16[64]{0:T(256)(128)(2,1)S(1)}, u32[]{:S(2)}, u32[]{:S(2)}) collective-permute-start(bf16[64]{0:T(256)(128)(2,1)S(1)} %slice_bitcast_fusion.17), channel_id=1, source_target_pairs={{0,32},{32,0},{1,33},{33,1},{2,34},{34,2},{3,35},{35,3},{4,36},{36... | collective-permute-start | bytes 392 | tf_op jit(solution)/shard_map/ppermute | solution.py:45
  (18 other events, 66.0 us)
Sparse Core Ops, SparseCore 0:
  16.4 53.5 all-gather.5
  72.2 71.5 all-gather.7
  152.5 63.8 all-gather.9
  272.4 89.2 reduce-scatter.2
  391.1 110.7 reduce-scatter.4

commit v4 on v3

--- a/solution.py
+++ b/solution.py
@@ -355,9 +355,14 @@
     )(flags, recv, grads, keep, lse, key_ids, query_ids)
 
 
+KEPT_C, KEPT_A, KEPT_MIX = slice(2048, 3072), slice(3072, 4096), slice(4096, 4608)
+KEPT_WIDTH = 4608
+TALL = BOTH + 16
+
+
 def mlp_kernel(
-    place_ref, rows_ref, recv_ref, vec_ref, bias_ref, out_weight_ref, one_ref, two_ref,
-    mixture_ref, branch_ref, middle_ref, normed_ref, pre_ref, act_ref, out_ref, acc_ref,
+    place_ref, rows_ref, normed_ref, recv_ref, vec_ref, bias_ref, out_weight_ref, one_ref, two_ref,
+    branch_ref, middle_ref, pre_ref, kept_ref, out_ref, acc_ref,
 ):
     at = pl.program_id(0)
 
@@ -367,7 +372,8 @@
         own = unpack_heads(recv_ref, 0, tensor * WIDE).astype(BF)
         partner = unpack_heads(recv_ref, 0, (1 - tensor) * WIDE).astype(BF)
         partner = jnp.concatenate([partner[ROWS:], partner[:ROWS]], axis=0)
-        mixture_ref[...] = own
+        kept_ref[:, KEPT_A] = normed_ref[...]
+        kept_ref[:, KEPT_MIX] = own
         proj = nn(own, out_weight_ref[:, 0:16, :].reshape(HALF_W, MODEL)) + nn(
             partner, out_weight_ref[:, 16:32, :].reshape(HALF_W, MODEL)
         )
@@ -376,30 +382,32 @@
         middle = rows_ref[...].astype(F32) + row_of(vec_ref, SCALE_A) * branch
         middle_ref[...] = middle
         hat, _ = norm_parts(middle)
-        normed_ref[...] = (hat * row_of(vec_ref, GAIN_C) + row_of(vec_ref, SHIFT_C)).astype(BF)
-
-    pre = nn(normed_ref[...], one_ref[...].reshape(MODEL, MODEL)) + bias_ref[...]
+        kept_ref[:, KEPT_C] = (hat * row_of(vec_ref, GAIN_C) + row_of(vec_ref, SHIFT_C)).astype(BF)
+
+    pre = nn(kept_ref[:, KEPT_C], one_ref[...].reshape(MODEL, MODEL)) + bias_ref[...]
     act = (0.5 * pre * (1.0 + lax.erf(pre * ROOT_HALF))).astype(BF)
     pre_ref[...] = pre
-    act_ref[...] = act
     part = nn(act, two_ref[...].reshape(MODEL, MODEL))
 
     @pl.when(at == 0)
     def _():
+        kept_ref[:, 0:MODEL] = act
         acc_ref[...] = part
 
     @pl.when(at == 1)
     def _():
+        kept_ref[:, MODEL:HIDDEN] = act
         out_ref[...] = (acc_ref[...] + part).astype(BF)
 
 
-def mlp_call(place, rows, recv, small, weights):
+def mlp_call(place, rows, normed, recv, small, weights):
     vec, _, bias = small
     return pl.pallas_call(
         mlp_kernel,
         grid=(2,),
         in_specs=[
             pl.BlockSpec(memory_space=pltpu.SMEM),
+            whole((BOTH, MODEL)),
             whole((BOTH, MODEL)),
             whole((2 * WIDE, 16, 128)),
             whole((8, MODEL)),
@@ -409,32 +417,28 @@
             pl.BlockSpec((16, 64, MODEL), lambda j: (j, 0, 0)),
         ],
         out_specs=[
-            whole((BOTH, HALF_W)),
-            whole((BOTH, MODEL)),
             whole((BOTH, MODEL)),
             whole((BOTH, MODEL)),
             pl.BlockSpec((BOTH, MODEL), lambda j: (0, j)),
-            pl.BlockSpec((BOTH, MODEL), lambda j: (0, j)),
+            whole((BOTH, KEPT_WIDTH)),
             whole((BOTH, MODEL)),
         ],
         out_shape=[
-            jax.ShapeDtypeStruct((BOTH, HALF_W), BF),
             jax.ShapeDtypeStruct((BOTH, MODEL), F32),
             jax.ShapeDtypeStruct((BOTH, MODEL), F32),
+            jax.ShapeDtypeStruct((BOTH, HIDDEN), F32),
+            jax.ShapeDtypeStruct((BOTH, KEPT_WIDTH), BF),
             jax.ShapeDtypeStruct((BOTH, MODEL), BF),
-            jax.ShapeDtypeStruct((BOTH, HIDDEN), F32),
-            jax.ShapeDtypeStruct((BOTH, HIDDEN), BF),
-            jax.ShapeDtypeStruct((BOTH, MODEL), BF),
         ],
         scratch_shapes=[pltpu.VMEM((BOTH, MODEL), F32)],
         compiler_params=params(),
         cost_estimate=cost(8),
-    )(place, rows, recv, vec, bias, weights, weights, weights)
+    )(place, rows, normed, recv, vec, bias, weights, weights, weights)
 
 
 def mlp_back_steps(
     grad, vec_ref, mlp_own_ref, mlp_recv_ref, pre_ref, one_ref, two_ref,
-    grad_ref, low_ref, grad_pre_ref, out_ref, sums_ref, acc_ref,
+    grad_ref, back_ref, out_ref, acc_ref, sums_ref,
 ):
     at = pl.program_id(0)
 
@@ -444,28 +448,31 @@
         grad_ref[...] = rows
         rows = rows.astype(F32)
         scaled = rows * row_of(vec_ref, SCALE_M)
-        low_ref[...] = scaled.astype(BF)
+        back_ref[0:BOTH, 2048:3072] = scaled.astype(BF)
         branch = joined(mlp_own_ref, mlp_recv_ref) + row_of(vec_ref, SHIFT_M)
-        sums_ref[...] = jnp.zeros((8, MODEL), F32)
+        sums_ref[...] = jnp.zeros((16, MODEL), F32)
         sums_ref[0:1, :] = column_sum(scaled)
         sums_ref[1:2, :] = column_sum(rows * branch)
 
     pre = pre_ref[...]
     slope = 0.5 * (1.0 + lax.erf(pre * ROOT_HALF)) + pre * jnp.exp(-0.5 * pre * pre) * INV_ROOT_TAU
-    grad_pre = (nt(low_ref[...], two_ref[...].reshape(MODEL, MODEL)) * slope).astype(BF)
-    grad_pre_ref[...] = grad_pre
+    grad_pre = (nt(back_ref[0:BOTH, 2048:3072], two_ref[...].reshape(MODEL, MODEL)) * slope).astype(BF)
     part = nt(grad_pre, one_ref[...].reshape(MODEL, MODEL))
     bias_sum = jnp.sum(grad_pre.astype(F32), axis=0, keepdims=True)
 
     @pl.when(at == 0)
     def _():
+        back_ref[0:BOTH, 0:MODEL] = grad_pre
         acc_ref[...] = part
         sums_ref[2:3, :] = bias_sum
 
     @pl.when(at == 1)
     def _():
+        back_ref[0:BOTH, MODEL:HIDDEN] = grad_pre
         out_ref[...] = (acc_ref[...] + part).astype(BF)
         sums_ref[3:4, :] = bias_sum
+        back_ref[BOTH:TALL, 0:MODEL] = sums_ref[...].astype(BF)
+        back_ref[BOTH:TALL, MODEL:3072] = jnp.zeros((16, 2048), BF)
 
 
 def mlp_back_first_kernel(own_ref, other_ref, *refs):
@@ -473,7 +480,7 @@
 
 
 def mlp_back_next_kernel(middle_grad_ref, part_own_ref, part_recv_ref, rows_ref, after_ref, *refs):
-    *refs, input_grad_ref, acc_ref = refs
+    *refs, input_grad_ref, acc_ref, sums_ref = refs
 
     def grad():
         hat, rstd = norm_parts(rows_ref[...].astype(F32))
@@ -482,7 +489,7 @@
         input_grad_ref[...] = total[:ROWS]
         return total.astype(BF)
 
-    mlp_back_steps(grad, *refs, acc_ref)
+    mlp_back_steps(grad, *refs, acc_ref, sums_ref)
 
 
 def mlp_back_call(inputs, small, mlp_own, mlp_recv, pre, weights):
@@ -500,23 +507,15 @@
             pl.BlockSpec((WIDE, 32, MODEL), lambda j: (0, 2 + j, 0)),
             pl.BlockSpec((16, 64, MODEL), lambda j: (j, 0, 0)),
         ],
-        out_specs=[
-            whole((BOTH, MODEL)),
-            whole((BOTH, MODEL)),
-            pl.BlockSpec((BOTH, MODEL), lambda j: (0, j)),
-            whole((BOTH, MODEL)),
-            whole((8, MODEL)),
-        ]
+        out_specs=[whole((BOTH, MODEL)), whole((TALL, 3072)), whole((BOTH, MODEL))]
         + [whole(shape) for shape in extra],
         out_shape=[
             jax.ShapeDtypeStruct((BOTH, MODEL), BF),
+            jax.ShapeDtypeStruct((TALL, 3072), BF),
             jax.ShapeDtypeStruct((BOTH, MODEL), BF),
-            jax.ShapeDtypeStruct((BOTH, HIDDEN), BF),
-            jax.ShapeDtypeStruct((BOTH, MODEL), BF),
-            jax.ShapeDtypeStruct((8, MODEL), F32),
         ]
         + [jax.ShapeDtypeStruct(shape, F32) for shape in extra],
-        scratch_shapes=[pltpu.VMEM((BOTH, MODEL), F32)],
+        scratch_shapes=[pltpu.VMEM((BOTH, MODEL), F32), pltpu.VMEM((16, MODEL), F32)],
         compiler_params=params(),
         cost_estimate=cost(8),
     )(*inputs, small[0], mlp_own, mlp_recv, pre, weights, weights)
@@ -526,92 +525,63 @@
 CHIPS = WIDE // 2
 
 
-def store_split(place_ref, value, mine_ref, away_ref, pairs, rows, columns):
+ANYWHERE = pl.BlockSpec(memory_space=pl.ANY)
+SCALARS = pl.BlockSpec(memory_space=pltpu.SMEM)
+EVERY = slice(None)
+
+
+def store_mine(place_ref, value, grad_ref, pairs, rows, columns):
     value = value.reshape(value.shape[0] // 2, 2, *value.shape[1:])
     for core in range(2):
 
         @pl.when(place_ref[1] == core)
         def _():
-            mine_ref[pairs, rows, columns] = value[:, core]
-            away_ref[pairs, rows, columns] = value[:, 1 - core]
-
-
-EVERY = slice(None)
-
-
-def split_spec(rows, index):
-    return [pl.BlockSpec((CHIPS, rows, MODEL), lambda *g: (0, index, 0))] * 2
-
-
-def split_shape(rows):
-    return [jax.ShapeDtypeStruct((CHIPS, rows, MODEL), BF)] * 2
-
-
-ANYWHERE = pl.BlockSpec(memory_space=pl.ANY)
-SCALARS = pl.BlockSpec(memory_space=pltpu.SMEM)
-
-
-def mlp_weight_grads(low_ref, normed_ref, act_ref, grad_pre_ref):
-    grad_two = tn(act_ref[...], low_ref[...]).astype(BF).reshape(16, 64, MODEL)
-    grad_one = tn(normed_ref[...], grad_pre_ref[...]).astype(BF).reshape(WIDE, 32, MODEL)
-    return grad_two, grad_one
-
-
-MLP_WEIGHT_SPECS = [
-    whole((BOTH, MODEL)),
-    whole((BOTH, MODEL)),
-    pl.BlockSpec((BOTH, MODEL), lambda j: (0, j)),
-    pl.BlockSpec((BOTH, MODEL), lambda j: (0, j)),
-]
-
-
-def mlp_weight_kernel(low_ref, normed_ref, act_ref, grad_pre_ref, after_ref, grad_ref):
-    grad_two, grad_one = mlp_weight_grads(low_ref, normed_ref, act_ref, grad_pre_ref)
+            grad_ref[pairs, rows, columns] = value[:, core].astype(BF)
+
+
+def both_cores(own_ref, other_ref):
+    return jnp.concatenate([own_ref[0:BOTH], other_ref[0:BOTH]], axis=0)
+
+
+def twice(spec):
+    return [spec, spec]
+
+
+def mlp_weight_kernel(place_ref, *refs):
+    act, normed, low, grad_pre = (both_cores(*refs[at : at + 2]) for at in range(0, 8, 2))
+    grad_ref = refs[-1]
+    grad_two = tn(act, low).reshape(16, 64, MODEL)
+    grad_one = tn(normed, grad_pre).reshape(WIDE, 32, MODEL)
     for at in range(2):
 
         @pl.when(pl.program_id(0) == at)
         def _():
-            grad_ref[16 * at : 16 * at + 16, 0:64, :] = grad_two
-            grad_ref[:, 64 + 32 * at : 96 + 32 * at, :] = grad_one
-
-
-def mlp_weight_call(low, normed, act, grad_pre, after):
+            store_mine(
+                place_ref, grad_two, grad_ref, slice(8 * at, 8 * at + 8), slice(0, 64), EVERY
+            )
+            rows = slice(64 + 32 * at, 96 + 32 * at)
+            store_mine(place_ref, grad_one, grad_ref, EVERY, rows, EVERY)
+
+
+def mlp_weight_call(place, kept, back, more, pack=None):
+    rows, extra, aliases = 128, [more], {}
+    if pack is not None:
+        rows, extra, aliases = PACK_ROWS, [pack], {9: 0}
     return pl.pallas_call(
         mlp_weight_kernel,
         grid=(2,),
-        in_specs=MLP_WEIGHT_SPECS + [ANYWHERE],
-        out_specs=whole((WIDE, 128, MODEL)),
-        out_shape=jax.ShapeDtypeStruct((WIDE, 128, MODEL), BF),
-        compiler_params=params(),
-        cost_estimate=cost(8),
-    )(low, normed, act, grad_pre, after)
-
-
-def mlp_weight_split_kernel(
-    place_ref, low_ref, normed_ref, act_ref, grad_pre_ref, mine_in, away_in, mine_ref, away_ref
-):
-    grad_two, grad_one = mlp_weight_grads(low_ref, normed_ref, act_ref, grad_pre_ref)
-    for at in range(2):
-
-        @pl.when(pl.program_id(0) == at)
-        def _():
-            half = slice(8 * at, 8 * at + 8)
-            store_split(place_ref, grad_two, mine_ref, away_ref, half, slice(0, 64), EVERY)
-            rows = slice(64 + 32 * at, 96 + 32 * at)
-            store_split(place_ref, grad_one, mine_ref, away_ref, EVERY, rows, EVERY)
-
-
-def mlp_weight_split_call(place, low, normed, act, grad_pre, pack):
-    return pl.pallas_call(
-        mlp_weight_split_kernel,
-        grid=(2,),
-        in_specs=[SCALARS] + MLP_WEIGHT_SPECS + [ANYWHERE] * 2,
-        out_specs=split_spec(128, 0),
-        out_shape=split_shape(PACK_ROWS),
-        input_output_aliases={5: 0, 6: 1},
-        compiler_params=params(),
-        cost_estimate=cost(8),
-    )(place, low, normed, act, grad_pre, *pack)
+        in_specs=[SCALARS]
+        + twice(pl.BlockSpec((BOTH, MODEL), lambda j: (0, j)))
+        + twice(pl.BlockSpec((BOTH, MODEL), lambda j: (0, 2)))
+        + twice(pl.BlockSpec((BOTH, MODEL), lambda j: (0, 2)))
+        + twice(pl.BlockSpec((BOTH, MODEL), lambda j: (0, j)))
+        + [ANYWHERE],
+        out_specs=pl.BlockSpec((CHIPS, 128, MODEL), lambda j: (0, 0, 0)),
+        out_shape=jax.ShapeDtypeStruct((CHIPS, rows, MODEL), BF),
+        input_output_aliases=aliases,
+        compiler_params=params(),
+        cost_estimate=cost(7),
+    )(place, *kept, *kept, *back, *back, *extra)
 
 
 def out_back_kernel(
@@ -624,15 +594,16 @@
     middle_grad_ref[...] = total
     scaled = total * row_of(vec_ref, SCALE_A)
     rows = scaled.astype(BF)
-    low_ref[...] = rows
+    low_ref[0:BOTH, :] = rows
     grad_mix = nt(rows, weight_ref[...].reshape(HALF_W, MODEL))
     for pair in range(HEADS_DEV // 2):
         pack_heads(grad_mix[:, pair * 128 : pair * 128 + 128], send_ref, pair, 0)
-    sums_ref[...] = jnp.zeros((8, MODEL), F32)
+    sums_ref[...] = jnp.zeros((16, MODEL), F32)
     sums_ref[0:1, :] = column_sum(grad_norm * hat)
     sums_ref[1:2, :] = column_sum(grad_norm)
     sums_ref[2:3, :] = column_sum(scaled)
     sums_ref[3:4, :] = column_sum(total * branch_ref[...])
+    low_ref[BOTH:TALL, :] = sums_ref[...].astype(BF)
 
 
 def out_back_call(grad, part_own, part_recv, middle, branch, small, weights):
@@ -641,62 +612,70 @@
         grid=(1,),
         in_specs=[whole((BOTH, MODEL))] * 5
         + [whole((8, MODEL)), pl.BlockSpec((WIDE, 16, MODEL), lambda i: (0, 8, 0))],
-        out_specs=[
-            whole((BOTH, MODEL)), whole((WIDE, 16, 128)), whole((BOTH, MODEL)), whole((8, MODEL))
-        ],
+        out_specs=[whole((BOTH, MODEL)), whole((WIDE, 16, 128)), whole((TALL, MODEL))],
         out_shape=[
             jax.ShapeDtypeStruct((BOTH, MODEL), F32),
             jax.ShapeDtypeStruct((WIDE, 16, 128), BF),
-            jax.ShapeDtypeStruct((BOTH, MODEL), BF),
-            jax.ShapeDtypeStruct((8, MODEL), F32),
-        ],
+            jax.ShapeDtypeStruct((TALL, MODEL), BF),
+        ],
+        scratch_shapes=[pltpu.VMEM((16, MODEL), F32)],
         compiler_params=params(),
         cost_estimate=cost(4),
     )(grad, part_own, part_recv, middle, branch, small[0], weights)
 
 
-def out_weight_kernel(place_ref, mixture_ref, low_ref, mine_ref, away_ref):
-    grad = tn(mixture_ref[...], low_ref[...]).astype(BF).reshape(WIDE, 16, MODEL)
-    store_split(place_ref, grad, mine_ref, away_ref, EVERY, EVERY, EVERY)
-
-
-def out_weight_last_kernel(place_ref, mixture_ref, low_ref, *refs):
-    *sums_refs, before_ref, mine_in, away_in, mine_ref, away_ref = refs
-    grad = tn(mixture_ref[...], low_ref[...]).astype(BF).reshape(WIDE, 16, MODEL)
-    store_split(place_ref, grad, mine_ref, away_ref, EVERY, slice(0, 16), EVERY)
-    parts = [ref[0:4, :] for ref in sums_refs] + [before_ref[0:12, :].astype(F32)]
-    rows = jnp.concatenate(parts, axis=0).astype(BF)
-    rows = jnp.broadcast_to(rows[None], (CHIPS, 32, MODEL))
-    mine_ref[:, 16:48, :] = rows
-    away_ref[:, 16:48, :] = rows
-
-
-def out_weight_call(place, mixture, low):
+def store_out_grads(place_ref, refs, grad_ref, rows):
+    grad = tn(both_cores(*refs[0:2]), both_cores(*refs[2:4])).reshape(WIDE, 16, MODEL)
+    store_mine(place_ref, grad, grad_ref, EVERY, rows, EVERY)
+
+
+def out_weight_kernel(place_ref, *refs):
+    store_out_grads(place_ref, refs, refs[-1], EVERY)
+
+
+def out_weight_last_kernel(place_ref, *refs):
+    *sums_refs, before_ref, _, grad_ref = refs[4:]
+    store_out_grads(place_ref, refs, grad_ref, slice(0, 16))
+    parts = [
+        own[0:4, :].astype(F32) + other[0:4, :].astype(F32)
+        for own, other in zip(sums_refs[0::2], sums_refs[1::2])
+    ]
+    rows = jnp.concatenate(parts + [before_ref[0:12, :].astype(F32)], axis=0).astype(BF)
+    grad_ref[:, 16:48, :] = jnp.broadcast_to(rows[None], (CHIPS, 32, MODEL))
+
+
+OUT_WEIGHT_SPECS = (
+    [SCALARS]
+    + twice(pl.BlockSpec((BOTH, HALF_W), lambda i: (0, 8)))
+    + twice(pl.BlockSpec((BOTH, MODEL), lambda i: (0, 0)))
+)
+SUMS_SPEC = pl.BlockSpec((16, MODEL), lambda i: (8, 0))
+
+
+def out_weight_call(place, kept, low):
     return pl.pallas_call(
         out_weight_kernel,
         grid=(1,),
-        in_specs=[SCALARS, whole((BOTH, HALF_W)), whole((BOTH, MODEL))],
-        out_specs=split_spec(16, 8),
-        out_shape=split_shape(PACK_ROWS),
+        in_specs=OUT_WEIGHT_SPECS,
+        out_specs=pl.BlockSpec((CHIPS, 16, MODEL), lambda i: (0, 8, 0)),
+        out_shape=jax.ShapeDtypeStruct((CHIPS, PACK_ROWS, MODEL), BF),
         compiler_params=params(),
         cost_estimate=cost(2),
-    )(place, mixture, low)
-
-
-def out_weight_last_call(place, mixture, low, sums, before, pack):
-    count = 4 + len(sums)
+    )(place, *kept, *low)
+
+
+def out_weight_last_call(place, kept, low, sums, before, pack):
+    flat = [array for pair in sums for array in pair]
     return pl.pallas_call(
         out_weight_last_kernel,
         grid=(1,),
-        in_specs=[SCALARS, whole((BOTH, HALF_W)), whole((BOTH, MODEL))]
-        + [whole((8, MODEL)) for _ in sums]
-        + [whole((16, MODEL)), ANYWHERE, ANYWHERE],
-        out_specs=split_spec(48, 4),
-        out_shape=split_shape(PACK_ROWS),
-        input_output_aliases={count: 0, count + 1: 1},
+        in_specs=OUT_WEIGHT_SPECS + [SUMS_SPEC] * len(flat) + [whole((16, MODEL)), ANYWHERE],
+        out_specs=pl.BlockSpec((CHIPS, 48, MODEL), lambda i: (0, 4, 0)),
+        out_shape=jax.ShapeDtypeStruct((CHIPS, PACK_ROWS, MODEL), BF),
+        input_output_aliases={6 + len(flat): 0},
         compiler_params=params(),
         cost_estimate=cost(3),
-    )(place, mixture, low, *sums, before, *pack)
+    )(place, *kept, *low, *flat, before, pack)
 
 
 def qkv_back_kernel(recv_ref, rows_ref, vec_ref, weight_ref, part_ref, grads_ref, sums_ref):
@@ -714,9 +693,9 @@
         value_columns.append(jnp.where(mask, turn(sums[0]), sums[1]))
     grad_k = jnp.concatenate(key_columns, axis=1).astype(BF)
     grad_v = jnp.concatenate(value_columns, axis=1).astype(BF)
-    grads_ref[:, 0:HALF_W] = grad_q
-    grads_ref[:, HALF_W:MODEL] = grad_k
-    grads_ref[:, MODEL : MODEL + HALF_W] = grad_v
+    grads_ref[0:BOTH, 0:HALF_W] = grad_q
+    grads_ref[0:BOTH, HALF_W:MODEL] = grad_k
+    grads_ref[0:BOTH, MODEL : MODEL + HALF_W] = grad_v
     result = (
         nt(grad_q, qkv_weight(weight_ref, 0))
         + nt(grad_k, qkv_weight(weight_ref, 1))
@@ -724,11 +703,13 @@
     )
     part_ref[...] = result.astype(BF)
     hat, _ = norm_parts(rows_ref[...].astype(F32))
-    sums_ref[...] = jnp.zeros((8, MODEL), F32)
+    sums_ref[...] = jnp.zeros((16, MODEL), F32)
     sums_ref[0:1, :] = column_sum(result * hat)
     sums_ref[1:2, :] = column_sum(result)
     sums_ref[2:3, 0:HALF_W] = column_sum(grad_q.astype(F32))
     sums_ref[2:3, HALF_W:MODEL] = column_sum(grad_v.astype(F32))
+    grads_ref[BOTH:TALL, 0:MODEL] = sums_ref[...].astype(BF)
+    grads_ref[BOTH:TALL, MODEL : MODEL + HALF_W] = jnp.zeros((16, HALF_W), BF)
 
 
 def qkv_back_call(recv, rows, small, weight, block_at):
@@ -741,66 +722,82 @@
             whole((8, MODEL)),
             qkv_block(block_at),
         ],
-        out_specs=[whole((BOTH, MODEL)), whole((BOTH, 3 * HALF_W)), whole((8, MODEL))],
+        out_specs=[whole((BOTH, MODEL)), whole((TALL, 3 * HALF_W))],
         out_shape=[
             jax.ShapeDtypeStruct((BOTH, MODEL), BF),
-            jax.ShapeDtypeStruct((BOTH, 3 * HALF_W), BF),
-            jax.ShapeDtypeStruct((8, MODEL), F32),
-        ],
+            jax.ShapeDtypeStruct((TALL, 3 * HALF_W), BF),
+        ],
+        scratch_shapes=[pltpu.VMEM((16, MODEL), F32)],
         compiler_params=params(),
         cost_estimate=cost(5),
     )(recv, rows, small[0], weight)
 
 
-def store_qkv_grads(place_ref, normed_ref, grads_ref, mine_ref, away_ref):
-    rows = normed_ref[...]
+def store_qkv_grads(place_ref, refs, grad_ref):
+    rows = both_cores(*refs[0:2])
 
     def part(which):
-        grads = grads_ref[:, which * HALF_W : which * HALF_W + HALF_W]
-        return tn(rows, grads).astype(BF).reshape(WIDE, 32, HALF_W)
+        columns = slice(which * HALF_W, which * HALF_W + HALF_W)
+        grads = jnp.concatenate([ref[0:BOTH, columns] for ref in refs[2:4]], axis=0)
+        return tn(rows, grads).reshape(WIDE, 32, HALF_W)
 
     low, high = slice(0, HALF_W), slice(HALF_W, MODEL)
-    store_split(place_ref, part(0), mine_ref, away_ref, EVERY, slice(0, 32), low)
-    store_split(place_ref, part(1), mine_ref, away_ref, EVERY, slice(0, 32), high)
+    store_mine(place_ref, part(0), grad_ref, EVERY, slice(0, 32), low)
+    store_mine(place_ref, part(1), grad_ref, EVERY, slice(0, 32), high)
     values = part(2)
-    store_split(place_ref, values[:, 0:16], mine_ref, away_ref, EVERY, slice(32, 48), low)
-    store_split(place_ref, values[:, 16:32], mine_ref, away_ref, EVERY, slice(32, 48), high)
-
-
-def qkv_weight_kernel(place_ref, normed_ref, grads_ref, mine_in, away_in, mine_ref, away_ref):
-    store_qkv_grads(place_ref, normed_ref, grads_ref, mine_ref, away_ref)
-
-
-def qkv_weight_last_kernel(place_ref, normed_ref, grads_ref, sums_ref, mine_ref, away_ref):
-    store_qkv_grads(place_ref, normed_ref, grads_ref, mine_ref, away_ref)
-    rows = jnp.broadcast_to(sums_ref[...].astype(BF)[None], (CHIPS, 8, MODEL))
-    mine_ref[:, 48:56, :] = rows
-    away_ref[:, 48:56, :] = rows
-
-
-def qkv_weight_call(place, normed, grads, pack):
+    store_mine(place_ref, values[:, 0:16], grad_ref, EVERY, slice(32, 48), low)
+    store_mine(place_ref, values[:, 16:32], grad_ref, EVERY, slice(32, 48), high)
+
+
+def qkv_weight_kernel(place_ref, *refs):
+    store_qkv_grads(place_ref, refs, refs[-1])
+
+
+def qkv_weight_last_kernel(place_ref, *refs):
+    grad_ref = refs[-1]
+    store_qkv_grads(place_ref, refs, grad_ref)
+    rows = sum(ref[BOTH : BOTH + 8, 0:MODEL].astype(F32) for ref in refs[2:4]).astype(BF)
+    grad_ref[:, 48:56, :] = jnp.broadcast_to(rows[None], (CHIPS, 8, MODEL))
+
+
+QKV_WEIGHT_SPECS = (
+    [SCALARS]
+    + twice(pl.BlockSpec((BOTH, MODEL), lambda i: (0, 3)))
+    + twice(whole((TALL, 3 * HALF_W)))
+)
+
+
+def qkv_weight_call(place, kept, grads, pack):
     return pl.pallas_call(
         qkv_weight_kernel,
         grid=(1,),
-        in_specs=[SCALARS, whole((BOTH, MODEL)), whole((BOTH, 3 * HALF_W)), ANYWHERE, ANYWHERE],
-        out_specs=split_spec(48, 3),
-        out_shape=split_shape(PACK_ROWS),
-        input_output_aliases={3: 0, 4: 1},
+        in_specs=QKV_WEIGHT_SPECS + [ANYWHERE],
+        out_specs=qkv_chips(3),
+        out_shape=jax.ShapeDtypeStruct((CHIPS, PACK_ROWS, MODEL), BF),
+        input_output_aliases={5: 0},
         compiler_params=params(),
         cost_estimate=cost(4),
-    )(place, normed, grads, *pack)
-
-
-def qkv_weight_last_call(place, normed, grads, sums):
+    )(place, *kept, *grads, pack)
+
+
+def qkv_chips(index):
+    return pl.BlockSpec((CHIPS, 48, MODEL), lambda i: (0, index, 0))
+
+
+def qkv_weight_last_call(place, kept, grads):
     return pl.pallas_call(
         qkv_weight_last_kernel,
         grid=(1,),
-        in_specs=[SCALARS, whole((BOTH, MODEL)), whole((BOTH, 3 * HALF_W)), whole((8, MODEL))],
-        out_specs=split_spec(56, 0),
-        out_shape=split_shape(56),
+        in_specs=QKV_WEIGHT_SPECS,
+        out_specs=whole((CHIPS, 56, MODEL)),
+        out_shape=jax.ShapeDtypeStruct((CHIPS, 56, MODEL), BF),
         compiler_params=params(),
         cost_estimate=cost(4),
-    )(place, normed, grads, sums)
+    )(place, *kept, *grads)
+
+
+def with_core(block):
+    return block, lax.ppermute(block, "wide", [(i, i ^ 1) for i in range(WIDE)])
 
 
 def all_to_all(block):
@@ -815,31 +812,28 @@
     mix_recv = lax.all_to_all(
         mix_sent.reshape(2 * WIDE, 16, 128), ("tensor", "wide"), 0, 0, tiled=True
     )
-    mixture, branch, middle, normed_c, pre, act, mlp = mlp_call(place, rows, mix_recv, small, rest)
+    branch, middle, pre, wide_kept, mlp = mlp_call(place, rows, normed_a, mix_recv, small, rest)
     mlp_recv = swap(mlp, "tensor")
     return dict(
-        rows=rows, normed_a=normed_a, recv=recv, keep=mix_keep, lse=lse, mixture=mixture,
-        branch=branch, middle=middle, normed_c=normed_c, pre=pre, act=act, mlp=mlp, mlp_recv=mlp_recv,
+        rows=rows, recv=recv, keep=mix_keep, lse=lse, branch=branch, middle=middle, pre=pre,
+        mlp=mlp, mlp_recv=mlp_recv, for_weights=with_core(wide_kept),
     )
 
 
 def layer_backward(inputs, kept, ids, qkv, rest, small):
     flags, key_ids, query_ids = ids
-    grad, low_m, grad_pre, part, mlp_sums, *input_grad = mlp_back_call(
+    grad, mlp_back, part, *input_grad = mlp_back_call(
         inputs, small, kept["mlp"], kept["mlp_recv"], kept["pre"], rest
     )
-    middle_grad, mix_grad, low_a, out_sums = out_back_call(
+    middle_grad, mix_grad, low_a = out_back_call(
         grad, part, swap(part, "tensor"), kept["middle"], kept["branch"], small, rest
     )
     back = attend_back_call(
         flags, kept["recv"], all_to_all(mix_grad), kept["keep"], kept["lse"], key_ids, query_ids
     )
-    qkv_part, qkv_grads, qkv_sums = qkv_back_call(all_to_all(back), kept["rows"], small, *qkv)
+    qkv_part, qkv_grads = qkv_back_call(all_to_all(back), kept["rows"], small, *qkv)
     carried = (middle_grad, qkv_part, swap(qkv_part, "tensor"), kept["rows"])
-    for_weights = dict(
-        low_m=low_m, grad_pre=grad_pre, low_a=low_a, qkv_grads=qkv_grads,
-        mlp_sums=mlp_sums, out_sums=out_sums, qkv_sums=qkv_sums,
-    )
+    for_weights = with_core(mlp_back), with_core(low_a), with_core(qkv_grads)
     return carried, for_weights, input_grad
 
 
@@ -937,50 +931,35 @@
     ).astype(BF)
     out0 = kept1["rows"][:ROWS]
 
-    def rs(pack):
+    same_core = [list(range(core, WIDE, 2)) for core in range(2)]
+
+    def over_chips(pack):
         return lax.psum_scatter(
-            pack.reshape(WIDE * pack.shape[1], MODEL), "wide", scatter_dimension=0, tiled=True
+            pack.reshape(CHIPS * pack.shape[1], MODEL),
+            "wide", scatter_dimension=0, axis_index_groups=same_core, tiled=True,
         )
 
     carried1, back1, _ = layer_backward(
         (own_cot, other_cot), kept1, ids, qkv_parts[1], rest[1], small[1]
     )
-    sum_mlp1 = rs(
-        mlp_weight_call(
-            back1["low_m"], kept1["normed_c"], kept1["act"], back1["grad_pre"], back1["out_sums"]
-        )
-    )
-    pack = out_weight_call(place, kept1["mixture"], back1["low_a"])
-    pack = qkv_weight_call(place, kept1["normed_a"], back1["qkv_grads"], pack)
+    kept_pair0, kept_pair1 = kept0["for_weights"], kept1["for_weights"]
+    mlp_back1, low1, grads1 = back1
+    sum_mlp1 = over_chips(mlp_weight_call(place, kept_pair1, mlp_back1, low1[0]))
+    pack = out_weight_call(place, kept_pair1, low1)
+    pack = qkv_weight_call(place, kept_pair1, grads1, pack)
 
     carried0, back0, (grad_x1,) = layer_backward(
         carried1 + (small[1][0],), kept0, ids, qkv_parts[0], rest[0], small[0]
     )
-    pack = mlp_weight_split_call(
-        place, back0["low_m"], kept0["normed_c"], kept0["act"], back0["grad_pre"], pack
-    )
+    mlp_back0, low0, grads0 = back0
+    pack = mlp_weight_call(place, kept_pair0, mlp_back0, None, pack)
     pack = out_weight_last_call(
-        place,
-        kept0["mixture"],
-        back0["low_a"],
-        (back1["mlp_sums"], back1["out_sums"], back1["qkv_sums"], back0["mlp_sums"], back0["out_sums"]),
-        sum_mlp1,
-        pack,
-    )
-
-    same_core = [list(range(core, WIDE, 2)) for core in range(2)]
-
-    def over_chip(mine, away):
-        came = lax.ppermute(away, "wide", [(i, i ^ 1) for i in range(WIDE)])
-        return (mine.astype(F32) + came.astype(F32)).astype(BF)
-
-    sum_mid = lax.psum_scatter(
-        over_chip(*pack).reshape(CHIPS * PACK_ROWS, MODEL),
-        "wide", scatter_dimension=0, axis_index_groups=same_core, tiled=True,
-    )
-    last_pack = qkv_weight_last_call(place, kept0["normed_a"], back0["qkv_grads"], back0["qkv_sums"])
+        place, kept_pair0, low0, (mlp_back1, low1, grads1, mlp_back0, low0), sum_mlp1, pack
+    )
+    sum_mid = over_chips(pack)
     last_recv = lax.all_to_all(
-        over_chip(*last_pack), "wide", 0, 0, axis_index_groups=same_core, tiled=True
+        qkv_weight_last_call(place, kept_pair0, grads0),
+        "wide", 0, 0, axis_index_groups=same_core, tiled=True,
     )
     sum_last = jnp.sum(last_recv.astype(F32), axis=0)
 

time: 542 us -> 532 us (0.982)
  other arithmetic: 35.2 us -> 15.9 us
  waiting for transfers between devices: 176 us -> 187 us
    convert_element_type x2 -> x0, other arithmetic: 16.5 us -> none  [over_chip(): return (mine.astype(F32) + came.astype(F32)).astype(BF)]
    ppermute x2 -> x8, waiting for transfers between devices: 12.7 us -> 0.73 us  [with_core(): lax.ppermute(block, 'wide', [(i, i ^ 1) for i in range(WIDE)])]
    ppermute x14, waiting for transfers between devices: 50.8 us -> 62.4 us  [swap(): return lax.ppermute(block, axis, [(0, 1), (1, 0)])]
    all_to_all x2, waiting for transfers between devices: 34 us -> 42.3 us  [all_to_all(): return lax.all_to_all(block, 'wide', 0, 0, tiled=True)]
    ppermute x14, starting transfers between devices: 24.6 us -> 19 us  [swap(): return lax.ppermute(block, axis, [(0, 1), (1, 0)])]
    unnamed x52 -> x84, local copies, waits for them, and re-layouts: 11.5 us -> 14.4 us
  transfers between devices with their start and end apart: 27 -> 33, of which waited for: 20 -> 19; matrix products, arithmetic and copies ran while one was open for 6% -> 4% of each run, Pallas kernels for 19% -> 22%
where the time goes in v4:
time: 532 us; the launch traced here: 523 us
  waiting for transfers between devices  187 us (35%)
  Pallas kernels  141 us (27%)
  blocking collectives  78.6 us (15%)
  starting transfers between devices  50.6 us (10%)
  local copies, waits for them, and re-layouts  35.5 us (7%)
  other arithmetic  15.9 us (3%)
  between operations  14.9 us (3%)
    all_to_all x4, blocking collectives, all_to_all(): return lax.all_to_all(block, 'wide', 0, 0, tiled=True)  78.6 us
    ppermute x14, waiting for transfers between devices, swap(): return lax.ppermute(block, axis, [(0, 1), (1, 0)])  62.4 us
    all_to_all x2, waiting for transfers between devices, all_to_all(): return lax.all_to_all(block, 'wide', 0, 0, tiled=True)  42.3 us
    all_gather x3, waiting for transfers between devices, gather(): return lax.all_gather(block, 'wide', axis=0, tiled=False)  40 us
    pallas_call x2, Pallas kernels, attend_back_call(): pl.pallas_call(attend_back_kernel, grid_spec=pltpu.PrefetchScalarGridSpec...  32.9 us
    pallas_call x2, Pallas kernels, attend_call(): pl.pallas_call(attend_kernel, grid_spec=pltpu.PrefetchScalarGridSpec(num_...  25.9 us
    all_to_all x2, waiting for transfers between devices, layer_forward(): lax.all_to_all(mix_sent.reshape(2 * WIDE, 16, 128), ('tensor', 'wide'), 0...  21.4 us
    all_to_all x1, waiting for transfers between devices, body(): lax.all_to_all(qkv_weight_last_call(place, kept_pair0, grads0), 'wide', 0...  20.1 us
  transfers between devices with their start and end apart: 33, of which 19 were waited for; matrix products, arithmetic and copies ran while one was open for 4% of the time, Pallas kernels for 22%

profile of v4, /device:TPU:0, one launch (start us, length us, event | category | flops | bytes accessed | tf_op | source)
XLA Modules:
  0.0 523.3 jit_solution(10569226278007611245)
XLA Ops:
  20.6 6.1 %collective-permute-done = bf16[144,1024]{1,0:T(8,128)(2,1)S(1)} collective-permute-done((bf16[144,1024]{1,0:T(8,128)(2,1)S(1)}, bf16[144,1024]{1,0:T(8,128)(2,1)S(1)}, u32[]{:S(2)}, u32[]{:S(2)}) %collective-permute-start) | collective-permute-done | bytes 294944 | tf_op jit(solution)/shard_map/ppermute | solution.py:45
  28.3 6.1 %collective-permute-done.2 = bf16[160,1024]{1,0:T(8,128)(2,1)S(1)} collective-permute-done((bf16[160,1024]{1,0:T(8,128)(2,1)S(1)}, bf16[160,1024]{1,0:T(8,128)(2,1)S(1)}, u32[]{:S(2)}, u32[]{:S(2)}) %collective-permute-start.2) | collective-permute-done | bytes 327712 | tf_op jit(solution)/shard_map/ppermute | solution.py:45
  34.5 35.5 %all-gather.6.cloned.1.call-done.weight_ref = bf16[32,112,1024]{2,1,0:T(8,128)(2,1)} async-done(((bf16[1,112,1024]{2,1,0:T(8,128)(2,1)}), bf16[32,112,1024]{2,1,0:T(8,128)(2,1)}) %all-gather.6.cloned.1.call-update) | async-done | bytes 7340048 | tf_op jit(solution)/shard_map/all_gather | solution.py:880
  78.9 5.2 %all-to-all-start = ((bf16[32,144,128]{2,1,0:T(8,128)(2,1)}), bf16[32,144,128]{2,1,0:T(8,128)(2,1)S(1)}, u32[]{:S(2)}, u32[]{:S(2)}) async-start(bf16[32,144,128]{2,1,0:T(8,128)(2,1)} %get-tuple-element.52), calls=%async_computation | async-start | bytes 2359296 | tf_op jit(solution)/shard_map/all_to_all | solution.py:804
  88.0 18.6 %all-to-all-done.recv_ref = bf16[32,144,128]{2,1,0:T(8,128)(2,1)S(1)} async-done(((bf16[32,144,128]{2,1,0:T(8,128)(2,1)}), bf16[32,144,128]{2,1,0:T(8,128)(2,1)S(1)}, u32[]{:S(2)}, u32[]{:S(2)}) %all-to-all-start) | async-done | bytes 1179680 | tf_op jit(solution)/shard_map/all_to_all | solution.py:804
  107.6 12.9 %shard_map.204 = (bf16[2,32,16,128]{3,2,1,0:T(8,128)(2,1)}, f32[32,16,128]{2,1,0:T(8,128)}, f32[1024,1]{1,0:T(8,128)}) custom-call(s32[4,8]{1,0:T(4,128)} %and_convert_fusion.flag_ref, bf16[32,144,128]{2,1,0:T(8,128)(2,1)} %copy-done.7, s32[8,1,512]{2,1,0:T(1,128)} %reshape.242.key_id_ref, s32[4,256,1]{2,1,0:T(8,128)} %reshape.261.query_id_ref), custom_call_target="tpu_custom_call" | custom-call | flops 12000000000 | bytes 100000 | tf_op jit(solution)/shard_map/pallas_call | solution.py:246
  120.5 6.5 %all-to-all-start.1 = ((bf16[64,16,128]{2,1,0:T(8,128)(2,1)}), bf16[64,16,128]{2,1,0:T(8,128)(2,1)S(1)}, u32[]{:S(2)}, u32[]{:S(2)}) async-start(bf16[64,16,128]{2,1,0:T(8,128)(2,1)} %bitcast.124), calls=%async_computation.1 | async-start | bytes 524288 | tf_op jit(solution)/shard_map/all_to_all | solution.py:812
  128.4 11.3 %all-to-all-done.1.recv_ref = bf16[64,16,128]{2,1,0:T(8,128)(2,1)S(1)} async-done(((bf16[64,16,128]{2,1,0:T(8,128)(2,1)}), bf16[64,16,128]{2,1,0:T(8,128)(2,1)S(1)}, u32[]{:S(2)}, u32[]{:S(2)}) %all-to-all-start.1) | async-done | bytes 262176 | tf_op jit(solution)/shard_map/all_to_all | solution.py:812
  144.1 7.3 %shard_map.205 = (f32[128,1024]{1,0:T(8,128)}, f32[128,1024]{1,0:T(8,128)}, f32[128,2048]{1,0:T(8,128)}, bf16[128,4608]{1,0:T(8,128)(2,1)}, bf16[128,1024]{1,0:T(8,128)(2,1)}) custom-call(s32[2]{0:T(128)} %pad_add_fusion.place_ref, bf16[128,1024]{1,0:T(8,128)(2,1)} %get-tuple-element.50.rows_ref, bf16[128,1024]{1,0:T(8,128)(2,1)} %get-tuple-element.51.normed_ref, ...), custom_call_target="tpu_custom_call" | custom-call | flops 8000000000 | bytes 100000 | tf_op jit(solution)/shard_map/pallas_call | solution.py:405
  157.4 5.7 %collective-permute-done.3.mlp_recv_ref.refs_2_ = bf16[128,1024]{1,0:T(8,128)(2,1)S(1)} collective-permute-done((bf16[128,1024]{1,0:T(8,128)(2,1)}, bf16[128,1024]{1,0:T(8,128)(2,1)S(1)}, u32[]{:S(2)}, u32[]{:S(2)}) %collective-permute-start.3) | collective-permute-done | bytes 262176 | tf_op jit(solution)/shard_map/ppermute | solution.py:45
  168.2 27.5 %all_to_all.45.recv_ref = bf16[32,144,128]{2,1,0:T(8,128)(2,1)} all-to-all(bf16[32,144,128]{2,1,0:T(8,128)(2,1)} %get-tuple-element.58), channel_id=1, replica_groups=mesh['section'=2,'tensor'=2,'wide'=32] {'wide'}, dimensions={0} | all-to-all | bytes 2359296 | tf_op jit(solution)/shard_map/all_to_all | solution.py:804
  195.7 13.0 %shard_map.207 = (bf16[2,32,16,128]{3,2,1,0:T(8,128)(2,1)}, f32[32,16,128]{2,1,0:T(8,128)}, f32[1024,1]{1,0:T(8,128)}) custom-call(s32[4,8]{1,0:T(4,128)} %and_convert_fusion.flag_ref, bf16[32,144,128]{2,1,0:T(8,128)(2,1)} %all_to_all.45.recv_ref, s32[8,1,512]{2,1,0:T(1,128)} %reshape.242.key_id_ref, s32[4,256,1]{2,1,0:T(8,128)} %reshape.261.query_id_ref), custom_call_target="tpu_custom_call" | custom-call | flops 12000000000 | bytes 100000 | tf_op jit(solution)/shard_map/pallas_call | solution.py:246
  208.7 7.1 %all-to-all-start.3 = ((bf16[64,16,128]{2,1,0:T(8,128)(2,1)}), bf16[64,16,128]{2,1,0:T(8,128)(2,1)S(1)}, u32[]{:S(2)}, u32[]{:S(2)}) async-start(bf16[64,16,128]{2,1,0:T(8,128)(2,1)} %bitcast.125), calls=%async_computation.3 | async-start | bytes 524288 | tf_op jit(solution)/shard_map/all_to_all | solution.py:812
  216.6 10.1 %all-to-all-done.3.recv_ref = bf16[64,16,128]{2,1,0:T(8,128)(2,1)S(1)} async-done(((bf16[64,16,128]{2,1,0:T(8,128)(2,1)}), bf16[64,16,128]{2,1,0:T(8,128)(2,1)S(1)}, u32[]{:S(2)}, u32[]{:S(2)}) %all-to-all-start.3) | async-done | bytes 262176 | tf_op jit(solution)/shard_map/all_to_all | solution.py:812
  227.4 7.3 %shard_map.208 = (f32[128,1024]{1,0:T(8,128)}, f32[128,1024]{1,0:T(8,128)}, f32[128,2048]{1,0:T(8,128)}, bf16[128,4608]{1,0:T(8,128)(2,1)}, bf16[128,1024]{1,0:T(8,128)(2,1)}) custom-call(s32[2]{0:T(128)} %pad_add_fusion.place_ref, bf16[128,1024]{1,0:T(8,128)(2,1)} %get-tuple-element.56.rows_ref, bf16[128,1024]{1,0:T(8,128)(2,1)} %get-tuple-element.57.normed_ref, ...), custom_call_target="tpu_custom_call" | custom-call | flops 8000000000 | bytes 100000 | tf_op jit(solution)/shard_map/pallas_call | solution.py:405
  236.2 8.7 %collective-permute-done.4.refs_2_ = bf16[128,1024]{1,0:T(8,128)(2,1)S(1)} collective-permute-done((bf16[128,1024]{1,0:T(8,128)(2,1)}, bf16[128,1024]{1,0:T(8,128)(2,1)S(1)}, u32[]{:S(2)}, u32[]{:S(2)}) %collective-permute-start.4) | collective-permute-done | bytes 262176 | tf_op jit(solution)/shard_map/ppermute | solution.py:45
  245.5 7.2 %shard_map.209 = (bf16[128,1024]{1,0:T(8,128)(2,1)}, bf16[144,3072]{1,0:T(8,128)(2,1)}, bf16[128,1024]{1,0:T(8,128)(2,1)}) custom-call(bf16[64,1024]{1,0:T(8,128)(2,1)} %copy-done.21, bf16[64,1024]{1,0:T(8,128)(2,1)} %get-tuple-element.123.other_ref, f32[8,1024]{1,0:T(8,128)} %reshape.246.vec_ref.refs_0_.after_ref, ...), custom_call_target="tpu_custom_call" | custom-call | flops 8000000000 | bytes 100000 | tf_op jit(solution)/shard_map/pallas_call | solution.py:498
  253.8 9.3 %collective-permute-done.6.part_recv_ref = bf16[128,1024]{1,0:T(8,128)(2,1)S(1)} collective-permute-done((bf16[128,1024]{1,0:T(8,128)(2,1)}, bf16[128,1024]{1,0:T(8,128)(2,1)S(1)}, u32[]{:S(2)}, u32[]{:S(2)}) %collective-permute-start.6) | collective-permute-done | bytes 262176 | tf_op jit(solution)/shard_map/ppermute | solution.py:45
  268.7 6.5 %shard_map.218 = bf16[16,128,1024]{2,1,0:T(8,128)(2,1)} custom-call(s32[2]{0:T(128)} %pad_add_fusion.place_ref, bf16[128,4608]{1,0:T(8,128)(2,1)} %get-tuple-element.88.refs_0_.refs_2_, bf16[128,4608]{1,0:T(8,128)(2,1)} %copy-done.2, bf16[128,4608]{1,0:T(8,128)(2,1)} %get-tuple-element.88.refs_0_.refs_2_, bf16[128,4608]{1,0:T(8,128)(2,1)} %copy-done.2, ...), custom_call_target="tpu_custom_call" | custom-call | flops 7000000000 | bytes 100000 | tf_op jit(solution)/shard_map/pallas_call | solution.py:570
  276.2 12.4 %all_to_all.46.grad_ref = bf16[32,16,128]{2,1,0:T(8,128)(2,1)} all-to-all(bf16[32,16,128]{2,1,0:T(8,128)(2,1)S(1)} %copy-done.27), channel_id=1, replica_groups=mesh['section'=2,'tensor'=2,'wide'=32] {'wide'}, dimensions={0} | all-to-all | bytes 262144 | tf_op jit(solution)/shard_map/all_to_all | solution.py:804
  288.6 16.5 %shard_map.211 = bf16[32,144,128]{2,1,0:T(8,128)(2,1)} custom-call(s32[4,8]{1,0:T(4,128)} %and_convert_fusion.flag_ref, bf16[32,144,128]{2,1,0:T(8,128)(2,1)} %all_to_all.45.recv_ref, bf16[32,16,128]{2,1,0:T(8,128)(2,1)} %all_to_all.46.grad_ref, f32[32,16,128]{2,1,0:T(8,128)} %get-tuple-element.68.keep_ref, f32[1024,1]{1,0:T(8,128)} %get-tuple-element.69.lse_ref, ...), custom_call_target="tpu_custom_call" | custom-call | flops 16000000000 | bytes 100000 | tf_op jit(solution)/shard_map/pallas_call | solution.py:333
  305.1 26.5 %all_to_all.47.recv_ref = bf16[32,144,128]{2,1,0:T(8,128)(2,1)} all-to-all(bf16[32,144,128]{2,1,0:T(8,128)(2,1)} %shard_map.211), channel_id=1, replica_groups=mesh['section'=2,'tensor'=2,'wide'=32] {'wide'}, dimensions={0} | all-to-all | bytes 2359296 | tf_op jit(solution)/shard_map/all_to_all | solution.py:804
  331.6 4.6 shard_map.212
  337.2 9.2 %collective-permute-done.7.part_recv_ref = bf16[128,1024]{1,0:T(8,128)(2,1)S(1)} collective-permute-done((bf16[128,1024]{1,0:T(8,128)(2,1)}, bf16[128,1024]{1,0:T(8,128)(2,1)S(1)}, u32[]{:S(2)}, u32[]{:S(2)}) %collective-permute-start.7) | collective-permute-done | bytes 262176 | tf_op jit(solution)/shard_map/ppermute | solution.py:45
  347.1 8.2 %shard_map.213 = (bf16[128,1024]{1,0:T(8,128)(2,1)}, bf16[144,3072]{1,0:T(8,128)(2,1)}, bf16[128,1024]{1,0:T(8,128)(2,1)}, f32[64,1024]{1,0:T(8,128)}) custom-call(f32[128,1024]{1,0:T(8,128)} %get-tuple-element.66.middle_grad_ref, bf16[128,1024]{1,0:T(8,128)(2,1)} %get-tuple-element.70.part_own_ref, bf16[128,1024]{1,0:T(8,128)(2,1)} %copy-done.36, ...), custom_call_target="tpu_custom_call" | custom-call | flops 8000000000 | bytes 100000 | tf_op jit(solution)/shard_map/pallas_call | solution.py:498
  363.8 5.0 collective-permute-done.8.part_recv_ref
  375.1 6.6 %shard_map.221.refs_15_ = bf16[16,240,1024]{2,1,0:T(8,128)(2,1)} custom-call(s32[2]{0:T(128)} %pad_add_fusion.place_ref, bf16[128,4608]{1,0:T(8,128)(2,1)} %get-tuple-element.81.refs_0_.refs_2_, bf16[128,4608]{1,0:T(8,128)(2,1)} %copy-done.10, bf16[128,4608]{1,0:T(8,128)(2,1)} %get-tuple-element.81.refs_0_.refs_2_, ...), custom_call_target="tpu_custom_call", output_to_operand_aliasing={{}: (9, {})} | custom-call | flops 7000000000 | bytes 100000 | tf_op jit(solution)/shard_map/pallas_call | solution.py:570
  386.4 12.2 %all_to_all.48.grad_ref = bf16[32,16,128]{2,1,0:T(8,128)(2,1)} all-to-all(bf16[32,16,128]{2,1,0:T(8,128)(2,1)S(1)} %copy-done.26), channel_id=1, replica_groups=mesh['section'=2,'tensor'=2,'wide'=32] {'wide'}, dimensions={0} | all-to-all | bytes 262144 | tf_op jit(solution)/shard_map/all_to_all | solution.py:804
  398.5 16.5 %shard_map.215 = bf16[32,144,128]{2,1,0:T(8,128)(2,1)} custom-call(s32[4,8]{1,0:T(4,128)} %and_convert_fusion.flag_ref, bf16[32,144,128]{2,1,0:T(8,128)(2,1)} %copy-done.7, bf16[32,16,128]{2,1,0:T(8,128)(2,1)} %all_to_all.48.grad_ref, f32[32,16,128]{2,1,0:T(8,128)} %get-tuple-element.77.keep_ref, f32[1024,1]{1,0:T(8,128)} %get-tuple-element.78.lse_ref, ...), custom_call_target="tpu_custom_call" | custom-call | flops 16000000000 | bytes 100000 | tf_op jit(solution)/shard_map/pallas_call | solution.py:333
  419.5 23.7 %all-to-all-done.7.recv_ref = bf16[32,144,128]{2,1,0:T(8,128)(2,1)S(1)} async-done(((bf16[32,144,128]{2,1,0:T(8,128)(2,1)}), bf16[32,144,128]{2,1,0:T(8,128)(2,1)S(1)}, u32[]{:S(2)}, u32[]{:S(2)}) %all-to-all-start.7) | async-done | bytes 1179680 | tf_op jit(solution)/shard_map/all_to_all | solution.py:804
  456.0 5.1 all-to-all-start.8
  474.0 20.1 %all-to-all-done.8 = bf16[16,56,1024]{2,1,0:T(8,128)(2,1)S(1)} async-done(((bf16[16,56,1024]{2,1,0:T(8,128)(2,1)}), bf16[16,56,1024]{2,1,0:T(8,128)(2,1)S(1)}, u32[]{:S(2)}, u32[]{:S(2)}) %all-to-all-start.8) | async-done | bytes 1835040 | tf_op jit(solution)/shard_map/all_to_all | solution.py:960
  (270 shorter events, 130.0 us)
Async XLA Ops:
  7.2 62.8 %all-gather.6.cloned.1.call-start = ((), (), s32[]{:S(2)}) async-start(), calls=%async_computation.11 | async-start | bytes 7569408 | tf_op jit(solution)/shard_map/all_gather | solution.py:880
  10.3 5.2 %collective-permute-start.1 = (bf16[64,1024]{1,0:T(8,128)(2,1)S(1)}, bf16[64,1024]{1,0:T(8,128)(2,1)S(1)}, u32[]{:S(2)}, u32[]{:S(2)}) collective-permute-start(bf16[64,1024]{1,0:T(8,128)(2,1)S(1)} %pad_maximum_fusion.5), channel_id=1, source_target_pairs={{0,64},{64,0},{1,65},{65,1},{2,66},{66,2},{3,67},{67,3},{4,68},{68... | collective-permute-start | bytes 393224 | tf_op jit(solution)/shard_map/ppermute | solution.py:45
  16.3 127.8 %all-gather.8.cloned.1.call-start = ((), (), s32[]{:S(2)}) async-start(), calls=%async_computation.14 | async-start | bytes 11894784 | tf_op jit(solution)/shard_map/all_gather | solution.py:880
  17.1 9.6 %collective-permute-start = (bf16[144,1024]{1,0:T(8,128)(2,1)S(1)}, bf16[144,1024]{1,0:T(8,128)(2,1)S(1)}, u32[]{:S(2)}, u32[]{:S(2)}) collective-permute-start(bf16[144,1024]{1,0:T(8,128)(2,1)S(1)} %pad_maximum_fusion.2), channel_id=1, source_target_pairs={{0,32},{32,0},{1,33},{33,1},{2,34},{34,2},{3,35},{35,3},{4,36},{36... | collective-permute-start | bytes 884744 | tf_op jit(solution)/shard_map/ppermute | solution.py:45
  26.6 7.8 %collective-permute-start.2 = (bf16[160,1024]{1,0:T(8,128)(2,1)S(1)}, bf16[160,1024]{1,0:T(8,128)(2,1)S(1)}, u32[]{:S(2)}, u32[]{:S(2)}) collective-permute-start(bf16[160,1024]{1,0:T(8,128)(2,1)S(1)} %slice_dynamic-update-slice_fusion.2), channel_id=1, source_target_pairs={{0,64},{64,0},{1,65},{65,1},{2,66},{66,2},{3,67},{67,3},{4,68},{68... | collective-permute-start | bytes 983048 | tf_op jit(solution)/shard_map/ppermute | solution.py:45
  78.9 27.7 %all-to-all-start = ((bf16[32,144,128]{2,1,0:T(8,128)(2,1)}), bf16[32,144,128]{2,1,0:T(8,128)(2,1)S(1)}, u32[]{:S(2)}, u32[]{:S(2)}) async-start(bf16[32,144,128]{2,1,0:T(8,128)(2,1)} %get-tuple-element.52), calls=%async_computation | async-start | bytes 2359296 | tf_op jit(solution)/shard_map/all_to_all | solution.py:804
  120.5 19.1 %all-to-all-start.1 = ((bf16[64,16,128]{2,1,0:T(8,128)(2,1)}), bf16[64,16,128]{2,1,0:T(8,128)(2,1)S(1)}, u32[]{:S(2)}, u32[]{:S(2)}) async-start(bf16[64,16,128]{2,1,0:T(8,128)(2,1)} %bitcast.124), calls=%async_computation.1 | async-start | bytes 524288 | tf_op jit(solution)/shard_map/all_to_all | solution.py:812
  127.0 99.7 %all-gather.10.cloned.1.call-start = ((), (), s32[]{:S(2)}) async-start(), calls=%async_computation.15 | async-start | bytes 11894784 | tf_op jit(solution)/shard_map/all_gather | solution.py:880
  152.9 10.3 %collective-permute-start.3 = (bf16[128,1024]{1,0:T(8,128)(2,1)}, bf16[128,1024]{1,0:T(8,128)(2,1)S(1)}, u32[]{:S(2)}, u32[]{:S(2)}) collective-permute-start(bf16[128,1024]{1,0:T(8,128)(2,1)} %get-tuple-element.55.mlp_own_ref.refs_1_), channel_id=1, source_target_pairs={{0,32},{32,0},{1,33},{33,1},{2,34},{34,2},{3,35},{35,3},{4,36},{36... | collective-permute-start | bytes 786440 | tf_op jit(solution)/shard_map/ppermute | solution.py:45
  208.7 18.0 %all-to-all-start.3 = ((bf16[64,16,128]{2,1,0:T(8,128)(2,1)}), bf16[64,16,128]{2,1,0:T(8,128)(2,1)S(1)}, u32[]{:S(2)}, u32[]{:S(2)}) async-start(bf16[64,16,128]{2,1,0:T(8,128)(2,1)} %bitcast.125), calls=%async_computation.3 | async-start | bytes 524288 | tf_op jit(solution)/shard_map/all_to_all | solution.py:812
  215.8 165.9 %reduce-scatter.3.cloned.1.call-start = ((), (), s32[]{:S(2)}) async-start(), calls=%async_computation.12 | async-start | bytes 4456448 | tf_op jit(solution)/shard_map/reduce_scatter | solution.py:937
  234.7 10.1 %collective-permute-start.4 = (bf16[128,1024]{1,0:T(8,128)(2,1)}, bf16[128,1024]{1,0:T(8,128)(2,1)S(1)}, u32[]{:S(2)}, u32[]{:S(2)}) collective-permute-start(bf16[128,1024]{1,0:T(8,128)(2,1)} %get-tuple-element.61.refs_1_), channel_id=1, source_target_pairs={{0,32},{32,0},{1,33},{33,1},{2,34},{34,2},{3,35},{35,3},{4,36},{36... | collective-permute-start | bytes 786440 | tf_op jit(solution)/shard_map/ppermute | solution.py:45
  236.2 31.3 %collective-permute-start.18 = (bf16[128,4608]{1,0:T(8,128)(2,1)}, bf16[128,4608]{1,0:T(8,128)(2,1)S(1)}, u32[]{:S(2)}, u32[]{:S(2)}) collective-permute-start(bf16[128,4608]{1,0:T(8,128)(2,1)} %get-tuple-element.88.refs_0_.refs_2_), channel_id=1, source_target_pairs={{0,1},{1,0},{2,3},{3,2},{4,5},{5,4},{6,7},{7,6},{8,9},{9,8},{10,11... | collective-permute-start | bytes 3538952 | tf_op jit(solution)/shard_map/ppermute | solution.py:800
  252.7 14.7 %collective-permute-start.14 = (bf16[144,3072]{1,0:T(8,128)(2,1)}, bf16[144,3072]{1,0:T(8,128)(2,1)S(1)}, u32[]{:S(2)}, u32[]{:S(2)}) collective-permute-start(bf16[144,3072]{1,0:T(8,128)(2,1)} %get-tuple-element.84.refs_4_.refs_6_), channel_id=1, source_target_pairs={{0,1},{1,0},{2,3},{3,2},{4,5},{5,4},{6,7},{7,6},{8,9},{9,8},{10,11... | collective-permute-start | bytes 2654216 | tf_op jit(solution)/shard_map/ppermute | solution.py:800
  252.7 10.4 %collective-permute-start.6 = (bf16[128,1024]{1,0:T(8,128)(2,1)}, bf16[128,1024]{1,0:T(8,128)(2,1)S(1)}, u32[]{:S(2)}, u32[]{:S(2)}) collective-permute-start(bf16[128,1024]{1,0:T(8,128)(2,1)} %get-tuple-element.64.part_own_ref), channel_id=1, source_target_pairs={{0,32},{32,0},{1,33},{33,1},{2,34},{34,2},{3,35},{35,3},{4,36},{36... | collective-permute-start | bytes 786440 | tf_op jit(solution)/shard_map/ppermute | solution.py:45
  275.3 219.4 %reduce-scatter.5.cloned.1.call-start = ((), (), s32[]{:S(2)}) async-start(), calls=%async_computation.13 | async-start | bytes 8355840 | tf_op jit(solution)/shard_map/reduce_scatter | solution.py:937
  336.1 10.2 %collective-permute-start.7 = (bf16[128,1024]{1,0:T(8,128)(2,1)}, bf16[128,1024]{1,0:T(8,128)(2,1)S(1)}, u32[]{:S(2)}, u32[]{:S(2)}) collective-permute-start(bf16[128,1024]{1,0:T(8,128)(2,1)} %get-tuple-element.70.part_own_ref), channel_id=1, source_target_pairs={{0,32},{32,0},{1,33},{33,1},{2,34},{34,2},{3,35},{35,3},{4,36},{36... | collective-permute-start | bytes 786440 | tf_op jit(solution)/shard_map/ppermute | solution.py:45
  336.6 36.6 %collective-permute-start.11 = (bf16[128,4608]{1,0:T(8,128)(2,1)S(1)}, bf16[128,4608]{1,0:T(8,128)(2,1)S(1)}, u32[]{:S(2)}, u32[]{:S(2)}) collective-permute-start(bf16[128,4608]{1,0:T(8,128)(2,1)S(1)} %copy-done.9), channel_id=1, source_target_pairs={{0,1},{1,0},{2,3},{3,2},{4,5},{5,4},{6,7},{7,6},{8,9},{9,8},{10,11... | collective-permute-start | bytes 3538952 | tf_op jit(solution)/shard_map/ppermute | solution.py:800
  336.6 18.7 %collective-permute-start.15 = (bf16[144,1024]{1,0:T(8,128)(2,1)S(1)}, bf16[144,1024]{1,0:T(8,128)(2,1)S(1)}, u32[]{:S(2)}, u32[]{:S(2)}) collective-permute-start(bf16[144,1024]{1,0:T(8,128)(2,1)S(1)} %copy-done.11), channel_id=1, source_target_pairs={{0,1},{1,0},{2,3},{3,2},{4,5},{5,4},{6,7},{7,6},{8,9},{9,8},{10,11... | collective-permute-start | bytes 884744 | tf_op jit(solution)/shard_map/ppermute | solution.py:800
  337.1 21.7 %collective-permute-start.16 = (bf16[144,1536]{1,0:T(8,128)(2,1)}, bf16[144,1536]{1,0:T(8,128)(2,1)S(1)}, u32[]{:S(2)}, u32[]{:S(2)}) collective-permute-start(bf16[144,1536]{1,0:T(8,128)(2,1)} %get-tuple-element.86.refs_2_.refs_8_), channel_id=1, source_target_pairs={{0,1},{1,0},{2,3},{3,2},{4,5},{5,4},{6,7},{7,6},{8,9},{9,8},{10,11... | collective-permute-start | bytes 1327112 | tf_op jit(solution)/shard_map/ppermute | solution.py:800
  355.2 17.9 %collective-permute-start.17 = (bf16[144,3072]{1,0:T(8,128)(2,1)}, bf16[144,3072]{1,0:T(8,128)(2,1)S(1)}, u32[]{:S(2)}, u32[]{:S(2)}) collective-permute-start(bf16[144,3072]{1,0:T(8,128)(2,1)} %get-tuple-element.87.refs_4_.refs_6_.refs_10_), channel_id=1, source_target_pairs={{0,1},{1,0},{2,3},{3,2},{4,5},{5,4},{6,7},{7,6},{8,9},{9,8},{10,11... | collective-permute-start | bytes 2654216 | tf_op jit(solution)/shard_map/ppermute | solution.py:800
  358.6 10.2 %collective-permute-start.8 = (bf16[128,1024]{1,0:T(8,128)(2,1)S(1)}, bf16[128,1024]{1,0:T(8,128)(2,1)S(1)}, u32[]{:S(2)}, u32[]{:S(2)}) collective-permute-start(bf16[128,1024]{1,0:T(8,128)(2,1)S(1)} %copy-done.35), channel_id=1, source_target_pairs={{0,32},{32,0},{1,33},{33,1},{2,34},{34,2},{3,35},{35,3},{4,36},{36... | collective-permute-start | bytes 786440 | tf_op jit(solution)/shard_map/ppermute | solution.py:45
  373.1 8.5 %collective-permute-start.13 = (bf16[144,1024]{1,0:T(8,128)(2,1)}, bf16[144,1024]{1,0:T(8,128)(2,1)S(1)}, u32[]{:S(2)}, u32[]{:S(2)}) collective-permute-start(bf16[144,1024]{1,0:T(8,128)(2,1)} %get-tuple-element.83.refs_2_.refs_12_), channel_id=1, source_target_pairs={{0,1},{1,0},{2,3},{3,2},{4,5},{5,4},{6,7},{7,6},{8,9},{9,8},{10,11... | collective-permute-start | bytes 884744 | tf_op jit(solution)/shard_map/ppermute | solution.py:800
  415.0 28.3 %all-to-all-start.7 = ((bf16[32,144,128]{2,1,0:T(8,128)(2,1)}), bf16[32,144,128]{2,1,0:T(8,128)(2,1)S(1)}, u32[]{:S(2)}, u32[]{:S(2)}) async-start(bf16[32,144,128]{2,1,0:T(8,128)(2,1)} %shard_map.215), calls=%async_computation.7 | async-start | bytes 2359296 | tf_op jit(solution)/shard_map/all_to_all | solution.py:804
  450.1 12.4 %collective-permute-start.9 = (bf16[128,1024]{1,0:T(8,128)(2,1)}, bf16[128,1024]{1,0:T(8,128)(2,1)S(1)}, u32[]{:S(2)}, u32[]{:S(2)}) collective-permute-start(bf16[128,1024]{1,0:T(8,128)(2,1)} %get-tuple-element.79), channel_id=1, source_target_pairs={{0,32},{32,0},{1,33},{33,1},{2,34},{34,2},{3,35},{35,3},{4,36},{36... | collective-permute-start | bytes 786440 | tf_op jit(solution)/shard_map/ppermute | solution.py:45
  456.0 38.2 %all-to-all-start.8 = ((bf16[16,56,1024]{2,1,0:T(8,128)(2,1)}), bf16[16,56,1024]{2,1,0:T(8,128)(2,1)S(1)}, u32[]{:S(2)}, u32[]{:S(2)}) async-start(bf16[16,56,1024]{2,1,0:T(8,128)(2,1)} %shard_map.217), calls=%async_computation.8 | async-start | bytes 3670016 | tf_op jit(solution)/shard_map/all_to_all | solution.py:960
  462.2 6.5 %collective-permute-start.5 = (bf16[64,1024]{1,0:T(8,128)(2,1)S(1)}, bf16[64,1024]{1,0:T(8,128)(2,1)S(1)}, u32[]{:S(2)}, u32[]{:S(2)}) collective-permute-start(bf16[64,1024]{1,0:T(8,128)(2,1)S(1)} %get-tuple-element.103), channel_id=1, source_target_pairs={{0,64},{64,0},{1,65},{65,1},{2,66},{66,2},{3,67},{67,3},{4,68},{68... | collective-permute-start | bytes 393224 | tf_op jit(solution)/shard_map/ppermute | solution.py:45
  463.9 9.2 %collective-permute-start.10 = (f32[64,1024]{1,0:T(8,128)S(1)}, f32[64,1024]{1,0:T(8,128)S(1)}, u32[]{:S(2)}, u32[]{:S(2)}) collective-permute-start(f32[64,1024]{1,0:T(8,128)S(1)} %get-tuple-element.99), channel_id=1, source_target_pairs={{0,64},{64,0},{1,65},{65,1},{2,66},{66,2},{3,67},{67,3},{4,68},{68... | collective-permute-start | bytes 786440 | tf_op jit(solution)/shard_map/ppermute | solution.py:45
  499.6 6.0 %collective-permute-start.19 = (bf16[49,1024]{1,0:T(8,128)(2,1)S(1)}, bf16[49,1024]{1,0:T(8,128)(2,1)S(1)}, u32[]{:S(2)}, u32[]{:S(2)}) collective-permute-start(bf16[49,1024]{1,0:T(8,128)(2,1)S(1)} %broadcast_select_fusion.7), channel_id=1, source_target_pairs={{0,64},{64,0},{1,65},{65,1},{2,66},{66,2},{3,67},{67,3},{4,68},{68... | collective-permute-start | bytes 301064 | tf_op jit(solution)/shard_map/ppermute | solution.py:45
  500.7 9.8 %collective-permute-start.22 = (bf16[64]{0:T(256)(128)(2,1)S(1)}, bf16[64]{0:T(256)(128)(2,1)S(1)}, u32[]{:S(2)}, u32[]{:S(2)}) collective-permute-start(bf16[64]{0:T(256)(128)(2,1)S(1)} %slice_bitcast_fusion.16), channel_id=1, source_target_pairs={{0,96},{96,0},{32,64},{64,32},{1,97},{97,1},{33,65},{65,33},{2,98}... | collective-permute-start | bytes 392 | tf_op jit(solution)/shard_map/ppermute | solution.py:998
  505.1 8.9 %collective-permute-start.20 = (bf16[144,1024]{1,0:T(8,128)(2,1)S(1)}, bf16[144,1024]{1,0:T(8,128)(2,1)S(1)}, u32[]{:S(2)}, u32[]{:S(2)}) collective-permute-start(bf16[144,1024]{1,0:T(8,128)(2,1)S(1)} %broadcast_select_fusion.2), channel_id=1, source_target_pairs={{0,64},{64,0},{1,65},{65,1},{2,66},{66,2},{3,67},{67,3},{4,68},{68... | collective-permute-start | bytes 884744 | tf_op jit(solution)/shard_map/ppermute | solution.py:45
  506.4 6.3 %collective-permute-start.21 = (bf16[64]{0:T(256)(128)(2,1)S(1)}, bf16[64]{0:T(256)(128)(2,1)S(1)}, u32[]{:S(2)}, u32[]{:S(2)}) collective-permute-start(bf16[64]{0:T(256)(128)(2,1)S(1)} %slice_bitcast_fusion.17), channel_id=1, source_target_pairs={{0,32},{32,0},{1,33},{33,1},{2,34},{34,2},{3,35},{35,3},{4,36},{36... | collective-permute-start | bytes 392 | tf_op jit(solution)/shard_map/ppermute | solution.py:45
  (40 other events, 280.7 us)
Sparse Core Ops, SparseCore 0:
  16.4 53.5 all-gather.5
  72.3 71.7 all-gather.7
  153.0 63.8 all-gather.9
  275.4 81.0 reduce-scatter.2
  385.6 107.3 reduce-scatter.4

commit v5 on v4

--- a/solution.py
+++ b/solution.py
@@ -39,6 +39,11 @@
 def whole(shape):
     count = len(shape)
     return pl.BlockSpec(shape, lambda *g: (0,) * count)
+
+
+ANYWHERE = pl.BlockSpec(memory_space=pl.ANY)
+SCALARS = pl.BlockSpec(memory_space=pltpu.SMEM)
+EVERY = slice(None)
 
 
 def swap(block, axis):
@@ -437,8 +442,7 @@
 
 
 def mlp_back_steps(
-    grad, vec_ref, mlp_own_ref, mlp_recv_ref, pre_ref, one_ref, two_ref,
-    grad_ref, back_ref, out_ref, acc_ref, sums_ref,
+    grad, vec_ref, pre_ref, one_ref, two_ref, grad_ref, back_ref, out_ref, acc_ref, sums_ref,
 ):
     at = pl.program_id(0)
 
@@ -449,10 +453,8 @@
         rows = rows.astype(F32)
         scaled = rows * row_of(vec_ref, SCALE_M)
         back_ref[0:BOTH, 2048:3072] = scaled.astype(BF)
-        branch = joined(mlp_own_ref, mlp_recv_ref) + row_of(vec_ref, SHIFT_M)
         sums_ref[...] = jnp.zeros((16, MODEL), F32)
         sums_ref[0:1, :] = column_sum(scaled)
-        sums_ref[1:2, :] = column_sum(rows * branch)
 
     pre = pre_ref[...]
     slope = 0.5 * (1.0 + lax.erf(pre * ROOT_HALF)) + pre * jnp.exp(-0.5 * pre * pre) * INV_ROOT_TAU
@@ -464,13 +466,13 @@
     def _():
         back_ref[0:BOTH, 0:MODEL] = grad_pre
         acc_ref[...] = part
-        sums_ref[2:3, :] = bias_sum
+        sums_ref[1:2, :] = bias_sum
 
     @pl.when(at == 1)
     def _():
         back_ref[0:BOTH, MODEL:HIDDEN] = grad_pre
         out_ref[...] = (acc_ref[...] + part).astype(BF)
-        sums_ref[3:4, :] = bias_sum
+        sums_ref[2:3, :] = bias_sum
         back_ref[BOTH:TALL, 0:MODEL] = sums_ref[...].astype(BF)
         back_ref[BOTH:TALL, MODEL:3072] = jnp.zeros((16, 2048), BF)
 
@@ -479,7 +481,9 @@
     mlp_back_steps(lambda: jnp.concatenate([own_ref[...], other_ref[...]], axis=0), *refs)
 
 
-def mlp_back_next_kernel(middle_grad_ref, part_own_ref, part_recv_ref, rows_ref, after_ref, *refs):
+def mlp_back_next_kernel(
+    middle_grad_ref, part_own_ref, part_recv_ref, rows_ref, after_ref, pack_ref, *refs
+):
     *refs, input_grad_ref, acc_ref, sums_ref = refs
 
     def grad():
@@ -492,17 +496,15 @@
     mlp_back_steps(grad, *refs, acc_ref, sums_ref)
 
 
-def mlp_back_call(inputs, small, mlp_own, mlp_recv, pre, weights):
+def mlp_back_call(inputs, small, pre, weights):
     first = len(inputs) == 2
     extra = [] if first else [(ROWS, MODEL)]
     return pl.pallas_call(
         mlp_back_first_kernel if first else mlp_back_next_kernel,
         grid=(2,),
-        in_specs=[whole(part.shape) for part in inputs]
+        in_specs=[ANYWHERE if part.ndim == 3 else whole(part.shape) for part in inputs]
         + [
             whole((8, MODEL)),
-            whole((BOTH, MODEL)),
-            whole((BOTH, MODEL)),
             pl.BlockSpec((BOTH, MODEL), lambda j: (0, j)),
             pl.BlockSpec((WIDE, 32, MODEL), lambda j: (0, 2 + j, 0)),
             pl.BlockSpec((16, 64, MODEL), lambda j: (j, 0, 0)),
@@ -518,16 +520,11 @@
         scratch_shapes=[pltpu.VMEM((BOTH, MODEL), F32), pltpu.VMEM((16, MODEL), F32)],
         compiler_params=params(),
         cost_estimate=cost(8),
-    )(*inputs, small[0], mlp_own, mlp_recv, pre, weights, weights)
+    )(*inputs, small[0], pre, weights, weights)
 
 
 PACK_ROWS = 240
 CHIPS = WIDE // 2
-
-
-ANYWHERE = pl.BlockSpec(memory_space=pl.ANY)
-SCALARS = pl.BlockSpec(memory_space=pltpu.SMEM)
-EVERY = slice(None)
 
 
 def store_mine(place_ref, value, grad_ref, pairs, rows, columns):
@@ -563,8 +560,8 @@
             store_mine(place_ref, grad_one, grad_ref, EVERY, rows, EVERY)
 
 
-def mlp_weight_call(place, kept, back, more, pack=None):
-    rows, extra, aliases = 128, [more], {}
+def mlp_weight_call(place, kept, back, pack=None):
+    rows, extra, aliases = 128, [], {}
     if pack is not None:
         rows, extra, aliases = PACK_ROWS, [pack], {9: 0}
     return pl.pallas_call(
@@ -575,7 +572,7 @@
         + twice(pl.BlockSpec((BOTH, MODEL), lambda j: (0, 2)))
         + twice(pl.BlockSpec((BOTH, MODEL), lambda j: (0, 2)))
         + twice(pl.BlockSpec((BOTH, MODEL), lambda j: (0, j)))
-        + [ANYWHERE],
+        + [ANYWHERE] * len(extra),
         out_specs=pl.BlockSpec((CHIPS, 128, MODEL), lambda j: (0, 0, 0)),
         out_shape=jax.ShapeDtypeStruct((CHIPS, rows, MODEL), BF),
         input_output_aliases=aliases,
@@ -585,8 +582,8 @@
 
 
 def out_back_kernel(
-    grad_ref, part_own_ref, part_recv_ref, middle_ref, branch_ref, vec_ref,
-    weight_ref, middle_grad_ref, send_ref, low_ref, sums_ref,
+    grad_ref, part_own_ref, part_recv_ref, middle_ref, branch_ref, mlp_own_ref, mlp_recv_ref, vec_ref,
+    weight_ref, pack_ref, middle_grad_ref, send_ref, low_ref, sums_ref,
 ):
     hat, rstd = norm_parts(middle_ref[...])
     grad_norm = joined(part_own_ref, part_recv_ref)
@@ -603,15 +600,17 @@
     sums_ref[1:2, :] = column_sum(grad_norm)
     sums_ref[2:3, :] = column_sum(scaled)
     sums_ref[3:4, :] = column_sum(total * branch_ref[...])
+    branch = joined(mlp_own_ref, mlp_recv_ref) + row_of(vec_ref, SHIFT_M)
+    sums_ref[4:5, :] = column_sum(grad_ref[...].astype(F32) * branch)
     low_ref[BOTH:TALL, :] = sums_ref[...].astype(BF)
 
 
-def out_back_call(grad, part_own, part_recv, middle, branch, small, weights):
+def out_back_call(grad, part_own, part_recv, middle, branch, mlp, mlp_recv, small, weights, pack):
     return pl.pallas_call(
         out_back_kernel,
         grid=(1,),
-        in_specs=[whole((BOTH, MODEL))] * 5
-        + [whole((8, MODEL)), pl.BlockSpec((WIDE, 16, MODEL), lambda i: (0, 8, 0))],
+        in_specs=[whole((BOTH, MODEL))] * 7
+        + [whole((8, MODEL)), pl.BlockSpec((WIDE, 16, MODEL), lambda i: (0, 8, 0)), ANYWHERE],
         out_specs=[whole((BOTH, MODEL)), whole((WIDE, 16, 128)), whole((TALL, MODEL))],
         out_shape=[
             jax.ShapeDtypeStruct((BOTH, MODEL), F32),
@@ -621,7 +620,7 @@
         scratch_shapes=[pltpu.VMEM((16, MODEL), F32)],
         compiler_params=params(),
         cost_estimate=cost(4),
-    )(grad, part_own, part_recv, middle, branch, small[0], weights)
+    )(grad, part_own, part_recv, middle, branch, mlp, mlp_recv, small[0], weights, pack)
 
 
 def store_out_grads(place_ref, refs, grad_ref, rows):
@@ -637,10 +636,10 @@
     *sums_refs, before_ref, _, grad_ref = refs[4:]
     store_out_grads(place_ref, refs, grad_ref, slice(0, 16))
     parts = [
-        own[0:4, :].astype(F32) + other[0:4, :].astype(F32)
-        for own, other in zip(sums_refs[0::2], sums_refs[1::2])
+        own[0:count, :].astype(F32) + other[0:count, :].astype(F32)
+        for own, other, count in zip(sums_refs[0::2], sums_refs[1::2], (8, 8, 4, 4, 4))
     ]
-    rows = jnp.concatenate(parts + [before_ref[0:12, :].astype(F32)], axis=0).astype(BF)
+    rows = jnp.concatenate(parts + [before_ref[0:4, :].astype(F32)], axis=0).astype(BF)
     grad_ref[:, 16:48, :] = jnp.broadcast_to(rows[None], (CHIPS, 32, MODEL))
 
 
@@ -820,21 +819,24 @@
     )
 
 
-def layer_backward(inputs, kept, ids, qkv, rest, small):
+def layer_backward(place, inputs, kept, ids, qkv, rest, small, pack=None):
     flags, key_ids, query_ids = ids
     grad, mlp_back, part, *input_grad = mlp_back_call(
-        inputs, small, kept["mlp"], kept["mlp_recv"], kept["pre"], rest
-    )
+        inputs, small, kept["pre"], rest
+    )
+    mlp_pair = with_core(mlp_back)
+    pack = mlp_weight_call(place, kept["for_weights"], mlp_pair, pack)
     middle_grad, mix_grad, low_a = out_back_call(
-        grad, part, swap(part, "tensor"), kept["middle"], kept["branch"], small, rest
+        grad, part, swap(part, "tensor"), kept["middle"], kept["branch"], kept["mlp"],
+        kept["mlp_recv"], small, rest, pack,
     )
     back = attend_back_call(
         flags, kept["recv"], all_to_all(mix_grad), kept["keep"], kept["lse"], key_ids, query_ids
     )
     qkv_part, qkv_grads = qkv_back_call(all_to_all(back), kept["rows"], small, *qkv)
     carried = (middle_grad, qkv_part, swap(qkv_part, "tensor"), kept["rows"])
-    for_weights = with_core(mlp_back), with_core(low_a), with_core(qkv_grads)
-    return carried, for_weights, input_grad
+    for_weights = mlp_pair, with_core(low_a), with_core(qkv_grads)
+    return carried, pack, for_weights, input_grad
 
 
 def body(
@@ -939,22 +941,21 @@
             "wide", scatter_dimension=0, axis_index_groups=same_core, tiled=True,
         )
 
-    carried1, back1, _ = layer_backward(
-        (own_cot, other_cot), kept1, ids, qkv_parts[1], rest[1], small[1]
+    carried1, pack1, back1, _ = layer_backward(
+        place, (own_cot, other_cot), kept1, ids, qkv_parts[1], rest[1], small[1]
     )
     kept_pair0, kept_pair1 = kept0["for_weights"], kept1["for_weights"]
     mlp_back1, low1, grads1 = back1
-    sum_mlp1 = over_chips(mlp_weight_call(place, kept_pair1, mlp_back1, low1[0]))
+    sum_mlp1 = over_chips(pack1)
     pack = out_weight_call(place, kept_pair1, low1)
     pack = qkv_weight_call(place, kept_pair1, grads1, pack)
 
-    carried0, back0, (grad_x1,) = layer_backward(
-        carried1 + (small[1][0],), kept0, ids, qkv_parts[0], rest[0], small[0]
+    carried0, pack, back0, (grad_x1,) = layer_backward(
+        place, carried1 + (small[1][0], pack), kept0, ids, qkv_parts[0], rest[0], small[0], pack
     )
     mlp_back0, low0, grads0 = back0
-    pack = mlp_weight_call(place, kept_pair0, mlp_back0, None, pack)
     pack = out_weight_last_call(
-        place, kept_pair0, low0, (mlp_back1, low1, grads1, mlp_back0, low0), sum_mlp1, pack
+        place, kept_pair0, low0, (low1, low0, grads1, mlp_back1, mlp_back0), sum_mlp1, pack
     )
     sum_mid = over_chips(pack)
     last_recv = lax.all_to_all(
@@ -971,42 +972,29 @@
     def lanes(rows, width):
         return lax.dynamic_slice_in_dim(rows, wide * width, width, rows.ndim - 1)
 
-    def own_sums(mlp, outs, qkv_rows):
-        norms = jnp.concatenate([mlp[0:2], outs, qkv_rows[0:2]], axis=0)
-        pair = qkv_rows[2].reshape(2, HALF_W)
-        return jnp.concatenate(
-            [lanes(norms, 32).reshape(-1), lanes(pair, 16).reshape(-1), lanes(mlp[2:4].reshape(-1), 64)]
-        )
-
-    sums = sum_mid[208:228]
-    mlp1, outs1, qkv1, mlp0, outs0 = (sums[at : at + 4] for at in range(0, 20, 4))
     mid0 = jnp.concatenate([sum_mid[0:128], sum_mid[192:208]], axis=0)
     mid1 = jnp.concatenate([sum_mlp1, sum_mid[128:144]], axis=0)
     mid_total = jnp.where(is_first, mid0, mid1).astype(F32) + swap(
         jnp.where(is_first, mid1, mid0), "section"
     ).astype(F32)
-
-    def with_sums(rows, vector):
-        return jnp.concatenate([rows, jnp.pad(vector, (0, 672)).reshape(1, MODEL)], axis=0)
-
-    late0 = with_sums(sum_last[0:48].astype(BF), own_sums(mlp0, outs0, sum_last[48:52].astype(BF)))
-    late1 = with_sums(sum_mid[144:192], own_sums(mlp1, outs1, qkv1))
+    late0 = jnp.concatenate([sum_last[0:52].astype(BF), sum_mid[232:236], sum_mid[216:224]], axis=0)
+    late1 = jnp.concatenate(
+        [sum_mid[144:192], sum_mid[224:228], sum_mid[228:232], sum_mid[208:216]], axis=0
+    )
     late_own = jnp.where(is_first, late0, late1)
     late_away = jnp.where(is_first, late1, late0)
     late_total = late_own.astype(F32) + swap(late_away, "section").astype(F32)
-    own_part, away_part = late_own[48, 192:256], late_away[48, 192:256]
-    across = lax.ppermute(away_part, ("section", "tensor"), [(0, 3), (3, 0), (1, 2), (2, 1)])
-    heads_total = late_total[48, 192:256] + (
-        swap(own_part, "tensor").astype(F32) + across.astype(F32)
-    )
-    mlp_total, out_total = mid_total[0:128], mid_total[128:144]
-    qkv_total, tiny = late_total[0:48], late_total[48]
-    norms = jnp.concatenate([tiny[0:192], heads_total]).reshape(8, 32)
-    g_gains = jnp.stack([norms[6], norms[2]])
-    g_shifts = jnp.stack([norms[7], norms[4], norms[3], norms[0]])
-    g_scales = jnp.stack([norms[5], norms[1]])
-    g_qv = tiny[256:288].reshape(2, 16)
-    g_fc1_bias = tiny[288:352]
+    across = lax.ppermute(late_away[48:50], ("section", "tensor"), [(0, 3), (3, 0), (1, 2), (2, 1)])
+    heads_total = late_total[48:50] + (
+        swap(late_own[48:50], "tensor").astype(F32) + across.astype(F32)
+    )
+    mlp_total, out_total, qkv_total = mid_total[0:128], mid_total[128:144], late_total[0:48]
+    norms = lanes(jnp.concatenate([heads_total, late_total[52:53], late_total[56:61]], axis=0), 32)
+    g_gains = jnp.stack([norms[0], norms[3]])
+    g_shifts = jnp.stack([norms[1], norms[5], norms[4], norms[2]])
+    g_scales = jnp.stack([norms[6], norms[7]])
+    g_qv = lanes(late_total[50].reshape(2, HALF_W), 16)
+    g_fc1_bias = lanes(late_total[53:55].reshape(HIDDEN), 64)
     g_fc2 = mlp_total[0:64]
     g_fc1 = jnp.concatenate([mlp_total[64:96], mlp_total[96:128]], axis=1)
     pairs = qkv_total[0:32]

time: 532 us -> 523 us (0.983)
  blocking collectives: 78.6 us -> 53.1 us
  waiting for transfers between devices: 187 us -> 202 us
  starting transfers between devices: 50.6 us -> 58.1 us
    all_to_all x4 -> x3, blocking collectives: 78.6 us -> 53.1 us  [all_to_all(): return lax.all_to_all(block, 'wide', 0, 0, tiled=True)]
    all_to_all x2 -> x3, waiting for transfers between devices: 42.3 us -> 62.7 us  [all_to_all(): return lax.all_to_all(block, 'wide', 0, 0, tiled=True)]
    ppermute x14, waiting for transfers between devices: 62.4 us -> 50.6 us  [swap(): return lax.ppermute(block, axis, [(0, 1), (1, 0)])]
    all_to_all x2 -> x3, starting transfers between devices: 9.51 us -> 13.4 us  [all_to_all(): return lax.all_to_all(block, 'wide', 0, 0, tiled=True)]
    unnamed x84 -> x89, local copies, waits for them, and re-layouts: 14.4 us -> 14.5 us
  transfers between devices with their start and end apart: 33 -> 34, of which waited for: 19 -> 25; matrix products, arithmetic and copies ran while one was open for 4% -> 5% of each run, Pallas kernels for 22% -> 22%
where the time goes in v5:
time: 523 us; the launch traced here: 515 us
  waiting for transfers between devices  202 us (39%)
  Pallas kernels  136 us (26%)
  starting transfers between devices  58.1 us (11%)
  blocking collectives  53.1 us (10%)
  local copies, waits for them, and re-layouts  34.6 us (7%)
  other arithmetic  16.1 us (3%)
  between operations  14.9 us (3%)
    all_to_all x3, waiting for transfers between devices, all_to_all(): return lax.all_to_all(block, 'wide', 0, 0, tiled=True)  62.7 us
    all_to_all x3, blocking collectives, all_to_all(): return lax.all_to_all(block, 'wide', 0, 0, tiled=True)  53.1 us
    ppermute x14, waiting for transfers between devices, swap(): return lax.ppermute(block, axis, [(0, 1), (1, 0)])  50.6 us
    all_gather x3, waiting for transfers between devices, gather(): return lax.all_gather(block, 'wide', axis=0, tiled=False)  40.5 us
    pallas_call x2, Pallas kernels, attend_back_call(): pl.pallas_call(attend_back_kernel, grid_spec=pltpu.PrefetchScalarGridSpec...  30.3 us
    pallas_call x2, Pallas kernels, attend_call(): pl.pallas_call(attend_kernel, grid_spec=pltpu.PrefetchScalarGridSpec(num_...  24.1 us
    ppermute x14, starting transfers between devices, swap(): return lax.ppermute(block, axis, [(0, 1), (1, 0)])  22.1 us
    all_to_all x2, waiting for transfers between devices, layer_forward(): lax.all_to_all(mix_sent.reshape(2 * WIDE, 16, 128), ('tensor', 'wide'), 0...  21.4 us
  transfers between devices with their start and end apart: 34, of which 25 were waited for; matrix products, arithmetic and copies ran while one was open for 5% of the time, Pallas kernels for 22%

profile of v5, /device:TPU:0, one launch (start us, length us, event | category | flops | bytes accessed | tf_op | source)
XLA Modules:
  0.0 514.7 jit_solution(7471111209726157478)
XLA Ops:
  20.6 6.1 %collective-permute-done = bf16[144,1024]{1,0:T(8,128)(2,1)S(1)} collective-permute-done((bf16[144,1024]{1,0:T(8,128)(2,1)S(1)}, bf16[144,1024]{1,0:T(8,128)(2,1)S(1)}, u32[]{:S(2)}, u32[]{:S(2)}) %collective-permute-start) | collective-permute-done | bytes 294944 | tf_op jit(solution)/shard_map/ppermute | solution.py:50
  28.3 6.1 %collective-permute-done.2 = bf16[160,1024]{1,0:T(8,128)(2,1)S(1)} collective-permute-done((bf16[160,1024]{1,0:T(8,128)(2,1)S(1)}, bf16[160,1024]{1,0:T(8,128)(2,1)S(1)}, u32[]{:S(2)}, u32[]{:S(2)}) %collective-permute-start.2) | collective-permute-done | bytes 327712 | tf_op jit(solution)/shard_map/ppermute | solution.py:50
  34.5 35.5 %all-gather.6.cloned.1.call-done.weight_ref = bf16[32,112,1024]{2,1,0:T(8,128)(2,1)} async-done(((bf16[1,112,1024]{2,1,0:T(8,128)(2,1)}), bf16[32,112,1024]{2,1,0:T(8,128)(2,1)}) %all-gather.6.cloned.1.call-update) | async-done | bytes 7340048 | tf_op jit(solution)/shard_map/all_gather | solution.py:882
  78.9 5.2 %all-to-all-start = ((bf16[32,144,128]{2,1,0:T(8,128)(2,1)}), bf16[32,144,128]{2,1,0:T(8,128)(2,1)S(1)}, u32[]{:S(2)}, u32[]{:S(2)}) async-start(bf16[32,144,128]{2,1,0:T(8,128)(2,1)} %get-tuple-element.52), calls=%async_computation | async-start | bytes 2359296 | tf_op jit(solution)/shard_map/all_to_all | solution.py:803
  88.0 18.6 %all-to-all-done.recv_ref = bf16[32,144,128]{2,1,0:T(8,128)(2,1)S(1)} async-done(((bf16[32,144,128]{2,1,0:T(8,128)(2,1)}), bf16[32,144,128]{2,1,0:T(8,128)(2,1)S(1)}, u32[]{:S(2)}, u32[]{:S(2)}) %all-to-all-start) | async-done | bytes 1179680 | tf_op jit(solution)/shard_map/all_to_all | solution.py:803
  107.6 12.0 %shard_map.204 = (bf16[2,32,16,128]{3,2,1,0:T(8,128)(2,1)}, f32[32,16,128]{2,1,0:T(8,128)}, f32[1024,1]{1,0:T(8,128)}) custom-call(s32[4,8]{1,0:T(4,128)} %and_convert_fusion.flag_ref, bf16[32,144,128]{2,1,0:T(8,128)(2,1)} %copy-done.9, s32[8,1,512]{2,1,0:T(1,128)} %reshape.195.key_id_ref, s32[4,256,1]{2,1,0:T(8,128)} %reshape.207.query_id_ref), custom_call_target="tpu_custom_call" | custom-call | flops 12000000000 | bytes 100000 | tf_op jit(solution)/shard_map/pallas_call | solution.py:251
  119.6 6.8 %all-to-all-start.1 = ((bf16[64,16,128]{2,1,0:T(8,128)(2,1)}), bf16[64,16,128]{2,1,0:T(8,128)(2,1)S(1)}, u32[]{:S(2)}, u32[]{:S(2)}) async-start(bf16[64,16,128]{2,1,0:T(8,128)(2,1)} %bitcast.114), calls=%async_computation.1 | async-start | bytes 524288 | tf_op jit(solution)/shard_map/all_to_all | solution.py:811
  127.8 11.3 %all-to-all-done.1.recv_ref = bf16[64,16,128]{2,1,0:T(8,128)(2,1)S(1)} async-done(((bf16[64,16,128]{2,1,0:T(8,128)(2,1)}), bf16[64,16,128]{2,1,0:T(8,128)(2,1)S(1)}, u32[]{:S(2)}, u32[]{:S(2)}) %all-to-all-start.1) | async-done | bytes 262176 | tf_op jit(solution)/shard_map/all_to_all | solution.py:811
  139.1 5.0 all-gather.8.cloned.1.call-done
  144.1 7.5 %shard_map.205 = (f32[128,1024]{1,0:T(8,128)}, f32[128,1024]{1,0:T(8,128)}, f32[128,2048]{1,0:T(8,128)}, bf16[128,4608]{1,0:T(8,128)(2,1)}, bf16[128,1024]{1,0:T(8,128)(2,1)}) custom-call(s32[2]{0:T(128)} %pad_add_fusion.place_ref, bf16[128,1024]{1,0:T(8,128)(2,1)} %get-tuple-element.50.rows_ref, bf16[128,1024]{1,0:T(8,128)(2,1)} %get-tuple-element.51.normed_ref, ...), custom_call_target="tpu_custom_call" | custom-call | flops 8000000000 | bytes 100000 | tf_op jit(solution)/shard_map/pallas_call | solution.py:410
  157.7 5.7 %collective-permute-done.3.mlp_recv_ref = bf16[128,1024]{1,0:T(8,128)(2,1)S(1)} collective-permute-done((bf16[128,1024]{1,0:T(8,128)(2,1)}, bf16[128,1024]{1,0:T(8,128)(2,1)S(1)}, u32[]{:S(2)}, u32[]{:S(2)}) %collective-permute-start.3) | collective-permute-done | bytes 262176 | tf_op jit(solution)/shard_map/ppermute | solution.py:50
  168.3 27.7 %all_to_all.45.recv_ref = bf16[32,144,128]{2,1,0:T(8,128)(2,1)} all-to-all(bf16[32,144,128]{2,1,0:T(8,128)(2,1)} %get-tuple-element.58), channel_id=1, replica_groups=mesh['section'=2,'tensor'=2,'wide'=32] {'wide'}, dimensions={0} | all-to-all | bytes 2359296 | tf_op jit(solution)/shard_map/all_to_all | solution.py:803
  196.0 12.1 %shard_map.207 = (bf16[2,32,16,128]{3,2,1,0:T(8,128)(2,1)}, f32[32,16,128]{2,1,0:T(8,128)}, f32[1024,1]{1,0:T(8,128)}) custom-call(s32[4,8]{1,0:T(4,128)} %and_convert_fusion.flag_ref, bf16[32,144,128]{2,1,0:T(8,128)(2,1)} %all_to_all.45.recv_ref, s32[8,1,512]{2,1,0:T(1,128)} %reshape.195.key_id_ref, s32[4,256,1]{2,1,0:T(8,128)} %reshape.207.query_id_ref), custom_call_target="tpu_custom_call" | custom-call | flops 12000000000 | bytes 100000 | tf_op jit(solution)/shard_map/pallas_call | solution.py:251
  208.1 6.9 %all-to-all-start.3 = ((bf16[64,16,128]{2,1,0:T(8,128)(2,1)}), bf16[64,16,128]{2,1,0:T(8,128)(2,1)S(1)}, u32[]{:S(2)}, u32[]{:S(2)}) async-start(bf16[64,16,128]{2,1,0:T(8,128)(2,1)} %bitcast.115), calls=%async_computation.3 | async-start | bytes 524288 | tf_op jit(solution)/shard_map/all_to_all | solution.py:811
  215.8 10.1 %all-to-all-done.3.recv_ref = bf16[64,16,128]{2,1,0:T(8,128)(2,1)S(1)} async-done(((bf16[64,16,128]{2,1,0:T(8,128)(2,1)}), bf16[64,16,128]{2,1,0:T(8,128)(2,1)S(1)}, u32[]{:S(2)}, u32[]{:S(2)}) %all-to-all-start.3) | async-done | bytes 262176 | tf_op jit(solution)/shard_map/all_to_all | solution.py:811
  226.6 7.3 %shard_map.208 = (f32[128,1024]{1,0:T(8,128)}, f32[128,1024]{1,0:T(8,128)}, f32[128,2048]{1,0:T(8,128)}, bf16[128,4608]{1,0:T(8,128)(2,1)}, bf16[128,1024]{1,0:T(8,128)(2,1)}) custom-call(s32[2]{0:T(128)} %pad_add_fusion.place_ref, bf16[128,1024]{1,0:T(8,128)(2,1)} %get-tuple-element.56.rows_ref, bf16[128,1024]{1,0:T(8,128)(2,1)} %get-tuple-element.57.normed_ref, ...), custom_call_target="tpu_custom_call" | custom-call | flops 8000000000 | bytes 100000 | tf_op jit(solution)/shard_map/pallas_call | solution.py:410
  234.1 6.9 %shard_map.209 = (bf16[128,1024]{1,0:T(8,128)(2,1)}, bf16[144,3072]{1,0:T(8,128)(2,1)}, bf16[128,1024]{1,0:T(8,128)(2,1)}) custom-call(bf16[64,1024]{1,0:T(8,128)(2,1)} %copy-done.27, bf16[64,1024]{1,0:T(8,128)(2,1)} %get-tuple-element.122.other_ref, f32[8,1024]{1,0:T(8,128)} %reshape.199.vec_ref.refs_0_.after_ref, f32[128,2048]{1,0:T(8,128)} %get-tuple-element.62.refs_1_, ...), custom_call_target="tpu_custom_call" | custom-call | flops 8000000000 | bytes 100000 | tf_op jit(solution)/shard_map/pallas_call | solution.py:502
  245.7 6.6 %shard_map.210.pack_ref = bf16[16,128,1024]{2,1,0:T(8,128)(2,1)} custom-call(s32[2]{0:T(128)} %pad_add_fusion.place_ref, bf16[128,4608]{1,0:T(8,128)(2,1)} %get-tuple-element.66.refs_0_.refs_2_, bf16[128,4608]{1,0:T(8,128)(2,1)} %copy-done.2, bf16[128,4608]{1,0:T(8,128)(2,1)} %get-tuple-element.66.refs_0_.refs_2_, bf16[128,4608]{1,0:T(8,128)(2,1)} %copy-done.2, ...), custom_call_target="tpu_custom_call" | custom-call | flops 7000000000 | bytes 100000 | tf_op jit(solution)/shard_map/pallas_call | solution.py:567
  256.7 7.1 %collective-permute-done.6.part_recv_ref = bf16[128,1024]{1,0:T(8,128)(2,1)S(1)} collective-permute-done((bf16[128,1024]{1,0:T(8,128)(2,1)S(1)}, bf16[128,1024]{1,0:T(8,128)(2,1)S(1)}, u32[]{:S(2)}, u32[]{:S(2)}) %collective-permute-start.6) | collective-permute-done | bytes 262176 | tf_op jit(solution)/shard_map/ppermute | solution.py:50
  263.8 5.1 collective-permute-done.4.mlp_recv_ref
  273.7 13.1 %all_to_all.46.grad_ref = bf16[32,16,128]{2,1,0:T(8,128)(2,1)} all-to-all(bf16[32,16,128]{2,1,0:T(8,128)(2,1)} %get-tuple-element.69), channel_id=1, replica_groups=mesh['section'=2,'tensor'=2,'wide'=32] {'wide'}, dimensions={0} | all-to-all | bytes 262144 | tf_op jit(solution)/shard_map/all_to_all | solution.py:803
  286.8 15.2 %shard_map.212 = bf16[32,144,128]{2,1,0:T(8,128)(2,1)} custom-call(s32[4,8]{1,0:T(4,128)} %and_convert_fusion.flag_ref, bf16[32,144,128]{2,1,0:T(8,128)(2,1)} %all_to_all.45.recv_ref, bf16[32,16,128]{2,1,0:T(8,128)(2,1)} %all_to_all.46.grad_ref, f32[32,16,128]{2,1,0:T(8,128)} %get-tuple-element.70.keep_ref, f32[1024,1]{1,0:T(8,128)} %get-tuple-element.71.lse_ref, ...), custom_call_target="tpu_custom_call" | custom-call | flops 16000000000 | bytes 100000 | tf_op jit(solution)/shard_map/pallas_call | solution.py:338
  306.4 19.9 %all-to-all-done.5.recv_ref = bf16[32,144,128]{2,1,0:T(8,128)(2,1)S(1)} async-done(((bf16[32,144,128]{2,1,0:T(8,128)(2,1)}), bf16[32,144,128]{2,1,0:T(8,128)(2,1)S(1)}, u32[]{:S(2)}, u32[]{:S(2)}) %all-to-all-start.5) | async-done | bytes 1179680 | tf_op jit(solution)/shard_map/all_to_all | solution.py:803
  340.8 4.9 collective-permute-done.9.part_recv_ref
  346.4 7.7 %shard_map.216 = (bf16[128,1024]{1,0:T(8,128)(2,1)}, bf16[144,3072]{1,0:T(8,128)(2,1)}, bf16[128,1024]{1,0:T(8,128)(2,1)}, f32[64,1024]{1,0:T(8,128)}) custom-call(f32[128,1024]{1,0:T(8,128)} %get-tuple-element.68.middle_grad_ref, bf16[128,1024]{1,0:T(8,128)(2,1)} %get-tuple-element.72.part_own_ref, bf16[128,1024]{1,0:T(8,128)(2,1)} %copy-done.33, ...), custom_call_target="tpu_custom_call" | custom-call | flops 8000000000 | bytes 100000 | tf_op jit(solution)/shard_map/pallas_call | solution.py:502
  357.7 6.6 %shard_map.217.pack_ref.refs_15_ = bf16[16,240,1024]{2,1,0:T(8,128)(2,1)} custom-call(s32[2]{0:T(128)} %pad_add_fusion.place_ref, bf16[128,4608]{1,0:T(8,128)(2,1)} %get-tuple-element.79.refs_0_.refs_2_, bf16[128,4608]{1,0:T(8,128)(2,1)} %copy-done.13, bf16[128,4608]{1,0:T(8,128)(2,1)} %get-tuple-element.79.refs_0_.refs_2_, ...), custom_call_target="tpu_custom_call", output_to_operand_aliasing={{}: (9, {})} | custom-call | flops 7000000000 | bytes 100000 | tf_op jit(solution)/shard_map/pallas_call | solution.py:567
  375.9 12.3 %all_to_all.47.grad_ref = bf16[32,16,128]{2,1,0:T(8,128)(2,1)} all-to-all(bf16[32,16,128]{2,1,0:T(8,128)(2,1)S(1)} %copy-done.37), channel_id=1, replica_groups=mesh['section'=2,'tensor'=2,'wide'=32] {'wide'}, dimensions={0} | all-to-all | bytes 262144 | tf_op jit(solution)/shard_map/all_to_all | solution.py:803
  388.1 15.2 %shard_map.219 = bf16[32,144,128]{2,1,0:T(8,128)(2,1)} custom-call(s32[4,8]{1,0:T(4,128)} %and_convert_fusion.flag_ref, bf16[32,144,128]{2,1,0:T(8,128)(2,1)} %copy-done.9, bf16[32,16,128]{2,1,0:T(8,128)(2,1)} %all_to_all.47.grad_ref, f32[32,16,128]{2,1,0:T(8,128)} %get-tuple-element.83.keep_ref, f32[1024,1]{1,0:T(8,128)} %get-tuple-element.84.lse_ref, ...), custom_call_target="tpu_custom_call" | custom-call | flops 16000000000 | bytes 100000 | tf_op jit(solution)/shard_map/pallas_call | solution.py:338
  407.6 24.2 %all-to-all-done.7.recv_ref = bf16[32,144,128]{2,1,0:T(8,128)(2,1)S(1)} async-done(((bf16[32,144,128]{2,1,0:T(8,128)(2,1)}), bf16[32,144,128]{2,1,0:T(8,128)(2,1)S(1)}, u32[]{:S(2)}, u32[]{:S(2)}) %all-to-all-start.7) | async-done | bytes 1179680 | tf_op jit(solution)/shard_map/all_to_all | solution.py:803
  446.4 5.4 %all-to-all-start.8 = ((bf16[16,56,1024]{2,1,0:T(8,128)(2,1)}), bf16[16,56,1024]{2,1,0:T(8,128)(2,1)S(1)}, u32[]{:S(2)}, u32[]{:S(2)}) async-start(bf16[16,56,1024]{2,1,0:T(8,128)(2,1)} %shard_map.221), calls=%async_computation.8 | async-start | bytes 3670016 | tf_op jit(solution)/shard_map/all_to_all | solution.py:961
  459.7 6.1 %collective-permute-done.16 = f32[64,1024]{1,0:T(8,128)S(1)} collective-permute-done((f32[64,1024]{1,0:T(8,128)S(1)}, f32[64,1024]{1,0:T(8,128)S(1)}, u32[]{:S(2)}, u32[]{:S(2)}) %collective-permute-start.16) | collective-permute-done | bytes 262176 | tf_op jit(solution)/shard_map/ppermute | solution.py:50
  466.7 19.1 %all-to-all-done.8 = bf16[16,56,1024]{2,1,0:T(8,128)(2,1)S(1)} async-done(((bf16[16,56,1024]{2,1,0:T(8,128)(2,1)}), bf16[16,56,1024]{2,1,0:T(8,128)(2,1)S(1)}, u32[]{:S(2)}, u32[]{:S(2)}) %all-to-all-start.8) | async-done | bytes 1835040 | tf_op jit(solution)/shard_map/all_to_all | solution.py:961
  (258 shorter events, 140.7 us)
Async XLA Ops:
  7.2 62.8 %all-gather.6.cloned.1.call-start = ((), (), s32[]{:S(2)}) async-start(), calls=%async_computation.11 | async-start | bytes 7569408 | tf_op jit(solution)/shard_map/all_gather | solution.py:882
  10.3 5.2 %collective-permute-start.1 = (bf16[64,1024]{1,0:T(8,128)(2,1)S(1)}, bf16[64,1024]{1,0:T(8,128)(2,1)S(1)}, u32[]{:S(2)}, u32[]{:S(2)}) collective-permute-start(bf16[64,1024]{1,0:T(8,128)(2,1)S(1)} %pad_maximum_fusion.5), channel_id=1, source_target_pairs={{0,64},{64,0},{1,65},{65,1},{2,66},{66,2},{3,67},{67,3},{4,68},{68... | collective-permute-start | bytes 393224 | tf_op jit(solution)/shard_map/ppermute | solution.py:50
  16.3 127.8 %all-gather.8.cloned.1.call-start = ((), (), s32[]{:S(2)}) async-start(), calls=%async_computation.14 | async-start | bytes 11894784 | tf_op jit(solution)/shard_map/all_gather | solution.py:882
  17.1 9.6 %collective-permute-start = (bf16[144,1024]{1,0:T(8,128)(2,1)S(1)}, bf16[144,1024]{1,0:T(8,128)(2,1)S(1)}, u32[]{:S(2)}, u32[]{:S(2)}) collective-permute-start(bf16[144,1024]{1,0:T(8,128)(2,1)S(1)} %pad_maximum_fusion.2), channel_id=1, source_target_pairs={{0,32},{32,0},{1,33},{33,1},{2,34},{34,2},{3,35},{35,3},{4,36},{36... | collective-permute-start | bytes 884744 | tf_op jit(solution)/shard_map/ppermute | solution.py:50
  26.6 7.8 %collective-permute-start.2 = (bf16[160,1024]{1,0:T(8,128)(2,1)S(1)}, bf16[160,1024]{1,0:T(8,128)(2,1)S(1)}, u32[]{:S(2)}, u32[]{:S(2)}) collective-permute-start(bf16[160,1024]{1,0:T(8,128)(2,1)S(1)} %slice_dynamic-update-slice_fusion.2), channel_id=1, source_target_pairs={{0,64},{64,0},{1,65},{65,1},{2,66},{66,2},{3,67},{67,3},{4,68},{68... | collective-permute-start | bytes 983048 | tf_op jit(solution)/shard_map/ppermute | solution.py:50
  78.9 27.7 %all-to-all-start = ((bf16[32,144,128]{2,1,0:T(8,128)(2,1)}), bf16[32,144,128]{2,1,0:T(8,128)(2,1)S(1)}, u32[]{:S(2)}, u32[]{:S(2)}) async-start(bf16[32,144,128]{2,1,0:T(8,128)(2,1)} %get-tuple-element.52), calls=%async_computation | async-start | bytes 2359296 | tf_op jit(solution)/shard_map/all_to_all | solution.py:803
  119.6 19.5 %all-to-all-start.1 = ((bf16[64,16,128]{2,1,0:T(8,128)(2,1)}), bf16[64,16,128]{2,1,0:T(8,128)(2,1)S(1)}, u32[]{:S(2)}, u32[]{:S(2)}) async-start(bf16[64,16,128]{2,1,0:T(8,128)(2,1)} %bitcast.114), calls=%async_computation.1 | async-start | bytes 524288 | tf_op jit(solution)/shard_map/all_to_all | solution.py:811
  126.5 99.5 %all-gather.10.cloned.1.call-start = ((), (), s32[]{:S(2)}) async-start(), calls=%async_computation.15 | async-start | bytes 11894784 | tf_op jit(solution)/shard_map/all_gather | solution.py:882
  153.1 10.3 %collective-permute-start.3 = (bf16[128,1024]{1,0:T(8,128)(2,1)}, bf16[128,1024]{1,0:T(8,128)(2,1)S(1)}, u32[]{:S(2)}, u32[]{:S(2)}) collective-permute-start(bf16[128,1024]{1,0:T(8,128)(2,1)} %get-tuple-element.55.mlp_own_ref), channel_id=1, source_target_pairs={{0,32},{32,0},{1,33},{33,1},{2,34},{34,2},{3,35},{35,3},{4,36},{36... | collective-permute-start | bytes 786440 | tf_op jit(solution)/shard_map/ppermute | solution.py:50
  208.1 17.8 %all-to-all-start.3 = ((bf16[64,16,128]{2,1,0:T(8,128)(2,1)}), bf16[64,16,128]{2,1,0:T(8,128)(2,1)S(1)}, u32[]{:S(2)}, u32[]{:S(2)}) async-start(bf16[64,16,128]{2,1,0:T(8,128)(2,1)} %bitcast.115), calls=%async_computation.3 | async-start | bytes 524288 | tf_op jit(solution)/shard_map/all_to_all | solution.py:811
  215.0 156.2 %reduce-scatter.3.cloned.1.call-start = ((), (), s32[]{:S(2)}) async-start(), calls=%async_computation.12 | async-start | bytes 4456448 | tf_op jit(solution)/shard_map/reduce_scatter | solution.py:939
  233.9 9.8 %collective-permute-start.7 = (bf16[128,4608]{1,0:T(8,128)(2,1)}, bf16[128,4608]{1,0:T(8,128)(2,1)S(1)}, u32[]{:S(2)}, u32[]{:S(2)}) collective-permute-start(bf16[128,4608]{1,0:T(8,128)(2,1)} %get-tuple-element.66.refs_0_.refs_2_), channel_id=1, source_target_pairs={{0,1},{1,0},{2,3},{3,2},{4,5},{5,4},{6,7},{7,6},{8,9},{9,8},{10,11... | collective-permute-start | bytes 3538952 | tf_op jit(solution)/shard_map/ppermute | solution.py:799
  241.0 2.7 collective-permute-start.8
  253.2 10.6 %collective-permute-start.6 = (bf16[128,1024]{1,0:T(8,128)(2,1)S(1)}, bf16[128,1024]{1,0:T(8,128)(2,1)S(1)}, u32[]{:S(2)}, u32[]{:S(2)}) collective-permute-start(bf16[128,1024]{1,0:T(8,128)(2,1)S(1)} %copy-done.29), channel_id=1, source_target_pairs={{0,32},{32,0},{1,33},{33,1},{2,34},{34,2},{3,35},{35,3},{4,36},{36... | collective-permute-start | bytes 786440 | tf_op jit(solution)/shard_map/ppermute | solution.py:50
  254.6 14.3 %collective-permute-start.4 = (bf16[128,1024]{1,0:T(8,128)(2,1)S(1)}, bf16[128,1024]{1,0:T(8,128)(2,1)S(1)}, u32[]{:S(2)}, u32[]{:S(2)}) collective-permute-start(bf16[128,1024]{1,0:T(8,128)(2,1)S(1)} %copy-done.24), channel_id=1, source_target_pairs={{0,32},{32,0},{1,33},{33,1},{2,34},{34,2},{3,35},{35,3},{4,36},{36... | collective-permute-start | bytes 786440 | tf_op jit(solution)/shard_map/ppermute | solution.py:50
  302.0 24.3 %all-to-all-start.5 = ((bf16[32,144,128]{2,1,0:T(8,128)(2,1)}), bf16[32,144,128]{2,1,0:T(8,128)(2,1)S(1)}, u32[]{:S(2)}, u32[]{:S(2)}) async-start(bf16[32,144,128]{2,1,0:T(8,128)(2,1)} %shard_map.212), calls=%async_computation.5 | async-start | bytes 2359296 | tf_op jit(solution)/shard_map/all_to_all | solution.py:803
  306.1 181.5 %reduce-scatter.5.cloned.1.call-start = ((), (), s32[]{:S(2)}) async-start(), calls=%async_computation.13 | async-start | bytes 8355840 | tf_op jit(solution)/shard_map/reduce_scatter | solution.py:939
  306.1 26.2 %collective-permute-start.11 = (bf16[144,1024]{1,0:T(8,128)(2,1)S(1)}, bf16[144,1024]{1,0:T(8,128)(2,1)S(1)}, u32[]{:S(2)}, u32[]{:S(2)}) collective-permute-start(bf16[144,1024]{1,0:T(8,128)(2,1)S(1)} %copy-done.14), channel_id=1, source_target_pairs={{0,1},{1,0},{2,3},{3,2},{4,5},{5,4},{6,7},{7,6},{8,9},{9,8},{10,11... | collective-permute-start | bytes 884744 | tf_op jit(solution)/shard_map/ppermute | solution.py:799
  331.8 4.3 collective-permute-start.10
  332.2 22.7 %collective-permute-start.13 = (bf16[128,4608]{1,0:T(8,128)(2,1)S(1)}, bf16[128,4608]{1,0:T(8,128)(2,1)S(1)}, u32[]{:S(2)}, u32[]{:S(2)}) collective-permute-start(bf16[128,4608]{1,0:T(8,128)(2,1)S(1)} %copy-done.12), channel_id=1, source_target_pairs={{0,1},{1,0},{2,3},{3,2},{4,5},{5,4},{6,7},{7,6},{8,9},{9,8},{10,11... | collective-permute-start | bytes 3538952 | tf_op jit(solution)/shard_map/ppermute | solution.py:799
  335.6 10.2 %collective-permute-start.9 = (bf16[128,1024]{1,0:T(8,128)(2,1)S(1)}, bf16[128,1024]{1,0:T(8,128)(2,1)S(1)}, u32[]{:S(2)}, u32[]{:S(2)}) collective-permute-start(bf16[128,1024]{1,0:T(8,128)(2,1)S(1)} %copy-done.30), channel_id=1, source_target_pairs={{0,32},{32,0},{1,33},{33,1},{2,34},{34,2},{3,35},{35,3},{4,36},{36... | collective-permute-start | bytes 786440 | tf_op jit(solution)/shard_map/ppermute | solution.py:50
  354.2 10.6 %collective-permute-start.12 = (bf16[128,1024]{1,0:T(8,128)(2,1)}, bf16[128,1024]{1,0:T(8,128)(2,1)S(1)}, u32[]{:S(2)}, u32[]{:S(2)}) collective-permute-start(bf16[128,1024]{1,0:T(8,128)(2,1)} %get-tuple-element.77.part_own_ref), channel_id=1, source_target_pairs={{0,32},{32,0},{1,33},{33,1},{2,34},{34,2},{3,35},{35,3},{4,36},{36... | collective-permute-start | bytes 786440 | tf_op jit(solution)/shard_map/ppermute | solution.py:50
  403.3 28.5 %all-to-all-start.7 = ((bf16[32,144,128]{2,1,0:T(8,128)(2,1)}), bf16[32,144,128]{2,1,0:T(8,128)(2,1)S(1)}, u32[]{:S(2)}, u32[]{:S(2)}) async-start(bf16[32,144,128]{2,1,0:T(8,128)(2,1)} %shard_map.219), calls=%async_computation.7 | async-start | bytes 2359296 | tf_op jit(solution)/shard_map/all_to_all | solution.py:803
  437.5 3.9 collective-permute-start.17
  439.8 15.7 %collective-permute-start.15 = (bf16[128,1024]{1,0:T(8,128)(2,1)}, bf16[128,1024]{1,0:T(8,128)(2,1)}, u32[]{:S(2)}, u32[]{:S(2)}) collective-permute-start(bf16[128,1024]{1,0:T(8,128)(2,1)} %get-tuple-element.85), channel_id=1, source_target_pairs={{0,32},{32,0},{1,33},{33,1},{2,34},{34,2},{3,35},{35,3},{4,36},{36... | collective-permute-start | bytes 786440 | tf_op jit(solution)/shard_map/ppermute | solution.py:50
  446.4 39.4 %all-to-all-start.8 = ((bf16[16,56,1024]{2,1,0:T(8,128)(2,1)}), bf16[16,56,1024]{2,1,0:T(8,128)(2,1)S(1)}, u32[]{:S(2)}, u32[]{:S(2)}) async-start(bf16[16,56,1024]{2,1,0:T(8,128)(2,1)} %shard_map.221), calls=%async_computation.8 | async-start | bytes 3670016 | tf_op jit(solution)/shard_map/all_to_all | solution.py:961
  452.8 6.2 %collective-permute-start.5 = (bf16[64,1024]{1,0:T(8,128)(2,1)S(1)}, bf16[64,1024]{1,0:T(8,128)(2,1)S(1)}, u32[]{:S(2)}, u32[]{:S(2)}) collective-permute-start(bf16[64,1024]{1,0:T(8,128)(2,1)S(1)} %get-tuple-element.103), channel_id=1, source_target_pairs={{0,64},{64,0},{1,65},{65,1},{2,66},{66,2},{3,67},{67,3},{4,68},{68... | collective-permute-start | bytes 393224 | tf_op jit(solution)/shard_map/ppermute | solution.py:50
  458.0 7.8 %collective-permute-start.16 = (f32[64,1024]{1,0:T(8,128)S(1)}, f32[64,1024]{1,0:T(8,128)S(1)}, u32[]{:S(2)}, u32[]{:S(2)}) collective-permute-start(f32[64,1024]{1,0:T(8,128)S(1)} %get-tuple-element.99), channel_id=1, source_target_pairs={{0,64},{64,0},{1,65},{65,1},{2,66},{66,2},{3,67},{67,3},{4,68},{68... | collective-permute-start | bytes 786440 | tf_op jit(solution)/shard_map/ppermute | solution.py:50
  490.0 6.4 %collective-permute-start.19 = (bf16[64,1024]{1,0:T(8,128)(2,1)S(1)}, bf16[64,1024]{1,0:T(8,128)(2,1)S(1)}, u32[]{:S(2)}, u32[]{:S(2)}) collective-permute-start(bf16[64,1024]{1,0:T(8,128)(2,1)S(1)} %broadcast_select_fusion.3), channel_id=1, source_target_pairs={{0,64},{64,0},{1,65},{65,1},{2,66},{66,2},{3,67},{67,3},{4,68},{68... | collective-permute-start | bytes 393224 | tf_op jit(solution)/shard_map/ppermute | solution.py:50
  492.9 12.6 %collective-permute-start.20 = (bf16[144,1024]{1,0:T(8,128)(2,1)S(1)}, bf16[144,1024]{1,0:T(8,128)(2,1)S(1)}, u32[]{:S(2)}, u32[]{:S(2)}) collective-permute-start(bf16[144,1024]{1,0:T(8,128)(2,1)S(1)} %broadcast_select_fusion.2), channel_id=1, source_target_pairs={{0,64},{64,0},{1,65},{65,1},{2,66},{66,2},{3,67},{67,3},{4,68},{68... | collective-permute-start | bytes 884744 | tf_op jit(solution)/shard_map/ppermute | solution.py:50
  494.1 4.8 collective-permute-start.22
  496.6 6.5 %collective-permute-start.21 = (bf16[2,1024]{1,0:T(2,128)(2,1)S(1)}, bf16[2,1024]{1,0:T(2,128)(2,1)S(1)}, u32[]{:S(2)}, u32[]{:S(2)}) collective-permute-start(bf16[2,1024]{1,0:T(2,128)(2,1)S(1)} %slice.317), channel_id=1, source_target_pairs={{0,32},{32,0},{1,33},{33,1},{2,34},{34,2},{3,35},{35,3},{4,36},{36... | collective-permute-start | bytes 12296 | tf_op jit(solution)/shard_map/ppermute | solution.py:50
  (44 other events, 396.9 us)
Sparse Core Ops, SparseCore 0:
  16.4 53.5 all-gather.5
  72.3 71.7 all-gather.7
  153.2 63.8 all-gather.9
  252.4 80.0 reduce-scatter.2
  375.1 112.4 reduce-scatter.4

commit v6 on v5

--- a/solution.py
+++ b/solution.py
@@ -560,8 +560,8 @@
             store_mine(place_ref, grad_one, grad_ref, EVERY, rows, EVERY)
 
 
-def mlp_weight_call(place, kept, back, pack=None):
-    rows, extra, aliases = 128, [], {}
+def mlp_weight_call(place, kept, back, part_recv, pack=None):
+    rows, extra, aliases = 128, [part_recv], {}
     if pack is not None:
         rows, extra, aliases = PACK_ROWS, [pack], {9: 0}
     return pl.pallas_call(
@@ -582,8 +582,8 @@
 
 
 def out_back_kernel(
-    grad_ref, part_own_ref, part_recv_ref, middle_ref, branch_ref, mlp_own_ref, mlp_recv_ref, vec_ref,
-    weight_ref, pack_ref, middle_grad_ref, send_ref, low_ref, sums_ref,
+    grad_ref, part_own_ref, part_recv_ref, middle_ref, branch_ref, vec_ref, weight_ref, pack_ref,
+     middle_grad_ref, send_ref, low_ref, sums_ref,
 ):
     hat, rstd = norm_parts(middle_ref[...])
     grad_norm = joined(part_own_ref, part_recv_ref)
@@ -600,16 +600,14 @@
     sums_ref[1:2, :] = column_sum(grad_norm)
     sums_ref[2:3, :] = column_sum(scaled)
     sums_ref[3:4, :] = column_sum(total * branch_ref[...])
-    branch = joined(mlp_own_ref, mlp_recv_ref) + row_of(vec_ref, SHIFT_M)
-    sums_ref[4:5, :] = column_sum(grad_ref[...].astype(F32) * branch)
     low_ref[BOTH:TALL, :] = sums_ref[...].astype(BF)
 
 
-def out_back_call(grad, part_own, part_recv, middle, branch, mlp, mlp_recv, small, weights, pack):
+def out_back_call(grad, part_own, part_recv, middle, branch, small, weights, pack):
     return pl.pallas_call(
         out_back_kernel,
         grid=(1,),
-        in_specs=[whole((BOTH, MODEL))] * 7
+        in_specs=[whole((BOTH, MODEL))] * 5
         + [whole((8, MODEL)), pl.BlockSpec((WIDE, 16, MODEL), lambda i: (0, 8, 0)), ANYWHERE],
         out_specs=[whole((BOTH, MODEL)), whole((WIDE, 16, 128)), whole((TALL, MODEL))],
         out_shape=[
@@ -620,7 +618,7 @@
         scratch_shapes=[pltpu.VMEM((16, MODEL), F32)],
         compiler_params=params(),
         cost_estimate=cost(4),
-    )(grad, part_own, part_recv, middle, branch, mlp, mlp_recv, small[0], weights, pack)
+    )(grad, part_own, part_recv, middle, branch, small[0], weights, pack)
 
 
 def store_out_grads(place_ref, refs, grad_ref, rows):
@@ -677,7 +675,10 @@
     )(place, *kept, *low, *flat, before, pack)
 
 
-def qkv_back_kernel(recv_ref, rows_ref, vec_ref, weight_ref, part_ref, grads_ref, sums_ref):
+def qkv_back_kernel(
+    recv_ref, rows_ref, grad_ref, mlp_own_ref, mlp_recv_ref, vec_ref, weight_ref,
+    part_ref, grads_ref, sums_ref,
+):
     grad_q = unpack_heads(recv_ref, BOTH).astype(BF)
     mask = low_lanes((BOTH, 128))
     key_columns, value_columns = [], []
@@ -707,17 +708,22 @@
     sums_ref[1:2, :] = column_sum(result)
     sums_ref[2:3, 0:HALF_W] = column_sum(grad_q.astype(F32))
     sums_ref[2:3, HALF_W:MODEL] = column_sum(grad_v.astype(F32))
+    branch = joined(mlp_own_ref, mlp_recv_ref) + row_of(vec_ref, SHIFT_M)
+    sums_ref[3:4, :] = column_sum(grad_ref[...].astype(F32) * branch)
     grads_ref[BOTH:TALL, 0:MODEL] = sums_ref[...].astype(BF)
     grads_ref[BOTH:TALL, MODEL : MODEL + HALF_W] = jnp.zeros((16, HALF_W), BF)
 
 
-def qkv_back_call(recv, rows, small, weight, block_at):
+def qkv_back_call(recv, rows, grad, mlp, mlp_recv, small, weight, block_at):
     return pl.pallas_call(
         qkv_back_kernel,
         grid=(1,),
         in_specs=[
             whole((WIDE, SEND_ROWS, 128)),
             whole((BOTH, MODEL)),
+            whole((BOTH, MODEL)),
+            whole((BOTH, MODEL)),
+            whole((BOTH, MODEL)),
             whole((8, MODEL)),
             qkv_block(block_at),
         ],
@@ -729,7 +735,7 @@
         scratch_shapes=[pltpu.VMEM((16, MODEL), F32)],
         compiler_params=params(),
         cost_estimate=cost(5),
-    )(recv, rows, small[0], weight)
+    )(recv, rows, grad, mlp, mlp_recv, small[0], weight)
 
 
 def store_qkv_grads(place_ref, refs, grad_ref):
@@ -825,15 +831,17 @@
         inputs, small, kept["pre"], rest
     )
     mlp_pair = with_core(mlp_back)
-    pack = mlp_weight_call(place, kept["for_weights"], mlp_pair, pack)
+    part_recv = swap(part, "tensor")
+    pack = mlp_weight_call(place, kept["for_weights"], mlp_pair, part_recv, pack)
     middle_grad, mix_grad, low_a = out_back_call(
-        grad, part, swap(part, "tensor"), kept["middle"], kept["branch"], kept["mlp"],
-        kept["mlp_recv"], small, rest, pack,
+        grad, part, part_recv, kept["middle"], kept["branch"], small, rest, pack
     )
     back = attend_back_call(
         flags, kept["recv"], all_to_all(mix_grad), kept["keep"], kept["lse"], key_ids, query_ids
     )
-    qkv_part, qkv_grads = qkv_back_call(all_to_all(back), kept["rows"], small, *qkv)
+    qkv_part, qkv_grads = qkv_back_call(
+        all_to_all(back), kept["rows"], grad, kept["mlp"], kept["mlp_recv"], small, *qkv
+    )
     carried = (middle_grad, qkv_part, swap(qkv_part, "tensor"), kept["rows"])
     for_weights = mlp_pair, with_core(low_a), with_core(qkv_grads)
     return carried, pack, for_weights, input_grad
@@ -989,7 +997,7 @@
         swap(late_own[48:50], "tensor").astype(F32) + across.astype(F32)
     )
     mlp_total, out_total, qkv_total = mid_total[0:128], mid_total[128:144], late_total[0:48]
-    norms = lanes(jnp.concatenate([heads_total, late_total[52:53], late_total[56:61]], axis=0), 32)
+    norms = lanes(jnp.concatenate([heads_total, late_total[52:53], late_total[56:60], late_total[51:52]], axis=0), 32)
     g_gains = jnp.stack([norms[0], norms[3]])
     g_shifts = jnp.stack([norms[1], norms[5], norms[4], norms[2]])
     g_scales = jnp.stack([norms[6], norms[7]])

time: 523 us -> 512 us (0.979)
  waiting for transfers between devices: 202 us -> 191 us
    all_to_all x3, waiting for transfers between devices: 62.7 us -> 52.8 us  [all_to_all(): return lax.all_to_all(block, 'wide', 0, 0, tiled=True)]
    unnamed x89 -> x87, local copies, waits for them, and re-layouts: 14.5 us -> 12.9 us
  transfers between devices with their start and end apart: 34 -> 34, of which waited for: 25 -> 21; matrix products, arithmetic and copies ran while one was open for 5% -> 5% of each run, Pallas kernels for 22% -> 22%
where the time goes in v6:
time: 512 us; the launch traced here: 503 us
  waiting for transfers between devices  191 us (37%)
  Pallas kernels  136 us (27%)
  starting transfers between devices  58.9 us (12%)
  blocking collectives  53.1 us (10%)
  local copies, waits for them, and re-layouts  33 us (6%)
  other arithmetic  16 us (3%)
  between operations  14.9 us (3%)
    ppermute x14, waiting for transfers between devices, swap(): return lax.ppermute(block, axis, [(0, 1), (1, 0)])  53.6 us
    all_to_all x3, blocking collectives, all_to_all(): return lax.all_to_all(block, 'wide', 0, 0, tiled=True)  53.1 us
    all_to_all x3, waiting for transfers between devices, all_to_all(): return lax.all_to_all(block, 'wide', 0, 0, tiled=True)  52.8 us
    all_gather x3, waiting for transfers between devices, gather(): return lax.all_gather(block, 'wide', axis=0, tiled=False)  40.5 us
    pallas_call x2, Pallas kernels, attend_back_call(): pl.pallas_call(attend_back_kernel, grid_spec=pltpu.PrefetchScalarGridSpec...  30.4 us
    pallas_call x2, Pallas kernels, attend_call(): pl.pallas_call(attend_kernel, grid_spec=pltpu.PrefetchScalarGridSpec(num_...  24.1 us
    ppermute x14, starting transfers between devices, swap(): return lax.ppermute(block, axis, [(0, 1), (1, 0)])  22.6 us
    all_to_all x2, waiting for transfers between devices, layer_forward(): lax.all_to_all(mix_sent.reshape(2 * WIDE, 16, 128), ('tensor', 'wide'), 0...  21.4 us
  transfers between devices with their start and end apart: 34, of which 21 were waited for; matrix products, arithmetic and copies ran while one was open for 5% of the time, Pallas kernels for 22%

profile of v6, /device:TPU:0, one launch (start us, length us, event | category | flops | bytes accessed | tf_op | source)
XLA Modules:
  0.0 502.8 jit_solution(629220557156183717)
XLA Ops:
  20.6 6.1 %collective-permute-done = bf16[144,1024]{1,0:T(8,128)(2,1)S(1)} collective-permute-done((bf16[144,1024]{1,0:T(8,128)(2,1)S(1)}, bf16[144,1024]{1,0:T(8,128)(2,1)S(1)}, u32[]{:S(2)}, u32[]{:S(2)}) %collective-permute-start) | collective-permute-done | bytes 294944 | tf_op jit(solution)/shard_map/ppermute | solution.py:50
  28.3 6.1 %collective-permute-done.2 = bf16[160,1024]{1,0:T(8,128)(2,1)S(1)} collective-permute-done((bf16[160,1024]{1,0:T(8,128)(2,1)S(1)}, bf16[160,1024]{1,0:T(8,128)(2,1)S(1)}, u32[]{:S(2)}, u32[]{:S(2)}) %collective-permute-start.2) | collective-permute-done | bytes 327712 | tf_op jit(solution)/shard_map/ppermute | solution.py:50
  34.5 35.5 %all-gather.6.cloned.1.call-done.weight_ref = bf16[32,112,1024]{2,1,0:T(8,128)(2,1)} async-done(((bf16[1,112,1024]{2,1,0:T(8,128)(2,1)}), bf16[32,112,1024]{2,1,0:T(8,128)(2,1)}) %all-gather.6.cloned.1.call-update) | async-done | bytes 7340048 | tf_op jit(solution)/shard_map/all_gather | solution.py:890
  78.9 5.2 %all-to-all-start = ((bf16[32,144,128]{2,1,0:T(8,128)(2,1)}), bf16[32,144,128]{2,1,0:T(8,128)(2,1)S(1)}, u32[]{:S(2)}, u32[]{:S(2)}) async-start(bf16[32,144,128]{2,1,0:T(8,128)(2,1)} %get-tuple-element.52), calls=%async_computation | async-start | bytes 2359296 | tf_op jit(solution)/shard_map/all_to_all | solution.py:809
  88.0 18.6 %all-to-all-done.recv_ref = bf16[32,144,128]{2,1,0:T(8,128)(2,1)S(1)} async-done(((bf16[32,144,128]{2,1,0:T(8,128)(2,1)}), bf16[32,144,128]{2,1,0:T(8,128)(2,1)S(1)}, u32[]{:S(2)}, u32[]{:S(2)}) %all-to-all-start) | async-done | bytes 1179680 | tf_op jit(solution)/shard_map/all_to_all | solution.py:809
  107.6 12.0 %shard_map.204 = (bf16[2,32,16,128]{3,2,1,0:T(8,128)(2,1)}, f32[32,16,128]{2,1,0:T(8,128)}, f32[1024,1]{1,0:T(8,128)}) custom-call(s32[4,8]{1,0:T(4,128)} %and_convert_fusion.flag_ref, bf16[32,144,128]{2,1,0:T(8,128)(2,1)} %copy-done.9, s32[8,1,512]{2,1,0:T(1,128)} %reshape.195.key_id_ref, s32[4,256,1]{2,1,0:T(8,128)} %reshape.207.query_id_ref), custom_call_target="tpu_custom_call" | custom-call | flops 12000000000 | bytes 100000 | tf_op jit(solution)/shard_map/pallas_call | solution.py:251
  119.6 6.9 %all-to-all-start.1 = ((bf16[64,16,128]{2,1,0:T(8,128)(2,1)}), bf16[64,16,128]{2,1,0:T(8,128)(2,1)S(1)}, u32[]{:S(2)}, u32[]{:S(2)}) async-start(bf16[64,16,128]{2,1,0:T(8,128)(2,1)} %bitcast.114), calls=%async_computation.1 | async-start | bytes 524288 | tf_op jit(solution)/shard_map/all_to_all | solution.py:817
  127.9 11.3 %all-to-all-done.1.recv_ref = bf16[64,16,128]{2,1,0:T(8,128)(2,1)S(1)} async-done(((bf16[64,16,128]{2,1,0:T(8,128)(2,1)}), bf16[64,16,128]{2,1,0:T(8,128)(2,1)S(1)}, u32[]{:S(2)}, u32[]{:S(2)}) %all-to-all-start.1) | async-done | bytes 262176 | tf_op jit(solution)/shard_map/all_to_all | solution.py:817
  139.1 5.0 all-gather.8.cloned.1.call-done
  144.1 7.3 %shard_map.205 = (f32[128,1024]{1,0:T(8,128)}, f32[128,1024]{1,0:T(8,128)}, f32[128,2048]{1,0:T(8,128)}, bf16[128,4608]{1,0:T(8,128)(2,1)}, bf16[128,1024]{1,0:T(8,128)(2,1)}) custom-call(s32[2]{0:T(128)} %pad_add_fusion.place_ref, bf16[128,1024]{1,0:T(8,128)(2,1)} %get-tuple-element.50.rows_ref, bf16[128,1024]{1,0:T(8,128)(2,1)} %get-tuple-element.51.normed_ref, ...), custom_call_target="tpu_custom_call" | custom-call | flops 8000000000 | bytes 100000 | tf_op jit(solution)/shard_map/pallas_call | solution.py:410
  157.5 5.7 %collective-permute-done.3.mlp_recv_ref = bf16[128,1024]{1,0:T(8,128)(2,1)S(1)} collective-permute-done((bf16[128,1024]{1,0:T(8,128)(2,1)}, bf16[128,1024]{1,0:T(8,128)(2,1)S(1)}, u32[]{:S(2)}, u32[]{:S(2)}) %collective-permute-start.3) | collective-permute-done | bytes 262176 | tf_op jit(solution)/shard_map/ppermute | solution.py:50
  168.2 27.6 %all_to_all.45.recv_ref = bf16[32,144,128]{2,1,0:T(8,128)(2,1)} all-to-all(bf16[32,144,128]{2,1,0:T(8,128)(2,1)} %get-tuple-element.58), channel_id=1, replica_groups=mesh['section'=2,'tensor'=2,'wide'=32] {'wide'}, dimensions={0} | all-to-all | bytes 2359296 | tf_op jit(solution)/shard_map/all_to_all | solution.py:809
  195.8 12.1 %shard_map.207 = (bf16[2,32,16,128]{3,2,1,0:T(8,128)(2,1)}, f32[32,16,128]{2,1,0:T(8,128)}, f32[1024,1]{1,0:T(8,128)}) custom-call(s32[4,8]{1,0:T(4,128)} %and_convert_fusion.flag_ref, bf16[32,144,128]{2,1,0:T(8,128)(2,1)} %all_to_all.45.recv_ref, s32[8,1,512]{2,1,0:T(1,128)} %reshape.195.key_id_ref, s32[4,256,1]{2,1,0:T(8,128)} %reshape.207.query_id_ref), custom_call_target="tpu_custom_call" | custom-call | flops 12000000000 | bytes 100000 | tf_op jit(solution)/shard_map/pallas_call | solution.py:251
  207.8 7.1 %all-to-all-start.3 = ((bf16[64,16,128]{2,1,0:T(8,128)(2,1)}), bf16[64,16,128]{2,1,0:T(8,128)(2,1)S(1)}, u32[]{:S(2)}, u32[]{:S(2)}) async-start(bf16[64,16,128]{2,1,0:T(8,128)(2,1)} %bitcast.115), calls=%async_computation.3 | async-start | bytes 524288 | tf_op jit(solution)/shard_map/all_to_all | solution.py:817
  215.7 10.1 %all-to-all-done.3.recv_ref = bf16[64,16,128]{2,1,0:T(8,128)(2,1)S(1)} async-done(((bf16[64,16,128]{2,1,0:T(8,128)(2,1)}), bf16[64,16,128]{2,1,0:T(8,128)(2,1)S(1)}, u32[]{:S(2)}, u32[]{:S(2)}) %all-to-all-start.3) | async-done | bytes 262176 | tf_op jit(solution)/shard_map/all_to_all | solution.py:817
  226.5 7.3 %shard_map.208 = (f32[128,1024]{1,0:T(8,128)}, f32[128,1024]{1,0:T(8,128)}, f32[128,2048]{1,0:T(8,128)}, bf16[128,4608]{1,0:T(8,128)(2,1)}, bf16[128,1024]{1,0:T(8,128)(2,1)}) custom-call(s32[2]{0:T(128)} %pad_add_fusion.place_ref, bf16[128,1024]{1,0:T(8,128)(2,1)} %get-tuple-element.56.rows_ref, bf16[128,1024]{1,0:T(8,128)(2,1)} %get-tuple-element.57.normed_ref, ...), custom_call_target="tpu_custom_call" | custom-call | flops 8000000000 | bytes 100000 | tf_op jit(solution)/shard_map/pallas_call | solution.py:410
  234.0 7.0 %shard_map.209 = (bf16[128,1024]{1,0:T(8,128)(2,1)}, bf16[144,3072]{1,0:T(8,128)(2,1)}, bf16[128,1024]{1,0:T(8,128)(2,1)}) custom-call(bf16[64,1024]{1,0:T(8,128)(2,1)} %copy-done.24, bf16[64,1024]{1,0:T(8,128)(2,1)} %get-tuple-element.122.other_ref, f32[8,1024]{1,0:T(8,128)} %reshape.199.vec_ref.refs_0_.after_ref, f32[128,2048]{1,0:T(8,128)} %get-tuple-element.62.refs_1_, ...), custom_call_target="tpu_custom_call" | custom-call | flops 8000000000 | bytes 100000 | tf_op jit(solution)/shard_map/pallas_call | solution.py:502
  242.7 8.6 %collective-permute-done.6.refs_8_.part_recv_ref = bf16[128,1024]{1,0:T(8,128)(2,1)S(1)} collective-permute-done((bf16[128,1024]{1,0:T(8,128)(2,1)}, bf16[128,1024]{1,0:T(8,128)(2,1)S(1)}, u32[]{:S(2)}, u32[]{:S(2)}) %collective-permute-start.6) | collective-permute-done | bytes 262176 | tf_op jit(solution)/shard_map/ppermute | solution.py:50
  253.4 6.6 %shard_map.210.pack_ref = bf16[16,128,1024]{2,1,0:T(8,128)(2,1)} custom-call(s32[2]{0:T(128)} %pad_add_fusion.place_ref, bf16[128,4608]{1,0:T(8,128)(2,1)} %get-tuple-element.66.refs_0_.refs_2_, bf16[128,4608]{1,0:T(8,128)(2,1)} %copy-done.2, bf16[128,4608]{1,0:T(8,128)(2,1)} %get-tuple-element.66.refs_0_.refs_2_, bf16[128,4608]{1,0:T(8,128)(2,1)} %copy-done.2, ...), custom_call_target="tpu_custom_call" | custom-call | flops 7000000000 | bytes 100000 | tf_op jit(solution)/shard_map/pallas_call | solution.py:567
  263.6 13.2 %all_to_all.46.grad_ref = bf16[32,16,128]{2,1,0:T(8,128)(2,1)} all-to-all(bf16[32,16,128]{2,1,0:T(8,128)(2,1)} %get-tuple-element.69), channel_id=1, replica_groups=mesh['section'=2,'tensor'=2,'wide'=32] {'wide'}, dimensions={0} | all-to-all | bytes 262144 | tf_op jit(solution)/shard_map/all_to_all | solution.py:809
  276.8 15.3 %shard_map.212 = bf16[32,144,128]{2,1,0:T(8,128)(2,1)} custom-call(s32[4,8]{1,0:T(4,128)} %and_convert_fusion.flag_ref, bf16[32,144,128]{2,1,0:T(8,128)(2,1)} %all_to_all.45.recv_ref, bf16[32,16,128]{2,1,0:T(8,128)(2,1)} %all_to_all.46.grad_ref, f32[32,16,128]{2,1,0:T(8,128)} %get-tuple-element.70.keep_ref, f32[1024,1]{1,0:T(8,128)} %get-tuple-element.71.lse_ref, ...), custom_call_target="tpu_custom_call" | custom-call | flops 16000000000 | bytes 100000 | tf_op jit(solution)/shard_map/pallas_call | solution.py:338
  297.5 8.7 %collective-permute-done.4.mlp_recv_ref = bf16[128,1024]{1,0:T(8,128)(2,1)S(1)} collective-permute-done((bf16[128,1024]{1,0:T(8,128)(2,1)S(1)}, bf16[128,1024]{1,0:T(8,128)(2,1)S(1)}, u32[]{:S(2)}, u32[]{:S(2)}) %collective-permute-start.4) | collective-permute-done | bytes 262176 | tf_op jit(solution)/shard_map/ppermute | solution.py:50
  306.2 10.2 %all-to-all-done.5.recv_ref = bf16[32,144,128]{2,1,0:T(8,128)(2,1)S(1)} async-done(((bf16[32,144,128]{2,1,0:T(8,128)(2,1)}), bf16[32,144,128]{2,1,0:T(8,128)(2,1)S(1)}, u32[]{:S(2)}, u32[]{:S(2)}) %all-to-all-start.5) | async-done | bytes 1179680 | tf_op jit(solution)/shard_map/all_to_all | solution.py:809
  317.4 4.8 shard_map.213
  337.3 7.8 %shard_map.216 = (bf16[128,1024]{1,0:T(8,128)(2,1)}, bf16[144,3072]{1,0:T(8,128)(2,1)}, bf16[128,1024]{1,0:T(8,128)(2,1)}, f32[64,1024]{1,0:T(8,128)}) custom-call(f32[128,1024]{1,0:T(8,128)} %get-tuple-element.68.middle_grad_ref, bf16[128,1024]{1,0:T(8,128)(2,1)} %get-tuple-element.72.part_own_ref, bf16[128,1024]{1,0:T(8,128)(2,1)} %copy-done.27, ...), custom_call_target="tpu_custom_call" | custom-call | flops 8000000000 | bytes 100000 | tf_op jit(solution)/shard_map/pallas_call | solution.py:502
  348.7 6.6 %shard_map.217.pack_ref.refs_15_ = bf16[16,240,1024]{2,1,0:T(8,128)(2,1)} custom-call(s32[2]{0:T(128)} %pad_add_fusion.place_ref, bf16[128,4608]{1,0:T(8,128)(2,1)} %get-tuple-element.79.refs_0_.refs_2_, bf16[128,4608]{1,0:T(8,128)(2,1)} %copy-done.13, bf16[128,4608]{1,0:T(8,128)(2,1)} %get-tuple-element.79.refs_0_.refs_2_, ...), custom_call_target="tpu_custom_call", output_to_operand_aliasing={{}: (9, {})} | custom-call | flops 7000000000 | bytes 100000 | tf_op jit(solution)/shard_map/pallas_call | solution.py:567
  366.5 12.3 %all_to_all.47.grad_ref = bf16[32,16,128]{2,1,0:T(8,128)(2,1)} all-to-all(bf16[32,16,128]{2,1,0:T(8,128)(2,1)S(1)} %copy-done.33), channel_id=1, replica_groups=mesh['section'=2,'tensor'=2,'wide'=32] {'wide'}, dimensions={0} | all-to-all | bytes 262144 | tf_op jit(solution)/shard_map/all_to_all | solution.py:809
  378.7 15.2 %shard_map.219 = bf16[32,144,128]{2,1,0:T(8,128)(2,1)} custom-call(s32[4,8]{1,0:T(4,128)} %and_convert_fusion.flag_ref, bf16[32,144,128]{2,1,0:T(8,128)(2,1)} %copy-done.9, bf16[32,16,128]{2,1,0:T(8,128)(2,1)} %all_to_all.47.grad_ref, f32[32,16,128]{2,1,0:T(8,128)} %get-tuple-element.83.keep_ref, f32[1024,1]{1,0:T(8,128)} %get-tuple-element.84.lse_ref, ...), custom_call_target="tpu_custom_call" | custom-call | flops 16000000000 | bytes 100000 | tf_op jit(solution)/shard_map/pallas_call | solution.py:338
  398.2 24.0 %all-to-all-done.7.recv_ref = bf16[32,144,128]{2,1,0:T(8,128)(2,1)S(1)} async-done(((bf16[32,144,128]{2,1,0:T(8,128)(2,1)}), bf16[32,144,128]{2,1,0:T(8,128)(2,1)S(1)}, u32[]{:S(2)}, u32[]{:S(2)}) %all-to-all-start.7) | async-done | bytes 1179680 | tf_op jit(solution)/shard_map/all_to_all | solution.py:809
  423.3 4.8 shard_map.220
  448.2 5.6 %collective-permute-done.16 = f32[64,1024]{1,0:T(8,128)S(1)} collective-permute-done((f32[64,1024]{1,0:T(8,128)S(1)}, f32[64,1024]{1,0:T(8,128)S(1)}, u32[]{:S(2)}, u32[]{:S(2)}) %collective-permute-start.16) | collective-permute-done | bytes 262176 | tf_op jit(solution)/shard_map/ppermute | solution.py:50
  454.7 20.0 %all-to-all-done.8 = bf16[16,56,1024]{2,1,0:T(8,128)(2,1)S(1)} async-done(((bf16[16,56,1024]{2,1,0:T(8,128)(2,1)}), bf16[16,56,1024]{2,1,0:T(8,128)(2,1)S(1)}, u32[]{:S(2)}, u32[]{:S(2)}) %all-to-all-start.8) | async-done | bytes 1835040 | tf_op jit(solution)/shard_map/all_to_all | solution.py:969
  (256 shorter events, 133.6 us)
Async XLA Ops:
  7.2 62.8 %all-gather.6.cloned.1.call-start = ((), (), s32[]{:S(2)}) async-start(), calls=%async_computation.11 | async-start | bytes 7569408 | tf_op jit(solution)/shard_map/all_gather | solution.py:890
  10.3 5.2 %collective-permute-start.1 = (bf16[64,1024]{1,0:T(8,128)(2,1)S(1)}, bf16[64,1024]{1,0:T(8,128)(2,1)S(1)}, u32[]{:S(2)}, u32[]{:S(2)}) collective-permute-start(bf16[64,1024]{1,0:T(8,128)(2,1)S(1)} %pad_maximum_fusion.5), channel_id=1, source_target_pairs={{0,64},{64,0},{1,65},{65,1},{2,66},{66,2},{3,67},{67,3},{4,68},{68... | collective-permute-start | bytes 393224 | tf_op jit(solution)/shard_map/ppermute | solution.py:50
  16.3 127.8 %all-gather.8.cloned.1.call-start = ((), (), s32[]{:S(2)}) async-start(), calls=%async_computation.14 | async-start | bytes 11894784 | tf_op jit(solution)/shard_map/all_gather | solution.py:890
  17.1 9.6 %collective-permute-start = (bf16[144,1024]{1,0:T(8,128)(2,1)S(1)}, bf16[144,1024]{1,0:T(8,128)(2,1)S(1)}, u32[]{:S(2)}, u32[]{:S(2)}) collective-permute-start(bf16[144,1024]{1,0:T(8,128)(2,1)S(1)} %pad_maximum_fusion.2), channel_id=1, source_target_pairs={{0,32},{32,0},{1,33},{33,1},{2,34},{34,2},{3,35},{35,3},{4,36},{36... | collective-permute-start | bytes 884744 | tf_op jit(solution)/shard_map/ppermute | solution.py:50
  26.6 7.8 %collective-permute-start.2 = (bf16[160,1024]{1,0:T(8,128)(2,1)S(1)}, bf16[160,1024]{1,0:T(8,128)(2,1)S(1)}, u32[]{:S(2)}, u32[]{:S(2)}) collective-permute-start(bf16[160,1024]{1,0:T(8,128)(2,1)S(1)} %slice_dynamic-update-slice_fusion.2), channel_id=1, source_target_pairs={{0,64},{64,0},{1,65},{65,1},{2,66},{66,2},{3,67},{67,3},{4,68},{68... | collective-permute-start | bytes 983048 | tf_op jit(solution)/shard_map/ppermute | solution.py:50
  78.9 27.7 %all-to-all-start = ((bf16[32,144,128]{2,1,0:T(8,128)(2,1)}), bf16[32,144,128]{2,1,0:T(8,128)(2,1)S(1)}, u32[]{:S(2)}, u32[]{:S(2)}) async-start(bf16[32,144,128]{2,1,0:T(8,128)(2,1)} %get-tuple-element.52), calls=%async_computation | async-start | bytes 2359296 | tf_op jit(solution)/shard_map/all_to_all | solution.py:809
  119.6 19.5 %all-to-all-start.1 = ((bf16[64,16,128]{2,1,0:T(8,128)(2,1)}), bf16[64,16,128]{2,1,0:T(8,128)(2,1)S(1)}, u32[]{:S(2)}, u32[]{:S(2)}) async-start(bf16[64,16,128]{2,1,0:T(8,128)(2,1)} %bitcast.114), calls=%async_computation.1 | async-start | bytes 524288 | tf_op jit(solution)/shard_map/all_to_all | solution.py:817
  126.5 99.3 %all-gather.10.cloned.1.call-start = ((), (), s32[]{:S(2)}) async-start(), calls=%async_computation.15 | async-start | bytes 11894784 | tf_op jit(solution)/shard_map/all_gather | solution.py:890
  152.9 10.3 %collective-permute-start.3 = (bf16[128,1024]{1,0:T(8,128)(2,1)}, bf16[128,1024]{1,0:T(8,128)(2,1)S(1)}, u32[]{:S(2)}, u32[]{:S(2)}) collective-permute-start(bf16[128,1024]{1,0:T(8,128)(2,1)} %get-tuple-element.55.mlp_own_ref), channel_id=1, source_target_pairs={{0,32},{32,0},{1,33},{33,1},{2,34},{34,2},{3,35},{35,3},{4,36},{36... | collective-permute-start | bytes 786440 | tf_op jit(solution)/shard_map/ppermute | solution.py:50
  207.8 18.0 %all-to-all-start.3 = ((bf16[64,16,128]{2,1,0:T(8,128)(2,1)}), bf16[64,16,128]{2,1,0:T(8,128)(2,1)S(1)}, u32[]{:S(2)}, u32[]{:S(2)}) async-start(bf16[64,16,128]{2,1,0:T(8,128)(2,1)} %bitcast.115), calls=%async_computation.3 | async-start | bytes 524288 | tf_op jit(solution)/shard_map/all_to_all | solution.py:817
  214.9 147.0 %reduce-scatter.3.cloned.1.call-start = ((), (), s32[]{:S(2)}) async-start(), calls=%async_computation.12 | async-start | bytes 4456448 | tf_op jit(solution)/shard_map/reduce_scatter | solution.py:947
  233.8 17.6 %collective-permute-start.7 = (bf16[128,4608]{1,0:T(8,128)(2,1)}, bf16[128,4608]{1,0:T(8,128)(2,1)S(1)}, u32[]{:S(2)}, u32[]{:S(2)}) collective-permute-start(bf16[128,4608]{1,0:T(8,128)(2,1)} %get-tuple-element.66.refs_0_.refs_2_), channel_id=1, source_target_pairs={{0,1},{1,0},{2,3},{3,2},{4,5},{5,4},{6,7},{7,6},{8,9},{9,8},{10,11... | collective-permute-start | bytes 3538952 | tf_op jit(solution)/shard_map/ppermute | solution.py:805
  240.9 10.4 %collective-permute-start.8 = (bf16[144,3072]{1,0:T(8,128)(2,1)}, bf16[144,3072]{1,0:T(8,128)(2,1)S(1)}, u32[]{:S(2)}, u32[]{:S(2)}) collective-permute-start(bf16[144,3072]{1,0:T(8,128)(2,1)} %get-tuple-element.67.refs_4_.refs_6_.refs_10_), channel_id=1, source_target_pairs={{0,1},{1,0},{2,3},{3,2},{4,5},{5,4},{6,7},{7,6},{8,9},{9,8},{10,11... | collective-permute-start | bytes 2654216 | tf_op jit(solution)/shard_map/ppermute | solution.py:805
  241.3 10.0 %collective-permute-start.6 = (bf16[128,1024]{1,0:T(8,128)(2,1)}, bf16[128,1024]{1,0:T(8,128)(2,1)S(1)}, u32[]{:S(2)}, u32[]{:S(2)}) collective-permute-start(bf16[128,1024]{1,0:T(8,128)(2,1)} %get-tuple-element.64.part_own_ref), channel_id=1, source_target_pairs={{0,32},{32,0},{1,33},{33,1},{2,34},{34,2},{3,35},{35,3},{4,36},{36... | collective-permute-start | bytes 786440 | tf_op jit(solution)/shard_map/ppermute | solution.py:50
  292.1 24.3 %all-to-all-start.5 = ((bf16[32,144,128]{2,1,0:T(8,128)(2,1)}), bf16[32,144,128]{2,1,0:T(8,128)(2,1)S(1)}, u32[]{:S(2)}, u32[]{:S(2)}) async-start(bf16[32,144,128]{2,1,0:T(8,128)(2,1)} %shard_map.212), calls=%async_computation.5 | async-start | bytes 2359296 | tf_op jit(solution)/shard_map/all_to_all | solution.py:809
  296.2 178.8 %reduce-scatter.5.cloned.1.call-start = ((), (), s32[]{:S(2)}) async-start(), calls=%async_computation.13 | async-start | bytes 8355840 | tf_op jit(solution)/shard_map/reduce_scatter | solution.py:947
  296.2 10.0 %collective-permute-start.4 = (bf16[128,1024]{1,0:T(8,128)(2,1)S(1)}, bf16[128,1024]{1,0:T(8,128)(2,1)S(1)}, u32[]{:S(2)}, u32[]{:S(2)}) collective-permute-start(bf16[128,1024]{1,0:T(8,128)(2,1)S(1)} %copy-done.34), channel_id=1, source_target_pairs={{0,32},{32,0},{1,33},{33,1},{2,34},{34,2},{3,35},{35,3},{4,36},{36... | collective-permute-start | bytes 786440 | tf_op jit(solution)/shard_map/ppermute | solution.py:50
  297.5 25.8 %collective-permute-start.11 = (bf16[144,1024]{1,0:T(8,128)(2,1)S(1)}, bf16[144,1024]{1,0:T(8,128)(2,1)S(1)}, u32[]{:S(2)}, u32[]{:S(2)}) collective-permute-start(bf16[144,1024]{1,0:T(8,128)(2,1)S(1)} %copy-done.14), channel_id=1, source_target_pairs={{0,1},{1,0},{2,3},{3,2},{4,5},{5,4},{6,7},{7,6},{8,9},{9,8},{10,11... | collective-permute-start | bytes 884744 | tf_op jit(solution)/shard_map/ppermute | solution.py:805
  322.2 5.9 %collective-permute-start.10 = (bf16[144,1536]{1,0:T(8,128)(2,1)}, bf16[144,1536]{1,0:T(8,128)(2,1)S(1)}, u32[]{:S(2)}, u32[]{:S(2)}) collective-permute-start(bf16[144,1536]{1,0:T(8,128)(2,1)} %get-tuple-element.73.refs_2_.refs_8_), channel_id=1, source_target_pairs={{0,1},{1,0},{2,3},{3,2},{4,5},{5,4},{6,7},{7,6},{8,9},{9,8},{10,11... | collective-permute-start | bytes 1327112 | tf_op jit(solution)/shard_map/ppermute | solution.py:805
  323.2 23.4 %collective-permute-start.13 = (bf16[128,4608]{1,0:T(8,128)(2,1)S(1)}, bf16[128,4608]{1,0:T(8,128)(2,1)S(1)}, u32[]{:S(2)}, u32[]{:S(2)}) collective-permute-start(bf16[128,4608]{1,0:T(8,128)(2,1)S(1)} %copy-done.12), channel_id=1, source_target_pairs={{0,1},{1,0},{2,3},{3,2},{4,5},{5,4},{6,7},{7,6},{8,9},{9,8},{10,11... | collective-permute-start | bytes 3538952 | tf_op jit(solution)/shard_map/ppermute | solution.py:805
  326.5 10.1 %collective-permute-start.9 = (bf16[128,1024]{1,0:T(8,128)(2,1)S(1)}, bf16[128,1024]{1,0:T(8,128)(2,1)S(1)}, u32[]{:S(2)}, u32[]{:S(2)}) collective-permute-start(bf16[128,1024]{1,0:T(8,128)(2,1)S(1)} %copy-done.25), channel_id=1, source_target_pairs={{0,32},{32,0},{1,33},{33,1},{2,34},{34,2},{3,35},{35,3},{4,36},{36... | collective-permute-start | bytes 786440 | tf_op jit(solution)/shard_map/ppermute | solution.py:50
  345.2 10.6 %collective-permute-start.12 = (bf16[128,1024]{1,0:T(8,128)(2,1)}, bf16[128,1024]{1,0:T(8,128)(2,1)S(1)}, u32[]{:S(2)}, u32[]{:S(2)}) collective-permute-start(bf16[128,1024]{1,0:T(8,128)(2,1)} %get-tuple-element.77.part_own_ref), channel_id=1, source_target_pairs={{0,32},{32,0},{1,33},{33,1},{2,34},{34,2},{3,35},{35,3},{4,36},{36... | collective-permute-start | bytes 786440 | tf_op jit(solution)/shard_map/ppermute | solution.py:50
  393.9 28.3 %all-to-all-start.7 = ((bf16[32,144,128]{2,1,0:T(8,128)(2,1)}), bf16[32,144,128]{2,1,0:T(8,128)(2,1)S(1)}, u32[]{:S(2)}, u32[]{:S(2)}) async-start(bf16[32,144,128]{2,1,0:T(8,128)(2,1)} %shard_map.219), calls=%async_computation.7 | async-start | bytes 2359296 | tf_op jit(solution)/shard_map/all_to_all | solution.py:809
  428.2 3.4 collective-permute-start.17
  430.4 13.0 %collective-permute-start.15 = (bf16[128,1024]{1,0:T(8,128)(2,1)}, bf16[128,1024]{1,0:T(8,128)(2,1)}, u32[]{:S(2)}, u32[]{:S(2)}) collective-permute-start(bf16[128,1024]{1,0:T(8,128)(2,1)} %get-tuple-element.85), channel_id=1, source_target_pairs={{0,32},{32,0},{1,33},{33,1},{2,34},{34,2},{3,35},{35,3},{4,36},{36... | collective-permute-start | bytes 786440 | tf_op jit(solution)/shard_map/ppermute | solution.py:50
  436.4 38.2 %all-to-all-start.8 = ((bf16[16,56,1024]{2,1,0:T(8,128)(2,1)}), bf16[16,56,1024]{2,1,0:T(8,128)(2,1)S(1)}, u32[]{:S(2)}, u32[]{:S(2)}) async-start(bf16[16,56,1024]{2,1,0:T(8,128)(2,1)} %shard_map.221), calls=%async_computation.8 | async-start | bytes 3670016 | tf_op jit(solution)/shard_map/all_to_all | solution.py:969
  442.1 5.4 %collective-permute-start.5 = (bf16[64,1024]{1,0:T(8,128)(2,1)S(1)}, bf16[64,1024]{1,0:T(8,128)(2,1)S(1)}, u32[]{:S(2)}, u32[]{:S(2)}) collective-permute-start(bf16[64,1024]{1,0:T(8,128)(2,1)S(1)} %get-tuple-element.103), channel_id=1, source_target_pairs={{0,64},{64,0},{1,65},{65,1},{2,66},{66,2},{3,67},{67,3},{4,68},{68... | collective-permute-start | bytes 393224 | tf_op jit(solution)/shard_map/ppermute | solution.py:50
  445.8 8.0 %collective-permute-start.16 = (f32[64,1024]{1,0:T(8,128)S(1)}, f32[64,1024]{1,0:T(8,128)S(1)}, u32[]{:S(2)}, u32[]{:S(2)}) collective-permute-start(f32[64,1024]{1,0:T(8,128)S(1)} %get-tuple-element.99), channel_id=1, source_target_pairs={{0,64},{64,0},{1,65},{65,1},{2,66},{66,2},{3,67},{67,3},{4,68},{68... | collective-permute-start | bytes 786440 | tf_op jit(solution)/shard_map/ppermute | solution.py:50
  477.4 6.6 %collective-permute-start.19 = (bf16[64,1024]{1,0:T(8,128)(2,1)S(1)}, bf16[64,1024]{1,0:T(8,128)(2,1)S(1)}, u32[]{:S(2)}, u32[]{:S(2)}) collective-permute-start(bf16[64,1024]{1,0:T(8,128)(2,1)S(1)} %broadcast_select_fusion.3), channel_id=1, source_target_pairs={{0,64},{64,0},{1,65},{65,1},{2,66},{66,2},{3,67},{67,3},{4,68},{68... | collective-permute-start | bytes 393224 | tf_op jit(solution)/shard_map/ppermute | solution.py:50
  480.7 12.9 %collective-permute-start.20 = (bf16[144,1024]{1,0:T(8,128)(2,1)S(1)}, bf16[144,1024]{1,0:T(8,128)(2,1)S(1)}, u32[]{:S(2)}, u32[]{:S(2)}) collective-permute-start(bf16[144,1024]{1,0:T(8,128)(2,1)S(1)} %broadcast_select_fusion.2), channel_id=1, source_target_pairs={{0,64},{64,0},{1,65},{65,1},{2,66},{66,2},{3,67},{67,3},{4,68},{68... | collective-permute-start | bytes 884744 | tf_op jit(solution)/shard_map/ppermute | solution.py:50
  481.5 5.5 %collective-permute-start.22 = (bf16[2,1024]{1,0:T(2,128)(2,1)S(1)}, bf16[2,1024]{1,0:T(2,128)(2,1)S(1)}, u32[]{:S(2)}, u32[]{:S(2)}) collective-permute-start(bf16[2,1024]{1,0:T(2,128)(2,1)S(1)} %slice.322), channel_id=1, source_target_pairs={{0,96},{96,0},{32,64},{64,32},{1,97},{97,1},{33,65},{65,33},{2,98}... | collective-permute-start | bytes 12296 | tf_op jit(solution)/shard_map/ppermute | solution.py:995
  484.2 7.0 %collective-permute-start.21 = (bf16[2,1024]{1,0:T(2,128)(2,1)S(1)}, bf16[2,1024]{1,0:T(2,128)(2,1)S(1)}, u32[]{:S(2)}, u32[]{:S(2)}) collective-permute-start(bf16[2,1024]{1,0:T(2,128)(2,1)S(1)} %slice.321), channel_id=1, source_target_pairs={{0,32},{32,0},{1,33},{33,1},{2,34},{34,2},{3,35},{35,3},{4,36},{36... | collective-permute-start | bytes 12296 | tf_op jit(solution)/shard_map/ppermute | solution.py:50
  (43 other events, 400.3 us)
Sparse Core Ops, SparseCore 0:
  16.4 53.5 all-gather.5
  72.3 71.7 all-gather.7
  153.1 63.8 all-gather.9
  260.2 81.8 reduce-scatter.2
  365.7 108.9 reduce-scatter.4

commit v7 on v6

--- a/solution.py
+++ b/solution.py
@@ -895,9 +895,8 @@
 
     attn_both = gather(jnp.where(is_first, joined_a(pack_a, other_a), joined_a(other_a, pack_a)))
 
-    rest_first = gather(
-        jnp.concatenate([jnp.where(is_first, pack_b, other_b), attn_both[0, 96:112]], axis=0)
-    )
+    first_here = is_first & (attn_both[0, 111, MODEL - 1] == 0)
+    rest_first = gather(jnp.where(first_here, pack_b, other_b))
 
     def rest_second(rows):
         return gather(jnp.concatenate([jnp.where(is_first, other_b, pack_b), rows], axis=0))

time: 512 us -> 512 us (level)
  starting transfers between devices: 58.9 us -> 70 us
  Pallas kernels: 136 us -> 130 us
    ppermute x14, waiting for transfers between devices: 53.6 us -> 48.2 us  [swap(): return lax.ppermute(block, axis, [(0, 1), (1, 0)])]
    unnamed x87 -> x89, local copies, waits for them, and re-layouts: 12.9 us -> 13.2 us
  transfers between devices with their start and end apart: 34 -> 34, of which waited for: 21 -> 20; matrix products, arithmetic and copies ran while one was open for 5% -> 5% of each run, Pallas kernels for 22% -> 21%
where the time goes in v7:
time: 512 us; the launch traced here: 504 us
  waiting for transfers between devices  188 us (37%)
  Pallas kernels  130 us (25%)
  starting transfers between devices  70 us (14%)
  blocking collectives  52.8 us (10%)
  local copies, waits for them, and re-layouts  33.9 us (7%)
  between operations  15.6 us (3%)
  other arithmetic  14.1 us (3%)
    all_to_all x3, blocking collectives, all_to_all(): return lax.all_to_all(block, 'wide', 0, 0, tiled=True)  52.8 us
    all_to_all x3, waiting for transfers between devices, all_to_all(): return lax.all_to_all(block, 'wide', 0, 0, tiled=True)  52.1 us
    ppermute x14, waiting for transfers between devices, swap(): return lax.ppermute(block, axis, [(0, 1), (1, 0)])  48.2 us
    all_gather x3, waiting for transfers between devices, gather(): return lax.all_gather(block, 'wide', axis=0, tiled=False)  44.6 us
    ppermute x14, starting transfers between devices, swap(): return lax.ppermute(block, axis, [(0, 1), (1, 0)])  26.7 us
    pallas_call x2, Pallas kernels, attend_back_call(): pl.pallas_call(attend_back_kernel, grid_spec=pltpu.PrefetchScalarGridSpec...  26.4 us
    all_to_all x2, waiting for transfers between devices, layer_forward(): lax.all_to_all(mix_sent.reshape(2 * WIDE, 16, 128), ('tensor', 'wide'), 0...  21.4 us
    pallas_call x2, Pallas kernels, attend_call(): pl.pallas_call(attend_kernel, grid_spec=pltpu.PrefetchScalarGridSpec(num_...  21.3 us
  transfers between devices with their start and end apart: 34, of which 20 were waited for; matrix products, arithmetic and copies ran while one was open for 5% of the time, Pallas kernels for 21%

profile of v7, /device:TPU:0, one launch (start us, length us, event | category | flops | bytes accessed | tf_op | source)
XLA Modules:
  0.0 503.9 jit_solution(653651402819958497)
XLA Ops:
  20.6 6.1 %collective-permute-done = bf16[144,1024]{1,0:T(8,128)(2,1)S(1)} collective-permute-done((bf16[144,1024]{1,0:T(8,128)(2,1)S(1)}, bf16[144,1024]{1,0:T(8,128)(2,1)S(1)}, u32[]{:S(2)}, u32[]{:S(2)}) %collective-permute-start) | collective-permute-done | bytes 294944 | tf_op jit(solution)/shard_map/ppermute | solution.py:50
  28.3 41.7 %all-gather.6.cloned.1.call-done.weight_ref = bf16[32,112,1024]{2,1,0:T(8,128)(2,1)} async-done(((bf16[1,112,1024]{2,1,0:T(8,128)(2,1)}), bf16[32,112,1024]{2,1,0:T(8,128)(2,1)}) %all-gather.6.cloned.1.call-update) | async-done | bytes 7340048 | tf_op jit(solution)/shard_map/all_gather | solution.py:890
  80.0 5.2 %all-to-all-start = ((bf16[32,144,128]{2,1,0:T(8,128)(2,1)}), bf16[32,144,128]{2,1,0:T(8,128)(2,1)S(1)}, u32[]{:S(2)}, u32[]{:S(2)}) async-start(bf16[32,144,128]{2,1,0:T(8,128)(2,1)} %get-tuple-element.52), calls=%async_computation | async-start | bytes 2359296 | tf_op jit(solution)/shard_map/all_to_all | solution.py:809
  89.1 18.1 %all-to-all-done.recv_ref = bf16[32,144,128]{2,1,0:T(8,128)(2,1)S(1)} async-done(((bf16[32,144,128]{2,1,0:T(8,128)(2,1)}), bf16[32,144,128]{2,1,0:T(8,128)(2,1)S(1)}, u32[]{:S(2)}, u32[]{:S(2)}) %all-to-all-start) | async-done | bytes 1179680 | tf_op jit(solution)/shard_map/all_to_all | solution.py:809
  108.2 10.6 %shard_map.204 = (bf16[2,32,16,128]{3,2,1,0:T(8,128)(2,1)}, f32[32,16,128]{2,1,0:T(8,128)}, f32[1024,1]{1,0:T(8,128)}) custom-call(s32[4,8]{1,0:T(4,128)} %and_convert_fusion.flag_ref, bf16[32,144,128]{2,1,0:T(8,128)(2,1)} %copy-done.9, s32[8,1,512]{2,1,0:T(1,128)} %reshape.197.key_id_ref, s32[4,256,1]{2,1,0:T(8,128)} %reshape.209.query_id_ref), custom_call_target="tpu_custom_call" | custom-call | flops 12000000000 | bytes 100000 | tf_op jit(solution)/shard_map/pallas_call | solution.py:251
  118.8 8.1 %all-to-all-start.1 = ((bf16[64,16,128]{2,1,0:T(8,128)(2,1)}), bf16[64,16,128]{2,1,0:T(8,128)(2,1)S(1)}, u32[]{:S(2)}, u32[]{:S(2)}) async-start(bf16[64,16,128]{2,1,0:T(8,128)(2,1)} %bitcast.113), calls=%async_computation.1 | async-start | bytes 524288 | tf_op jit(solution)/shard_map/all_to_all | solution.py:817
  128.4 11.3 %all-to-all-done.1.recv_ref = bf16[64,16,128]{2,1,0:T(8,128)(2,1)S(1)} async-done(((bf16[64,16,128]{2,1,0:T(8,128)(2,1)}), bf16[64,16,128]{2,1,0:T(8,128)(2,1)S(1)}, u32[]{:S(2)}, u32[]{:S(2)}) %all-to-all-start.1) | async-done | bytes 262176 | tf_op jit(solution)/shard_map/all_to_all | solution.py:817
  142.5 7.4 %shard_map.205 = (f32[128,1024]{1,0:T(8,128)}, f32[128,1024]{1,0:T(8,128)}, f32[128,2048]{1,0:T(8,128)}, bf16[128,4608]{1,0:T(8,128)(2,1)}, bf16[128,1024]{1,0:T(8,128)(2,1)}) custom-call(s32[2]{0:T(128)} %pad_add_fusion.place_ref, bf16[128,1024]{1,0:T(8,128)(2,1)} %get-tuple-element.50.rows_ref, bf16[128,1024]{1,0:T(8,128)(2,1)} %get-tuple-element.51.normed_ref, ...), custom_call_target="tpu_custom_call" | custom-call | flops 8000000000 | bytes 100000 | tf_op jit(solution)/shard_map/pallas_call | solution.py:410
  156.0 5.7 %collective-permute-done.3.mlp_recv_ref = bf16[128,1024]{1,0:T(8,128)(2,1)S(1)} collective-permute-done((bf16[128,1024]{1,0:T(8,128)(2,1)}, bf16[128,1024]{1,0:T(8,128)(2,1)S(1)}, u32[]{:S(2)}, u32[]{:S(2)}) %collective-permute-start.3) | collective-permute-done | bytes 262176 | tf_op jit(solution)/shard_map/ppermute | solution.py:50
  166.7 27.7 %all_to_all.45.recv_ref = bf16[32,144,128]{2,1,0:T(8,128)(2,1)} all-to-all(bf16[32,144,128]{2,1,0:T(8,128)(2,1)} %get-tuple-element.58), channel_id=1, replica_groups=mesh['section'=2,'tensor'=2,'wide'=32] {'wide'}, dimensions={0} | all-to-all | bytes 2359296 | tf_op jit(solution)/shard_map/all_to_all | solution.py:809
  194.4 10.7 %shard_map.207 = (bf16[2,32,16,128]{3,2,1,0:T(8,128)(2,1)}, f32[32,16,128]{2,1,0:T(8,128)}, f32[1024,1]{1,0:T(8,128)}) custom-call(s32[4,8]{1,0:T(4,128)} %and_convert_fusion.flag_ref, bf16[32,144,128]{2,1,0:T(8,128)(2,1)} %all_to_all.45.recv_ref, s32[8,1,512]{2,1,0:T(1,128)} %reshape.197.key_id_ref, s32[4,256,1]{2,1,0:T(8,128)} %reshape.209.query_id_ref), custom_call_target="tpu_custom_call" | custom-call | flops 12000000000 | bytes 100000 | tf_op jit(solution)/shard_map/pallas_call | solution.py:251
  205.1 8.4 %all-to-all-start.3 = ((bf16[64,16,128]{2,1,0:T(8,128)(2,1)}), bf16[64,16,128]{2,1,0:T(8,128)(2,1)S(1)}, u32[]{:S(2)}, u32[]{:S(2)}) async-start(bf16[64,16,128]{2,1,0:T(8,128)(2,1)} %bitcast.114), calls=%async_computation.3 | async-start | bytes 524288 | tf_op jit(solution)/shard_map/all_to_all | solution.py:817
  214.4 10.1 %all-to-all-done.3.recv_ref = bf16[64,16,128]{2,1,0:T(8,128)(2,1)S(1)} async-done(((bf16[64,16,128]{2,1,0:T(8,128)(2,1)}), bf16[64,16,128]{2,1,0:T(8,128)(2,1)S(1)}, u32[]{:S(2)}, u32[]{:S(2)}) %all-to-all-start.3) | async-done | bytes 262176 | tf_op jit(solution)/shard_map/all_to_all | solution.py:817
  225.2 7.3 %shard_map.208 = (f32[128,1024]{1,0:T(8,128)}, f32[128,1024]{1,0:T(8,128)}, f32[128,2048]{1,0:T(8,128)}, bf16[128,4608]{1,0:T(8,128)(2,1)}, bf16[128,1024]{1,0:T(8,128)(2,1)}) custom-call(s32[2]{0:T(128)} %pad_add_fusion.place_ref, bf16[128,1024]{1,0:T(8,128)(2,1)} %get-tuple-element.56.rows_ref, bf16[128,1024]{1,0:T(8,128)(2,1)} %get-tuple-element.57.normed_ref, ...), custom_call_target="tpu_custom_call" | custom-call | flops 8000000000 | bytes 100000 | tf_op jit(solution)/shard_map/pallas_call | solution.py:410
  232.7 7.0 %shard_map.209 = (bf16[128,1024]{1,0:T(8,128)(2,1)}, bf16[144,3072]{1,0:T(8,128)(2,1)}, bf16[128,1024]{1,0:T(8,128)(2,1)}) custom-call(bf16[64,1024]{1,0:T(8,128)(2,1)} %copy-done.24, bf16[64,1024]{1,0:T(8,128)(2,1)} %get-tuple-element.122.other_ref, f32[8,1024]{1,0:T(8,128)} %reshape.201.vec_ref.refs_0_.after_ref, f32[128,2048]{1,0:T(8,128)} %get-tuple-element.62.refs_1_, ...), custom_call_target="tpu_custom_call" | custom-call | flops 8000000000 | bytes 100000 | tf_op jit(solution)/shard_map/pallas_call | solution.py:502
  241.4 8.6 %collective-permute-done.6.refs_8_.part_recv_ref = bf16[128,1024]{1,0:T(8,128)(2,1)S(1)} collective-permute-done((bf16[128,1024]{1,0:T(8,128)(2,1)}, bf16[128,1024]{1,0:T(8,128)(2,1)S(1)}, u32[]{:S(2)}, u32[]{:S(2)}) %collective-permute-start.6) | collective-permute-done | bytes 262176 | tf_op jit(solution)/shard_map/ppermute | solution.py:50
  252.1 6.5 %shard_map.210.pack_ref = bf16[16,128,1024]{2,1,0:T(8,128)(2,1)} custom-call(s32[2]{0:T(128)} %pad_add_fusion.place_ref, bf16[128,4608]{1,0:T(8,128)(2,1)} %get-tuple-element.66.refs_0_.refs_2_, bf16[128,4608]{1,0:T(8,128)(2,1)} %copy-done.2, bf16[128,4608]{1,0:T(8,128)(2,1)} %get-tuple-element.66.refs_0_.refs_2_, bf16[128,4608]{1,0:T(8,128)(2,1)} %copy-done.2, ...), custom_call_target="tpu_custom_call" | custom-call | flops 7000000000 | bytes 100000 | tf_op jit(solution)/shard_map/pallas_call | solution.py:567
  262.3 13.2 %all_to_all.46.grad_ref = bf16[32,16,128]{2,1,0:T(8,128)(2,1)} all-to-all(bf16[32,16,128]{2,1,0:T(8,128)(2,1)} %get-tuple-element.69), channel_id=1, replica_groups=mesh['section'=2,'tensor'=2,'wide'=32] {'wide'}, dimensions={0} | all-to-all | bytes 262144 | tf_op jit(solution)/shard_map/all_to_all | solution.py:809
  275.5 13.2 %shard_map.212 = bf16[32,144,128]{2,1,0:T(8,128)(2,1)} custom-call(s32[4,8]{1,0:T(4,128)} %and_convert_fusion.flag_ref, bf16[32,144,128]{2,1,0:T(8,128)(2,1)} %all_to_all.45.recv_ref, bf16[32,16,128]{2,1,0:T(8,128)(2,1)} %all_to_all.46.grad_ref, f32[32,16,128]{2,1,0:T(8,128)} %get-tuple-element.70.keep_ref, f32[1024,1]{1,0:T(8,128)} %get-tuple-element.71.lse_ref, ...), custom_call_target="tpu_custom_call" | custom-call | flops 16000000000 | bytes 100000 | tf_op jit(solution)/shard_map/pallas_call | solution.py:338
  288.7 6.0 %all-to-all-start.5 = ((bf16[32,144,128]{2,1,0:T(8,128)(2,1)}), bf16[32,144,128]{2,1,0:T(8,128)(2,1)S(1)}, u32[]{:S(2)}, u32[]{:S(2)}) async-start(bf16[32,144,128]{2,1,0:T(8,128)(2,1)} %shard_map.212), calls=%async_computation.5 | async-start | bytes 2359296 | tf_op jit(solution)/shard_map/all_to_all | solution.py:809
  295.6 9.4 %collective-permute-done.4.mlp_recv_ref = bf16[128,1024]{1,0:T(8,128)(2,1)S(1)} collective-permute-done((bf16[128,1024]{1,0:T(8,128)(2,1)S(1)}, bf16[128,1024]{1,0:T(8,128)(2,1)S(1)}, u32[]{:S(2)}, u32[]{:S(2)}) %collective-permute-start.4) | collective-permute-done | bytes 262176 | tf_op jit(solution)/shard_map/ppermute | solution.py:50
  305.0 10.8 %all-to-all-done.5.recv_ref = bf16[32,144,128]{2,1,0:T(8,128)(2,1)S(1)} async-done(((bf16[32,144,128]{2,1,0:T(8,128)(2,1)}), bf16[32,144,128]{2,1,0:T(8,128)(2,1)S(1)}, u32[]{:S(2)}, u32[]{:S(2)}) %all-to-all-start.5) | async-done | bytes 1179680 | tf_op jit(solution)/shard_map/all_to_all | solution.py:809
  316.8 4.8 shard_map.213
  336.0 7.9 %shard_map.216 = (bf16[128,1024]{1,0:T(8,128)(2,1)}, bf16[144,3072]{1,0:T(8,128)(2,1)}, bf16[128,1024]{1,0:T(8,128)(2,1)}, f32[64,1024]{1,0:T(8,128)}) custom-call(f32[128,1024]{1,0:T(8,128)} %get-tuple-element.68.middle_grad_ref, bf16[128,1024]{1,0:T(8,128)(2,1)} %get-tuple-element.72.part_own_ref, bf16[128,1024]{1,0:T(8,128)(2,1)} %copy-done.27, ...), custom_call_target="tpu_custom_call" | custom-call | flops 8000000000 | bytes 100000 | tf_op jit(solution)/shard_map/pallas_call | solution.py:502
  347.8 6.7 %shard_map.217.pack_ref.refs_15_ = bf16[16,240,1024]{2,1,0:T(8,128)(2,1)} custom-call(s32[2]{0:T(128)} %pad_add_fusion.place_ref, bf16[128,4608]{1,0:T(8,128)(2,1)} %get-tuple-element.79.refs_0_.refs_2_, bf16[128,4608]{1,0:T(8,128)(2,1)} %copy-done.13, bf16[128,4608]{1,0:T(8,128)(2,1)} %get-tuple-element.79.refs_0_.refs_2_, ...), custom_call_target="tpu_custom_call", output_to_operand_aliasing={{}: (9, {})} | custom-call | flops 7000000000 | bytes 100000 | tf_op jit(solution)/shard_map/pallas_call | solution.py:567
  365.2 11.8 %all_to_all.47.grad_ref = bf16[32,16,128]{2,1,0:T(8,128)(2,1)} all-to-all(bf16[32,16,128]{2,1,0:T(8,128)(2,1)S(1)} %copy-done.33), channel_id=1, replica_groups=mesh['section'=2,'tensor'=2,'wide'=32] {'wide'}, dimensions={0} | all-to-all | bytes 262144 | tf_op jit(solution)/shard_map/all_to_all | solution.py:809
  377.1 13.2 %shard_map.219 = bf16[32,144,128]{2,1,0:T(8,128)(2,1)} custom-call(s32[4,8]{1,0:T(4,128)} %and_convert_fusion.flag_ref, bf16[32,144,128]{2,1,0:T(8,128)(2,1)} %copy-done.9, bf16[32,16,128]{2,1,0:T(8,128)(2,1)} %all_to_all.47.grad_ref, f32[32,16,128]{2,1,0:T(8,128)} %get-tuple-element.83.keep_ref, f32[1024,1]{1,0:T(8,128)} %get-tuple-element.84.lse_ref, ...), custom_call_target="tpu_custom_call" | custom-call | flops 16000000000 | bytes 100000 | tf_op jit(solution)/shard_map/pallas_call | solution.py:338
  390.3 5.7 %all-to-all-start.7 = ((bf16[32,144,128]{2,1,0:T(8,128)(2,1)}), bf16[32,144,128]{2,1,0:T(8,128)(2,1)S(1)}, u32[]{:S(2)}, u32[]{:S(2)}) async-start(bf16[32,144,128]{2,1,0:T(8,128)(2,1)} %shard_map.219), calls=%async_computation.7 | async-start | bytes 2359296 | tf_op jit(solution)/shard_map/all_to_all | solution.py:809
  396.2 23.2 %all-to-all-done.7.recv_ref = bf16[32,144,128]{2,1,0:T(8,128)(2,1)S(1)} async-done(((bf16[32,144,128]{2,1,0:T(8,128)(2,1)}), bf16[32,144,128]{2,1,0:T(8,128)(2,1)S(1)}, u32[]{:S(2)}, u32[]{:S(2)}) %all-to-all-start.7) | async-done | bytes 1179680 | tf_op jit(solution)/shard_map/all_to_all | solution.py:809
  420.4 5.0 shard_map.220
  435.3 5.4 %all-to-all-start.8 = ((bf16[16,56,1024]{2,1,0:T(8,128)(2,1)}), bf16[16,56,1024]{2,1,0:T(8,128)(2,1)S(1)}, u32[]{:S(2)}, u32[]{:S(2)}) async-start(bf16[16,56,1024]{2,1,0:T(8,128)(2,1)} %shard_map.221), calls=%async_computation.8 | async-start | bytes 3670016 | tf_op jit(solution)/shard_map/all_to_all | solution.py:968
  455.7 18.9 %all-to-all-done.8 = bf16[16,56,1024]{2,1,0:T(8,128)(2,1)S(1)} async-done(((bf16[16,56,1024]{2,1,0:T(8,128)(2,1)}), bf16[16,56,1024]{2,1,0:T(8,128)(2,1)S(1)}, u32[]{:S(2)}, u32[]{:S(2)}) %all-to-all-start.8) | async-done | bytes 1835040 | tf_op jit(solution)/shard_map/all_to_all | solution.py:968
  (257 shorter events, 132.4 us)
Async XLA Ops:
  7.2 62.8 %all-gather.6.cloned.1.call-start = ((), (), s32[]{:S(2)}) async-start(), calls=%async_computation.11 | async-start | bytes 7569408 | tf_op jit(solution)/shard_map/all_gather | solution.py:890
  10.2 5.2 %collective-permute-start.1 = (bf16[64,1024]{1,0:T(8,128)(2,1)S(1)}, bf16[64,1024]{1,0:T(8,128)(2,1)S(1)}, u32[]{:S(2)}, u32[]{:S(2)}) collective-permute-start(bf16[64,1024]{1,0:T(8,128)(2,1)S(1)} %pad_maximum_fusion.4), channel_id=1, source_target_pairs={{0,64},{64,0},{1,65},{65,1},{2,66},{66,2},{3,67},{67,3},{4,68},{68... | collective-permute-start | bytes 393224 | tf_op jit(solution)/shard_map/ppermute | solution.py:50
  16.3 126.2 %all-gather.8.cloned.1.call-start = ((), (), s32[]{:S(2)}) async-start(), calls=%async_computation.14 | async-start | bytes 10813440 | tf_op jit(solution)/shard_map/all_gather | solution.py:890
  17.1 9.6 %collective-permute-start = (bf16[144,1024]{1,0:T(8,128)(2,1)S(1)}, bf16[144,1024]{1,0:T(8,128)(2,1)S(1)}, u32[]{:S(2)}, u32[]{:S(2)}) collective-permute-start(bf16[144,1024]{1,0:T(8,128)(2,1)S(1)} %pad_maximum_fusion.1), channel_id=1, source_target_pairs={{0,32},{32,0},{1,33},{33,1},{2,34},{34,2},{3,35},{35,3},{4,36},{36... | collective-permute-start | bytes 884744 | tf_op jit(solution)/shard_map/ppermute | solution.py:50
  26.6 45.3 %collective-permute-start.2 = (bf16[160,1024]{1,0:T(8,128)(2,1)S(1)}, bf16[160,1024]{1,0:T(8,128)(2,1)S(1)}, u32[]{:S(2)}, u32[]{:S(2)}) collective-permute-start(bf16[160,1024]{1,0:T(8,128)(2,1)S(1)} %slice_dynamic-update-slice_fusion.2), channel_id=1, source_target_pairs={{0,64},{64,0},{1,65},{65,1},{2,66},{66,2},{3,67},{67,3},{4,68},{68... | collective-permute-start | bytes 983048 | tf_op jit(solution)/shard_map/ppermute | solution.py:50
  80.0 27.2 %all-to-all-start = ((bf16[32,144,128]{2,1,0:T(8,128)(2,1)}), bf16[32,144,128]{2,1,0:T(8,128)(2,1)S(1)}, u32[]{:S(2)}, u32[]{:S(2)}) async-start(bf16[32,144,128]{2,1,0:T(8,128)(2,1)} %get-tuple-element.52), calls=%async_computation | async-start | bytes 2359296 | tf_op jit(solution)/shard_map/all_to_all | solution.py:809
  118.8 20.8 %all-to-all-start.1 = ((bf16[64,16,128]{2,1,0:T(8,128)(2,1)}), bf16[64,16,128]{2,1,0:T(8,128)(2,1)S(1)}, u32[]{:S(2)}, u32[]{:S(2)}) async-start(bf16[64,16,128]{2,1,0:T(8,128)(2,1)} %bitcast.113), calls=%async_computation.1 | async-start | bytes 524288 | tf_op jit(solution)/shard_map/all_to_all | solution.py:817
  127.0 97.5 %all-gather.10.cloned.1.call-start = ((), (), s32[]{:S(2)}) async-start(), calls=%async_computation.15 | async-start | bytes 11894784 | tf_op jit(solution)/shard_map/all_gather | solution.py:890
  151.4 10.3 %collective-permute-start.3 = (bf16[128,1024]{1,0:T(8,128)(2,1)}, bf16[128,1024]{1,0:T(8,128)(2,1)S(1)}, u32[]{:S(2)}, u32[]{:S(2)}) collective-permute-start(bf16[128,1024]{1,0:T(8,128)(2,1)} %get-tuple-element.55.mlp_own_ref), channel_id=1, source_target_pairs={{0,32},{32,0},{1,33},{33,1},{2,34},{34,2},{3,35},{35,3},{4,36},{36... | collective-permute-start | bytes 786440 | tf_op jit(solution)/shard_map/ppermute | solution.py:50
  205.1 19.3 %all-to-all-start.3 = ((bf16[64,16,128]{2,1,0:T(8,128)(2,1)}), bf16[64,16,128]{2,1,0:T(8,128)(2,1)S(1)}, u32[]{:S(2)}, u32[]{:S(2)}) async-start(bf16[64,16,128]{2,1,0:T(8,128)(2,1)} %bitcast.114), calls=%async_computation.3 | async-start | bytes 524288 | tf_op jit(solution)/shard_map/all_to_all | solution.py:817
  213.6 147.0 %reduce-scatter.3.cloned.1.call-start = ((), (), s32[]{:S(2)}) async-start(), calls=%async_computation.12 | async-start | bytes 4456448 | tf_op jit(solution)/shard_map/reduce_scatter | solution.py:946
  232.5 17.6 %collective-permute-start.7 = (bf16[128,4608]{1,0:T(8,128)(2,1)}, bf16[128,4608]{1,0:T(8,128)(2,1)S(1)}, u32[]{:S(2)}, u32[]{:S(2)}) collective-permute-start(bf16[128,4608]{1,0:T(8,128)(2,1)} %get-tuple-element.66.refs_0_.refs_2_), channel_id=1, source_target_pairs={{0,1},{1,0},{2,3},{3,2},{4,5},{5,4},{6,7},{7,6},{8,9},{9,8},{10,11... | collective-permute-start | bytes 3538952 | tf_op jit(solution)/shard_map/ppermute | solution.py:805
  239.6 10.4 %collective-permute-start.8 = (bf16[144,3072]{1,0:T(8,128)(2,1)}, bf16[144,3072]{1,0:T(8,128)(2,1)S(1)}, u32[]{:S(2)}, u32[]{:S(2)}) collective-permute-start(bf16[144,3072]{1,0:T(8,128)(2,1)} %get-tuple-element.67.refs_4_.refs_6_.refs_10_), channel_id=1, source_target_pairs={{0,1},{1,0},{2,3},{3,2},{4,5},{5,4},{6,7},{7,6},{8,9},{9,8},{10,11... | collective-permute-start | bytes 2654216 | tf_op jit(solution)/shard_map/ppermute | solution.py:805
  240.1 10.0 %collective-permute-start.6 = (bf16[128,1024]{1,0:T(8,128)(2,1)}, bf16[128,1024]{1,0:T(8,128)(2,1)S(1)}, u32[]{:S(2)}, u32[]{:S(2)}) collective-permute-start(bf16[128,1024]{1,0:T(8,128)(2,1)} %get-tuple-element.64.part_own_ref), channel_id=1, source_target_pairs={{0,32},{32,0},{1,33},{33,1},{2,34},{34,2},{3,35},{35,3},{4,36},{36... | collective-permute-start | bytes 786440 | tf_op jit(solution)/shard_map/ppermute | solution.py:50
  288.7 27.0 %all-to-all-start.5 = ((bf16[32,144,128]{2,1,0:T(8,128)(2,1)}), bf16[32,144,128]{2,1,0:T(8,128)(2,1)S(1)}, u32[]{:S(2)}, u32[]{:S(2)}) async-start(bf16[32,144,128]{2,1,0:T(8,128)(2,1)} %shard_map.212), calls=%async_computation.5 | async-start | bytes 2359296 | tf_op jit(solution)/shard_map/all_to_all | solution.py:809
  294.8 180.5 %reduce-scatter.5.cloned.1.call-start = ((), (), s32[]{:S(2)}) async-start(), calls=%async_computation.13 | async-start | bytes 8355840 | tf_op jit(solution)/shard_map/reduce_scatter | solution.py:946
  294.8 10.2 %collective-permute-start.4 = (bf16[128,1024]{1,0:T(8,128)(2,1)S(1)}, bf16[128,1024]{1,0:T(8,128)(2,1)S(1)}, u32[]{:S(2)}, u32[]{:S(2)}) collective-permute-start(bf16[128,1024]{1,0:T(8,128)(2,1)S(1)} %copy-done.35), channel_id=1, source_target_pairs={{0,32},{32,0},{1,33},{33,1},{2,34},{34,2},{3,35},{35,3},{4,36},{36... | collective-permute-start | bytes 786440 | tf_op jit(solution)/shard_map/ppermute | solution.py:50
  295.6 26.5 %collective-permute-start.11 = (bf16[144,1024]{1,0:T(8,128)(2,1)S(1)}, bf16[144,1024]{1,0:T(8,128)(2,1)S(1)}, u32[]{:S(2)}, u32[]{:S(2)}) collective-permute-start(bf16[144,1024]{1,0:T(8,128)(2,1)S(1)} %copy-done.14), channel_id=1, source_target_pairs={{0,1},{1,0},{2,3},{3,2},{4,5},{5,4},{6,7},{7,6},{8,9},{9,8},{10,11... | collective-permute-start | bytes 884744 | tf_op jit(solution)/shard_map/ppermute | solution.py:805
  321.6 5.5 %collective-permute-start.10 = (bf16[144,1536]{1,0:T(8,128)(2,1)}, bf16[144,1536]{1,0:T(8,128)(2,1)S(1)}, u32[]{:S(2)}, u32[]{:S(2)}) collective-permute-start(bf16[144,1536]{1,0:T(8,128)(2,1)} %get-tuple-element.73.refs_2_.refs_8_), channel_id=1, source_target_pairs={{0,1},{1,0},{2,3},{3,2},{4,5},{5,4},{6,7},{7,6},{8,9},{9,8},{10,11... | collective-permute-start | bytes 1327112 | tf_op jit(solution)/shard_map/ppermute | solution.py:805
  321.6 24.2 %collective-permute-start.13 = (bf16[128,4608]{1,0:T(8,128)(2,1)S(1)}, bf16[128,4608]{1,0:T(8,128)(2,1)S(1)}, u32[]{:S(2)}, u32[]{:S(2)}) collective-permute-start(bf16[128,4608]{1,0:T(8,128)(2,1)S(1)} %copy-done.12), channel_id=1, source_target_pairs={{0,1},{1,0},{2,3},{3,2},{4,5},{5,4},{6,7},{7,6},{8,9},{9,8},{10,11... | collective-permute-start | bytes 3538952 | tf_op jit(solution)/shard_map/ppermute | solution.py:805
  325.4 9.8 %collective-permute-start.9 = (bf16[128,1024]{1,0:T(8,128)(2,1)S(1)}, bf16[128,1024]{1,0:T(8,128)(2,1)S(1)}, u32[]{:S(2)}, u32[]{:S(2)}) collective-permute-start(bf16[128,1024]{1,0:T(8,128)(2,1)S(1)} %copy-done.25), channel_id=1, source_target_pairs={{0,32},{32,0},{1,33},{33,1},{2,34},{34,2},{3,35},{35,3},{4,36},{36... | collective-permute-start | bytes 786440 | tf_op jit(solution)/shard_map/ppermute | solution.py:50
  343.9 10.7 %collective-permute-start.12 = (bf16[128,1024]{1,0:T(8,128)(2,1)}, bf16[128,1024]{1,0:T(8,128)(2,1)S(1)}, u32[]{:S(2)}, u32[]{:S(2)}) collective-permute-start(bf16[128,1024]{1,0:T(8,128)(2,1)} %get-tuple-element.77.part_own_ref), channel_id=1, source_target_pairs={{0,32},{32,0},{1,33},{33,1},{2,34},{34,2},{3,35},{35,3},{4,36},{36... | collective-permute-start | bytes 786440 | tf_op jit(solution)/shard_map/ppermute | solution.py:50
  390.3 29.1 %all-to-all-start.7 = ((bf16[32,144,128]{2,1,0:T(8,128)(2,1)}), bf16[32,144,128]{2,1,0:T(8,128)(2,1)S(1)}, u32[]{:S(2)}, u32[]{:S(2)}) async-start(bf16[32,144,128]{2,1,0:T(8,128)(2,1)} %shard_map.219), calls=%async_computation.7 | async-start | bytes 2359296 | tf_op jit(solution)/shard_map/all_to_all | solution.py:809
  425.4 4.9 collective-permute-start.17
  427.7 18.0 %collective-permute-start.15 = (bf16[128,1024]{1,0:T(8,128)(2,1)}, bf16[128,1024]{1,0:T(8,128)(2,1)S(1)}, u32[]{:S(2)}, u32[]{:S(2)}) collective-permute-start(bf16[128,1024]{1,0:T(8,128)(2,1)} %get-tuple-element.85), channel_id=1, source_target_pairs={{0,32},{32,0},{1,33},{33,1},{2,34},{34,2},{3,35},{35,3},{4,36},{36... | collective-permute-start | bytes 786440 | tf_op jit(solution)/shard_map/ppermute | solution.py:50
  435.3 39.3 %all-to-all-start.8 = ((bf16[16,56,1024]{2,1,0:T(8,128)(2,1)}), bf16[16,56,1024]{2,1,0:T(8,128)(2,1)S(1)}, u32[]{:S(2)}, u32[]{:S(2)}) async-start(bf16[16,56,1024]{2,1,0:T(8,128)(2,1)} %shard_map.221), calls=%async_computation.8 | async-start | bytes 3670016 | tf_op jit(solution)/shard_map/all_to_all | solution.py:968
  441.8 8.2 %collective-permute-start.5 = (bf16[64,1024]{1,0:T(8,128)(2,1)S(1)}, bf16[64,1024]{1,0:T(8,128)(2,1)S(1)}, u32[]{:S(2)}, u32[]{:S(2)}) collective-permute-start(bf16[64,1024]{1,0:T(8,128)(2,1)S(1)} %get-tuple-element.103), channel_id=1, source_target_pairs={{0,64},{64,0},{1,65},{65,1},{2,66},{66,2},{3,67},{67,3},{4,68},{68... | collective-permute-start | bytes 393224 | tf_op jit(solution)/shard_map/ppermute | solution.py:50
  446.1 8.7 %collective-permute-start.16 = (f32[64,1024]{1,0:T(8,128)S(1)}, f32[64,1024]{1,0:T(8,128)S(1)}, u32[]{:S(2)}, u32[]{:S(2)}) collective-permute-start(f32[64,1024]{1,0:T(8,128)S(1)} %get-tuple-element.99), channel_id=1, source_target_pairs={{0,64},{64,0},{1,65},{65,1},{2,66},{66,2},{3,67},{67,3},{4,68},{68... | collective-permute-start | bytes 786440 | tf_op jit(solution)/shard_map/ppermute | solution.py:50
  477.7 7.7 %collective-permute-start.19 = (bf16[64,1024]{1,0:T(8,128)(2,1)S(1)}, bf16[64,1024]{1,0:T(8,128)(2,1)S(1)}, u32[]{:S(2)}, u32[]{:S(2)}) collective-permute-start(bf16[64,1024]{1,0:T(8,128)(2,1)S(1)} %broadcast_select_fusion.3), channel_id=1, source_target_pairs={{0,64},{64,0},{1,65},{65,1},{2,66},{66,2},{3,67},{67,3},{4,68},{68... | collective-permute-start | bytes 393224 | tf_op jit(solution)/shard_map/ppermute | solution.py:50
  482.4 12.3 %collective-permute-start.20 = (bf16[144,1024]{1,0:T(8,128)(2,1)S(1)}, bf16[144,1024]{1,0:T(8,128)(2,1)S(1)}, u32[]{:S(2)}, u32[]{:S(2)}) collective-permute-start(bf16[144,1024]{1,0:T(8,128)(2,1)S(1)} %broadcast_select_fusion.2), channel_id=1, source_target_pairs={{0,64},{64,0},{1,65},{65,1},{2,66},{66,2},{3,67},{67,3},{4,68},{68... | collective-permute-start | bytes 884744 | tf_op jit(solution)/shard_map/ppermute | solution.py:50
  482.5 5.8 %collective-permute-start.22 = (bf16[2,1024]{1,0:T(2,128)(2,1)S(1)}, bf16[2,1024]{1,0:T(2,128)(2,1)S(1)}, u32[]{:S(2)}, u32[]{:S(2)}) collective-permute-start(bf16[2,1024]{1,0:T(2,128)(2,1)S(1)} %slice.322), channel_id=1, source_target_pairs={{0,96},{96,0},{32,64},{64,32},{1,97},{97,1},{33,65},{65,33},{2,98}... | collective-permute-start | bytes 12296 | tf_op jit(solution)/shard_map/ppermute | solution.py:994
  485.6 6.7 %collective-permute-start.21 = (bf16[2,1024]{1,0:T(2,128)(2,1)S(1)}, bf16[2,1024]{1,0:T(2,128)(2,1)S(1)}, u32[]{:S(2)}, u32[]{:S(2)}) collective-permute-start(bf16[2,1024]{1,0:T(2,128)(2,1)S(1)} %slice.321), channel_id=1, source_target_pairs={{0,32},{32,0},{1,33},{33,1},{2,34},{34,2},{3,35},{35,3},{4,36},{36... | collective-permute-start | bytes 12296 | tf_op jit(solution)/shard_map/ppermute | solution.py:50
  (44 other events, 370.1 us)
Sparse Core Ops, SparseCore 0:
  16.4 53.5 all-gather.5
  72.8 69.5 all-gather.7
  151.5 63.8 all-gather.9
  258.8 83.3 reduce-scatter.2
  364.5 110.8 reduce-scatter.4
